TPU v7x, 32 devices: a whole 2x2x4 slice. The times are simulated.
32 devices in a mesh: groups: 2 (over x), cols: 4 (over y, core), rows: 4 (over z).
Axes of the slice: x: 2, y: 2, z: 4, core: 2. Of those that a mesh axis runs over, the one named last changes fastest.
Arguments:
- camera_tokens: bfloat16 [1024, 6144], P(('groups', 'rows'), 'cols'), parts along dimension 0, may hold values from -150 to 150, as said below
- norm_gain: float32 [6144], P('cols'), may hold values from 0.25 to 1.75
- query_weight: bfloat16 [6144, 6144], P('cols', 'rows'), may hold values from -0.078125 to 0.078125
- key_weight: bfloat16 [6144, 6144], P('cols', 'rows'), may hold values from -0.078125 to 0.078125
- value_weight: bfloat16 [6144, 6144], P('cols', 'rows'), may hold values from -0.078125 to 0.078125
- query_gain: float32 [6144], P('rows'), may hold values from 0.5 to 14, as said below
- key_gain: float32 [6144], P('rows'), may hold values from 0.5 to 14, as said below
- out_weight: bfloat16 [6144, 6144], P('rows', 'cols'), may hold values from -0.078125 to 0.078125
- up_weight: bfloat16 [6144, 24576], P('cols', 'rows'), may hold values from -0.078125 to 0.078125
- up_bias: float32 [24576], P('rows'), may hold values from -3 to 3
- down_weight: bfloat16 [24576, 6144], P('rows', 'cols'), may hold values from -0.0390625 to 0.0390625
- down_bias: float32 [6144], P('cols'), may hold values from -3 to 3
- join_gain: float32 [6144], P('cols'), may hold values from 0.25 to 1.75
- join_query: bfloat16 [6144, 6144], P('cols', 'rows'), may hold values from -0.078125 to 0.078125
- join_key: bfloat16 [6144, 6144], P('cols', 'rows'), may hold values from -0.078125 to 0.078125
- join_value: bfloat16 [6144, 6144], P('cols', 'rows'), may hold values from -0.078125 to 0.078125
- join_query_gain: float32 [6144], P('rows'), may hold values from 0.5 to 14, as said below
- join_key_gain: float32 [6144], P('rows'), may hold values from 0.5 to 14, as said below
- join_out: bfloat16 [6144, 6144], P('rows', 'cols'), may hold values from -0.078125 to 0.078125
Outputs:
- joined_tokens: bfloat16 [1024, 6144], P(('groups', 'rows'), 'cols'), parts along dimension 0
There are 2 independent parts, one for each index of `groups`. A program takes and returns all parts, laid end to end along the dimension named above; an argument that names none is the same for every part. Nothing has to cross between parts.
Inputs may be any that keep to these rules, and one draw needn't show every extreme that they name: `camera_tokens`: real valued tokens. `query_gain`: Positive. `key_gain`: Positive. `join_query_gain`: Positive. `join_key_gain`: Positive.
All inputs are finite; a program needn't handle non-finite values.
Results may differ from a plain program's by a relative error of at most 0.012.
Values may be sent and summed in bfloat16 or wider, within the bound.
No kernel may reach another device: no remote copies, remote signals or barrier semaphores. Data moves between devices by JAX's collectives and lax.ppermute only.
A program may use at most 192 MiB of HBM per device.

v0:
```python
import math

import jax
import jax.numpy as jnp
from jax import lax
from jax.sharding import PartitionSpec as P

HEAD_DIM = 128
TOK_CAM = 64
D = 6144


EPS = 1e-06


def partner_2(array, axis, bit):
    return lax.ppermute(array, axis, [(i, i ^ 1 << bit) for i in range(lax.axis_size(axis))])


def normalize(values, scales, moments):
    row_mean = moments[0] / D
    row_var = moments[1] / D - row_mean * row_mean
    return ((values - row_mean[:, None]) * lax.rsqrt(row_var[:, None] + EPS) * scales).astype(
        jnp.bfloat16
    )


def shard_moments(values):
    return lax.psum((jnp.sum(values, 1), jnp.sum(values * values, 1)), "cols")


def head_norm(values, scales):
    row_count = values.shape[0]
    grouped = values.reshape(row_count, -1, HEAD_DIM)
    row_mean = jnp.mean(grouped, -1, keepdims=True)
    row_var = jnp.mean(grouped * grouped, -1, keepdims=True) - row_mean * row_mean
    normed = (grouped - row_mean) * lax.rsqrt(row_var + EPS)
    return (normed.reshape(row_count, -1) * scales).astype(jnp.bfloat16)


def attend(queries, key_rows, val_rows):
    inv_root = 1.0 / math.sqrt(HEAD_DIM)
    scores = (
        jnp.einsum("bqhd,bkhd->bhqk", queries, key_rows, preferred_element_type=jnp.float32)
        * inv_root
    )
    row_max = jnp.max(scores, -1, keepdims=True)
    weights = jnp.exp(scores - row_max)
    row_sum = jnp.sum(weights, -1)
    blended = jnp.einsum(
        "bhqk,bkhd->bqhd",
        weights.astype(jnp.bfloat16),
        val_rows,
        preferred_element_type=jnp.float32,
    )
    return blended / jnp.transpose(row_sum, (0, 2, 1))[..., None]


def to_heads(matrix, blocks):
    return matrix.reshape(blocks, -1, matrix.shape[1] // HEAD_DIM, HEAD_DIM)


def camera_attention(queries, key_rows, val_rows):
    local_rows = queries.shape[0]
    if local_rows >= TOK_CAM:
        blocks = local_rows // TOK_CAM
        result = attend(
            to_heads(queries, blocks), to_heads(key_rows, blocks), to_heads(val_rows, blocks)
        )
    else:
        cam_span = TOK_CAM // local_rows
        position = lax.axis_index("cols")
        key_value = jnp.stack((key_rows, val_rows))
        for which_bit in range(cam_span.bit_length() - 1):
            partner = partner_2(key_value, "cols", which_bit)
            is_lower = position >> which_bit & 1 == 0
            key_value = jnp.where(
                is_lower,
                jnp.concatenate((key_value, partner), 1),
                jnp.concatenate((partner, key_value), 1),
            )
        result = attend(to_heads(queries, 1), to_heads(key_value[0], 1), to_heads(key_value[1], 1))
    return result.reshape(local_rows, -1).astype(jnp.bfloat16)


def body(
    camera_tokens,
    norm_gain,
    query_weight,
    key_weight,
    value_weight,
    query_gain,
    key_gain,
    out_weight,
    up_weight,
    up_bias,
    down_weight,
    down_bias,
    join_gain,
    join_query,
    join_key,
    join_value,
    join_query_gain,
    join_key_gain,
    join_out,
):
    own_rows = camera_tokens.shape[0]
    all_rows = own_rows * lax.axis_size("rows")
    col_rows = all_rows // lax.axis_size("cols")
    attn_width = query_weight.shape[1]
    start_f32 = camera_tokens.astype(jnp.float32)
    normed_all = lax.all_gather(
        normalize(start_f32, norm_gain, shard_moments(start_f32)), "rows", axis=0, tiled=True
    )
    joint_weight = jnp.concatenate((query_weight, key_weight, value_weight, up_weight), 1)
    joint = lax.psum_scatter(
        jnp.dot(normed_all, joint_weight, preferred_element_type=jnp.float32),
        "cols",
        scatter_dimension=0,
        tiled=True,
    )
    up_sum = joint[:, 3 * attn_width :]
    hidden = jax.nn.gelu(up_sum + up_bias, approximate=False).astype(jnp.bfloat16)
    attended = camera_attention(
        head_norm(joint[:, :attn_width], query_gain),
        head_norm(joint[:, attn_width : 2 * attn_width], key_gain),
        joint[:, 2 * attn_width : 3 * attn_width].astype(jnp.bfloat16),
    )
    attn_all, hidden_all = (
        lax.all_gather(attended, "cols", axis=0, tiled=True),
        lax.all_gather(hidden, "cols", axis=0, tiled=True),
    )
    mixed = lax.psum_scatter(
        jnp.dot(attn_all, out_weight, preferred_element_type=jnp.float32)
        + jnp.dot(hidden_all, down_weight, preferred_element_type=jnp.float32),
        "rows",
        scatter_dimension=0,
        tiled=True,
    )
    layer_own = (start_f32 + mixed + down_bias).astype(jnp.bfloat16)
    layer_f32 = layer_own.astype(jnp.float32)
    join_in = lax.all_gather(
        normalize(layer_f32, join_gain, shard_moments(layer_f32)), "rows", axis=0, tiled=True
    )
    join_weight = jnp.concatenate((join_query, join_key, join_value), 1)
    join_joint = lax.psum_scatter(
        jnp.dot(join_in, join_weight, preferred_element_type=jnp.float32),
        "cols",
        scatter_dimension=0,
        tiled=True,
    )
    join_q = head_norm(join_joint[:, :attn_width], join_query_gain)
    join_k = head_norm(join_joint[:, attn_width : 2 * attn_width], join_key_gain)
    join_v = join_joint[:, 2 * attn_width :].astype(jnp.bfloat16)
    heads_here = attn_width // HEAD_DIM
    query_heads = join_q.reshape(col_rows, heads_here, HEAD_DIM)
    inv_root = 1.0 / math.sqrt(HEAD_DIM)
    run_max = jnp.full((heads_here, col_rows), -jnp.inf, jnp.float32)
    run_sum = jnp.zeros((heads_here, col_rows), jnp.float32)
    accum = jnp.zeros((col_rows, heads_here, HEAD_DIM), jnp.float32)
    key_part = lax.all_gather(join_k, "cols", axis=0, tiled=True)
    val_part = lax.all_gather(join_v, "cols", axis=0, tiled=True)
    row_count = key_part.shape[0]
    key_heads = key_part.reshape(row_count, heads_here, HEAD_DIM)
    val_heads = val_part.reshape(row_count, heads_here, HEAD_DIM)
    scores = (
        jnp.einsum("qhd,khd->hqk", query_heads, key_heads, preferred_element_type=jnp.float32)
        * inv_root
    )
    new_max = jnp.max(scores, -1)
    factor = jnp.exp(run_max - new_max)
    weights = jnp.exp(scores - new_max[..., None])
    run_sum = run_sum * factor + jnp.sum(weights, -1)
    accum = accum * jnp.transpose(factor)[..., None] + jnp.einsum(
        "hqk,khd->qhd", weights.astype(jnp.bfloat16), val_heads, preferred_element_type=jnp.float32
    )
    run_max, run_sum, accum = (new_max, run_sum, accum)
    joined_attn = (
        (accum / jnp.transpose(run_sum)[..., None])
        .reshape(col_rows, attn_width)
        .astype(jnp.bfloat16)
    )
    joined_all = lax.all_gather(joined_attn, "cols", axis=0, tiled=True)
    result = lax.psum_scatter(
        jnp.dot(joined_all, join_out, preferred_element_type=jnp.float32),
        "rows",
        scatter_dimension=0,
        tiled=True,
    )
    return (layer_own.astype(jnp.float32) + result).astype(jnp.bfloat16)


def solution(mesh):
    in_specs = (
        P(("groups", "rows"), "cols"),
        P("cols"),
        P("cols", "rows"),
        P("cols", "rows"),
        P("cols", "rows"),
        P("rows"),
        P("rows"),
        P("rows", "cols"),
        P("cols", "rows"),
        P("rows"),
        P("rows", "cols"),
        P("cols"),
        P("cols"),
        P("cols", "rows"),
        P("cols", "rows"),
        P("cols", "rows"),
        P("rows"),
        P("rows"),
        P("rows", "cols"),
    )
    out_specs = P(("groups", "rows"), "cols")
    return jax.shard_map(body, mesh=mesh, in_specs=in_specs, out_specs=out_specs, check_vma=False)
```

profile of v0, /device:TPU:0, one launch (start us, length us, event | category | flops | bytes accessed | tf_op | source)
XLA Modules:
  0.0 699.6 jit_solution(5860410591741534853)
XLA Ops:
  6.5 1.2 convert_reduce_fusion.1
  7.7 8.4 %all-reduce.1 = (f32[128]{0:T(128)S(1)}, f32[128]{0:T(128)S(1)}) all-reduce(f32[128]{0:T(128)S(1)} %get-tuple-element.16, f32[128]{0:T(128)S(1)} %get-tuple-element.15), channel_id=1, replica_groups=mesh['groups'=2,'cols'=4,'rows'=4] {'cols'}, use_global_device_ids=true, to_apply=%region_3.0 | all-reduce | flops 256 | bytes 2048 | tf_op jit(solution)/shard_map/psum | solution.py:29
  16.1 2.0 fusion.46
  18.2 37.5 %all-gather.8.cloned.1.call-done = bf16[512,1536]{1,0:T(8,128)(2,1)} async-done(((bf16[128,1536]{1,0:T(8,128)(2,1)}), bf16[512,1536]{1,0:T(8,128)(2,1)}) %all-gather.8.cloned.1.call-update) | async-done | bytes 1572880 | tf_op jit(solution)/shard_map/all_gather | solution.py:112
  55.7 35.7 %fusion = f32[512,10752]{1,0:T(8,128)} fusion(bf16[512,1536]{1,0:T(8,128)(2,1)} %all-gather.8.cloned.1.call-done, bf16[1536,6144]{1,0:T(8,128)(2,1)} %param.27, bf16[1536,1536]{1,0:T(8,128)(2,1)} %param.23, bf16[1536,1536]{1,0:T(8,128)(2,1)} %param.22, bf16[1536,1536]{1,0:T(8,128)(2,1)} %param.21), kind=kOutput, calls=%fused_computation | convolution fusion | flops 17043554304 | bytes 56623104 | tf_op jit(solution)/shard_map/dot_general | solution.py:117
  91.5 158.9 %reduce-scatter.5.cloned.1.call-done = f32[128,10752]{1,0:T(8,128)} async-done(((f32[512,10752]{1,0:T(8,128)}), f32[128,10752]{1,0:T(8,128)}) %reduce-scatter.5.cloned.1.call-update) | async-done | bytes 5505040 | tf_op jit(solution)/shard_map/reduce_scatter | solution.py:116
  252.6 1.5 fusion.70
  257.1 2.1 multiply_convert_fusion.3
  262.0 8.8 %fusion.16 = bf16[128,6144]{1,0:T(8,128)(2,1)} fusion(f32[128,10752]{1,0:T(8,128)} %reduce-scatter.5.cloned.1.call-done, f32[6144]{0:T(1024)S(1)} %copy-done.3), kind=kLoop, calls=%fused_computation.18 | loop fusion | flops 51904512 | bytes 4743168 | tf_op jit(solution)/shard_map/convert_element_type | solution.py:123
  271.0 10.7 %all-gather.10.cloned.1.call-done = bf16[512,1536]{1,0:T(8,128)(2,1)} async-done(((bf16[128,1536]{1,0:T(8,128)(2,1)}), bf16[512,1536]{1,0:T(8,128)(2,1)}) %all-gather.10.cloned.1.call-update) | async-done | bytes 1572880 | tf_op jit(solution)/shard_map/all_gather | solution.py:130
  281.7 4.9 fusion.73
  286.7 43.0 %all-gather.12.cloned.1.call-done = bf16[512,6144]{1,0:T(8,128)(2,1)} async-done(((bf16[128,6144]{1,0:T(8,128)(2,1)}), bf16[512,6144]{1,0:T(8,128)(2,1)}) %all-gather.12.cloned.1.call-update) | async-done | bytes 6291472 | tf_op jit(solution)/shard_map/all_gather | solution.py:131
  329.7 16.8 %convolution_add_fusion = f32[512,1536]{1,0:T(8,128)} fusion(f32[512,1536]{1,0:T(8,128)S(1)} %fusion.73, bf16[512,6144]{1,0:T(8,128)(2,1)} %all-gather.12.cloned.1.call-done, bf16[6144,1536]{1,0:T(8,128)(2,1)} %param.29), kind=kOutput, calls=%fused_computation.15 | convolution fusion | flops 9664462848 | bytes 31457280 | tf_op jit(solution)/shard_map/dot_general | solution.py:135
  346.6 60.4 %reduce-scatter.7.cloned.1.call-done = f32[128,1536]{1,0:T(8,128)} async-done(((f32[512,1536]{1,0:T(8,128)}), f32[128,1536]{1,0:T(8,128)}) %reduce-scatter.7.cloned.1.call-update) | async-done | bytes 786448 | tf_op jit(solution)/shard_map/reduce_scatter | solution.py:133
  406.9 1.4 convert_reduce_fusion
  408.3 6.4 all-reduce
  415.9 36.8 %all-gather.14.cloned.1.call-done = bf16[512,1536]{1,0:T(8,128)(2,1)} async-done(((bf16[128,1536]{1,0:T(8,128)(2,1)}), bf16[512,1536]{1,0:T(8,128)(2,1)}) %all-gather.14.cloned.1.call-update) | async-done | bytes 1572880 | tf_op jit(solution)/shard_map/all_gather | solution.py:142
  452.6 16.6 %fusion.8 = f32[512,4608]{1,0:T(8,128)} fusion(bf16[512,1536]{1,0:T(8,128)(2,1)} %all-gather.14.cloned.1.call-done, bf16[1536,1536]{1,0:T(8,128)(2,1)} %param.34, bf16[1536,1536]{1,0:T(8,128)(2,1)} %param.33, bf16[1536,1536]{1,0:T(8,128)(2,1)} %param.32), kind=kOutput, calls=%fused_computation.8 | convolution fusion | flops 7290224640 | bytes 25165824 | tf_op jit(solution)/shard_map/dot_general | solution.py:147
  469.3 77.4 %reduce-scatter.9.cloned.1.call-done = f32[128,4608]{1,0:T(8,128)} async-done(((f32[512,4608]{1,0:T(8,128)}), f32[128,4608]{1,0:T(8,128)}) %reduce-scatter.9.cloned.1.call-update) | async-done | bytes 2359312 | tf_op jit(solution)/shard_map/reduce_scatter | solution.py:146
  546.7 1.5 fusion.71
  550.3 1.2 copy.43
  553.9 2.9 multiply_convert_fusion
  558.9 17.7 %all-gather.16.cloned.1.call-done = bf16[512,1536]{1,0:T(8,128)(2,1)} async-done(((bf16[128,1536]{1,0:T(8,128)(2,1)}), bf16[512,1536]{1,0:T(8,128)(2,1)}) %all-gather.16.cloned.1.call-update) | async-done | bytes 1572880 | tf_op jit(solution)/shard_map/all_gather | solution.py:161
  576.7 2.6 copy.45
  579.2 2.2 multiply_reduce_fusion
  583.0 15.0 %all-gather.18.cloned.1.call-done = bf16[512,1536]{1,0:T(8,128)(2,1)} async-done(((bf16[128,1536]{1,0:T(8,128)(2,1)}), bf16[512,1536]{1,0:T(8,128)(2,1)}) %all-gather.18.cloned.1.call-update) | async-done | bytes 1572880 | tf_op jit(solution)/shard_map/all_gather | solution.py:162
  598.0 2.6 copy.48
  600.6 2.9 fusion.41
  603.6 19.9 %all-gather.20.cloned.1.call-done = bf16[512,1536]{0,1:T(8,128)(2,1)} async-done(((bf16[128,1536]{0,1:T(8,128)(2,1)}), bf16[512,1536]{0,1:T(8,128)(2,1)}) %all-gather.20.cloned.1.call-update) | async-done | bytes 1572880 | tf_op jit(solution)/shard_map/all_gather | solution.py:183
  623.6 7.1 %fusion.74 = f32[512,1536]{1,0:T(8,128)} fusion(bf16[512,1536]{0,1:T(8,128)(2,1)} %all-gather.20.cloned.1.call-done, bf16[1536,1536]{1,0:T(8,128)(2,1)} %param.37), kind=kOutput, calls=%fused_computation.112 | convolution fusion | flops 2415919104 | bytes 9437184 | tf_op jit(solution)/shard_map/dot_general | solution.py:185
  630.7 60.4 %reduce-scatter.11.cloned.1.call-done = f32[128,1536]{1,0:T(8,128)} async-done(((f32[512,1536]{1,0:T(8,128)}), f32[128,1536]{1,0:T(8,128)}) %reduce-scatter.11.cloned.1.call-update) | async-done | bytes 786448 | tf_op jit(solution)/shard_map/reduce_scatter | solution.py:184
  691.1 1.9 fusion.54
  (83 shorter events, 17.6 us)
Async XLA Ops:
  6.5 49.2 %all-gather.8.cloned.1.call-start = ((), (), s32[]{:S(2)}) async-start(), calls=%async_computation.4 | async-start | bytes 1966080 | tf_op jit(solution)/shard_map/all_gather | solution.py:112
  18.2 232.2 %reduce-scatter.5.cloned.1.call-start = ((), (), s32[]{:S(2)}) async-start(), calls=%async_computation.5 | async-start | bytes 27525120 | tf_op jit(solution)/shard_map/reduce_scatter | solution.py:116
  91.4 190.3 %all-gather.10.cloned.1.call-start = ((), (), s32[]{:S(2)}) async-start(), calls=%async_computation.6 | async-start | bytes 1966080 | tf_op jit(solution)/shard_map/all_gather | solution.py:130
  255.4 1.7 copy-start.4
  255.4 1.7 copy-start.5
  259.2 1.1 copy-start.2
  260.3 1.7 copy-start.3
  261.9 67.7 %all-gather.12.cloned.1.call-start = ((), (), s32[]{:S(2)}) async-start(), calls=%async_computation.7 | async-start | bytes 7864320 | tf_op jit(solution)/shard_map/all_gather | solution.py:131
  270.8 136.1 %reduce-scatter.7.cloned.1.call-start = ((), (), s32[]{:S(2)}) async-start(), calls=%async_computation.8 | async-start | bytes 3932160 | tf_op jit(solution)/shard_map/reduce_scatter | solution.py:133
  346.5 60.4 %copy-start.1 = (bf16[128,1536]{1,0:T(8,128)(2,1)S(1)}, bf16[128,1536]{1,0:T(8,128)(2,1)}, u32[]{:S(2)}) copy-start(bf16[128,1536]{1,0:T(8,128)(2,1)} %param.19) | copy-start | bytes 1179652
  346.5 60.4 %copy-start.6 = (f32[1536]{0:T(1024)S(1)}, f32[1536]{0:T(1024)}, u32[]{:S(2)}) copy-start(f32[1536]{0:T(1024)} %param.30) | copy-start | bytes 18436
  346.5 68.3 %copy-start.7 = (f32[1536]{0:T(1024)S(1)}, f32[1536]{0:T(1024)}, u32[]{:S(2)}) copy-start(f32[1536]{0:T(1024)} %param.31) | copy-start | bytes 18436
  346.5 106.1 %all-gather.14.cloned.1.call-start = ((), (), s32[]{:S(2)}) async-start(), calls=%async_computation.9 | async-start | bytes 1966080 | tf_op jit(solution)/shard_map/all_gather | solution.py:142
  415.8 130.9 %reduce-scatter.9.cloned.1.call-start = ((), (), s32[]{:S(2)}) async-start(), calls=%async_computation.10 | async-start | bytes 11796480 | tf_op jit(solution)/shard_map/reduce_scatter | solution.py:146
  469.3 107.4 %all-gather.16.cloned.1.call-start = ((), (), s32[]{:S(2)}) async-start(), calls=%async_computation.11 | async-start | bytes 1966080 | tf_op jit(solution)/shard_map/all_gather | solution.py:161
  550.3 3.6 copy-start
  551.5 2.4 copy-start.8
  556.8 41.2 %all-gather.18.cloned.1.call-start = ((), (), s32[]{:S(2)}) async-start(), calls=%async_computation.12 | async-start | bytes 1966080 | tf_op jit(solution)/shard_map/all_gather | solution.py:162
  557.7 65.9 %all-gather.20.cloned.1.call-start = ((), (), s32[]{:S(2)}) async-start(), calls=%async_computation.13 | async-start | bytes 1966080 | tf_op jit(solution)/shard_map/all_gather | solution.py:183
  603.6 87.5 %reduce-scatter.11.cloned.1.call-start = ((), (), s32[]{:S(2)}) async-start(), calls=%async_computation.14 | async-start | bytes 3932160 | tf_op jit(solution)/shard_map/reduce_scatter | solution.py:184
Sparse Core Ops, SparseCore 0:
  18.3 37.3 all-gather.7
  91.5 158.7 reduce-scatter.4
  262.0 19.6 all-gather.9
  283.2 46.3 all-gather.11
  346.7 60.2 reduce-scatter.6
  415.9 36.6 all-gather.13
  469.4 77.2 reduce-scatter.8
  557.0 19.6 all-gather.15
  578.3 19.6 all-gather.17
  603.7 19.8 all-gather.19
  630.8 60.2 reduce-scatter.10
where the time goes:
time: 700 us
  waiting for transfers between devices  538 us (77%)
  matrix products  87.2 us (12%)
  other arithmetic  23.5 us (3%)
  local copies, waits for them, and re-layouts  21.9 us (3%)
  blocking collectives  14.8 us (2%)
  between operations  13.5 us (2%)
    reduce_scatter x1, waiting for transfers between devices, body(): lax.psum_scatter(jnp.dot(normed_all, joint_weight, preferred_element_type...  159 us
    reduce_scatter x1, waiting for transfers between devices, body(): lax.psum_scatter(jnp.dot(join_in, join_weight, preferred_element_type=jnp...  77.4 us
    reduce_scatter x1, waiting for transfers between devices, body(): lax.psum_scatter(jnp.dot(joined_all, join_out, preferred_element_type=jnp...  60.4 us
    reduce_scatter x1, waiting for transfers between devices, body(): lax.psum_scatter(jnp.dot(attn_all, out_weight, preferred_element_type=jnp...  60.4 us
    all_gather x1, waiting for transfers between devices, body(): lax.all_gather(hidden, 'cols', axis=0, tiled=True)  43 us
    all_gather x1, waiting for transfers between devices, body(): lax.all_gather(normalize(start_f32, norm_gain, shard_moments(start_f32)),...  37.5 us
    all_gather x1, waiting for transfers between devices, body(): lax.all_gather(normalize(layer_f32, join_gain, shard_moments(layer_f32)),...  36.8 us
    dot_general x1, matrix products, body(): jnp.dot(normed_all, joint_weight, preferred_element_type=jnp.float32)  35.7 us
  transfers between devices with their start and end apart: 11, of which 11 were waited for; matrix products, arithmetic and copies ran while one was open for 3% of the time, Pallas kernels for 0%

commit v1 on v0

--- a/solution.py
+++ b/solution.py
@@ -3,6 +3,8 @@
 import jax
 import jax.numpy as jnp
 from jax import lax
+from jax.experimental import pallas as pl
+from jax.experimental.pallas import tpu as pltpu
 from jax.sharding import PartitionSpec as P
 
 HEAD_DIM = 128
@@ -83,7 +85,7 @@
     return result.reshape(local_rows, -1).astype(jnp.bfloat16)
 
 
-def body(
+def generic_body(
     camera_tokens,
     norm_gain,
     query_weight,
@@ -190,6 +192,475 @@
     return (layer_own.astype(jnp.float32) + result).astype(jnp.bfloat16)
 
 
+VMEM_BYTES = 48 * 1024 * 1024
+
+
+def flip(array, mask):
+    size = lax.axis_size("cols")
+    return lax.ppermute(array, "cols", [(i, i ^ mask) for i in range(size)])
+
+
+def core_swap(array):
+    return flip(array, 1)
+
+
+def y_swap(array):
+    return flip(array, 2)
+
+
+def row_shift(array, shift):
+    size = lax.axis_size("rows")
+    return lax.ppermute(array, "rows", [(i, (i + shift) % size) for i in range(size)])
+
+
+class Runner:
+    def __init__(self, position):
+        self.position = position
+        self.last = None
+
+    def __call__(self, kernel, grid, operands, in_specs, out_shape, out_spec, flops, scratch=()):
+        in_specs = list(in_specs)
+        operands = list(operands)
+        count = len(operands)
+        if self.last is not None:
+            operands.append(self.last)
+            in_specs.append(pl.BlockSpec(memory_space=pl.ANY))
+        total = len(operands)
+
+        def inner(position_ref, *refs):
+            kernel(position_ref, *refs[:count], *refs[total:])
+
+        self.last = pl.pallas_call(
+            inner,
+            out_shape=out_shape,
+            grid_spec=pltpu.PrefetchScalarGridSpec(
+                num_scalar_prefetch=1,
+                grid=grid,
+                in_specs=in_specs,
+                out_specs=out_spec,
+                scratch_shapes=scratch,
+            ),
+            compiler_params=pltpu.CompilerParams(vmem_limit_bytes=VMEM_BYTES),
+            cost_estimate=pl.CostEstimate(flops=1, bytes_accessed=1, transcendentals=0),
+        )(self.position, *operands)
+        return self.last
+
+
+def whole(array):
+    return pl.BlockSpec(array.shape, lambda s, pos: (0,) * array.ndim)
+
+
+def mine_of(pos):
+    return 2 * pos[0] + pos[1]
+
+
+def across_of(pos):
+    return 2 * pos[0] + 1 - pos[1]
+
+
+def dot_f32(a, b):
+    return jnp.dot(a, b, preferred_element_type=jnp.float32)
+
+
+def project_send(run, tokens, weights, width, sub):
+    rows, depth = tokens.shape
+    block = width // sub
+    wide = len(weights) * block
+
+    def kernel(pos, tokens_ref, *refs):
+        for i in range(len(weights)):
+            refs[-1][:, i * block : (i + 1) * block] = dot_f32(
+                tokens_ref[...], refs[i][...]
+            ).astype(jnp.bfloat16)
+
+    spec = pl.BlockSpec((depth, block), lambda s, pos: (0, 2 * (1 - pos[0]) * sub + s))
+    return run(
+        kernel,
+        (2 * sub,),
+        (tokens, *weights),
+        (whole(tokens), *[spec] * len(weights)),
+        jax.ShapeDtypeStruct((rows, 2 * sub * wide), jnp.bfloat16),
+        pl.BlockSpec((rows, wide), lambda s, pos: (0, s)),
+        rows * depth * 2 * sub * wide,
+    )
+
+
+def project_across(run, tokens, weights, width, sub, arrived):
+    rows, depth = tokens.shape
+    block = width // sub
+    wide = len(weights) * block
+
+    def kernel(pos, tokens_ref, *refs):
+        for i in range(len(weights)):
+            at = slice(i * block, (i + 1) * block)
+            part = dot_f32(tokens_ref[...], refs[i][...])
+            part = part + refs[-2][:, at].astype(jnp.float32)
+            refs[-1][:, at] = part.astype(jnp.bfloat16)
+
+    spec = pl.BlockSpec((depth, block), lambda s, pos: (0, across_of(pos) * sub + s))
+    return run(
+        kernel,
+        (sub,),
+        (tokens, *weights, arrived),
+        (
+            whole(tokens),
+            *[spec] * len(weights),
+            pl.BlockSpec((rows, wide), lambda s, pos: (0, (1 - pos[1]) * sub + s)),
+        ),
+        jax.ShapeDtypeStruct((rows, sub * wide), jnp.bfloat16),
+        pl.BlockSpec((rows, wide), lambda s, pos: (0, s)),
+        rows * depth * sub * wide,
+    )
+
+
+def project_hidden(run, tokens, weight, bias, width, sub, arrived, from_side):
+    rows, depth = tokens.shape
+    block = width // sub
+
+    def kernel(pos, tokens_ref, weight_ref, bias_ref, arrived_ref, side_ref, out_ref):
+        total = dot_f32(tokens_ref[...], weight_ref[...])
+        total = total + arrived_ref[...].astype(jnp.float32) + side_ref[...].astype(jnp.float32)
+        total = total + bias_ref[...]
+        out_ref[...] = (total * (1.0 + lax.erf(total * math.sqrt(0.5))) * 0.5).astype(jnp.bfloat16)
+
+    return run(
+        kernel,
+        (sub,),
+        (tokens, weight, bias, arrived, from_side),
+        (
+            whole(tokens),
+            pl.BlockSpec((depth, block), lambda s, pos: (0, mine_of(pos) * sub + s)),
+            pl.BlockSpec((1, block), lambda s, pos: (0, mine_of(pos) * sub + s)),
+            pl.BlockSpec((rows, block), lambda s, pos: (0, pos[1] * sub + s)),
+            pl.BlockSpec((rows, block), lambda s, pos: (0, s)),
+        ),
+        jax.ShapeDtypeStruct((rows, width), jnp.bfloat16),
+        pl.BlockSpec((rows, block), lambda s, pos: (0, s)),
+        rows * depth * width,
+    )
+
+
+def unit_norm(values, scales):
+    row_mean = jnp.mean(values, -1, keepdims=True)
+    row_var = jnp.mean(values * values, -1, keepdims=True) - row_mean * row_mean
+    return ((values - row_mean) * lax.rsqrt(row_var + EPS) * scales).astype(jnp.bfloat16)
+
+
+def softmax_blend(query, key, value, keep=None):
+    scores = lax.dot_general(
+        query, key, (((1,), (1,)), ((), ())), preferred_element_type=jnp.float32
+    ) * (1.0 / math.sqrt(HEAD_DIM))
+    if keep is not None:
+        scores = jnp.where(keep, scores, -jnp.inf)
+    weights = jnp.exp(scores - jnp.max(scores, -1, keepdims=True))
+    row_sum = jnp.sum(weights, -1, keepdims=True)
+    blended = dot_f32(weights.astype(jnp.bfloat16), value)
+    return (blended / row_sum).astype(jnp.bfloat16)
+
+
+def project_heads(run, tokens, weights, scales, width, arrived, from_side, attend_camera):
+    rows, depth = tokens.shape
+    heads = width // HEAD_DIM
+    out_width = width if attend_camera else 3 * width
+
+    def kernel(pos, tokens_ref, *refs):
+        weight_refs, scale_refs = refs[:3], refs[3:5]
+        arrived_ref, side_ref, out_ref = refs[5:]
+        raws = []
+        for i in range(3):
+            at = slice(i * width, (i + 1) * width)
+            raw = dot_f32(tokens_ref[...], weight_refs[i][...])
+            raw = raw + arrived_ref[:, at].astype(jnp.float32)
+            raws.append(raw + side_ref[:, at].astype(jnp.float32))
+        if attend_camera:
+            row_cam = lax.broadcasted_iota(jnp.int32, (rows, rows), 0) // TOK_CAM
+            col_cam = lax.broadcasted_iota(jnp.int32, (rows, rows), 1) // TOK_CAM
+            same = row_cam == col_cam
+        for h in range(heads):
+            at = slice(h * HEAD_DIM, (h + 1) * HEAD_DIM)
+            query = unit_norm(raws[0][:, at], scale_refs[0][:, at])
+            key = unit_norm(raws[1][:, at], scale_refs[1][:, at])
+            value = raws[2][:, at].astype(jnp.bfloat16)
+            if attend_camera:
+                out_ref[:, at] = softmax_blend(query, key, value, same)
+            else:
+                out_ref[:, at] = query
+                out_ref[:, width + h * HEAD_DIM : width + (h + 1) * HEAD_DIM] = key
+                out_ref[:, 2 * width + h * HEAD_DIM : 2 * width + (h + 1) * HEAD_DIM] = value
+
+    weight_spec = pl.BlockSpec((depth, width), lambda s, pos: (0, mine_of(pos)))
+    scale_spec = pl.BlockSpec((1, width), lambda s, pos: (0, mine_of(pos)))
+    return run(
+        kernel,
+        (1,),
+        (tokens, *weights, *scales, arrived, from_side),
+        (
+            whole(tokens),
+            *[weight_spec] * 3,
+            *[scale_spec] * 2,
+            pl.BlockSpec((rows, 3 * width), lambda s, pos: (0, pos[1])),
+            whole(from_side),
+        ),
+        jax.ShapeDtypeStruct((rows, out_width), jnp.bfloat16),
+        pl.BlockSpec((rows, out_width), lambda s, pos: (0, 0)),
+        3 * rows * depth * width,
+    )
+
+
+def contract(run, parts, weight, sub, first=0, start=None):
+    rows, width = parts[0].shape
+    count = len(parts)
+    out_width = weight.shape[1]
+    block = width // sub
+
+    def kernel(pos, weight_ref, *refs):
+        out_ref = refs[-1]
+        step = pl.program_id(0)
+        for i in range(count):
+
+            @pl.when(step // sub == i)
+            def _(i=i):
+                term = dot_f32(refs[i][...], weight_ref[...])
+                if i > 0:
+                    out_ref[...] += term
+                elif sub == 1:
+                    out_ref[...] = term if start is None else term + refs[count][...]
+                else:
+
+                    @pl.when(step == 0)
+                    def _():
+                        out_ref[...] = term if start is None else term + refs[count][...]
+
+                    @pl.when(step > 0)
+                    def _():
+                        out_ref[...] += term
+
+    def weight_block(s, pos):
+        i = s // sub + first
+        return (2 * (pos[0] ^ (i & 1)) + (pos[1] ^ (i >> 1))) * sub + s % sub, 0
+
+    def part_spec(i):
+        return pl.BlockSpec((rows, block), lambda s, pos: (0, jnp.clip(s - i * sub, 0, sub - 1)))
+
+    operands = [weight, *parts]
+    in_specs = [pl.BlockSpec((block, out_width), weight_block)]
+    in_specs += [part_spec(i) for i in range(count)]
+    if start is not None:
+        operands.append(start)
+        in_specs.append(whole(start))
+    return run(
+        kernel,
+        (count * sub,),
+        operands,
+        in_specs,
+        jax.ShapeDtypeStruct((rows, out_width), jnp.float32),
+        pl.BlockSpec((rows, out_width), lambda s, pos: (0, 0)),
+        rows * width * count * out_width,
+    )
+
+
+def join_blend(run, parts):
+    rows = sum(part.shape[0] for part in parts)
+    heads = parts[0].shape[1] // 3 // HEAD_DIM
+    count = len(parts)
+
+    def kernel(pos, *refs):
+        query, key, value = (
+            jnp.concatenate([ref[...] for ref in refs[i * count : (i + 1) * count]])
+            for i in range(3)
+        )
+        refs[-1][...] = softmax_blend(query, key, value)
+
+    def specs(which):
+        return [
+            pl.BlockSpec((part.shape[0], HEAD_DIM), lambda h, pos: (0, which * heads + h))
+            for part in parts
+        ]
+
+    return run(
+        kernel,
+        (heads,),
+        (*parts, *parts, *parts),
+        (*specs(0), *specs(1), *specs(2)),
+        jax.ShapeDtypeStruct((rows, heads * HEAD_DIM), jnp.bfloat16),
+        pl.BlockSpec((rows, HEAD_DIM), lambda h, pos: (0, h)),
+        2 * rows * rows * heads * HEAD_DIM,
+    )
+
+
+def all_moments(values):
+    pair = jnp.stack((jnp.sum(values, 1), jnp.sum(values * values, 1)))
+    return (pair + flip(pair, 1)) + (flip(pair, 2) + flip(pair, 3))
+
+
+def gather_rows(own):
+    return jnp.concatenate((own, row_shift(own, 1), row_shift(own, -1), row_shift(own, 2)))
+
+
+def scatter_rows(terms):
+    own, before, after, away = jnp.split(terms, 4)
+
+    def send(array, shift):
+        return row_shift(array.astype(jnp.bfloat16), shift).astype(jnp.float32)
+
+    return own + send(after, 1) + send(before, -1) + send(away, 2)
+
+
+def scatter_rows_long(terms):
+    own, before, after, away = jnp.split(terms, 4)
+    half = own.shape[0] // 2
+
+    def send(array, shift):
+        return row_shift(array.astype(jnp.bfloat16), shift).astype(jnp.float32)
+
+    to_after = send(away[:half], 1)
+    to_before = send(away[half:], -1)
+    from_before = jnp.concatenate((send(after[:half] + to_after, 1), send(after[half:], 1)))
+    from_after = jnp.concatenate((send(before[:half], -1), send(before[half:] + to_before, -1)))
+    return own + from_before + from_after
+
+
+def fast_body(
+    camera_tokens,
+    norm_gain,
+    query_weight,
+    key_weight,
+    value_weight,
+    query_gain,
+    key_gain,
+    out_weight,
+    up_weight,
+    up_bias,
+    down_weight,
+    down_bias,
+    join_gain,
+    join_query,
+    join_key,
+    join_value,
+    join_query_gain,
+    join_key_gain,
+    join_out,
+):
+    own_rows = camera_tokens.shape[0]
+    index = lax.axis_index("cols")
+    run = Runner(jnp.stack((index & 1, index >> 1)).astype(jnp.int32))
+    head_width = query_weight.shape[1] // 4
+    unit_width = up_weight.shape[1] // 4
+    sub = 3 if unit_width % (3 * 256) == 0 else 1
+    heads_in = (query_weight, key_weight, value_weight)
+    join_in = (join_query, join_key, join_value)
+    scales = (query_gain[None], key_gain[None])
+    join_scales = (join_query_gain[None], join_key_gain[None])
+    bias = up_bias[None]
+    spans = range(0, own_rows, TOK_CAM)
+    last = len(spans) - 1
+
+    start_f32 = camera_tokens.astype(jnp.float32)
+    normed = normalize(start_f32, norm_gain, all_moments(start_f32))
+    tokens = [gather_rows(normed[at : at + TOK_CAM]) for at in spans]
+
+    def collect(own):
+        own_across = y_swap(own)
+        return own, core_swap(own), own_across, core_swap(own_across)
+
+    def heads_begin(i):
+        sent = core_swap(project_send(run, tokens[i], heads_in, head_width, 1))
+        heads_arrived.append(sent)
+
+    def units_begin(i):
+        sent = core_swap(project_send(run, tokens[i], (up_weight,), unit_width, sub))
+        units_arrived.append(sent)
+
+    def heads_cross(i):
+        heads_side.append(
+            y_swap(project_across(run, tokens[i], heads_in, head_width, 1, heads_arrived[i]))
+        )
+
+    def units_cross(i):
+        units_side.append(
+            y_swap(
+                project_across(run, tokens[i], (up_weight,), unit_width, sub, units_arrived[i])
+            )
+        )
+
+    def heads_end(i):
+        own = project_heads(
+            run, tokens[i], heads_in, scales, head_width, heads_arrived[i], heads_side[i], True
+        )
+        blended.append(collect(own))
+
+    def units_end(i):
+        own = project_hidden(
+            run, tokens[i], up_weight, bias, unit_width, sub, units_arrived[i], units_side[i]
+        )
+        hidden.append(collect(own))
+
+    def out_terms(i):
+        return contract(run, blended[i], out_weight, 1)
+
+    def camera_end(i, mixed):
+        summed = scatter_rows(mixed)
+        rows = slice(spans[i], spans[i] + TOK_CAM)
+        layer = (start_f32[rows] + summed + down_bias).astype(jnp.bfloat16)
+        layers.append(layer)
+        layer_f32 = layer.astype(jnp.float32)
+        join_tokens.append(gather_rows(normalize(layer_f32, join_gain, all_moments(layer_f32))))
+
+    def join_begin(i):
+        arrived = core_swap(project_send(run, join_tokens[i], join_in, head_width, 1))
+        side = y_swap(project_across(run, join_tokens[i], join_in, head_width, 1, arrived))
+        join_sums.append((arrived, side))
+
+    def join_end(i):
+        join_parts.append(
+            project_heads(
+                run, join_tokens[i], join_in, join_scales, head_width, *join_sums[i], False
+            )
+        )
+
+    heads_arrived, units_arrived, heads_side, units_side = [], [], [], []
+    blended, hidden, layers, join_tokens, join_sums, join_parts = [], [], [], [], [], []
+    for i in range(len(spans)):
+        heads_begin(i)
+        units_begin(i)
+        heads_cross(i)
+        if i > 0:
+            heads_end(i - 1)
+        units_cross(i)
+        if i > 0:
+            units_end(i - 1)
+    heads_end(last)
+    for i in range(last):
+        mixed = contract(run, hidden[i], down_weight, 2, 0, out_terms(i))
+        if i == last - 1:
+            units_end(last)
+        camera_end(i, mixed)
+    if last == 0:
+        units_end(last)
+    mixed = contract(run, hidden[last][:2], down_weight, 2, 0, out_terms(last))
+    mixed = contract(run, hidden[last][2:], down_weight, 2, 2, mixed)
+    camera_end(last, mixed)
+    for i in range(len(spans)):
+        join_begin(i)
+        if i > 0:
+            join_end(i - 1)
+    join_end(last)
+
+    joined = join_blend(run, join_parts)
+    joined = joined.reshape(len(spans), 4, TOK_CAM, head_width).swapaxes(0, 1)
+    joined = joined.reshape(4 * own_rows, head_width)
+    summed = scatter_rows_long(contract(run, collect(joined), join_out, 1))
+    layer_own = jnp.concatenate(layers)
+    return (layer_own.astype(jnp.float32) + summed).astype(jnp.bfloat16)
+
+
+def layer(*arrays):
+    own_rows, heads_width = arrays[0].shape[0], arrays[2].shape[1]
+    fits = lax.axis_size("cols") == 4 and lax.axis_size("rows") == 4
+    fits = fits and own_rows % TOK_CAM == 0 and heads_width % (4 * HEAD_DIM) == 0
+    return (fast_body if fits else generic_body)(*arrays)
+
+
 def solution(mesh):
     in_specs = (
         P(("groups", "rows"), "cols"),
@@ -213,4 +684,4 @@
         P("rows", "cols"),
     )
     out_specs = P(("groups", "rows"), "cols")
-    return jax.shard_map(body, mesh=mesh, in_specs=in_specs, out_specs=out_specs, check_vma=False)
+    return jax.shard_map(layer, mesh=mesh, in_specs=in_specs, out_specs=out_specs, check_vma=False)

time: 700 us -> 433 us (0.62)
  waiting for transfers between devices: 538 us -> 229 us
  Pallas kernels: 0 us -> 135 us
  matrix products: 87.2 us -> 0 us
  starting transfers between devices: 0.82 us -> 56.6 us
  local copies, waits for them, and re-layouts: 21.9 us -> 1.44 us
  other arithmetic: 23.5 us -> 4.93 us
  blocking collectives: 14.8 us -> 0 us
  between operations: 13.5 us -> 1.11 us
    reduce_scatter x4 -> x0, waiting for transfers between devices: 357 us -> none  [the longest x1 159 us: body(): lax.psum_scatter(jnp.dot(normed_all, joint_weight, preferred_element_type...]
    ppermute x0 -> x60, waiting for transfers between devices: none -> 229 us  [the longest x36 133 us: flip(): return lax.ppermute(array, 'cols', [(i, i ^ mask) for i in range(size)])]
    all_gather x7 -> x0, waiting for transfers between devices: 181 us -> none  [the longest x1 43 us: body(): lax.all_gather(hidden, 'cols', axis=0, tiled=True)]
    pallas_call x0 -> x25, Pallas kernels: none -> 135 us  [__call__(): pl.pallas_call(inner, out_shape=out_shape, grid_spec=pltpu.PrefetchScalar...]
    dot_general x9 -> x0, matrix products: 87.2 us -> none  [the longest x1 35.7 us: body(): jnp.dot(normed_all, joint_weight, preferred_element_type=jnp.float32)]
    ppermute x0 -> x60, starting transfers between devices: none -> 56.6 us  [the longest x24 35.8 us: row_shift(): lax.ppermute(array, 'rows', [(i, (i + shift) % size) for i in range(size)])]
    psum x2 -> x0, blocking collectives: 14.8 us -> none  [shard_moments(): return lax.psum((jnp.sum(values, 1), jnp.sum(values * values, 1)), 'cols')]
    convert_element_type x4 -> x3, other arithmetic: 15.8 us -> 1.06 us  [the longest x1 0.92 us: fast_body(): return (layer_own.astype(jnp.float32) + summed).astype(jnp.bfloat16)]
  transfers between devices with their start and end apart: 11 -> 60, of which waited for: 11 -> 34; matrix products, arithmetic and copies ran while one was open for 3% -> 0% of each run, Pallas kernels for 0% -> 16%
where the time goes in v1:
time: 433 us; the launch traced here: 428 us
  waiting for transfers between devices  229 us (53%)
  Pallas kernels  135 us (31%)
  starting transfers between devices  56.6 us (13%)
  other arithmetic  4.93 us (1%)
    pallas_call x25, Pallas kernels, __call__(): pl.pallas_call(inner, out_shape=out_shape, grid_spec=pltpu.PrefetchScalar...  135 us
    ppermute x36, waiting for transfers between devices, flip(): return lax.ppermute(array, 'cols', [(i, i ^ mask) for i in range(size)])  133 us
    ppermute x24, waiting for transfers between devices, row_shift(): lax.ppermute(array, 'rows', [(i, (i + shift) % size) for i in range(size)])  95.9 us
    ppermute x24, starting transfers between devices, row_shift(): lax.ppermute(array, 'rows', [(i, (i + shift) % size) for i in range(size)])  35.8 us
    ppermute x36, starting transfers between devices, flip(): return lax.ppermute(array, 'cols', [(i, i ^ mask) for i in range(size)])  20.8 us
  transfers between devices with their start and end apart: 60, of which 34 were waited for; matrix products, arithmetic and copies ran while one was open for 0% of the time, Pallas kernels for 16%

profile of v1, /device:TPU:0, one launch (start us, length us, event | category | flops | bytes accessed | tf_op | source)
XLA Modules:
  0.0 428.4 jit_solution(3671528389970178898)
XLA Ops:
  13.4 4.9 %collective-permute-done.3 = bf16[64,1536]{1,0:T(8,128)(2,1)S(1)} collective-permute-done((bf16[64,1536]{1,0:T(8,128)(2,1)S(1)}, bf16[64,1536]{1,0:T(8,128)(2,1)S(1)}, u32[]{:S(2)}, u32[]{:S(2)}) %collective-permute-start.3) | collective-permute-done | bytes 196640 | tf_op jit(solution)/shard_map/ppermute | solution.py:213
  21.2 9.0 %collective-permute-done.5 = bf16[64,1536]{1,0:T(8,128)(2,1)S(1)} collective-permute-done((bf16[64,1536]{1,0:T(8,128)(2,1)S(1)}, bf16[64,1536]{1,0:T(8,128)(2,1)S(1)}, u32[]{:S(2)}, u32[]{:S(2)}) %collective-permute-start.5) | collective-permute-done | bytes 196640 | tf_op jit(solution)/shard_map/ppermute | solution.py:213
  30.2 5.5 %shard_map.181.refs_2_ = bf16[256,2304]{1,0:T(8,128)(2,1)S(1)} custom-call(s32[2]{0:T(128)S(1)} %pad_add_fusion.position_ref, bf16[256,1536]{1,0:T(8,128)(2,1)S(1)} %pad_maximum_fusion.refs_0_, bf16[1536,1536]{1,0:T(8,128)(2,1)} %refs_1_.28, bf16[1536,1536]{1,0:T(8,128)(2,1)} %refs_2_.17, bf16[1536,1536]{1,0:T(8,128)(2,1)} %refs_3_.17), custom_call_target="tpu_custom_call" | custom-call | flops 1 | bytes 1 | tf_op jit(solution)/shard_map/pallas_call | solution.py:233
  35.8 7.4 %shard_map.182.refs_5_ = bf16[256,3072]{1,0:T(8,128)(2,1)S(1)} custom-call(s32[2]{0:T(128)S(1)} %pad_add_fusion.position_ref, bf16[256,1536]{1,0:T(8,128)(2,1)S(1)} %pad_maximum_fusion.refs_0_, bf16[1536,6144]{1,0:T(8,128)(2,1)} %refs_1_.29, bf16[256,2304]{1,0:T(8,128)(2,1)S(1)} %shard_map.181.refs_2_), custom_call_target="tpu_custom_call" | custom-call | flops 1 | bytes 1 | tf_op jit(solution)/shard_map/pallas_call | solution.py:233
  45.9 6.3 %collective-permute-done.10 = bf16[64,1536]{1,0:T(8,128)(2,1)S(1)} collective-permute-done((bf16[64,1536]{1,0:T(8,128)(2,1)S(1)}, bf16[64,1536]{1,0:T(8,128)(2,1)S(1)}, u32[]{:S(2)}, u32[]{:S(2)}) %collective-permute-start.10) | collective-permute-done | bytes 196640 | tf_op jit(solution)/shard_map/ppermute | solution.py:213
  52.3 9.3 %collective-permute-done.11 = bf16[64,1536]{1,0:T(8,128)(2,1)S(1)} collective-permute-done((bf16[64,1536]{1,0:T(8,128)(2,1)S(1)}, bf16[64,1536]{1,0:T(8,128)(2,1)S(1)}, u32[]{:S(2)}, u32[]{:S(2)}) %collective-permute-start.11) | collective-permute-done | bytes 196640 | tf_op jit(solution)/shard_map/ppermute | solution.py:213
  70.4 5.5 %shard_map.185.refs_2_ = bf16[256,2304]{1,0:T(8,128)(2,1)S(1)} custom-call(s32[2]{0:T(128)S(1)} %pad_add_fusion.position_ref, bf16[256,1536]{1,0:T(8,128)(2,1)S(1)} %pad_maximum_fusion.1.refs_0_, bf16[1536,1536]{1,0:T(8,128)(2,1)} %refs_1_.28, bf16[1536,1536]{1,0:T(8,128)(2,1)} %refs_2_.17, bf16[1536,1536]{1,0:T(8,128)(2,1)} %refs_3_.17, ...), custom_call_target="tpu_custom_call" | custom-call | flops 1 | bytes 1 | tf_op jit(solution)/shard_map/pallas_call | solution.py:233
  76.0 7.4 %shard_map.186.refs_5_ = bf16[256,3072]{1,0:T(8,128)(2,1)S(1)} custom-call(s32[2]{0:T(128)S(1)} %pad_add_fusion.position_ref, bf16[256,1536]{1,0:T(8,128)(2,1)S(1)} %pad_maximum_fusion.1.refs_0_, bf16[1536,6144]{1,0:T(8,128)(2,1)} %refs_1_.29, bf16[256,2304]{1,0:T(8,128)(2,1)S(1)} %shard_map.185.refs_2_), custom_call_target="tpu_custom_call" | custom-call | flops 1 | bytes 1 | tf_op jit(solution)/shard_map/pallas_call | solution.py:233
  92.5 23.6 %collective-permute-done.13.refs_7_ = bf16[256,1152]{1,0:T(8,128)(2,1)S(1)} collective-permute-done((bf16[256,1152]{1,0:T(8,128)(2,1)S(1)}, bf16[256,1152]{1,0:T(8,128)(2,1)S(1)}, u32[]{:S(2)}, u32[]{:S(2)}) %collective-permute-start.13) | collective-permute-done | bytes 589856 | tf_op jit(solution)/shard_map/ppermute | solution.py:200
  125.2 4.8 %shard_map.190.refs_8_.refs_1_ = bf16[256,1536]{1,0:T(8,128)(2,1)S(1)} custom-call(s32[2]{0:T(128)S(1)} %pad_add_fusion.position_ref, bf16[256,1536]{1,0:T(8,128)(2,1)S(1)} %pad_maximum_fusion.refs_0_, bf16[1536,6144]{1,0:T(8,128)(2,1)} %refs_1_.29, f32[1,6144]{1,0:T(1,128)S(1)} %bitcast.47, bf16[256,3072]{1,0:T(8,128)(2,1)S(1)} %collective-permute-done.6.refs_2_.refs_3_, ...), custom_call_target="tpu_custom_call" | custom-call | flops 1 | bytes 1 | tf_op jit(solution)/shard_map/pallas_call | solution.py:233
  132.1 18.4 %collective-permute-done.16.refs_3_ = bf16[256,1536]{1,0:T(8,128)(2,1)S(1)} collective-permute-done((bf16[256,1536]{1,0:T(8,128)(2,1)S(1)}, bf16[256,1536]{1,0:T(8,128)(2,1)S(1)}, u32[]{:S(2)}, u32[]{:S(2)}) %collective-permute-start.16) | collective-permute-done | bytes 786464 | tf_op jit(solution)/shard_map/ppermute | solution.py:200
  152.6 29.9 %collective-permute-done.19.refs_3_ = bf16[256,384]{1,0:T(8,128)(2,1)S(1)} collective-permute-done((bf16[256,384]{1,0:T(8,128)(2,1)S(1)}, bf16[256,384]{1,0:T(8,128)(2,1)S(1)}, u32[]{:S(2)}, u32[]{:S(2)}) %collective-permute-start.19) | collective-permute-done | bytes 196640 | tf_op jit(solution)/shard_map/ppermute | solution.py:200
  187.4 5.0 %shard_map.192.refs_5_.refs_6_ = f32[256,1536]{1,0:T(8,128)S(1)} custom-call(s32[2]{0:T(128)S(1)} %pad_add_fusion.position_ref, bf16[1536,1536]{1,0:T(8,128)(2,1)} %refs_0_.8, bf16[256,384]{1,0:T(8,128)(2,1)S(1)} %shard_map.188.refs_3_.refs_1_, bf16[256,384]{1,0:T(8,128)(2,1)S(1)} %collective-permute-done.18.refs_2_, ...), custom_call_target="tpu_custom_call" | custom-call | flops 1 | bytes 1 | tf_op jit(solution)/shard_map/pallas_call | solution.py:233
  193.6 13.0 %shard_map.193.refs_5_ = f32[256,1536]{1,0:T(8,128)S(1)} custom-call(s32[2]{0:T(128)S(1)} %pad_add_fusion.position_ref, bf16[6144,1536]{1,0:T(8,128)(2,1)} %refs_0_.10, bf16[256,1536]{1,0:T(8,128)(2,1)S(1)} %shard_map.190.refs_8_.refs_1_, bf16[256,1536]{1,0:T(8,128)(2,1)S(1)} %collective-permute-done.15.refs_2_, ...), custom_call_target="tpu_custom_call" | custom-call | flops 1 | bytes 1 | tf_op jit(solution)/shard_map/pallas_call | solution.py:233
  212.1 18.9 %collective-permute-done.26.refs_1_ = bf16[256,1536]{1,0:T(8,128)(2,1)S(1)} collective-permute-done((bf16[256,1536]{1,0:T(8,128)(2,1)S(1)}, bf16[256,1536]{1,0:T(8,128)(2,1)S(1)}, u32[]{:S(2)}, u32[]{:S(2)}) %collective-permute-start.26) | collective-permute-done | bytes 786464 | tf_op jit(solution)/shard_map/ppermute | solution.py:200
  231.8 6.6 %collective-permute-done.30.refs_3_ = bf16[256,384]{1,0:T(8,128)(2,1)S(1)} collective-permute-done((bf16[256,384]{1,0:T(8,128)(2,1)S(1)}, bf16[256,384]{1,0:T(8,128)(2,1)S(1)}, u32[]{:S(2)}, u32[]{:S(2)}) %collective-permute-start.30) | collective-permute-done | bytes 196640 | tf_op jit(solution)/shard_map/ppermute | solution.py:200
  244.0 5.0 %shard_map.195.refs_3_.refs_4_ = f32[256,1536]{1,0:T(8,128)S(1)} custom-call(s32[2]{0:T(128)S(1)} %pad_add_fusion.position_ref, bf16[1536,1536]{1,0:T(8,128)(2,1)} %refs_0_.8, bf16[256,384]{1,0:T(8,128)(2,1)S(1)} %shard_map.191.refs_5_.refs_1_, bf16[256,384]{1,0:T(8,128)(2,1)S(1)} %collective-permute-done.29.refs_2_, ...), custom_call_target="tpu_custom_call" | custom-call | flops 1 | bytes 1 | tf_op jit(solution)/shard_map/pallas_call | solution.py:233
  249.0 7.0 %shard_map.196.refs_3_.refs_4_ = f32[256,1536]{1,0:T(8,128)S(1)} custom-call(s32[2]{0:T(128)S(1)} %pad_add_fusion.position_ref, bf16[6144,1536]{1,0:T(8,128)(2,1)} %refs_0_.10, bf16[256,1536]{1,0:T(8,128)(2,1)S(1)} %shard_map.194.refs_5_.refs_1_, bf16[256,1536]{1,0:T(8,128)(2,1)S(1)} %collective-permute-done.28.refs_2_, ...), custom_call_target="tpu_custom_call" | custom-call | flops 1 | bytes 1 | tf_op jit(solution)/shard_map/pallas_call | solution.py:233
  256.0 7.0 %shard_map.197.refs_4_ = f32[256,1536]{1,0:T(8,128)S(1)} custom-call(s32[2]{0:T(128)S(1)} %pad_add_fusion.position_ref, bf16[6144,1536]{1,0:T(8,128)(2,1)} %refs_0_.10, bf16[256,1536]{1,0:T(8,128)(2,1)S(1)} %collective-permute-done.26.refs_1_, bf16[256,1536]{1,0:T(8,128)(2,1)S(1)} %collective-permute-done.27.refs_2_, ...), custom_call_target="tpu_custom_call" | custom-call | flops 1 | bytes 1 | tf_op jit(solution)/shard_map/pallas_call | solution.py:233
  267.1 5.7 %collective-permute-done.32 = bf16[64,1536]{1,0:T(8,128)(2,1)S(1)} collective-permute-done((bf16[64,1536]{1,0:T(8,128)(2,1)S(1)}, bf16[64,1536]{1,0:T(8,128)(2,1)S(1)}, u32[]{:S(2)}, u32[]{:S(2)}) %collective-permute-start.32) | collective-permute-done | bytes 196640 | tf_op jit(solution)/shard_map/ppermute | solution.py:213
  274.0 9.4 %collective-permute-done.34 = bf16[64,1536]{1,0:T(8,128)(2,1)S(1)} collective-permute-done((bf16[64,1536]{1,0:T(8,128)(2,1)S(1)}, bf16[64,1536]{1,0:T(8,128)(2,1)S(1)}, u32[]{:S(2)}, u32[]{:S(2)}) %collective-permute-start.34) | collective-permute-done | bytes 196640 | tf_op jit(solution)/shard_map/ppermute | solution.py:213
  293.9 5.8 %collective-permute-done.38 = bf16[64,1536]{1,0:T(8,128)(2,1)S(1)} collective-permute-done((bf16[64,1536]{1,0:T(8,128)(2,1)S(1)}, bf16[64,1536]{1,0:T(8,128)(2,1)S(1)}, u32[]{:S(2)}, u32[]{:S(2)}) %collective-permute-start.38) | collective-permute-done | bytes 196640 | tf_op jit(solution)/shard_map/ppermute | solution.py:213
  302.9 6.4 %collective-permute-done.40 = bf16[64,1536]{1,0:T(8,128)(2,1)S(1)} collective-permute-done((bf16[64,1536]{1,0:T(8,128)(2,1)S(1)}, bf16[64,1536]{1,0:T(8,128)(2,1)S(1)}, u32[]{:S(2)}, u32[]{:S(2)}) %collective-permute-start.40) | collective-permute-done | bytes 196640 | tf_op jit(solution)/shard_map/ppermute | solution.py:213
  309.4 5.5 %shard_map.198.refs_5_ = bf16[256,2304]{1,0:T(8,128)(2,1)S(1)} custom-call(s32[2]{0:T(128)S(1)} %pad_add_fusion.position_ref, bf16[256,1536]{1,0:T(8,128)(2,1)S(1)} %pad_maximum_fusion.2.refs_0_, bf16[1536,1536]{1,0:T(8,128)(2,1)} %refs_1_.35, bf16[1536,1536]{1,0:T(8,128)(2,1)} %refs_2_.23, bf16[1536,1536]{1,0:T(8,128)(2,1)} %refs_3_.23, ...), custom_call_target="tpu_custom_call" | custom-call | flops 1 | bytes 1 | tf_op jit(solution)/shard_map/pallas_call | solution.py:233
  319.1 5.5 %collective-permute-done.46 = bf16[64,1536]{1,0:T(8,128)(2,1)S(1)} collective-permute-done((bf16[64,1536]{1,0:T(8,128)(2,1)S(1)}, bf16[64,1536]{1,0:T(8,128)(2,1)S(1)}, u32[]{:S(2)}, u32[]{:S(2)}) %collective-permute-start.46) | collective-permute-done | bytes 196640 | tf_op jit(solution)/shard_map/ppermute | solution.py:213
  329.1 5.4 %collective-permute-done.48 = bf16[64,1536]{1,0:T(8,128)(2,1)S(1)} collective-permute-done((bf16[64,1536]{1,0:T(8,128)(2,1)S(1)}, bf16[64,1536]{1,0:T(8,128)(2,1)S(1)}, u32[]{:S(2)}, u32[]{:S(2)}) %collective-permute-start.48) | collective-permute-done | bytes 196640 | tf_op jit(solution)/shard_map/ppermute | solution.py:213
  338.6 5.5 %shard_map.200.refs_5_ = bf16[256,2304]{1,0:T(8,128)(2,1)S(1)} custom-call(s32[2]{0:T(128)S(1)} %pad_add_fusion.position_ref, bf16[256,1536]{1,0:T(8,128)(2,1)S(1)} %pad_maximum_fusion.3.refs_0_, bf16[1536,1536]{1,0:T(8,128)(2,1)} %refs_1_.35, bf16[1536,1536]{1,0:T(8,128)(2,1)} %refs_2_.23, bf16[1536,1536]{1,0:T(8,128)(2,1)} %refs_3_.23, ...), custom_call_target="tpu_custom_call" | custom-call | flops 1 | bytes 1 | tf_op jit(solution)/shard_map/pallas_call | solution.py:233
  352.6 7.8 %collective-permute-done.42.refs_7_ = bf16[256,1152]{1,0:T(8,128)(2,1)S(1)} collective-permute-done((bf16[256,1152]{1,0:T(8,128)(2,1)S(1)}, bf16[256,1152]{1,0:T(8,128)(2,1)S(1)}, u32[]{:S(2)}, u32[]{:S(2)}) %collective-permute-start.42) | collective-permute-done | bytes 589856 | tf_op jit(solution)/shard_map/ppermute | solution.py:200
  364.5 8.1 %collective-permute-done.50.refs_7_ = bf16[256,1152]{1,0:T(8,128)(2,1)S(1)} collective-permute-done((bf16[256,1152]{1,0:T(8,128)(2,1)S(1)}, bf16[256,1152]{1,0:T(8,128)(2,1)S(1)}, u32[]{:S(2)}, u32[]{:S(2)}) %collective-permute-start.50) | collective-permute-done | bytes 589856 | tf_op jit(solution)/shard_map/ppermute | solution.py:200
  381.6 9.2 %collective-permute-done.52.refs_3_ = bf16[512,384]{1,0:T(8,128)(2,1)S(1)} collective-permute-done((bf16[512,384]{1,0:T(8,128)(2,1)S(1)}, bf16[512,384]{1,0:T(8,128)(2,1)S(1)}, u32[]{:S(2)}, u32[]{:S(2)}) %collective-permute-start.52) | collective-permute-done | bytes 393248 | tf_op jit(solution)/shard_map/ppermute | solution.py:200
  392.5 6.2 %shard_map.205 = f32[512,1536]{1,0:T(8,128)S(1)} custom-call(s32[2]{0:T(128)S(1)} %pad_add_fusion.position_ref, bf16[1536,1536]{1,0:T(8,128)(2,1)} %refs_0_.11, bf16[512,384]{1,0:T(8,128)(2,1)S(1)} %bitcast.46, bf16[512,384]{1,0:T(8,128)(2,1)S(1)} %collective-permute-done.51.refs_2_, bf16[512,384]{1,0:T(8,128)(2,1)S(1)} %collective-permute-done.52.refs_3_, ...), custom_call_target="tpu_custom_call" | custom-call | flops 1 | bytes 1 | tf_op jit(solution)/shard_map/pallas_call | solution.py:233
  419.5 6.1 %collective-permute-done.55 = bf16[64,1536]{1,0:T(8,128)(2,1)S(1)} collective-permute-done((bf16[64,1536]{1,0:T(8,128)(2,1)S(1)}, bf16[64,1536]{1,0:T(8,128)(2,1)S(1)}, u32[]{:S(2)}, u32[]{:S(2)}) %collective-permute-start.55) | collective-permute-done | bytes 196640 | tf_op jit(solution)/shard_map/ppermute | solution.py:213
  (167 shorter events, 146.1 us)
Async XLA Ops:
  12.5 17.6 %collective-permute-start.5 = (bf16[64,1536]{1,0:T(8,128)(2,1)S(1)}, bf16[64,1536]{1,0:T(8,128)(2,1)S(1)}, u32[]{:S(2)}, u32[]{:S(2)}) collective-permute-start(bf16[64,1536]{1,0:T(8,128)(2,1)S(1)} %get-tuple-element.29), channel_id=1, source_target_pairs={{0,2},{1,3},{2,0},{3,1},{4,6},{5,7},{6,4},{7,5},{8,10},{9,11},{10,... | collective-permute-start | bytes 589832 | tf_op jit(solution)/shard_map/ppermute | solution.py:213
  43.2 22.4 %collective-permute-start.6 = (bf16[256,3072]{1,0:T(8,128)(2,1)S(1)}, bf16[256,3072]{1,0:T(8,128)(2,1)S(1)}, u32[]{:S(2)}, u32[]{:S(2)}) collective-permute-start(bf16[256,3072]{1,0:T(8,128)(2,1)S(1)} %shard_map.182.refs_5_), channel_id=1, source_target_pairs={{0,4},{4,0},{8,12},{12,8},{1,5},{5,1},{9,13},{13,9},{2,6},{6,2},{1... | collective-permute-start | bytes 4718600 | tf_op jit(solution)/shard_map/ppermute | solution.py:200
  43.3 18.3 %collective-permute-start.7 = (bf16[256,2304]{1,0:T(8,128)(2,1)S(1)}, bf16[256,2304]{1,0:T(8,128)(2,1)S(1)}, u32[]{:S(2)}, u32[]{:S(2)}) collective-permute-start(bf16[256,2304]{1,0:T(8,128)(2,1)S(1)} %shard_map.181.refs_2_), channel_id=1, source_target_pairs={{0,4},{4,0},{8,12},{12,8},{1,5},{5,1},{9,13},{13,9},{2,6},{6,2},{1... | collective-permute-start | bytes 3538952 | tf_op jit(solution)/shard_map/ppermute | solution.py:200
  45.4 16.2 %collective-permute-start.11 = (bf16[64,1536]{1,0:T(8,128)(2,1)S(1)}, bf16[64,1536]{1,0:T(8,128)(2,1)S(1)}, u32[]{:S(2)}, u32[]{:S(2)}) collective-permute-start(bf16[64,1536]{1,0:T(8,128)(2,1)S(1)} %get-tuple-element.28), channel_id=1, source_target_pairs={{0,2},{1,3},{2,0},{3,1},{4,6},{5,7},{6,4},{7,5},{8,10},{9,11},{10,... | collective-permute-start | bytes 589832 | tf_op jit(solution)/shard_map/ppermute | solution.py:213
  45.4 16.2 %collective-permute-start.9 = (bf16[64,1536]{1,0:T(8,128)(2,1)S(1)}, bf16[64,1536]{1,0:T(8,128)(2,1)S(1)}, u32[]{:S(2)}, u32[]{:S(2)}) collective-permute-start(bf16[64,1536]{1,0:T(8,128)(2,1)S(1)} %get-tuple-element.28), channel_id=1, source_target_pairs={{0,1},{1,2},{2,3},{3,0},{4,5},{5,6},{6,7},{7,4},{8,9},{9,10},{10,1... | collective-permute-start | bytes 589832 | tf_op jit(solution)/shard_map/ppermute | solution.py:213
  83.3 37.2 %collective-permute-start.12 = (bf16[256,3072]{1,0:T(8,128)(2,1)S(1)}, bf16[256,3072]{1,0:T(8,128)(2,1)S(1)}, u32[]{:S(2)}, u32[]{:S(2)}) collective-permute-start(bf16[256,3072]{1,0:T(8,128)(2,1)S(1)} %shard_map.186.refs_5_), channel_id=1, source_target_pairs={{0,4},{4,0},{8,12},{12,8},{1,5},{5,1},{9,13},{13,9},{2,6},{6,2},{1... | collective-permute-start | bytes 4718600 | tf_op jit(solution)/shard_map/ppermute | solution.py:200
  83.9 41.2 %collective-permute-start.8 = (bf16[256,1536]{1,0:T(8,128)(2,1)S(1)}, bf16[256,1536]{1,0:T(8,128)(2,1)S(1)}, u32[]{:S(2)}, u32[]{:S(2)}) collective-permute-start(bf16[256,1536]{1,0:T(8,128)(2,1)S(1)} %shard_map.184.refs_4_), channel_id=1, source_target_pairs={{0,8},{4,12},{8,0},{12,4},{1,9},{5,13},{9,1},{13,5},{2,10},{6,14},... | collective-permute-start | bytes 2359304 | tf_op jit(solution)/shard_map/ppermute | solution.py:200
  84.4 31.6 %collective-permute-start.13 = (bf16[256,1152]{1,0:T(8,128)(2,1)S(1)}, bf16[256,1152]{1,0:T(8,128)(2,1)S(1)}, u32[]{:S(2)}, u32[]{:S(2)}) collective-permute-start(bf16[256,1152]{1,0:T(8,128)(2,1)S(1)} %shard_map.183.refs_3_), channel_id=1, source_target_pairs={{0,8},{4,12},{8,0},{12,4},{1,9},{5,13},{9,1},{13,5},{2,10},{6,14},... | collective-permute-start | bytes 1769480 | tf_op jit(solution)/shard_map/ppermute | solution.py:200
  130.0 20.5 %collective-permute-start.16 = (bf16[256,1536]{1,0:T(8,128)(2,1)S(1)}, bf16[256,1536]{1,0:T(8,128)(2,1)S(1)}, u32[]{:S(2)}, u32[]{:S(2)}) collective-permute-start(bf16[256,1536]{1,0:T(8,128)(2,1)S(1)} %shard_map.190.refs_8_.refs_1_), channel_id=1, source_target_pairs={{0,8},{4,12},{8,0},{12,4},{1,9},{5,13},{9,1},{13,5},{2,10},{6,14},... | collective-permute-start | bytes 2359304 | tf_op jit(solution)/shard_map/ppermute | solution.py:200
  130.6 51.9 %collective-permute-start.21 = (bf16[256,1152]{1,0:T(8,128)(2,1)S(1)}, bf16[256,1152]{1,0:T(8,128)(2,1)S(1)}, u32[]{:S(2)}, u32[]{:S(2)}) collective-permute-start(bf16[256,1152]{1,0:T(8,128)(2,1)S(1)} %shard_map.187.refs_8_), channel_id=1, source_target_pairs={{0,8},{4,12},{8,0},{12,4},{1,9},{5,13},{9,1},{13,5},{2,10},{6,14},... | collective-permute-start | bytes 1769480 | tf_op jit(solution)/shard_map/ppermute | solution.py:200
  132.1 61.5 %collective-permute-start.15 = (bf16[256,1536]{1,0:T(8,128)(2,1)S(1)}, bf16[256,1536]{1,0:T(8,128)(2,1)S(1)}, u32[]{:S(2)}, u32[]{:S(2)}) collective-permute-start(bf16[256,1536]{1,0:T(8,128)(2,1)S(1)} %shard_map.190.refs_8_.refs_1_), channel_id=1, source_target_pairs={{0,4},{4,0},{8,12},{12,8},{1,5},{5,1},{9,13},{13,9},{2,6},{6,2},{1... | collective-permute-start | bytes 2359304 | tf_op jit(solution)/shard_map/ppermute | solution.py:200
  150.6 43.1 %collective-permute-start.17 = (bf16[256,1536]{1,0:T(8,128)(2,1)S(1)}, bf16[256,1536]{1,0:T(8,128)(2,1)S(1)}, u32[]{:S(2)}, u32[]{:S(2)}) collective-permute-start(bf16[256,1536]{1,0:T(8,128)(2,1)S(1)} %collective-permute-done.16.refs_3_), channel_id=1, source_target_pairs={{0,4},{4,0},{8,12},{12,8},{1,5},{5,1},{9,13},{13,9},{2,6},{6,2},{1... | collective-permute-start | bytes 2359304 | tf_op jit(solution)/shard_map/ppermute | solution.py:200
  150.6 56.1 %collective-permute-start.25 = (bf16[256,1536]{1,0:T(8,128)(2,1)S(1)}, bf16[256,1536]{1,0:T(8,128)(2,1)S(1)}, u32[]{:S(2)}, u32[]{:S(2)}) collective-permute-start(bf16[256,1536]{1,0:T(8,128)(2,1)S(1)} %shard_map.189.refs_5_), channel_id=1, source_target_pairs={{0,8},{4,12},{8,0},{12,4},{1,9},{5,13},{9,1},{13,5},{2,10},{6,14},... | collective-permute-start | bytes 2359304 | tf_op jit(solution)/shard_map/ppermute | solution.py:200
  151.1 31.4 %collective-permute-start.19 = (bf16[256,384]{1,0:T(8,128)(2,1)S(1)}, bf16[256,384]{1,0:T(8,128)(2,1)S(1)}, u32[]{:S(2)}, u32[]{:S(2)}) collective-permute-start(bf16[256,384]{1,0:T(8,128)(2,1)S(1)} %shard_map.188.refs_3_.refs_1_), channel_id=1, source_target_pairs={{0,8},{4,12},{8,0},{12,4},{1,9},{5,13},{9,1},{13,5},{2,10},{6,14},... | collective-permute-start | bytes 589832 | tf_op jit(solution)/shard_map/ppermute | solution.py:200
  211.5 19.5 %collective-permute-start.26 = (bf16[256,1536]{1,0:T(8,128)(2,1)S(1)}, bf16[256,1536]{1,0:T(8,128)(2,1)S(1)}, u32[]{:S(2)}, u32[]{:S(2)}) collective-permute-start(bf16[256,1536]{1,0:T(8,128)(2,1)S(1)} %shard_map.194.refs_5_.refs_1_), channel_id=1, source_target_pairs={{0,8},{4,12},{8,0},{12,4},{1,9},{5,13},{9,1},{13,5},{2,10},{6,14},... | collective-permute-start | bytes 2359304 | tf_op jit(solution)/shard_map/ppermute | solution.py:200
  212.1 36.9 %collective-permute-start.28 = (bf16[256,1536]{1,0:T(8,128)(2,1)S(1)}, bf16[256,1536]{1,0:T(8,128)(2,1)S(1)}, u32[]{:S(2)}, u32[]{:S(2)}) collective-permute-start(bf16[256,1536]{1,0:T(8,128)(2,1)S(1)} %shard_map.194.refs_5_.refs_1_), channel_id=1, source_target_pairs={{0,4},{4,0},{8,12},{12,8},{1,5},{5,1},{9,13},{13,9},{2,6},{6,2},{1... | collective-permute-start | bytes 2359304 | tf_op jit(solution)/shard_map/ppermute | solution.py:200
  231.0 25.0 %collective-permute-start.27 = (bf16[256,1536]{1,0:T(8,128)(2,1)S(1)}, bf16[256,1536]{1,0:T(8,128)(2,1)S(1)}, u32[]{:S(2)}, u32[]{:S(2)}) collective-permute-start(bf16[256,1536]{1,0:T(8,128)(2,1)S(1)} %collective-permute-done.26.refs_1_), channel_id=1, source_target_pairs={{0,4},{4,0},{8,12},{12,8},{1,5},{5,1},{9,13},{13,9},{2,6},{6,2},{1... | collective-permute-start | bytes 2359304 | tf_op jit(solution)/shard_map/ppermute | solution.py:200
  238.5 28.5 %collective-permute-start.22 = (bf16[64,1536]{1,0:T(8,128)(2,1)S(1)}, bf16[64,1536]{1,0:T(8,128)(2,1)S(1)}, u32[]{:S(2)}, u32[]{:S(2)}) collective-permute-start(bf16[64,1536]{1,0:T(8,128)(2,1)S(1)} %get-tuple-element.25), channel_id=1, source_target_pairs={{0,1},{1,2},{2,3},{3,0},{4,5},{5,6},{6,7},{7,4},{8,9},{9,10},{10,1... | collective-permute-start | bytes 589832 | tf_op jit(solution)/shard_map/ppermute | solution.py:213
  240.0 27.1 %collective-permute-start.23 = (bf16[64,1536]{1,0:T(8,128)(2,1)S(1)}, bf16[64,1536]{1,0:T(8,128)(2,1)S(1)}, u32[]{:S(2)}, u32[]{:S(2)}) collective-permute-start(bf16[64,1536]{1,0:T(8,128)(2,1)S(1)} %get-tuple-element.27), channel_id=1, source_target_pairs={{0,3},{1,0},{2,1},{3,2},{4,7},{5,4},{6,5},{7,6},{8,11},{9,8},{10,9... | collective-permute-start | bytes 589832 | tf_op jit(solution)/shard_map/ppermute | solution.py:213
  242.4 24.8 %collective-permute-start.24 = (bf16[64,1536]{1,0:T(8,128)(2,1)S(1)}, bf16[64,1536]{1,0:T(8,128)(2,1)S(1)}, u32[]{:S(2)}, u32[]{:S(2)}) collective-permute-start(bf16[64,1536]{1,0:T(8,128)(2,1)S(1)} %get-tuple-element.26), channel_id=1, source_target_pairs={{0,2},{1,3},{2,0},{3,1},{4,6},{5,7},{6,4},{7,5},{8,10},{9,11},{10,... | collective-permute-start | bytes 589832 | tf_op jit(solution)/shard_map/ppermute | solution.py:213
  267.0 16.3 %collective-permute-start.34 = (bf16[64,1536]{1,0:T(8,128)(2,1)S(1)}, bf16[64,1536]{1,0:T(8,128)(2,1)S(1)}, u32[]{:S(2)}, u32[]{:S(2)}) collective-permute-start(bf16[64,1536]{1,0:T(8,128)(2,1)S(1)} %get-tuple-element.23), channel_id=1, source_target_pairs={{0,2},{1,3},{2,0},{3,1},{4,6},{5,7},{6,4},{7,5},{8,10},{9,11},{10,... | collective-permute-start | bytes 589832 | tf_op jit(solution)/shard_map/ppermute | solution.py:213
  290.0 12.8 %collective-permute-start.39 = (bf16[64,1536]{1,0:T(8,128)(2,1)S(1)}, bf16[64,1536]{1,0:T(8,128)(2,1)S(1)}, u32[]{:S(2)}, u32[]{:S(2)}) collective-permute-start(bf16[64,1536]{1,0:T(8,128)(2,1)S(1)} %get-tuple-element.31), channel_id=1, source_target_pairs={{0,3},{1,0},{2,1},{3,2},{4,7},{5,4},{6,5},{7,6},{8,11},{9,8},{10,9... | collective-permute-start | bytes 589832 | tf_op jit(solution)/shard_map/ppermute | solution.py:213
  293.9 15.5 %collective-permute-start.40 = (bf16[64,1536]{1,0:T(8,128)(2,1)S(1)}, bf16[64,1536]{1,0:T(8,128)(2,1)S(1)}, u32[]{:S(2)}, u32[]{:S(2)}) collective-permute-start(bf16[64,1536]{1,0:T(8,128)(2,1)S(1)} %get-tuple-element.31), channel_id=1, source_target_pairs={{0,2},{1,3},{2,0},{3,1},{4,6},{5,7},{6,4},{7,5},{8,10},{9,11},{10,... | collective-permute-start | bytes 589832 | tf_op jit(solution)/shard_map/ppermute | solution.py:213
  314.9 19.7 %collective-permute-start.41 = (bf16[256,2304]{1,0:T(8,128)(2,1)S(1)}, bf16[256,2304]{1,0:T(8,128)(2,1)S(1)}, u32[]{:S(2)}, u32[]{:S(2)}) collective-permute-start(bf16[256,2304]{1,0:T(8,128)(2,1)S(1)} %shard_map.198.refs_5_), channel_id=1, source_target_pairs={{0,4},{4,0},{8,12},{12,8},{1,5},{5,1},{9,13},{13,9},{2,6},{6,2},{1... | collective-permute-start | bytes 3538952 | tf_op jit(solution)/shard_map/ppermute | solution.py:200
  315.1 14.0 %collective-permute-start.47 = (bf16[64,1536]{1,0:T(8,128)(2,1)S(1)}, bf16[64,1536]{1,0:T(8,128)(2,1)S(1)}, u32[]{:S(2)}, u32[]{:S(2)}) collective-permute-start(bf16[64,1536]{1,0:T(8,128)(2,1)S(1)} %get-tuple-element.30), channel_id=1, source_target_pairs={{0,3},{1,0},{2,1},{3,2},{4,7},{5,4},{6,5},{7,6},{8,11},{9,8},{10,9... | collective-permute-start | bytes 589832 | tf_op jit(solution)/shard_map/ppermute | solution.py:213
  319.1 15.4 %collective-permute-start.48 = (bf16[64,1536]{1,0:T(8,128)(2,1)S(1)}, bf16[64,1536]{1,0:T(8,128)(2,1)S(1)}, u32[]{:S(2)}, u32[]{:S(2)}) collective-permute-start(bf16[64,1536]{1,0:T(8,128)(2,1)S(1)} %get-tuple-element.30), channel_id=1, source_target_pairs={{0,2},{1,3},{2,0},{3,1},{4,6},{5,7},{6,4},{7,5},{8,10},{9,11},{10,... | collective-permute-start | bytes 589832 | tf_op jit(solution)/shard_map/ppermute | solution.py:213
  344.2 16.2 %collective-permute-start.42 = (bf16[256,1152]{1,0:T(8,128)(2,1)S(1)}, bf16[256,1152]{1,0:T(8,128)(2,1)S(1)}, u32[]{:S(2)}, u32[]{:S(2)}) collective-permute-start(bf16[256,1152]{1,0:T(8,128)(2,1)S(1)} %shard_map.199.refs_4_), channel_id=1, source_target_pairs={{0,8},{4,12},{8,0},{12,4},{1,9},{5,13},{9,1},{13,5},{2,10},{6,14},... | collective-permute-start | bytes 1769480 | tf_op jit(solution)/shard_map/ppermute | solution.py:200
  351.0 21.6 %collective-permute-start.50 = (bf16[256,1152]{1,0:T(8,128)(2,1)S(1)}, bf16[256,1152]{1,0:T(8,128)(2,1)S(1)}, u32[]{:S(2)}, u32[]{:S(2)}) collective-permute-start(bf16[256,1152]{1,0:T(8,128)(2,1)S(1)} %shard_map.201.refs_8_), channel_id=1, source_target_pairs={{0,8},{4,12},{8,0},{12,4},{1,9},{5,13},{9,1},{13,5},{2,10},{6,14},... | collective-permute-start | bytes 1769480 | tf_op jit(solution)/shard_map/ppermute | solution.py:200
  402.8 14.2 %collective-permute-start.56 = (bf16[64,1536]{1,0:T(8,128)(2,1)S(1)}, bf16[64,1536]{1,0:T(8,128)(2,1)S(1)}, u32[]{:S(2)}, u32[]{:S(2)}) collective-permute-start(bf16[64,1536]{1,0:T(8,128)(2,1)S(1)} %get-tuple-element.17), channel_id=1, source_target_pairs={{0,1},{1,2},{2,3},{3,0},{4,5},{5,6},{6,7},{7,4},{8,9},{9,10},{10,1... | collective-permute-start | bytes 589832 | tf_op jit(solution)/shard_map/ppermute | solution.py:213
  402.8 16.6 %collective-permute-start.57 = (bf16[64,1536]{1,0:T(8,128)(2,1)S(1)}, bf16[64,1536]{1,0:T(8,128)(2,1)S(1)}, u32[]{:S(2)}, u32[]{:S(2)}) collective-permute-start(bf16[64,1536]{1,0:T(8,128)(2,1)S(1)} %get-tuple-element.15), channel_id=1, source_target_pairs={{0,3},{1,0},{2,1},{3,2},{4,7},{5,4},{6,5},{7,6},{8,11},{9,8},{10,9... | collective-permute-start | bytes 589832 | tf_op jit(solution)/shard_map/ppermute | solution.py:213
  411.1 14.4 %collective-permute-start.55 = (bf16[64,1536]{1,0:T(8,128)(2,1)S(1)}, bf16[64,1536]{1,0:T(8,128)(2,1)S(1)}, u32[]{:S(2)}, u32[]{:S(2)}) collective-permute-start(bf16[64,1536]{1,0:T(8,128)(2,1)S(1)} %get-tuple-element.14), channel_id=1, source_target_pairs={{0,1},{1,2},{2,3},{3,0},{4,5},{5,6},{6,7},{7,4},{8,9},{9,10},{10,1... | collective-permute-start | bytes 589832 | tf_op jit(solution)/shard_map/ppermute | solution.py:213
  411.2 15.9 %collective-permute-start.59 = (bf16[64,1536]{1,0:T(8,128)(2,1)S(1)}, bf16[64,1536]{1,0:T(8,128)(2,1)S(1)}, u32[]{:S(2)}, u32[]{:S(2)}) collective-permute-start(bf16[64,1536]{1,0:T(8,128)(2,1)S(1)} %get-tuple-element.13), channel_id=1, source_target_pairs={{0,3},{1,0},{2,1},{3,2},{4,7},{5,4},{6,5},{7,6},{8,11},{9,8},{10,9... | collective-permute-start | bytes 589832 | tf_op jit(solution)/shard_map/ppermute | solution.py:213
  (37 other events, 267.9 us)

commit v2 on v1

--- a/solution.py
+++ b/solution.py
@@ -216,34 +216,27 @@
 class Runner:
     def __init__(self, position):
         self.position = position
-        self.last = None
-
-    def __call__(self, kernel, grid, operands, in_specs, out_shape, out_spec, flops, scratch=()):
-        in_specs = list(in_specs)
-        operands = list(operands)
-        count = len(operands)
-        if self.last is not None:
-            operands.append(self.last)
-            in_specs.append(pl.BlockSpec(memory_space=pl.ANY))
-        total = len(operands)
-
-        def inner(position_ref, *refs):
-            kernel(position_ref, *refs[:count], *refs[total:])
-
-        self.last = pl.pallas_call(
-            inner,
+
+    def __call__(self, kernel, grid, operands, in_specs, out_shape, out_spec):
+        return pl.pallas_call(
+            kernel,
             out_shape=out_shape,
             grid_spec=pltpu.PrefetchScalarGridSpec(
-                num_scalar_prefetch=1,
-                grid=grid,
-                in_specs=in_specs,
-                out_specs=out_spec,
-                scratch_shapes=scratch,
+                num_scalar_prefetch=1, grid=grid, in_specs=list(in_specs), out_specs=out_spec
             ),
             compiler_params=pltpu.CompilerParams(vmem_limit_bytes=VMEM_BYTES),
             cost_estimate=pl.CostEstimate(flops=1, bytes_accessed=1, transcendentals=0),
         )(self.position, *operands)
-        return self.last
+
+
+def joined_rows(refs, at=slice(None)):
+    return jnp.concatenate([ref[:, at] for ref in refs])
+
+
+def store_rows(refs, at, values):
+    piece = values.shape[0] // len(refs)
+    for j, ref in enumerate(refs):
+        ref[:, at] = values[j * piece : (j + 1) * piece].astype(ref.dtype)
 
 
 def whole(array):
@@ -281,11 +274,10 @@
         (whole(tokens), *[spec] * len(weights)),
         jax.ShapeDtypeStruct((rows, 2 * sub * wide), jnp.bfloat16),
         pl.BlockSpec((rows, wide), lambda s, pos: (0, s)),
-        rows * depth * 2 * sub * wide,
-    )
-
-
-def project_across(run, tokens, weights, width, sub, arrived):
+    )
+
+
+def project_across(run, tokens, weights, width, sub, arrived, pieces=1):
     rows, depth = tokens.shape
     block = width // sub
     wide = len(weights) * block
@@ -294,8 +286,8 @@
         for i in range(len(weights)):
             at = slice(i * block, (i + 1) * block)
             part = dot_f32(tokens_ref[...], refs[i][...])
-            part = part + refs[-2][:, at].astype(jnp.float32)
-            refs[-1][:, at] = part.astype(jnp.bfloat16)
+            part = part + refs[len(weights)][:, at].astype(jnp.float32)
+            store_rows(refs[len(weights) + 1 :], at, part)
 
     spec = pl.BlockSpec((depth, block), lambda s, pos: (0, across_of(pos) * sub + s))
     return run(
@@ -307,36 +299,37 @@
             *[spec] * len(weights),
             pl.BlockSpec((rows, wide), lambda s, pos: (0, (1 - pos[1]) * sub + s)),
         ),
-        jax.ShapeDtypeStruct((rows, sub * wide), jnp.bfloat16),
-        pl.BlockSpec((rows, wide), lambda s, pos: (0, s)),
-        rows * depth * sub * wide,
-    )
-
-
-def project_hidden(run, tokens, weight, bias, width, sub, arrived, from_side):
+        (jax.ShapeDtypeStruct((rows // pieces, sub * wide), jnp.bfloat16),) * pieces,
+        (pl.BlockSpec((rows // pieces, wide), lambda s, pos: (0, s)),) * pieces,
+    )
+
+
+def project_hidden(run, tokens, weight, bias, width, sub, arrived, from_side, pieces=1):
     rows, depth = tokens.shape
     block = width // sub
-
-    def kernel(pos, tokens_ref, weight_ref, bias_ref, arrived_ref, side_ref, out_ref):
+    sides = len(from_side)
+
+    def kernel(pos, tokens_ref, weight_ref, bias_ref, arrived_ref, *refs):
         total = dot_f32(tokens_ref[...], weight_ref[...])
-        total = total + arrived_ref[...].astype(jnp.float32) + side_ref[...].astype(jnp.float32)
+        total = total + arrived_ref[...].astype(jnp.float32)
+        total = total + joined_rows(refs[:sides]).astype(jnp.float32)
         total = total + bias_ref[...]
-        out_ref[...] = (total * (1.0 + lax.erf(total * math.sqrt(0.5))) * 0.5).astype(jnp.bfloat16)
+        unit = total * (1.0 + lax.erf(total * math.sqrt(0.5))) * 0.5
+        store_rows(refs[sides:], slice(None), unit)
 
     return run(
         kernel,
         (sub,),
-        (tokens, weight, bias, arrived, from_side),
+        (tokens, weight, bias, arrived, *from_side),
         (
             whole(tokens),
             pl.BlockSpec((depth, block), lambda s, pos: (0, mine_of(pos) * sub + s)),
             pl.BlockSpec((1, block), lambda s, pos: (0, mine_of(pos) * sub + s)),
             pl.BlockSpec((rows, block), lambda s, pos: (0, pos[1] * sub + s)),
-            pl.BlockSpec((rows, block), lambda s, pos: (0, s)),
+            *[pl.BlockSpec((rows // sides, block), lambda s, pos: (0, s))] * sides,
         ),
-        jax.ShapeDtypeStruct((rows, width), jnp.bfloat16),
-        pl.BlockSpec((rows, block), lambda s, pos: (0, s)),
-        rows * depth * width,
+        (jax.ShapeDtypeStruct((rows // pieces, width), jnp.bfloat16),) * pieces,
+        (pl.BlockSpec((rows // pieces, block), lambda s, pos: (0, s)),) * pieces,
     )
 
 
@@ -403,13 +396,13 @@
         ),
         jax.ShapeDtypeStruct((rows, out_width), jnp.bfloat16),
         pl.BlockSpec((rows, out_width), lambda s, pos: (0, 0)),
-        3 * rows * depth * width,
     )
 
 
 def contract(run, parts, weight, sub, first=0, start=None):
-    rows, width = parts[0].shape
-    count = len(parts)
+    rows = sum(piece.shape[0] for piece in parts[0])
+    width = parts[0][0].shape[1]
+    count, pieces = len(parts), len(parts[0])
     out_width = weight.shape[1]
     block = width // sub
 
@@ -420,16 +413,17 @@
 
             @pl.when(step // sub == i)
             def _(i=i):
-                term = dot_f32(refs[i][...], weight_ref[...])
+                part = joined_rows(refs[i * pieces : (i + 1) * pieces])
+                term = dot_f32(part, weight_ref[...])
                 if i > 0:
                     out_ref[...] += term
                 elif sub == 1:
-                    out_ref[...] = term if start is None else term + refs[count][...]
+                    out_ref[...] = term if start is None else term + refs[-2][...]
                 else:
 
                     @pl.when(step == 0)
                     def _():
-                        out_ref[...] = term if start is None else term + refs[count][...]
+                        out_ref[...] = term if start is None else term + refs[-2][...]
 
                     @pl.when(step > 0)
                     def _():
@@ -440,11 +434,13 @@
         return (2 * (pos[0] ^ (i & 1)) + (pos[1] ^ (i >> 1))) * sub + s % sub, 0
 
     def part_spec(i):
-        return pl.BlockSpec((rows, block), lambda s, pos: (0, jnp.clip(s - i * sub, 0, sub - 1)))
-
-    operands = [weight, *parts]
+        return pl.BlockSpec(
+            (rows // pieces, block), lambda s, pos: (0, jnp.clip(s - i * sub, 0, sub - 1))
+        )
+
+    operands = [weight, *[piece for part in parts for piece in part]]
     in_specs = [pl.BlockSpec((block, out_width), weight_block)]
-    in_specs += [part_spec(i) for i in range(count)]
+    in_specs += [part_spec(i) for i in range(count) for _ in range(pieces)]
     if start is not None:
         operands.append(start)
         in_specs.append(whole(start))
@@ -455,7 +451,6 @@
         in_specs,
         jax.ShapeDtypeStruct((rows, out_width), jnp.float32),
         pl.BlockSpec((rows, out_width), lambda s, pos: (0, 0)),
-        rows * width * count * out_width,
     )
 
 
@@ -484,26 +479,27 @@
         (*specs(0), *specs(1), *specs(2)),
         jax.ShapeDtypeStruct((rows, heads * HEAD_DIM), jnp.bfloat16),
         pl.BlockSpec((rows, HEAD_DIM), lambda h, pos: (0, h)),
-        2 * rows * rows * heads * HEAD_DIM,
-    )
-
-
-def all_moments(values):
-    pair = jnp.stack((jnp.sum(values, 1), jnp.sum(values * values, 1)))
-    return (pair + flip(pair, 1)) + (flip(pair, 2) + flip(pair, 3))
-
-
-def gather_rows(own):
-    return jnp.concatenate((own, row_shift(own, 1), row_shift(own, -1), row_shift(own, 2)))
-
-
-def scatter_rows(terms):
-    own, before, after, away = jnp.split(terms, 4)
-
-    def send(array, shift):
-        return row_shift(array.astype(jnp.bfloat16), shift).astype(jnp.float32)
-
-    return own + send(after, 1) + send(before, -1) + send(away, 2)
+    )
+
+
+def moment_pair(values):
+    return jnp.stack((jnp.sum(values, 1), jnp.sum(values * values, 1)))
+
+
+def moment_flips(pair):
+    return pair, flip(pair, 1), flip(pair, 2), flip(pair, 3)
+
+
+def moment_sum(pairs):
+    return (pairs[0] + pairs[1]) + (pairs[2] + pairs[3])
+
+
+def sent(array, shift):
+    return row_shift(array.astype(jnp.bfloat16), shift)
+
+
+def sync(*values):
+    return lax.optimization_barrier(values)
 
 
 def scatter_rows_long(terms):
@@ -541,7 +537,7 @@
     join_key_gain,
     join_out,
 ):
-    own_rows = camera_tokens.shape[0]
+    half = TOK_CAM
     index = lax.axis_index("cols")
     run = Runner(jnp.stack((index & 1, index >> 1)).astype(jnp.int32))
     head_width = query_weight.shape[1] // 4
@@ -552,112 +548,180 @@
     scales = (query_gain[None], key_gain[None])
     join_scales = (join_query_gain[None], join_key_gain[None])
     bias = up_bias[None]
-    spans = range(0, own_rows, TOK_CAM)
-    last = len(spans) - 1
+
+    def heads_send(tokens, weights):
+        return project_send(run, tokens, weights, head_width, 1)
+
+    def heads_across(tokens, weights, arrived):
+        return project_across(run, tokens, weights, head_width, 1, arrived)[0]
+
+    def units_send(tokens):
+        return project_send(run, tokens, (up_weight,), unit_width, sub)
+
+    def units_across(tokens, arrived, pieces):
+        return project_across(run, tokens, (up_weight,), unit_width, sub, arrived, pieces)
+
+    def units_end(tokens, arrived, side, pieces):
+        return project_hidden(
+            run, tokens, up_weight, bias, unit_width, sub, arrived, side, pieces
+        )
+
+    def layer_end(start, own, *arrived):
+        total = own
+        for term in arrived:
+            total = total + term.astype(jnp.float32)
+        return (start + total + down_bias).astype(jnp.bfloat16)
 
     start_f32 = camera_tokens.astype(jnp.float32)
-    normed = normalize(start_f32, norm_gain, all_moments(start_f32))
-    tokens = [gather_rows(normed[at : at + TOK_CAM]) for at in spans]
-
-    def collect(own):
-        own_across = y_swap(own)
-        return own, core_swap(own), own_across, core_swap(own_across)
-
-    def heads_begin(i):
-        sent = core_swap(project_send(run, tokens[i], heads_in, head_width, 1))
-        heads_arrived.append(sent)
-
-    def units_begin(i):
-        sent = core_swap(project_send(run, tokens[i], (up_weight,), unit_width, sub))
-        units_arrived.append(sent)
-
-    def heads_cross(i):
-        heads_side.append(
-            y_swap(project_across(run, tokens[i], heads_in, head_width, 1, heads_arrived[i]))
-        )
-
-    def units_cross(i):
-        units_side.append(
-            y_swap(
-                project_across(run, tokens[i], (up_weight,), unit_width, sub, units_arrived[i])
-            )
-        )
-
-    def heads_end(i):
-        own = project_heads(
-            run, tokens[i], heads_in, scales, head_width, heads_arrived[i], heads_side[i], True
-        )
-        blended.append(collect(own))
-
-    def units_end(i):
-        own = project_hidden(
-            run, tokens[i], up_weight, bias, unit_width, sub, units_arrived[i], units_side[i]
-        )
-        hidden.append(collect(own))
-
-    def out_terms(i):
-        return contract(run, blended[i], out_weight, 1)
-
-    def camera_end(i, mixed):
-        summed = scatter_rows(mixed)
-        rows = slice(spans[i], spans[i] + TOK_CAM)
-        layer = (start_f32[rows] + summed + down_bias).astype(jnp.bfloat16)
-        layers.append(layer)
-        layer_f32 = layer.astype(jnp.float32)
-        join_tokens.append(gather_rows(normalize(layer_f32, join_gain, all_moments(layer_f32))))
-
-    def join_begin(i):
-        arrived = core_swap(project_send(run, join_tokens[i], join_in, head_width, 1))
-        side = y_swap(project_across(run, join_tokens[i], join_in, head_width, 1, arrived))
-        join_sums.append((arrived, side))
-
-    def join_end(i):
-        join_parts.append(
-            project_heads(
-                run, join_tokens[i], join_in, join_scales, head_width, *join_sums[i], False
-            )
-        )
-
-    heads_arrived, units_arrived, heads_side, units_side = [], [], [], []
-    blended, hidden, layers, join_tokens, join_sums, join_parts = [], [], [], [], [], []
-    for i in range(len(spans)):
-        heads_begin(i)
-        units_begin(i)
-        heads_cross(i)
-        if i > 0:
-            heads_end(i - 1)
-        units_cross(i)
-        if i > 0:
-            units_end(i - 1)
-    heads_end(last)
-    for i in range(last):
-        mixed = contract(run, hidden[i], down_weight, 2, 0, out_terms(i))
-        if i == last - 1:
-            units_end(last)
-        camera_end(i, mixed)
-    if last == 0:
-        units_end(last)
-    mixed = contract(run, hidden[last][:2], down_weight, 2, 0, out_terms(last))
-    mixed = contract(run, hidden[last][2:], down_weight, 2, 2, mixed)
-    camera_end(last, mixed)
-    for i in range(len(spans)):
-        join_begin(i)
-        if i > 0:
-            join_end(i - 1)
-    join_end(last)
-
-    joined = join_blend(run, join_parts)
-    joined = joined.reshape(len(spans), 4, TOK_CAM, head_width).swapaxes(0, 1)
-    joined = joined.reshape(4 * own_rows, head_width)
-    summed = scatter_rows_long(contract(run, collect(joined), join_out, 1))
-    layer_own = jnp.concatenate(layers)
+    pairs = sync(*moment_flips(moment_pair(start_f32)))
+    normed = normalize(start_f32, norm_gain, moment_sum(pairs))
+    own_a, own_b = normed[:half], normed[half:]
+    gathered = sync(own_b, own_a, sent(own_a, 1), sent(own_a, -1), sent(own_a, 2))
+    own_b, tok_a = gathered[0], jnp.concatenate(gathered[1:])
+
+    b_before = sent(own_b, 1)
+    qs_a = heads_send(tok_a, heads_in)
+    tok_a, own_b, b_before, qs_a = sync(tok_a, own_b, b_before, qs_a)
+
+    b_after, qc_a = sent(own_b, -1), core_swap(qs_a)
+    us_a = units_send(tok_a)
+    tok_a, own_b, b_after, qc_a, us_a = sync(tok_a, own_b, b_after, qc_a, us_a)
+
+    uc_a = core_swap(us_a)
+    qx_a = heads_across(tok_a, heads_in, qc_a)
+    tok_a, own_b, qc_a, uc_a, qx_a = sync(tok_a, own_b, qc_a, uc_a, qx_a)
+
+    qy_a, b_away = y_swap(qx_a), sent(own_b, 2)
+    (ux_a,) = units_across(tok_a, uc_a, 1)
+    tok_a, qc_a, uc_a, ux_a, qy_a, own_b, b_before, b_after, b_away = sync(
+        tok_a, qc_a, uc_a, ux_a, qy_a, own_b, b_before, b_after, b_away
+    )
+
+    uy_a = y_swap(ux_a)
+    tok_b = jnp.concatenate((own_b, b_before, b_after, b_away))
+    qs_b = heads_send(tok_b, heads_in)
+    us_b = units_send(tok_b)
+    at_a = project_heads(run, tok_a, heads_in, scales, head_width, qc_a, qy_a, True)
+    tok_a, tok_b, qs_b, us_b, at_a, uc_a, uy_a = sync(
+        tok_a, tok_b, qs_b, us_b, at_a, uc_a, uy_a
+    )
+
+    at_ya, at_ca, qc_b, uc_b = y_swap(at_a), core_swap(at_a), core_swap(qs_b), core_swap(us_b)
+    (hd_a,) = units_end(tok_a, uc_a, (uy_a,), 1)
+    tok_b, at_a, at_ya, at_ca, qc_b, uc_b, hd_a = sync(
+        tok_b, at_a, at_ya, at_ca, qc_b, uc_b, hd_a
+    )
+
+    hd_ya, hd_ca, at_fa = y_swap(hd_a), core_swap(hd_a), core_swap(at_ya)
+    qx_b = heads_across(tok_b, heads_in, qc_b)
+    ux_b = units_across(tok_b, uc_b, 2)
+    tok_b, at_a, at_ya, at_ca, at_fa, hd_a, hd_ya, hd_ca, qc_b, uc_b, qx_b, *ux_b = sync(
+        tok_b, at_a, at_ya, at_ca, at_fa, hd_a, hd_ya, hd_ca, qc_b, uc_b, qx_b, *ux_b
+    )
+
+    qy_b, hd_fa = y_swap(qx_b), core_swap(hd_ya)
+    mixed_a = contract(run, ((at_a,), (at_ca,), (at_ya,), (at_fa,)), out_weight, 1)
+    mixed_a = contract(run, ((hd_a,), (hd_ca,)), down_weight, 2, 0, mixed_a)
+    tok_b, hd_ya, hd_fa, mixed_a, qc_b, qy_b, uc_b, ux_b0, ux_b1 = sync(
+        tok_b, hd_ya, hd_fa, mixed_a, qc_b, qy_b, uc_b, *ux_b
+    )
+
+    uy_b0 = y_swap(ux_b0)
+    mixed_a = contract(run, ((hd_ya,), (hd_fa,)), down_weight, 2, 2, mixed_a)
+    tok_b, mixed_a, qc_b, qy_b, uc_b, uy_b0, ux_b1 = sync(
+        tok_b, mixed_a, qc_b, qy_b, uc_b, uy_b0, ux_b1
+    )
+
+    uy_b1 = y_swap(ux_b1)
+    mine_a, before_a, after_a, away_a = jnp.split(mixed_a, 4)
+    from_before, from_after = sent(after_a, 1), sent(before_a, -1)
+    at_b = project_heads(run, tok_b, heads_in, scales, head_width, qc_b, qy_b, True)
+    tok_b, uc_b, uy_b0, uy_b1, at_b, mine_a, away_a, from_before, from_after = sync(
+        tok_b, uc_b, uy_b0, uy_b1, at_b, mine_a, away_a.astype(jnp.bfloat16), from_before, from_after
+    )
+
+    at_yb, at_cb, from_away = y_swap(at_b), core_swap(at_b), sent(away_a, 2)
+    hd_b = units_end(tok_b, uc_b, (uy_b0, uy_b1), 2)
+    at_b, at_yb, at_cb, hd_b0, hd_b1, mine_a, from_before, from_after, from_away = sync(
+        at_b, at_yb, at_cb, *hd_b, mine_a, from_before, from_after, from_away
+    )
+
+    hd_yb0, at_fb = y_swap(hd_b0), core_swap(at_yb)
+    layer_a = layer_end(start_f32[:half], mine_a, from_before, from_after, from_away)
+    pairs = moment_flips(moment_pair(layer_a.astype(jnp.float32)))
+    at_b, at_yb, at_cb, at_fb, hd_b0, hd_b1, hd_yb0, layer_a, *pairs = sync(
+        at_b, at_yb, at_cb, at_fb, hd_b0, hd_b1, hd_yb0, layer_a, *pairs
+    )
+
+    hd_yb1, hd_cb0, hd_cb1 = y_swap(hd_b1), core_swap(hd_b0), core_swap(hd_b1)
+    join_a = normalize(layer_a.astype(jnp.float32), join_gain, moment_sum(pairs))
+    ja_before, ja_after = sent(join_a, 1), sent(join_a, -1)
+    mixed_b = contract(run, ((at_b,), (at_cb,), (at_yb,), (at_fb,)), out_weight, 1)
+    hd_b0, hd_b1, hd_cb0, hd_cb1, hd_yb0, hd_yb1, mixed_b, join_a, ja_before, ja_after = sync(
+        hd_b0, hd_b1, hd_cb0, hd_cb1, hd_yb0, hd_yb1, mixed_b, join_a, ja_before, ja_after
+    )
+
+    hd_fb0, hd_fb1, ja_away = core_swap(hd_yb0), core_swap(hd_yb1), sent(join_a, 2)
+    mixed_b = contract(run, ((hd_b0, hd_b1), (hd_cb0, hd_cb1)), down_weight, 2, 0, mixed_b)
+    hd_yb0, hd_yb1, hd_fb0, hd_fb1, mixed_b, join_a, ja_before, ja_after, ja_away = sync(
+        hd_yb0, hd_yb1, hd_fb0, hd_fb1, mixed_b, join_a, ja_before, ja_after, ja_away
+    )
+
+    mixed_b = contract(run, ((hd_yb0, hd_yb1), (hd_fb0, hd_fb1)), down_weight, 2, 2, mixed_b)
+    mixed_b, join_a, ja_before, ja_after, ja_away = sync(
+        mixed_b, join_a, ja_before, ja_after, ja_away
+    )
+
+    mine_b, before_b, after_b, away_b = jnp.split(mixed_b, 4)
+    from_before, from_after = sent(after_b, 1), sent(before_b, -1)
+    tok_ja = jnp.concatenate((join_a, ja_before, ja_after, ja_away))
+    js_a = heads_send(tok_ja, join_in)
+    tok_ja, js_a, mine_b, away_b, from_before, from_after = sync(
+        tok_ja, js_a, mine_b, away_b.astype(jnp.bfloat16), from_before, from_after
+    )
+
+    from_away, jc_a = sent(away_b, 2), core_swap(js_a)
+    tok_ja, jc_a, mine_b, from_before, from_after, from_away = sync(
+        tok_ja, jc_a, mine_b, from_before, from_after, from_away
+    )
+
+    layer_b = layer_end(start_f32[half:], mine_b, from_before, from_after, from_away)
+    pairs = moment_flips(moment_pair(layer_b.astype(jnp.float32)))
+    jx_a = heads_across(tok_ja, join_in, jc_a)
+    tok_ja, jc_a, jx_a, layer_b, *pairs = sync(tok_ja, jc_a, jx_a, layer_b, *pairs)
+
+    join_b = normalize(layer_b.astype(jnp.float32), join_gain, moment_sum(pairs))
+    jb_before, jb_after, jb_away = sent(join_b, 1), sent(join_b, -1), sent(join_b, 2)
+    jy_a = y_swap(jx_a)
+    tok_ja, jc_a, jy_a, join_b, jb_before, jb_after, jb_away = sync(
+        tok_ja, jc_a, jy_a, join_b, jb_before, jb_after, jb_away
+    )
+
+    tok_jb = jnp.concatenate((join_b, jb_before, jb_after, jb_away))
+    js_b = heads_send(tok_jb, join_in)
+    tok_ja, jc_a, jy_a, tok_jb, js_b = sync(tok_ja, jc_a, jy_a, tok_jb, js_b)
+
+    jc_b = core_swap(js_b)
+    parts_a = project_heads(run, tok_ja, join_in, join_scales, head_width, jc_a, jy_a, False)
+    tok_jb, jc_b, parts_a = sync(tok_jb, jc_b, parts_a)
+
+    jy_b = y_swap(heads_across(tok_jb, join_in, jc_b))
+    parts_b = project_heads(run, tok_jb, join_in, join_scales, head_width, jc_b, jy_b, False)
+
+    joined = join_blend(run, (parts_a, parts_b))
+    joined = joined.reshape(2, 4, half, head_width).swapaxes(0, 1).reshape(8 * half, head_width)
+    jo_y, jo_c = y_swap(joined), core_swap(joined)
+    jo_f = core_swap(jo_y)
+    result = contract(run, ((joined,), (jo_c,), (jo_y,), (jo_f,)), join_out, 1)
+    summed = scatter_rows_long(result)
+    layer_own = jnp.concatenate((layer_a, layer_b))
     return (layer_own.astype(jnp.float32) + summed).astype(jnp.bfloat16)
 
 
 def layer(*arrays):
     own_rows, heads_width = arrays[0].shape[0], arrays[2].shape[1]
     fits = lax.axis_size("cols") == 4 and lax.axis_size("rows") == 4
-    fits = fits and own_rows % TOK_CAM == 0 and heads_width % (4 * HEAD_DIM) == 0
+    fits = fits and own_rows == 2 * TOK_CAM and heads_width % (4 * HEAD_DIM) == 0
     return (fast_body if fits else generic_body)(*arrays)
 
 

time: 433 us -> 347 us (0.80)
  waiting for transfers between devices: 229 us -> 138 us
  starting transfers between devices: 56.6 us -> 62 us
    ppermute x36 -> x40, waiting for transfers between devices: 133 us -> 54.5 us  [flip(): return lax.ppermute(array, 'cols', [(i, i ^ mask) for i in range(size)])]
    ppermute x24, waiting for transfers between devices: 95.9 us -> 83.9 us  [row_shift(): lax.ppermute(array, 'rows', [(i, (i + shift) % size) for i in range(size)])]
    ppermute x36 -> x40, starting transfers between devices: 20.8 us -> 23 us  [flip(): return lax.ppermute(array, 'cols', [(i, i ^ mask) for i in range(size)])]
    pallas_call x25 -> x26, Pallas kernels: 135 us -> 137 us  [__call__(): pl.pallas_call(kernel, out_shape=out_shape, grid_spec=pltpu.PrefetchScala...]
  transfers between devices with their start and end apart: 60 -> 64, of which waited for: 34 -> 34; matrix products, arithmetic and copies ran while one was open for 0% -> 0% of each run, Pallas kernels for 16% -> 31%
where the time goes in v2:
time: 347 us; the launch traced here: 344 us
  waiting for transfers between devices  138 us (40%)
  Pallas kernels  137 us (39%)
  starting transfers between devices  62 us (18%)
  other arithmetic  4.81 us (1%)
    pallas_call x26, Pallas kernels, __call__(): pl.pallas_call(kernel, out_shape=out_shape, grid_spec=pltpu.PrefetchScala...  137 us
    ppermute x24, waiting for transfers between devices, row_shift(): lax.ppermute(array, 'rows', [(i, (i + shift) % size) for i in range(size)])  83.9 us
    ppermute x40, waiting for transfers between devices, flip(): return lax.ppermute(array, 'cols', [(i, i ^ mask) for i in range(size)])  54.5 us
    ppermute x24, starting transfers between devices, row_shift(): lax.ppermute(array, 'rows', [(i, (i + shift) % size) for i in range(size)])  39 us
    ppermute x40, starting transfers between devices, flip(): return lax.ppermute(array, 'cols', [(i, i ^ mask) for i in range(size)])  23 us
  transfers between devices with their start and end apart: 64, of which 34 were waited for; matrix products, arithmetic and copies ran while one was open for 0% of the time, Pallas kernels for 31%

profile of v2, /device:TPU:0, one launch (start us, length us, event | category | flops | bytes accessed | tf_op | source)
XLA Modules:
  0.0 343.6 jit_solution(10031855277025826371)
XLA Ops:
  13.4 4.9 %collective-permute-done.3 = bf16[64,1536]{1,0:T(8,128)(2,1)S(1)} collective-permute-done((bf16[64,1536]{1,0:T(8,128)(2,1)S(1)}, bf16[64,1536]{1,0:T(8,128)(2,1)S(1)}, u32[]{:S(2)}, u32[]{:S(2)}) %collective-permute-start.3) | collective-permute-done | bytes 196640 | tf_op jit(solution)/shard_map/ppermute | solution.py:213
  21.2 9.0 %collective-permute-done.5 = bf16[64,1536]{1,0:T(8,128)(2,1)S(1)} collective-permute-done((bf16[64,1536]{1,0:T(8,128)(2,1)S(1)}, bf16[64,1536]{1,0:T(8,128)(2,1)S(1)}, u32[]{:S(2)}, u32[]{:S(2)}) %collective-permute-start.5) | collective-permute-done | bytes 196640 | tf_op jit(solution)/shard_map/ppermute | solution.py:213
  30.3 5.5 %shard_map.181 = bf16[256,2304]{1,0:T(8,128)(2,1)S(1)} custom-call(s32[2]{0:T(128)S(1)} %pad_add_fusion.pos, bf16[256,1536]{1,0:T(8,128)(2,1)S(1)} %constant_dynamic-update-slice_fusion.tokens_ref, bf16[1536,1536]{1,0:T(8,128)(2,1)} %refs_0_.25, bf16[1536,1536]{1,0:T(8,128)(2,1)} %refs_1_.17, bf16[1536,1536]{1,0:T(8,128)(2,1)} %refs_2_.17), custom_call_target="tpu_custom_call" | custom-call | flops 1 | bytes 1 | tf_op jit(solution)/shard_map/pallas_call | solution.py:221
  39.8 7.6 %shard_map.182 = bf16[256,3072]{1,0:T(8,128)(2,1)S(1)} custom-call(s32[2]{0:T(128)S(1)} %pad_add_fusion.pos, bf16[256,1536]{1,0:T(8,128)(2,1)S(1)} %constant_dynamic-update-slice_fusion.tokens_ref, bf16[1536,6144]{1,0:T(8,128)(2,1)} %weight_ref.13), custom_call_target="tpu_custom_call" | custom-call | flops 1 | bytes 1 | tf_op jit(solution)/shard_map/pallas_call | solution.py:221
  52.2 4.6 %shard_map.184 = bf16[256,1536]{1,0:T(8,128)(2,1)S(1)} custom-call(s32[2]{0:T(128)S(1)} %pad_add_fusion.pos, bf16[256,1536]{1,0:T(8,128)(2,1)S(1)} %constant_dynamic-update-slice_fusion.tokens_ref, bf16[1536,6144]{1,0:T(8,128)(2,1)} %weight_ref.13, bf16[256,3072]{1,0:T(8,128)(2,1)S(1)} %collective-permute-done.9.refs_1_.arrived_ref), custom_call_target="tpu_custom_call" | custom-call | flops 1 | bytes 1 | tf_op jit(solution)/shard_map/pallas_call | solution.py:221
  56.9 7.3 %collective-permute-done.11 = bf16[64,1536]{1,0:T(8,128)(2,1)S(1)} collective-permute-done((bf16[64,1536]{1,0:T(8,128)(2,1)S(1)}, bf16[64,1536]{1,0:T(8,128)(2,1)S(1)}, u32[]{:S(2)}, u32[]{:S(2)}) %collective-permute-start.11) | collective-permute-done | bytes 196640 | tf_op jit(solution)/shard_map/ppermute | solution.py:213
  67.9 7.4 %shard_map.186 = bf16[256,3072]{1,0:T(8,128)(2,1)S(1)} custom-call(s32[2]{0:T(128)S(1)} %pad_add_fusion.pos, bf16[256,1536]{1,0:T(8,128)(2,1)S(1)} %constant_dynamic-update-slice_fusion.4.tokens_ref, bf16[1536,6144]{1,0:T(8,128)(2,1)} %weight_ref.13), custom_call_target="tpu_custom_call" | custom-call | flops 1 | bytes 1 | tf_op jit(solution)/shard_map/pallas_call | solution.py:221
  75.3 5.5 %shard_map.185 = bf16[256,2304]{1,0:T(8,128)(2,1)S(1)} custom-call(s32[2]{0:T(128)S(1)} %pad_add_fusion.pos, bf16[256,1536]{1,0:T(8,128)(2,1)S(1)} %constant_dynamic-update-slice_fusion.4.tokens_ref, bf16[1536,1536]{1,0:T(8,128)(2,1)} %refs_0_.25, bf16[1536,1536]{1,0:T(8,128)(2,1)} %refs_1_.17, bf16[1536,1536]{1,0:T(8,128)(2,1)} %refs_2_.17), custom_call_target="tpu_custom_call" | custom-call | flops 1 | bytes 1 | tf_op jit(solution)/shard_map/pallas_call | solution.py:221
  80.9 4.4 %shard_map.187.refs_0_ = bf16[256,384]{1,0:T(8,128)(2,1)S(1)} custom-call(s32[2]{0:T(128)S(1)} %pad_add_fusion.pos, bf16[256,1536]{1,0:T(8,128)(2,1)S(1)} %constant_dynamic-update-slice_fusion.tokens_ref, bf16[1536,1536]{1,0:T(8,128)(2,1)} %refs_0_.25, bf16[1536,1536]{1,0:T(8,128)(2,1)} %refs_1_.17, bf16[1536,1536]{1,0:T(8,128)(2,1)} %refs_2_.17, ...), custom_call_target="tpu_custom_call" | custom-call | flops 1 | bytes 1 | tf_op jit(solution)/shard_map/pallas_call | solution.py:221
  87.4 4.8 %shard_map.188.refs_0_ = bf16[256,1536]{1,0:T(8,128)(2,1)S(1)} custom-call(s32[2]{0:T(128)S(1)} %pad_add_fusion.pos, bf16[256,1536]{1,0:T(8,128)(2,1)S(1)} %constant_dynamic-update-slice_fusion.tokens_ref, bf16[1536,6144]{1,0:T(8,128)(2,1)} %weight_ref.13, f32[1,6144]{1,0:T(1,128)S(1)} %bitcast.47, ...), custom_call_target="tpu_custom_call" | custom-call | flops 1 | bytes 1 | tf_op jit(solution)/shard_map/pallas_call | solution.py:221
  94.9 4.6 %shard_map.190 = (bf16[128,1536]{1,0:T(8,128)(2,1)S(1)}, bf16[128,1536]{1,0:T(8,128)(2,1)S(1)}) custom-call(s32[2]{0:T(128)S(1)} %pad_add_fusion.pos, bf16[256,1536]{1,0:T(8,128)(2,1)S(1)} %constant_dynamic-update-slice_fusion.4.tokens_ref, bf16[1536,6144]{1,0:T(8,128)(2,1)} %weight_ref.13, bf16[256,3072]{1,0:T(8,128)(2,1)S(1)} %collective-permute-done.16.refs_1_.arrived_ref), custom_call_target="tpu_custom_call" | custom-call | flops 1 | bytes 1 | tf_op jit(solution)/shard_map/pallas_call | solution.py:221
  103.5 8.8 %collective-permute-done.18.refs_0_ = bf16[256,1536]{1,0:T(8,128)(2,1)S(1)} collective-permute-done((bf16[256,1536]{1,0:T(8,128)(2,1)S(1)}, bf16[256,1536]{1,0:T(8,128)(2,1)S(1)}, u32[]{:S(2)}, u32[]{:S(2)}) %collective-permute-start.18) | collective-permute-done | bytes 786464 | tf_op jit(solution)/shard_map/ppermute | solution.py:200
  113.7 5.0 %shard_map.191.refs_2_ = f32[256,1536]{1,0:T(8,128)S(1)} custom-call(s32[2]{0:T(128)S(1)} %pad_add_fusion.pos, bf16[1536,1536]{1,0:T(8,128)(2,1)} %weight_ref.14, bf16[256,384]{1,0:T(8,128)(2,1)S(1)} %shard_map.187.refs_0_, bf16[256,384]{1,0:T(8,128)(2,1)S(1)} %collective-permute-done.14.refs_1_, bf16[256,384]{1,0:T(8,128)(2,1)S(1)} %collective-permute-done.13.refs_2_, ...), custom_call_target="tpu_custom_call" | custom-call | flops 1 | bytes 1 | tf_op jit(solution)/shard_map/pallas_call | solution.py:221
  118.7 7.4 %shard_map.192.refs_2_ = f32[256,1536]{1,0:T(8,128)S(1)} custom-call(s32[2]{0:T(128)S(1)} %pad_add_fusion.pos, bf16[6144,1536]{1,0:T(8,128)(2,1)} %weight_ref.16, bf16[256,1536]{1,0:T(8,128)(2,1)S(1)} %shard_map.188.refs_0_, bf16[256,1536]{1,0:T(8,128)(2,1)S(1)} %collective-permute-done.19.refs_1_, f32[256,1536]{1,0:T(8,128)S(1)} %shard_map.191.refs_2_), custom_call_target="tpu_custom_call" | custom-call | flops 1 | bytes 1 | tf_op jit(solution)/shard_map/pallas_call | solution.py:221
  129.5 7.0 %shard_map.193 = f32[256,1536]{1,0:T(8,128)S(1)} custom-call(s32[2]{0:T(128)S(1)} %pad_add_fusion.pos, bf16[6144,1536]{1,0:T(8,128)(2,1)} %weight_ref.16, bf16[256,1536]{1,0:T(8,128)(2,1)S(1)} %collective-permute-done.18.refs_0_, bf16[256,1536]{1,0:T(8,128)(2,1)S(1)} %collective-permute-done.20.refs_1_, f32[256,1536]{1,0:T(8,128)S(1)} %shard_map.192.refs_2_), custom_call_target="tpu_custom_call" | custom-call | flops 1 | bytes 1 | tf_op jit(solution)/shard_map/pallas_call | solution.py:221
  144.3 4.4 %shard_map.194.refs_0_ = bf16[256,384]{1,0:T(8,128)(2,1)S(1)} custom-call(s32[2]{0:T(128)S(1)} %pad_add_fusion.pos, bf16[256,1536]{1,0:T(8,128)(2,1)S(1)} %constant_dynamic-update-slice_fusion.4.tokens_ref, bf16[1536,1536]{1,0:T(8,128)(2,1)} %refs_0_.25, bf16[1536,1536]{1,0:T(8,128)(2,1)} %refs_1_.17, bf16[1536,1536]{1,0:T(8,128)(2,1)} %refs_2_.17, ...), custom_call_target="tpu_custom_call" | custom-call | flops 1 | bytes 1 | tf_op jit(solution)/shard_map/pallas_call | solution.py:221
  153.1 4.8 %shard_map.195 = (bf16[128,1536]{1,0:T(8,128)(2,1)S(1)}, bf16[128,1536]{1,0:T(8,128)(2,1)S(1)}) custom-call(s32[2]{0:T(128)S(1)} %pad_add_fusion.pos, bf16[256,1536]{1,0:T(8,128)(2,1)S(1)} %constant_dynamic-update-slice_fusion.4.tokens_ref, bf16[1536,6144]{1,0:T(8,128)(2,1)} %weight_ref.13, f32[1,6144]{1,0:T(1,128)S(1)} %bitcast.48, ...), custom_call_target="tpu_custom_call" | custom-call | flops 1 | bytes 1 | tf_op jit(solution)/shard_map/pallas_call | solution.py:221
  158.0 5.7 %collective-permute-done.28 = bf16[64,1536]{1,0:T(8,128)(2,1)S(1)} collective-permute-done((bf16[64,1536]{1,0:T(8,128)(2,1)S(1)}, bf16[64,1536]{1,0:T(8,128)(2,1)S(1)}, u32[]{:S(2)}, u32[]{:S(2)}) %collective-permute-start.28) | collective-permute-done | bytes 196640 | tf_op jit(solution)/shard_map/ppermute | solution.py:213
  167.5 7.4 %collective-permute-done.32 = f32[2,64]{1,0:T(2,128)S(1)} collective-permute-done((f32[2,64]{1,0:T(2,128)S(1)}, f32[2,64]{1,0:T(2,128)S(1)}, u32[]{:S(2)}, u32[]{:S(2)}) %collective-permute-start.32) | collective-permute-done | bytes 544 | tf_op jit(solution)/shard_map/ppermute | solution.py:200
  180.6 5.0 %shard_map.196.refs_4_ = f32[256,1536]{1,0:T(8,128)S(1)} custom-call(s32[2]{0:T(128)S(1)} %pad_add_fusion.pos, bf16[1536,1536]{1,0:T(8,128)(2,1)} %weight_ref.14, bf16[256,384]{1,0:T(8,128)(2,1)S(1)} %shard_map.194.refs_0_, bf16[256,384]{1,0:T(8,128)(2,1)S(1)} %collective-permute-done.27.refs_1_, bf16[256,384]{1,0:T(8,128)(2,1)S(1)} %collective-permute-done.26.refs_2_, ...), custom_call_target="tpu_custom_call" | custom-call | flops 1 | bytes 1 | tf_op jit(solution)/shard_map/pallas_call | solution.py:221
  191.2 7.0 %shard_map.197.refs_4_ = f32[256,1536]{1,0:T(8,128)S(1)} custom-call(s32[2]{0:T(128)S(1)} %pad_add_fusion.pos, bf16[6144,1536]{1,0:T(8,128)(2,1)} %weight_ref.16, bf16[128,1536]{1,0:T(8,128)(2,1)S(1)} %get-tuple-element.284.refs_0_, bf16[128,1536]{1,0:T(8,128)(2,1)S(1)} %get-tuple-element.285.refs_1_, bf16[128,1536]{1,0:T(8,128)(2,1)S(1)} %collective-permute-done.34.refs_2_, ...), custom_call_target="tpu_custom_call" | custom-call | flops 1 | bytes 1 | tf_op jit(solution)/shard_map/pallas_call | solution.py:221
  200.8 7.0 %shard_map.198 = f32[256,1536]{1,0:T(8,128)S(1)} custom-call(s32[2]{0:T(128)S(1)} %pad_add_fusion.pos, bf16[6144,1536]{1,0:T(8,128)(2,1)} %weight_ref.16, bf16[128,1536]{1,0:T(8,128)(2,1)S(1)} %collective-permute-done.30.refs_0_, bf16[128,1536]{1,0:T(8,128)(2,1)S(1)} %collective-permute-done.36.refs_1_, ...), custom_call_target="tpu_custom_call" | custom-call | flops 1 | bytes 1 | tf_op jit(solution)/shard_map/pallas_call | solution.py:221
  211.9 5.7 %shard_map.199 = bf16[256,2304]{1,0:T(8,128)(2,1)S(1)} custom-call(s32[2]{0:T(128)S(1)} %pad_add_fusion.pos, bf16[256,1536]{1,0:T(8,128)(2,1)S(1)} %constant_dynamic-update-slice_fusion.8.tokens_ref, bf16[1536,1536]{1,0:T(8,128)(2,1)} %refs_0_.31, bf16[1536,1536]{1,0:T(8,128)(2,1)} %refs_1_.23, bf16[1536,1536]{1,0:T(8,128)(2,1)} %refs_2_.23), custom_call_target="tpu_custom_call" | custom-call | flops 1 | bytes 1 | tf_op jit(solution)/shard_map/pallas_call | solution.py:221
  220.7 10.1 %collective-permute-done.45 = bf16[64,1536]{1,0:T(8,128)(2,1)S(1)} collective-permute-done((bf16[64,1536]{1,0:T(8,128)(2,1)S(1)}, bf16[64,1536]{1,0:T(8,128)(2,1)S(1)}, u32[]{:S(2)}, u32[]{:S(2)}) %collective-permute-start.45) | collective-permute-done | bytes 196640 | tf_op jit(solution)/shard_map/ppermute | solution.py:213
  241.8 5.8 %collective-permute-done.50 = bf16[64,1536]{1,0:T(8,128)(2,1)S(1)} collective-permute-done((bf16[64,1536]{1,0:T(8,128)(2,1)S(1)}, bf16[64,1536]{1,0:T(8,128)(2,1)S(1)}, u32[]{:S(2)}, u32[]{:S(2)}) %collective-permute-start.50) | collective-permute-done | bytes 196640 | tf_op jit(solution)/shard_map/ppermute | solution.py:213
  249.2 9.1 %collective-permute-done.52 = bf16[64,1536]{1,0:T(8,128)(2,1)S(1)} collective-permute-done((bf16[64,1536]{1,0:T(8,128)(2,1)S(1)}, bf16[64,1536]{1,0:T(8,128)(2,1)S(1)}, u32[]{:S(2)}, u32[]{:S(2)}) %collective-permute-start.52) | collective-permute-done | bytes 196640 | tf_op jit(solution)/shard_map/ppermute | solution.py:213
  258.4 5.5 %shard_map.201 = bf16[256,2304]{1,0:T(8,128)(2,1)S(1)} custom-call(s32[2]{0:T(128)S(1)} %pad_add_fusion.pos, bf16[256,1536]{1,0:T(8,128)(2,1)S(1)} %constant_dynamic-update-slice_fusion.12.tokens_ref, bf16[1536,1536]{1,0:T(8,128)(2,1)} %refs_0_.31, bf16[1536,1536]{1,0:T(8,128)(2,1)} %refs_1_.23, bf16[1536,1536]{1,0:T(8,128)(2,1)} %refs_2_.23), custom_call_target="tpu_custom_call" | custom-call | flops 1 | bytes 1 | tf_op jit(solution)/shard_map/pallas_call | solution.py:221
  264.1 4.0 %shard_map.202.refs_0_.refs_2_.refs_4_ = bf16[256,1152]{1,0:T(8,128)(2,1)S(1)} custom-call(s32[2]{0:T(128)S(1)} %pad_add_fusion.pos, bf16[256,1536]{1,0:T(8,128)(2,1)S(1)} %constant_dynamic-update-slice_fusion.8.tokens_ref, bf16[1536,1536]{1,0:T(8,128)(2,1)} %refs_0_.31, bf16[1536,1536]{1,0:T(8,128)(2,1)} %refs_1_.23, bf16[1536,1536]{1,0:T(8,128)(2,1)} %refs_2_.23, ...), custom_call_target="tpu_custom_call" | custom-call | flops 1 | bytes 1 | tf_op jit(solution)/shard_map/pallas_call | solution.py:221
  273.5 14.5 %collective-permute-done.54.refs_6_ = bf16[256,1152]{1,0:T(8,128)(2,1)S(1)} collective-permute-done((bf16[256,1152]{1,0:T(8,128)(2,1)S(1)}, bf16[256,1152]{1,0:T(8,128)(2,1)S(1)}, u32[]{:S(2)}, u32[]{:S(2)}) %collective-permute-start.54) | collective-permute-done | bytes 589856 | tf_op jit(solution)/shard_map/ppermute | solution.py:200
  296.7 9.5 %collective-permute-done.56.refs_2_ = bf16[512,384]{1,0:T(8,128)(2,1)S(1)} collective-permute-done((bf16[512,384]{1,0:T(8,128)(2,1)S(1)}, bf16[512,384]{1,0:T(8,128)(2,1)S(1)}, u32[]{:S(2)}, u32[]{:S(2)}) %collective-permute-start.56) | collective-permute-done | bytes 393248 | tf_op jit(solution)/shard_map/ppermute | solution.py:200
  307.9 6.2 %shard_map.206 = f32[512,1536]{1,0:T(8,128)S(1)} custom-call(s32[2]{0:T(128)S(1)} %pad_add_fusion.pos, bf16[1536,1536]{1,0:T(8,128)(2,1)} %weight_ref.17, bf16[512,384]{1,0:T(8,128)(2,1)S(1)} %bitcast.45, bf16[512,384]{1,0:T(8,128)(2,1)S(1)} %collective-permute-done.55.refs_1_, bf16[512,384]{1,0:T(8,128)(2,1)S(1)} %collective-permute-done.56.refs_2_, ...), custom_call_target="tpu_custom_call" | custom-call | flops 1 | bytes 1 | tf_op jit(solution)/shard_map/pallas_call | solution.py:221
  334.8 6.1 %collective-permute-done.59 = bf16[64,1536]{1,0:T(8,128)(2,1)S(1)} collective-permute-done((bf16[64,1536]{1,0:T(8,128)(2,1)S(1)}, bf16[64,1536]{1,0:T(8,128)(2,1)S(1)}, u32[]{:S(2)}, u32[]{:S(2)}) %collective-permute-start.59) | collective-permute-done | bytes 196640 | tf_op jit(solution)/shard_map/ppermute | solution.py:213
  (193 shorter events, 131.0 us)
Async XLA Ops:
  10.3 10.9 %collective-permute-start.4 = (bf16[64,1536]{1,0:T(8,128)(2,1)S(1)}, bf16[64,1536]{1,0:T(8,128)(2,1)S(1)}, u32[]{:S(2)}, u32[]{:S(2)}) collective-permute-start(bf16[64,1536]{1,0:T(8,128)(2,1)S(1)} %get-tuple-element.177), channel_id=1, source_target_pairs={{0,3},{1,0},{2,1},{3,2},{4,7},{5,4},{6,5},{7,6},{8,11},{9,8},{10,9... | collective-permute-start | bytes 589832 | tf_op jit(solution)/shard_map/ppermute | solution.py:213
  12.5 17.6 %collective-permute-start.5 = (bf16[64,1536]{1,0:T(8,128)(2,1)S(1)}, bf16[64,1536]{1,0:T(8,128)(2,1)S(1)}, u32[]{:S(2)}, u32[]{:S(2)}) collective-permute-start(bf16[64,1536]{1,0:T(8,128)(2,1)S(1)} %get-tuple-element.177), channel_id=1, source_target_pairs={{0,2},{1,3},{2,0},{3,1},{4,6},{5,7},{6,4},{7,5},{8,10},{9,11},{10,... | collective-permute-start | bytes 589832 | tf_op jit(solution)/shard_map/ppermute | solution.py:213
  51.6 15.6 %collective-permute-start.10 = (bf16[256,1152]{1,0:T(8,128)(2,1)S(1)}, bf16[256,1152]{1,0:T(8,128)(2,1)S(1)}, u32[]{:S(2)}, u32[]{:S(2)}) collective-permute-start(bf16[256,1152]{1,0:T(8,128)(2,1)S(1)} %shard_map.183), channel_id=1, source_target_pairs={{0,8},{4,12},{8,0},{12,4},{1,9},{5,13},{9,1},{13,5},{2,10},{6,14},... | collective-permute-start | bytes 1769480 | tf_op jit(solution)/shard_map/ppermute | solution.py:200
  52.2 12.0 %collective-permute-start.11 = (bf16[64,1536]{1,0:T(8,128)(2,1)S(1)}, bf16[64,1536]{1,0:T(8,128)(2,1)S(1)}, u32[]{:S(2)}, u32[]{:S(2)}) collective-permute-start(bf16[64,1536]{1,0:T(8,128)(2,1)S(1)} %get-tuple-element.197), channel_id=1, source_target_pairs={{0,2},{1,3},{2,0},{3,1},{4,6},{5,7},{6,4},{7,5},{8,10},{9,11},{10,... | collective-permute-start | bytes 589832 | tf_op jit(solution)/shard_map/ppermute | solution.py:213
  67.3 19.0 %collective-permute-start.12 = (bf16[256,1536]{1,0:T(8,128)(2,1)S(1)}, bf16[256,1536]{1,0:T(8,128)(2,1)S(1)}, u32[]{:S(2)}, u32[]{:S(2)}) collective-permute-start(bf16[256,1536]{1,0:T(8,128)(2,1)S(1)} %shard_map.184), channel_id=1, source_target_pairs={{0,8},{4,12},{8,0},{12,4},{1,9},{5,13},{9,1},{13,5},{2,10},{6,14},... | collective-permute-start | bytes 2359304 | tf_op jit(solution)/shard_map/ppermute | solution.py:200
  93.6 18.7 %collective-permute-start.18 = (bf16[256,1536]{1,0:T(8,128)(2,1)S(1)}, bf16[256,1536]{1,0:T(8,128)(2,1)S(1)}, u32[]{:S(2)}, u32[]{:S(2)}) collective-permute-start(bf16[256,1536]{1,0:T(8,128)(2,1)S(1)} %shard_map.188.refs_0_), channel_id=1, source_target_pairs={{0,8},{4,12},{8,0},{12,4},{1,9},{5,13},{9,1},{13,5},{2,10},{6,14},... | collective-permute-start | bytes 2359304 | tf_op jit(solution)/shard_map/ppermute | solution.py:200
  94.4 17.9 %collective-permute-start.19 = (bf16[256,1536]{1,0:T(8,128)(2,1)S(1)}, bf16[256,1536]{1,0:T(8,128)(2,1)S(1)}, u32[]{:S(2)}, u32[]{:S(2)}) collective-permute-start(bf16[256,1536]{1,0:T(8,128)(2,1)S(1)} %shard_map.188.refs_0_), channel_id=1, source_target_pairs={{0,4},{4,0},{8,12},{12,8},{1,5},{5,1},{9,13},{13,9},{2,6},{6,2},{1... | collective-permute-start | bytes 2359304 | tf_op jit(solution)/shard_map/ppermute | solution.py:200
  112.3 15.7 %collective-permute-start.20 = (bf16[256,1536]{1,0:T(8,128)(2,1)S(1)}, bf16[256,1536]{1,0:T(8,128)(2,1)S(1)}, u32[]{:S(2)}, u32[]{:S(2)}) collective-permute-start(bf16[256,1536]{1,0:T(8,128)(2,1)S(1)} %collective-permute-done.18.refs_0_), channel_id=1, source_target_pairs={{0,4},{4,0},{8,12},{12,8},{1,5},{5,1},{9,13},{13,9},{2,6},{6,2},{1... | collective-permute-start | bytes 2359304 | tf_op jit(solution)/shard_map/ppermute | solution.py:200
  112.3 15.7 %collective-permute-start.21 = (bf16[256,1152]{1,0:T(8,128)(2,1)S(1)}, bf16[256,1152]{1,0:T(8,128)(2,1)S(1)}, u32[]{:S(2)}, u32[]{:S(2)}) collective-permute-start(bf16[256,1152]{1,0:T(8,128)(2,1)S(1)} %shard_map.189), channel_id=1, source_target_pairs={{0,8},{4,12},{8,0},{12,4},{1,9},{5,13},{9,1},{13,5},{2,10},{6,14},... | collective-permute-start | bytes 1769480 | tf_op jit(solution)/shard_map/ppermute | solution.py:200
  128.0 10.7 %collective-permute-start.22 = (bf16[128,1536]{1,0:T(8,128)(2,1)S(1)}, bf16[128,1536]{1,0:T(8,128)(2,1)S(1)}, u32[]{:S(2)}, u32[]{:S(2)}) collective-permute-start(bf16[128,1536]{1,0:T(8,128)(2,1)S(1)} %get-tuple-element.241), channel_id=1, source_target_pairs={{0,8},{4,12},{8,0},{12,4},{1,9},{5,13},{9,1},{13,5},{2,10},{6,14},... | collective-permute-start | bytes 1179656 | tf_op jit(solution)/shard_map/ppermute | solution.py:200
  138.9 11.9 %collective-permute-start.23 = (bf16[128,1536]{1,0:T(8,128)(2,1)S(1)}, bf16[128,1536]{1,0:T(8,128)(2,1)S(1)}, u32[]{:S(2)}, u32[]{:S(2)}) collective-permute-start(bf16[128,1536]{1,0:T(8,128)(2,1)S(1)} %get-tuple-element.246), channel_id=1, source_target_pairs={{0,8},{4,12},{8,0},{12,4},{1,9},{5,13},{9,1},{13,5},{2,10},{6,14},... | collective-permute-start | bytes 1179656 | tf_op jit(solution)/shard_map/ppermute | solution.py:200
  151.5 12.2 %collective-permute-start.28 = (bf16[64,1536]{1,0:T(8,128)(2,1)S(1)}, bf16[64,1536]{1,0:T(8,128)(2,1)S(1)}, u32[]{:S(2)}, u32[]{:S(2)}) collective-permute-start(bf16[64,1536]{1,0:T(8,128)(2,1)S(1)} %get-tuple-element.260), channel_id=1, source_target_pairs={{0,2},{1,3},{2,0},{3,1},{4,6},{5,7},{6,4},{7,5},{8,10},{9,11},{10,... | collective-permute-start | bytes 589832 | tf_op jit(solution)/shard_map/ppermute | solution.py:213
  163.7 11.2 %collective-permute-start.30 = (bf16[128,1536]{1,0:T(8,128)(2,1)S(1)}, bf16[128,1536]{1,0:T(8,128)(2,1)S(1)}, u32[]{:S(2)}, u32[]{:S(2)}) collective-permute-start(bf16[128,1536]{1,0:T(8,128)(2,1)S(1)} %get-tuple-element.284.refs_0_), channel_id=1, source_target_pairs={{0,8},{4,12},{8,0},{12,4},{1,9},{5,13},{9,1},{13,5},{2,10},{6,14},... | collective-permute-start | bytes 1179656 | tf_op jit(solution)/shard_map/ppermute | solution.py:200
  175.0 13.3 %collective-permute-start.35 = (bf16[128,1536]{1,0:T(8,128)(2,1)S(1)}, bf16[128,1536]{1,0:T(8,128)(2,1)S(1)}, u32[]{:S(2)}, u32[]{:S(2)}) collective-permute-start(bf16[128,1536]{1,0:T(8,128)(2,1)S(1)} %get-tuple-element.285.refs_1_), channel_id=1, source_target_pairs={{0,4},{4,0},{8,12},{12,8},{1,5},{5,1},{9,13},{13,9},{2,6},{6,2},{1... | collective-permute-start | bytes 1179656 | tf_op jit(solution)/shard_map/ppermute | solution.py:200
  175.1 13.2 %collective-permute-start.36 = (bf16[128,1536]{1,0:T(8,128)(2,1)S(1)}, bf16[128,1536]{1,0:T(8,128)(2,1)S(1)}, u32[]{:S(2)}, u32[]{:S(2)}) collective-permute-start(bf16[128,1536]{1,0:T(8,128)(2,1)S(1)} %get-tuple-element.285.refs_1_), channel_id=1, source_target_pairs={{0,8},{4,12},{8,0},{12,4},{1,9},{5,13},{9,1},{13,5},{2,10},{6,14},... | collective-permute-start | bytes 1179656 | tf_op jit(solution)/shard_map/ppermute | solution.py:200
  176.4 11.8 %collective-permute-start.34 = (bf16[128,1536]{1,0:T(8,128)(2,1)S(1)}, bf16[128,1536]{1,0:T(8,128)(2,1)S(1)}, u32[]{:S(2)}, u32[]{:S(2)}) collective-permute-start(bf16[128,1536]{1,0:T(8,128)(2,1)S(1)} %get-tuple-element.284.refs_0_), channel_id=1, source_target_pairs={{0,4},{4,0},{8,12},{12,8},{1,5},{5,1},{9,13},{13,9},{2,6},{6,2},{1... | collective-permute-start | bytes 1179656 | tf_op jit(solution)/shard_map/ppermute | solution.py:200
  176.8 11.4 %collective-permute-start.38 = (bf16[64,1536]{1,0:T(8,128)(2,1)S(1)}, bf16[64,1536]{1,0:T(8,128)(2,1)S(1)}, u32[]{:S(2)}, u32[]{:S(2)}) collective-permute-start(bf16[64,1536]{1,0:T(8,128)(2,1)S(1)} %multiply_convert_fusion.2), channel_id=1, source_target_pairs={{0,3},{1,0},{2,1},{3,2},{4,7},{5,4},{6,5},{7,6},{8,11},{9,8},{10,9... | collective-permute-start | bytes 589832 | tf_op jit(solution)/shard_map/ppermute | solution.py:213
  188.2 12.6 %collective-permute-start.39 = (bf16[128,1536]{1,0:T(8,128)(2,1)S(1)}, bf16[128,1536]{1,0:T(8,128)(2,1)S(1)}, u32[]{:S(2)}, u32[]{:S(2)}) collective-permute-start(bf16[128,1536]{1,0:T(8,128)(2,1)S(1)} %collective-permute-done.30.refs_0_), channel_id=1, source_target_pairs={{0,4},{4,0},{8,12},{12,8},{1,5},{5,1},{9,13},{13,9},{2,6},{6,2},{1... | collective-permute-start | bytes 1179656 | tf_op jit(solution)/shard_map/ppermute | solution.py:200
  188.3 12.5 %collective-permute-start.40 = (bf16[128,1536]{1,0:T(8,128)(2,1)S(1)}, bf16[128,1536]{1,0:T(8,128)(2,1)S(1)}, u32[]{:S(2)}, u32[]{:S(2)}) collective-permute-start(bf16[128,1536]{1,0:T(8,128)(2,1)S(1)} %collective-permute-done.36.refs_1_), channel_id=1, source_target_pairs={{0,4},{4,0},{8,12},{12,8},{1,5},{5,1},{9,13},{13,9},{2,6},{6,2},{1... | collective-permute-start | bytes 1179656 | tf_op jit(solution)/shard_map/ppermute | solution.py:200
  188.8 12.0 %collective-permute-start.41 = (bf16[64,1536]{1,0:T(8,128)(2,1)S(1)}, bf16[64,1536]{1,0:T(8,128)(2,1)S(1)}, u32[]{:S(2)}, u32[]{:S(2)}) collective-permute-start(bf16[64,1536]{1,0:T(8,128)(2,1)S(1)} %multiply_convert_fusion.2), channel_id=1, source_target_pairs={{0,2},{1,3},{2,0},{3,1},{4,6},{5,7},{6,4},{7,5},{8,10},{9,11},{10,... | collective-permute-start | bytes 589832 | tf_op jit(solution)/shard_map/ppermute | solution.py:213
  218.3 12.4 %collective-permute-start.44 = (bf16[256,2304]{1,0:T(8,128)(2,1)S(1)}, bf16[256,2304]{1,0:T(8,128)(2,1)S(1)}, u32[]{:S(2)}, u32[]{:S(2)}) collective-permute-start(bf16[256,2304]{1,0:T(8,128)(2,1)S(1)} %shard_map.199), channel_id=1, source_target_pairs={{0,4},{4,0},{8,12},{12,8},{1,5},{5,1},{9,13},{13,9},{2,6},{6,2},{1... | collective-permute-start | bytes 3538952 | tf_op jit(solution)/shard_map/ppermute | solution.py:200
  218.3 12.4 %collective-permute-start.45 = (bf16[64,1536]{1,0:T(8,128)(2,1)S(1)}, bf16[64,1536]{1,0:T(8,128)(2,1)S(1)}, u32[]{:S(2)}, u32[]{:S(2)}) collective-permute-start(bf16[64,1536]{1,0:T(8,128)(2,1)S(1)} %get-tuple-element.311), channel_id=1, source_target_pairs={{0,2},{1,3},{2,0},{3,1},{4,6},{5,7},{6,4},{7,5},{8,10},{9,11},{10,... | collective-permute-start | bytes 589832 | tf_op jit(solution)/shard_map/ppermute | solution.py:213
  237.0 21.3 %collective-permute-start.49 = (bf16[256,1152]{1,0:T(8,128)(2,1)S(1)}, bf16[256,1152]{1,0:T(8,128)(2,1)S(1)}, u32[]{:S(2)}, u32[]{:S(2)}) collective-permute-start(bf16[256,1152]{1,0:T(8,128)(2,1)S(1)} %shard_map.200), channel_id=1, source_target_pairs={{0,8},{4,12},{8,0},{12,4},{1,9},{5,13},{9,1},{13,5},{2,10},{6,14},... | collective-permute-start | bytes 1769480 | tf_op jit(solution)/shard_map/ppermute | solution.py:200
  238.0 11.2 %collective-permute-start.51 = (bf16[64,1536]{1,0:T(8,128)(2,1)S(1)}, bf16[64,1536]{1,0:T(8,128)(2,1)S(1)}, u32[]{:S(2)}, u32[]{:S(2)}) collective-permute-start(bf16[64,1536]{1,0:T(8,128)(2,1)S(1)} %multiply_convert_fusion.1), channel_id=1, source_target_pairs={{0,3},{1,0},{2,1},{3,2},{4,7},{5,4},{6,5},{7,6},{8,11},{9,8},{10,9... | collective-permute-start | bytes 589832 | tf_op jit(solution)/shard_map/ppermute | solution.py:213
  241.8 16.5 %collective-permute-start.52 = (bf16[64,1536]{1,0:T(8,128)(2,1)S(1)}, bf16[64,1536]{1,0:T(8,128)(2,1)S(1)}, u32[]{:S(2)}, u32[]{:S(2)}) collective-permute-start(bf16[64,1536]{1,0:T(8,128)(2,1)S(1)} %multiply_convert_fusion.1), channel_id=1, source_target_pairs={{0,2},{1,3},{2,0},{3,1},{4,6},{5,7},{6,4},{7,5},{8,10},{9,11},{10,... | collective-permute-start | bytes 589832 | tf_op jit(solution)/shard_map/ppermute | solution.py:213
  272.2 15.8 %collective-permute-start.54 = (bf16[256,1152]{1,0:T(8,128)(2,1)S(1)}, bf16[256,1152]{1,0:T(8,128)(2,1)S(1)}, u32[]{:S(2)}, u32[]{:S(2)}) collective-permute-start(bf16[256,1152]{1,0:T(8,128)(2,1)S(1)} %shard_map.203), channel_id=1, source_target_pairs={{0,8},{4,12},{8,0},{12,4},{1,9},{5,13},{9,1},{13,5},{2,10},{6,14},... | collective-permute-start | bytes 1769480 | tf_op jit(solution)/shard_map/ppermute | solution.py:200
  295.4 10.8 %collective-permute-start.56 = (bf16[512,384]{1,0:T(8,128)(2,1)S(1)}, bf16[512,384]{1,0:T(8,128)(2,1)S(1)}, u32[]{:S(2)}, u32[]{:S(2)}) collective-permute-start(bf16[512,384]{1,0:T(8,128)(2,1)S(1)} %bitcast.43), channel_id=1, source_target_pairs={{0,8},{4,12},{8,0},{12,4},{1,9},{5,13},{9,1},{13,5},{2,10},{6,14},... | collective-permute-start | bytes 1179656 | tf_op jit(solution)/shard_map/ppermute | solution.py:200
  314.4 12.0 %collective-permute-start.62 = (bf16[64,1536]{1,0:T(8,128)(2,1)S(1)}, bf16[64,1536]{1,0:T(8,128)(2,1)S(1)}, u32[]{:S(2)}, u32[]{:S(2)}) collective-permute-start(bf16[64,1536]{1,0:T(8,128)(2,1)S(1)} %get-tuple-element.352), channel_id=1, source_target_pairs={{0,3},{1,0},{2,1},{3,2},{4,7},{5,4},{6,5},{7,6},{8,11},{9,8},{10,9... | collective-permute-start | bytes 589832 | tf_op jit(solution)/shard_map/ppermute | solution.py:213
  318.2 14.2 %collective-permute-start.60 = (bf16[64,1536]{1,0:T(8,128)(2,1)S(1)}, bf16[64,1536]{1,0:T(8,128)(2,1)S(1)}, u32[]{:S(2)}, u32[]{:S(2)}) collective-permute-start(bf16[64,1536]{1,0:T(8,128)(2,1)S(1)} %get-tuple-element.353), channel_id=1, source_target_pairs={{0,1},{1,2},{2,3},{3,0},{4,5},{5,6},{6,7},{7,4},{8,9},{9,10},{10,1... | collective-permute-start | bytes 589832 | tf_op jit(solution)/shard_map/ppermute | solution.py:213
  318.2 16.6 %collective-permute-start.61 = (bf16[64,1536]{1,0:T(8,128)(2,1)S(1)}, bf16[64,1536]{1,0:T(8,128)(2,1)S(1)}, u32[]{:S(2)}, u32[]{:S(2)}) collective-permute-start(bf16[64,1536]{1,0:T(8,128)(2,1)S(1)} %get-tuple-element.351), channel_id=1, source_target_pairs={{0,3},{1,0},{2,1},{3,2},{4,7},{5,4},{6,5},{7,6},{8,11},{9,8},{10,9... | collective-permute-start | bytes 589832 | tf_op jit(solution)/shard_map/ppermute | solution.py:213
  326.5 14.4 %collective-permute-start.59 = (bf16[64,1536]{1,0:T(8,128)(2,1)S(1)}, bf16[64,1536]{1,0:T(8,128)(2,1)S(1)}, u32[]{:S(2)}, u32[]{:S(2)}) collective-permute-start(bf16[64,1536]{1,0:T(8,128)(2,1)S(1)} %get-tuple-element.350), channel_id=1, source_target_pairs={{0,1},{1,2},{2,3},{3,0},{4,5},{5,6},{6,7},{7,4},{8,9},{9,10},{10,1... | collective-permute-start | bytes 589832 | tf_op jit(solution)/shard_map/ppermute | solution.py:213
  326.6 15.8 %collective-permute-start.63 = (bf16[64,1536]{1,0:T(8,128)(2,1)S(1)}, bf16[64,1536]{1,0:T(8,128)(2,1)S(1)}, u32[]{:S(2)}, u32[]{:S(2)}) collective-permute-start(bf16[64,1536]{1,0:T(8,128)(2,1)S(1)} %get-tuple-element.349), channel_id=1, source_target_pairs={{0,3},{1,0},{2,1},{3,2},{4,7},{5,4},{6,5},{7,6},{8,11},{9,8},{10,9... | collective-permute-start | bytes 589832 | tf_op jit(solution)/shard_map/ppermute | solution.py:213
  (42 other events, 336.9 us)

commit v3 on v2

--- a/solution.py
+++ b/solution.py
@@ -358,13 +358,13 @@
 
     def kernel(pos, tokens_ref, *refs):
         weight_refs, scale_refs = refs[:3], refs[3:5]
-        arrived_ref, side_ref, out_ref = refs[5:]
+        arrived_ref, *side_refs, out_ref = refs[5:]
         raws = []
         for i in range(3):
             at = slice(i * width, (i + 1) * width)
             raw = dot_f32(tokens_ref[...], weight_refs[i][...])
             raw = raw + arrived_ref[:, at].astype(jnp.float32)
-            raws.append(raw + side_ref[:, at].astype(jnp.float32))
+            raws.append(raw + joined_rows(side_refs, at).astype(jnp.float32))
         if attend_camera:
             row_cam = lax.broadcasted_iota(jnp.int32, (rows, rows), 0) // TOK_CAM
             col_cam = lax.broadcasted_iota(jnp.int32, (rows, rows), 1) // TOK_CAM
@@ -386,13 +386,13 @@
     return run(
         kernel,
         (1,),
-        (tokens, *weights, *scales, arrived, from_side),
+        (tokens, *weights, *scales, arrived, *from_side),
         (
             whole(tokens),
             *[weight_spec] * 3,
             *[scale_spec] * 2,
             pl.BlockSpec((rows, 3 * width), lambda s, pos: (0, pos[1])),
-            whole(from_side),
+            *[whole(piece) for piece in from_side],
         ),
         jax.ShapeDtypeStruct((rows, out_width), jnp.bfloat16),
         pl.BlockSpec((rows, out_width), lambda s, pos: (0, 0)),
@@ -496,6 +496,16 @@
 
 def sent(array, shift):
     return row_shift(array.astype(jnp.bfloat16), shift)
+
+
+def moment_shards(total):
+    return total, row_shift(total, 1), row_shift(total, -1), row_shift(total, 2)
+
+
+def normed_shards(shards, scales, totals):
+    return jnp.concatenate(
+        [normalize(x.astype(jnp.float32), scales, m) for x, m in zip(shards, totals)]
+    )
 
 
 def sync(*values):
@@ -552,8 +562,14 @@
     def heads_send(tokens, weights):
         return project_send(run, tokens, weights, head_width, 1)
 
-    def heads_across(tokens, weights, arrived):
-        return project_across(run, tokens, weights, head_width, 1, arrived)[0]
+    def heads_across(tokens, weights, arrived, pieces=1):
+        return project_across(run, tokens, weights, head_width, 1, arrived, pieces)
+
+    def heads_out(parts, first=0, start=None):
+        return contract(run, [(part,) for part in parts], out_weight, 1, first, start)
+
+    def units_down(parts, first, start):
+        return contract(run, parts, down_weight, 2, first, start)
 
     def units_send(tokens):
         return project_send(run, tokens, (up_weight,), unit_width, sub)
@@ -573,13 +589,21 @@
         return (start + total + down_bias).astype(jnp.bfloat16)
 
     start_f32 = camera_tokens.astype(jnp.float32)
-    pairs = sync(*moment_flips(moment_pair(start_f32)))
-    normed = normalize(start_f32, norm_gain, moment_sum(pairs))
-    own_a, own_b = normed[:half], normed[half:]
-    gathered = sync(own_b, own_a, sent(own_a, 1), sent(own_a, -1), sent(own_a, 2))
-    own_b, tok_a = gathered[0], jnp.concatenate(gathered[1:])
+    own_a, own_b = camera_tokens[:half], camera_tokens[half:]
+    pairs = moment_flips(moment_pair(start_f32))
+    own_a, own_b, a_before, a_after, *pairs = sync(
+        own_a, own_b, sent(own_a, 1), sent(own_a, -1), *pairs
+    )
+
+    totals = moment_shards(moment_sum(pairs))
+    own_a, own_b, a_before, a_after, a_away, *totals = sync(
+        own_a, own_b, a_before, a_after, sent(own_a, 2), *totals
+    )
+    totals_a = [total[:, :half] for total in totals]
+    totals_b = [total[:, half:] for total in totals]
 
     b_before = sent(own_b, 1)
+    tok_a = normed_shards((own_a, a_before, a_after, a_away), norm_gain, totals_a)
     qs_a = heads_send(tok_a, heads_in)
     tok_a, own_b, b_before, qs_a = sync(tok_a, own_b, b_before, qs_a)
 
@@ -588,7 +612,7 @@
     tok_a, own_b, b_after, qc_a, us_a = sync(tok_a, own_b, b_after, qc_a, us_a)
 
     uc_a = core_swap(us_a)
-    qx_a = heads_across(tok_a, heads_in, qc_a)
+    (qx_a,) = heads_across(tok_a, heads_in, qc_a)
     tok_a, own_b, qc_a, uc_a, qx_a = sync(tok_a, own_b, qc_a, uc_a, qx_a)
 
     qy_a, b_away = y_swap(qx_a), sent(own_b, 2)
@@ -598,10 +622,10 @@
     )
 
     uy_a = y_swap(ux_a)
-    tok_b = jnp.concatenate((own_b, b_before, b_after, b_away))
+    tok_b = normed_shards((own_b, b_before, b_after, b_away), norm_gain, totals_b)
     qs_b = heads_send(tok_b, heads_in)
     us_b = units_send(tok_b)
-    at_a = project_heads(run, tok_a, heads_in, scales, head_width, qc_a, qy_a, True)
+    at_a = project_heads(run, tok_a, heads_in, scales, head_width, qc_a, (qy_a,), True)
     tok_a, tok_b, qs_b, us_b, at_a, uc_a, uy_a = sync(
         tok_a, tok_b, qs_b, us_b, at_a, uc_a, uy_a
     )
@@ -613,61 +637,61 @@
     )
 
     hd_ya, hd_ca, at_fa = y_swap(hd_a), core_swap(hd_a), core_swap(at_ya)
-    qx_b = heads_across(tok_b, heads_in, qc_b)
+    (qx_b,) = heads_across(tok_b, heads_in, qc_b)
     ux_b = units_across(tok_b, uc_b, 2)
-    tok_b, at_a, at_ya, at_ca, at_fa, hd_a, hd_ya, hd_ca, qc_b, uc_b, qx_b, *ux_b = sync(
-        tok_b, at_a, at_ya, at_ca, at_fa, hd_a, hd_ya, hd_ca, qc_b, uc_b, qx_b, *ux_b
+    mixed_a = units_down(((hd_a,),), 0, heads_out((at_a, at_ca, at_ya)))
+    tok_b, at_fa, hd_ya, hd_ca, qc_b, uc_b, qx_b, mixed_a, *ux_b = sync(
+        tok_b, at_fa, hd_ya, hd_ca, qc_b, uc_b, qx_b, mixed_a, *ux_b
     )
 
     qy_b, hd_fa = y_swap(qx_b), core_swap(hd_ya)
-    mixed_a = contract(run, ((at_a,), (at_ca,), (at_ya,), (at_fa,)), out_weight, 1)
-    mixed_a = contract(run, ((hd_a,), (hd_ca,)), down_weight, 2, 0, mixed_a)
-    tok_b, hd_ya, hd_fa, mixed_a, qc_b, qy_b, uc_b, ux_b0, ux_b1 = sync(
-        tok_b, hd_ya, hd_fa, mixed_a, qc_b, qy_b, uc_b, *ux_b
+    mixed_a = units_down(((hd_ca,),), 1, heads_out((at_fa,), 3, mixed_a))
+    mixed_a = units_down(((hd_ya,), (hd_fa,)), 2, mixed_a)
+    tok_b, mixed_a, qc_b, qy_b, uc_b, ux_b0, ux_b1 = sync(
+        tok_b, mixed_a, qc_b, qy_b, uc_b, *ux_b
     )
 
     uy_b0 = y_swap(ux_b0)
-    mixed_a = contract(run, ((hd_ya,), (hd_fa,)), down_weight, 2, 2, mixed_a)
-    tok_b, mixed_a, qc_b, qy_b, uc_b, uy_b0, ux_b1 = sync(
-        tok_b, mixed_a, qc_b, qy_b, uc_b, uy_b0, ux_b1
-    )
-
-    uy_b1 = y_swap(ux_b1)
     mine_a, before_a, after_a, away_a = jnp.split(mixed_a, 4)
     from_before, from_after = sent(after_a, 1), sent(before_a, -1)
-    at_b = project_heads(run, tok_b, heads_in, scales, head_width, qc_b, qy_b, True)
-    tok_b, uc_b, uy_b0, uy_b1, at_b, mine_a, away_a, from_before, from_after = sync(
-        tok_b, uc_b, uy_b0, uy_b1, at_b, mine_a, away_a.astype(jnp.bfloat16), from_before, from_after
-    )
-
-    at_yb, at_cb, from_away = y_swap(at_b), core_swap(at_b), sent(away_a, 2)
+    at_b = project_heads(run, tok_b, heads_in, scales, head_width, qc_b, (qy_b,), True)
+    at_yb = y_swap(at_b)
+    tok_b, uc_b, uy_b0, ux_b1, at_b, at_yb, mine_a, away_a, from_before, from_after = sync(
+        tok_b, uc_b, uy_b0, ux_b1, at_b, at_yb, mine_a, away_a.astype(jnp.bfloat16),
+        from_before, from_after,
+    )
+
+    uy_b1, from_away, at_cb, at_fb = (
+        y_swap(ux_b1), sent(away_a, 2), core_swap(at_b), core_swap(at_yb)
+    )
+    tok_b, uc_b, uy_b0, uy_b1, at_b, at_cb, at_yb, at_fb, mine_a, *arrived = sync(
+        tok_b, uc_b, uy_b0, uy_b1, at_b, at_cb, at_yb, at_fb, mine_a,
+        from_before, from_after, from_away,
+    )
+
+    layer_a = layer_end(start_f32[:half], mine_a, *arrived)
+    pairs = moment_flips(moment_pair(layer_a.astype(jnp.float32)))
     hd_b = units_end(tok_b, uc_b, (uy_b0, uy_b1), 2)
-    at_b, at_yb, at_cb, hd_b0, hd_b1, mine_a, from_before, from_after, from_away = sync(
-        at_b, at_yb, at_cb, *hd_b, mine_a, from_before, from_after, from_away
-    )
-
-    hd_yb0, at_fb = y_swap(hd_b0), core_swap(at_yb)
-    layer_a = layer_end(start_f32[:half], mine_a, from_before, from_after, from_away)
-    pairs = moment_flips(moment_pair(layer_a.astype(jnp.float32)))
-    at_b, at_yb, at_cb, at_fb, hd_b0, hd_b1, hd_yb0, layer_a, *pairs = sync(
-        at_b, at_yb, at_cb, at_fb, hd_b0, hd_b1, hd_yb0, layer_a, *pairs
-    )
-
-    hd_yb1, hd_cb0, hd_cb1 = y_swap(hd_b1), core_swap(hd_b0), core_swap(hd_b1)
+    at_b, at_cb, at_yb, at_fb, hd_b0, hd_b1, layer_a, *pairs = sync(
+        at_b, at_cb, at_yb, at_fb, *hd_b, layer_a, *pairs
+    )
+
+    hd_yb0, hd_cb0, hd_cb1 = y_swap(hd_b0), core_swap(hd_b0), core_swap(hd_b1)
     join_a = normalize(layer_a.astype(jnp.float32), join_gain, moment_sum(pairs))
     ja_before, ja_after = sent(join_a, 1), sent(join_a, -1)
-    mixed_b = contract(run, ((at_b,), (at_cb,), (at_yb,), (at_fb,)), out_weight, 1)
-    hd_b0, hd_b1, hd_cb0, hd_cb1, hd_yb0, hd_yb1, mixed_b, join_a, ja_before, ja_after = sync(
-        hd_b0, hd_b1, hd_cb0, hd_cb1, hd_yb0, hd_yb1, mixed_b, join_a, ja_before, ja_after
-    )
-
-    hd_fb0, hd_fb1, ja_away = core_swap(hd_yb0), core_swap(hd_yb1), sent(join_a, 2)
-    mixed_b = contract(run, ((hd_b0, hd_b1), (hd_cb0, hd_cb1)), down_weight, 2, 0, mixed_b)
-    hd_yb0, hd_yb1, hd_fb0, hd_fb1, mixed_b, join_a, ja_before, ja_after, ja_away = sync(
-        hd_yb0, hd_yb1, hd_fb0, hd_fb1, mixed_b, join_a, ja_before, ja_after, ja_away
-    )
-
-    mixed_b = contract(run, ((hd_yb0, hd_yb1), (hd_fb0, hd_fb1)), down_weight, 2, 2, mixed_b)
+    mixed_b = units_down(((hd_b0, hd_b1),), 0, heads_out((at_b, at_cb, at_yb, at_fb)))
+    hd_b1, hd_cb0, hd_cb1, hd_yb0, mixed_b, layer_a, join_a, ja_before, ja_after = sync(
+        hd_b1, hd_cb0, hd_cb1, hd_yb0, mixed_b, layer_a, join_a, ja_before, ja_after
+    )
+
+    hd_yb1, ja_away = y_swap(hd_b1), sent(join_a, 2)
+    mixed_b = units_down(((hd_cb0, hd_cb1),), 1, mixed_b)
+    hd_yb0, hd_yb1, mixed_b, join_a, ja_before, ja_after, ja_away = sync(
+        hd_yb0, hd_yb1, mixed_b, join_a, ja_before, ja_after, ja_away
+    )
+
+    hd_fb0, hd_fb1 = core_swap(hd_yb0), core_swap(hd_yb1)
+    mixed_b = units_down(((hd_yb0, hd_yb1), (hd_fb0, hd_fb1)), 2, mixed_b)
     mixed_b, join_a, ja_before, ja_after, ja_away = sync(
         mixed_b, join_a, ja_before, ja_after, ja_away
     )
@@ -681,33 +705,38 @@
     )
 
     from_away, jc_a = sent(away_b, 2), core_swap(js_a)
-    tok_ja, jc_a, mine_b, from_before, from_after, from_away = sync(
-        tok_ja, jc_a, mine_b, from_before, from_after, from_away
-    )
-
-    layer_b = layer_end(start_f32[half:], mine_b, from_before, from_after, from_away)
+    jx_a = heads_across(tok_ja, join_in, jc_a, 2)
+    tok_ja, jc_a, jx_a0, jx_a1, mine_b, *arrived = sync(
+        tok_ja, jc_a, *jx_a, mine_b, from_before, from_after, from_away
+    )
+
+    layer_b = layer_end(start_f32[half:], mine_b, *arrived)
     pairs = moment_flips(moment_pair(layer_b.astype(jnp.float32)))
-    jx_a = heads_across(tok_ja, join_in, jc_a)
-    tok_ja, jc_a, jx_a, layer_b, *pairs = sync(tok_ja, jc_a, jx_a, layer_b, *pairs)
-
-    join_b = normalize(layer_b.astype(jnp.float32), join_gain, moment_sum(pairs))
-    jb_before, jb_after, jb_away = sent(join_b, 1), sent(join_b, -1), sent(join_b, 2)
-    jy_a = y_swap(jx_a)
-    tok_ja, jc_a, jy_a, join_b, jb_before, jb_after, jb_away = sync(
-        tok_ja, jc_a, jy_a, join_b, jb_before, jb_after, jb_away
-    )
-
-    tok_jb = jnp.concatenate((join_b, jb_before, jb_after, jb_away))
-    js_b = heads_send(tok_jb, join_in)
-    tok_ja, jc_a, jy_a, tok_jb, js_b = sync(tok_ja, jc_a, jy_a, tok_jb, js_b)
-
-    jc_b = core_swap(js_b)
-    parts_a = project_heads(run, tok_ja, join_in, join_scales, head_width, jc_a, jy_a, False)
-    tok_jb, jc_b, parts_a = sync(tok_jb, jc_b, parts_a)
-
-    jy_b = y_swap(heads_across(tok_jb, join_in, jc_b))
-    parts_b = project_heads(run, tok_jb, join_in, join_scales, head_width, jc_b, jy_b, False)
-
+    jb_before, jb_after, jy_a0 = sent(layer_b, 1), sent(layer_b, -1), y_swap(jx_a0)
+    tok_ja, jc_a, jy_a0, jx_a1, layer_b, jb_before, jb_after, *pairs = sync(
+        tok_ja, jc_a, jy_a0, jx_a1, layer_b, jb_before, jb_after, *pairs
+    )
+
+    totals = moment_shards(moment_sum(pairs))
+    jb_away, jy_a1 = sent(layer_b, 2), y_swap(jx_a1)
+    tok_ja, jc_a, jy_a0, jy_a1, layer_b, jb_before, jb_after, jb_away, *totals = sync(
+        tok_ja, jc_a, jy_a0, jy_a1, layer_b, jb_before, jb_after, jb_away, *totals
+    )
+
+    tok_jb = normed_shards((layer_b, jb_before, jb_after, jb_away), join_gain, totals)
+    jc_b = core_swap(heads_send(tok_jb, join_in))
+    (jx_b,) = heads_across(tok_jb, join_in, jc_b)
+    tok_ja, jc_a, jy_a0, jy_a1, tok_jb, jc_b, jx_b = sync(
+        tok_ja, jc_a, jy_a0, jy_a1, tok_jb, jc_b, jx_b
+    )
+
+    jy_b = y_swap(jx_b)
+    parts_a = project_heads(
+        run, tok_ja, join_in, join_scales, head_width, jc_a, (jy_a0, jy_a1), False
+    )
+    tok_jb, jc_b, jy_b, parts_a = sync(tok_jb, jc_b, jy_b, parts_a)
+
+    parts_b = project_heads(run, tok_jb, join_in, join_scales, head_width, jc_b, (jy_b,), False)
     joined = join_blend(run, (parts_a, parts_b))
     joined = joined.reshape(2, 4, half, head_width).swapaxes(0, 1).reshape(8 * half, head_width)
     jo_y, jo_c = y_swap(joined), core_swap(joined)

time: 347 us -> 332 us (0.957)
  waiting for transfers between devices: 138 us -> 104 us
  starting transfers between devices: 62 us -> 74.3 us
  Pallas kernels: 137 us -> 141 us
    ppermute x24 -> x30, waiting for transfers between devices: 83.9 us -> 62.9 us  [row_shift(): lax.ppermute(array, 'rows', [(i, (i + shift) % size) for i in range(size)])]
    ppermute x40 -> x41, waiting for transfers between devices: 54.5 us -> 41.3 us  [flip(): return lax.ppermute(array, 'cols', [(i, i ^ mask) for i in range(size)])]
    ppermute x24 -> x30, starting transfers between devices: 39 us -> 50.5 us  [row_shift(): lax.ppermute(array, 'rows', [(i, (i + shift) % size) for i in range(size)])]
    pallas_call x26 -> x29, Pallas kernels: 137 us -> 141 us  [__call__(): pl.pallas_call(kernel, out_shape=out_shape, grid_spec=pltpu.PrefetchScala...]
    ppermute x40 -> x41, starting transfers between devices: 23 us -> 23.8 us  [flip(): return lax.ppermute(array, 'cols', [(i, i ^ mask) for i in range(size)])]
  transfers between devices with their start and end apart: 64 -> 71, of which waited for: 34 -> 40; matrix products, arithmetic and copies ran while one was open for 0% -> 1% of each run, Pallas kernels for 31% -> 34%
where the time goes in v3:
time: 332 us; the launch traced here: 328 us
  Pallas kernels  141 us (42%)
  waiting for transfers between devices  104 us (31%)
  starting transfers between devices  74.3 us (22%)
  other arithmetic  5.5 us (2%)
    pallas_call x29, Pallas kernels, __call__(): pl.pallas_call(kernel, out_shape=out_shape, grid_spec=pltpu.PrefetchScala...  141 us
    ppermute x30, waiting for transfers between devices, row_shift(): lax.ppermute(array, 'rows', [(i, (i + shift) % size) for i in range(size)])  62.9 us
    ppermute x30, starting transfers between devices, row_shift(): lax.ppermute(array, 'rows', [(i, (i + shift) % size) for i in range(size)])  50.5 us
    ppermute x41, waiting for transfers between devices, flip(): return lax.ppermute(array, 'cols', [(i, i ^ mask) for i in range(size)])  41.3 us
    ppermute x41, starting transfers between devices, flip(): return lax.ppermute(array, 'cols', [(i, i ^ mask) for i in range(size)])  23.8 us
  transfers between devices with their start and end apart: 71, of which 40 were waited for; matrix products, arithmetic and copies ran while one was open for 1% of the time, Pallas kernels for 34%

profile of v3, /device:TPU:0, one launch (start us, length us, event | category | flops | bytes accessed | tf_op | source)
XLA Modules:
  0.0 328.1 jit_solution(1094051181285094699)
XLA Ops:
  28.1 5.5 %shard_map.181 = bf16[256,2304]{1,0:T(8,128)(2,1)S(1)} custom-call(s32[2]{0:T(128)S(1)} %pad_add_fusion.pos, bf16[256,1536]{1,0:T(8,128)(2,1)S(1)} %pad_maximum_fusion.tokens_ref, bf16[1536,1536]{1,0:T(8,128)(2,1)} %refs_0_.25, bf16[1536,1536]{1,0:T(8,128)(2,1)} %refs_1_.17, bf16[1536,1536]{1,0:T(8,128)(2,1)} %refs_2_.17), custom_call_target="tpu_custom_call" | custom-call | flops 1 | bytes 1 | tf_op jit(solution)/shard_map/pallas_call | solution.py:221
  37.2 7.4 %shard_map.182 = bf16[256,3072]{1,0:T(8,128)(2,1)S(1)} custom-call(s32[2]{0:T(128)S(1)} %pad_add_fusion.pos, bf16[256,1536]{1,0:T(8,128)(2,1)S(1)} %pad_maximum_fusion.tokens_ref, bf16[1536,6144]{1,0:T(8,128)(2,1)} %weight_ref.18), custom_call_target="tpu_custom_call" | custom-call | flops 1 | bytes 1 | tf_op jit(solution)/shard_map/pallas_call | solution.py:221
  50.5 4.6 %shard_map.184 = bf16[256,1536]{1,0:T(8,128)(2,1)S(1)} custom-call(s32[2]{0:T(128)S(1)} %pad_add_fusion.pos, bf16[256,1536]{1,0:T(8,128)(2,1)S(1)} %pad_maximum_fusion.tokens_ref, bf16[1536,6144]{1,0:T(8,128)(2,1)} %weight_ref.18, bf16[256,3072]{1,0:T(8,128)(2,1)S(1)} %collective-permute-done.12.refs_1_.arrived_ref), custom_call_target="tpu_custom_call" | custom-call | flops 1 | bytes 1 | tf_op jit(solution)/shard_map/pallas_call | solution.py:221
  55.1 6.3 %collective-permute-done.14 = bf16[64,1536]{1,0:T(8,128)(2,1)S(1)} collective-permute-done((bf16[64,1536]{1,0:T(8,128)(2,1)S(1)}, bf16[64,1536]{1,0:T(8,128)(2,1)S(1)}, u32[]{:S(2)}, u32[]{:S(2)}) %collective-permute-start.14) | collective-permute-done | bytes 196640 | tf_op jit(solution)/shard_map/ppermute | solution.py:213
  66.8 7.4 %shard_map.186 = bf16[256,3072]{1,0:T(8,128)(2,1)S(1)} custom-call(s32[2]{0:T(128)S(1)} %pad_add_fusion.pos, bf16[256,1536]{1,0:T(8,128)(2,1)S(1)} %pad_maximum_fusion.1.tokens_ref, bf16[1536,6144]{1,0:T(8,128)(2,1)} %weight_ref.18), custom_call_target="tpu_custom_call" | custom-call | flops 1 | bytes 1 | tf_op jit(solution)/shard_map/pallas_call | solution.py:221
  74.1 5.5 %shard_map.185 = bf16[256,2304]{1,0:T(8,128)(2,1)S(1)} custom-call(s32[2]{0:T(128)S(1)} %pad_add_fusion.pos, bf16[256,1536]{1,0:T(8,128)(2,1)S(1)} %pad_maximum_fusion.1.tokens_ref, bf16[1536,1536]{1,0:T(8,128)(2,1)} %refs_0_.25, bf16[1536,1536]{1,0:T(8,128)(2,1)} %refs_1_.17, bf16[1536,1536]{1,0:T(8,128)(2,1)} %refs_2_.17), custom_call_target="tpu_custom_call" | custom-call | flops 1 | bytes 1 | tf_op jit(solution)/shard_map/pallas_call | solution.py:221
  79.7 4.4 %shard_map.187.refs_0_ = bf16[256,384]{1,0:T(8,128)(2,1)S(1)} custom-call(s32[2]{0:T(128)S(1)} %pad_add_fusion.pos, bf16[256,1536]{1,0:T(8,128)(2,1)S(1)} %pad_maximum_fusion.tokens_ref, bf16[1536,1536]{1,0:T(8,128)(2,1)} %refs_0_.25, bf16[1536,1536]{1,0:T(8,128)(2,1)} %refs_1_.17, bf16[1536,1536]{1,0:T(8,128)(2,1)} %refs_2_.17, ...), custom_call_target="tpu_custom_call" | custom-call | flops 1 | bytes 1 | tf_op jit(solution)/shard_map/pallas_call | solution.py:221
  85.6 4.8 %shard_map.188.refs_0_ = bf16[256,1536]{1,0:T(8,128)(2,1)S(1)} custom-call(s32[2]{0:T(128)S(1)} %pad_add_fusion.pos, bf16[256,1536]{1,0:T(8,128)(2,1)S(1)} %pad_maximum_fusion.tokens_ref, bf16[1536,6144]{1,0:T(8,128)(2,1)} %weight_ref.18, f32[1,6144]{1,0:T(1,128)S(1)} %bitcast.147, bf16[256,3072]{1,0:T(8,128)(2,1)S(1)} %collective-permute-done.12.refs_1_.arrived_ref, ...), custom_call_target="tpu_custom_call" | custom-call | flops 1 | bytes 1 | tf_op jit(solution)/shard_map/pallas_call | solution.py:221
  92.9 4.6 %shard_map.192 = (bf16[128,1536]{1,0:T(8,128)(2,1)S(1)}, bf16[128,1536]{1,0:T(8,128)(2,1)S(1)}) custom-call(s32[2]{0:T(128)S(1)} %pad_add_fusion.pos, bf16[256,1536]{1,0:T(8,128)(2,1)S(1)} %pad_maximum_fusion.1.tokens_ref, bf16[1536,6144]{1,0:T(8,128)(2,1)} %weight_ref.18, bf16[256,3072]{1,0:T(8,128)(2,1)S(1)} %collective-permute-done.19.refs_1_.arrived_ref), custom_call_target="tpu_custom_call" | custom-call | flops 1 | bytes 1 | tf_op jit(solution)/shard_map/pallas_call | solution.py:221
  97.6 4.0 %shard_map.189 = bf16[256,1152]{1,0:T(8,128)(2,1)S(1)} custom-call(s32[2]{0:T(128)S(1)} %pad_add_fusion.pos, bf16[256,1536]{1,0:T(8,128)(2,1)S(1)} %pad_maximum_fusion.1.tokens_ref, bf16[1536,1536]{1,0:T(8,128)(2,1)} %refs_0_.25, bf16[1536,1536]{1,0:T(8,128)(2,1)} %refs_1_.17, bf16[1536,1536]{1,0:T(8,128)(2,1)} %refs_2_.17, ...), custom_call_target="tpu_custom_call" | custom-call | flops 1 | bytes 1 | tf_op jit(solution)/shard_map/pallas_call | solution.py:221
  101.5 4.3 %shard_map.190.refs_1_ = f32[256,1536]{1,0:T(8,128)S(1)} custom-call(s32[2]{0:T(128)S(1)} %pad_add_fusion.pos, bf16[1536,1536]{1,0:T(8,128)(2,1)} %weight_ref.19, bf16[256,384]{1,0:T(8,128)(2,1)S(1)} %shard_map.187.refs_0_, bf16[256,384]{1,0:T(8,128)(2,1)S(1)} %collective-permute-done.17.refs_1_, bf16[256,384]{1,0:T(8,128)(2,1)S(1)} %collective-permute-done.16.refs_2_), custom_call_target="tpu_custom_call" | custom-call | flops 1 | bytes 1 | tf_op jit(solution)/shard_map/pallas_call | solution.py:221
  105.8 4.2 %shard_map.191.refs_1_ = f32[256,1536]{1,0:T(8,128)S(1)} custom-call(s32[2]{0:T(128)S(1)} %pad_add_fusion.pos, bf16[6144,1536]{1,0:T(8,128)(2,1)} %weight_ref.22, bf16[256,1536]{1,0:T(8,128)(2,1)S(1)} %shard_map.188.refs_0_, f32[256,1536]{1,0:T(8,128)S(1)} %shard_map.190.refs_1_), custom_call_target="tpu_custom_call" | custom-call | flops 1 | bytes 1 | tf_op jit(solution)/shard_map/pallas_call | solution.py:221
  114.1 4.6 %shard_map.194.refs_2_ = f32[256,1536]{1,0:T(8,128)S(1)} custom-call(s32[2]{0:T(128)S(1)} %pad_add_fusion.pos, bf16[6144,1536]{1,0:T(8,128)(2,1)} %weight_ref.22, bf16[256,1536]{1,0:T(8,128)(2,1)S(1)} %collective-permute-done.22.refs_0_, f32[256,1536]{1,0:T(8,128)S(1)} %shard_map.193.refs_1_), custom_call_target="tpu_custom_call" | custom-call | flops 1 | bytes 1 | tf_op jit(solution)/shard_map/pallas_call | solution.py:221
  118.7 7.0 %shard_map.195 = f32[256,1536]{1,0:T(8,128)S(1)} custom-call(s32[2]{0:T(128)S(1)} %pad_add_fusion.pos, bf16[6144,1536]{1,0:T(8,128)(2,1)} %weight_ref.22, bf16[256,1536]{1,0:T(8,128)(2,1)S(1)} %collective-permute-done.21.refs_0_, bf16[256,1536]{1,0:T(8,128)(2,1)S(1)} %collective-permute-done.23.refs_1_, f32[256,1536]{1,0:T(8,128)S(1)} %shard_map.194.refs_2_), custom_call_target="tpu_custom_call" | custom-call | flops 1 | bytes 1 | tf_op jit(solution)/shard_map/pallas_call | solution.py:221
  131.5 4.4 %shard_map.196.refs_0_ = bf16[256,384]{1,0:T(8,128)(2,1)S(1)} custom-call(s32[2]{0:T(128)S(1)} %pad_add_fusion.pos, bf16[256,1536]{1,0:T(8,128)(2,1)S(1)} %pad_maximum_fusion.1.tokens_ref, bf16[1536,1536]{1,0:T(8,128)(2,1)} %refs_0_.25, bf16[1536,1536]{1,0:T(8,128)(2,1)} %refs_1_.17, bf16[1536,1536]{1,0:T(8,128)(2,1)} %refs_2_.17, ...), custom_call_target="tpu_custom_call" | custom-call | flops 1 | bytes 1 | tf_op jit(solution)/shard_map/pallas_call | solution.py:221
  144.3 9.6 %collective-permute-done.32 = bf16[64,1536]{1,0:T(8,128)(2,1)S(1)} collective-permute-done((bf16[64,1536]{1,0:T(8,128)(2,1)S(1)}, bf16[64,1536]{1,0:T(8,128)(2,1)S(1)}, u32[]{:S(2)}, u32[]{:S(2)}) %collective-permute-start.32) | collective-permute-done | bytes 196640 | tf_op jit(solution)/shard_map/ppermute | solution.py:213
  156.1 4.8 %shard_map.197 = (bf16[128,1536]{1,0:T(8,128)(2,1)S(1)}, bf16[128,1536]{1,0:T(8,128)(2,1)S(1)}) custom-call(s32[2]{0:T(128)S(1)} %pad_add_fusion.pos, bf16[256,1536]{1,0:T(8,128)(2,1)S(1)} %pad_maximum_fusion.1.tokens_ref, bf16[1536,6144]{1,0:T(8,128)(2,1)} %weight_ref.18, f32[1,6144]{1,0:T(1,128)S(1)} %bitcast.148, ...), custom_call_target="tpu_custom_call" | custom-call | flops 1 | bytes 1 | tf_op jit(solution)/shard_map/pallas_call | solution.py:221
  166.5 5.0 %shard_map.198.refs_2_ = f32[256,1536]{1,0:T(8,128)S(1)} custom-call(s32[2]{0:T(128)S(1)} %pad_add_fusion.pos, bf16[1536,1536]{1,0:T(8,128)(2,1)} %weight_ref.19, bf16[256,384]{1,0:T(8,128)(2,1)S(1)} %shard_map.196.refs_0_, bf16[256,384]{1,0:T(8,128)(2,1)S(1)} %collective-permute-done.30.refs_1_, bf16[256,384]{1,0:T(8,128)(2,1)S(1)} %collective-permute-done.26.refs_2_, ...), custom_call_target="tpu_custom_call" | custom-call | flops 1 | bytes 1 | tf_op jit(solution)/shard_map/pallas_call | solution.py:221
  171.5 4.2 %shard_map.199.refs_2_ = f32[256,1536]{1,0:T(8,128)S(1)} custom-call(s32[2]{0:T(128)S(1)} %pad_add_fusion.pos, bf16[6144,1536]{1,0:T(8,128)(2,1)} %weight_ref.22, bf16[128,1536]{1,0:T(8,128)(2,1)S(1)} %get-tuple-element.282.refs_0_, bf16[128,1536]{1,0:T(8,128)(2,1)S(1)} %get-tuple-element.294.refs_1_, f32[256,1536]{1,0:T(8,128)S(1)} %shard_map.198.refs_2_), custom_call_target="tpu_custom_call" | custom-call | flops 1 | bytes 1 | tf_op jit(solution)/shard_map/pallas_call | solution.py:221
  177.7 4.2 %shard_map.200.refs_4_ = f32[256,1536]{1,0:T(8,128)S(1)} custom-call(s32[2]{0:T(128)S(1)} %pad_add_fusion.pos, bf16[6144,1536]{1,0:T(8,128)(2,1)} %weight_ref.22, bf16[128,1536]{1,0:T(8,128)(2,1)S(1)} %collective-permute-done.36.refs_0_, bf16[128,1536]{1,0:T(8,128)(2,1)S(1)} %collective-permute-done.37.refs_1_, f32[256,1536]{1,0:T(8,128)S(1)} %shard_map.199.refs_2_), custom_call_target="tpu_custom_call" | custom-call | flops 1 | bytes 1 | tf_op jit(solution)/shard_map/pallas_call | solution.py:221
  181.9 5.5 %collective-permute-done.42 = bf16[64,1536]{1,0:T(8,128)(2,1)S(1)} collective-permute-done((bf16[64,1536]{1,0:T(8,128)(2,1)S(1)}, bf16[64,1536]{1,0:T(8,128)(2,1)S(1)}, u32[]{:S(2)}, u32[]{:S(2)}) %collective-permute-start.42) | collective-permute-done | bytes 196640 | tf_op jit(solution)/shard_map/ppermute | solution.py:213
  189.7 7.0 %shard_map.201 = f32[256,1536]{1,0:T(8,128)S(1)} custom-call(s32[2]{0:T(128)S(1)} %pad_add_fusion.pos, bf16[6144,1536]{1,0:T(8,128)(2,1)} %weight_ref.22, bf16[128,1536]{1,0:T(8,128)(2,1)S(1)} %collective-permute-done.38.refs_0_, bf16[128,1536]{1,0:T(8,128)(2,1)S(1)} %collective-permute-done.41.refs_1_, ...), custom_call_target="tpu_custom_call" | custom-call | flops 1 | bytes 1 | tf_op jit(solution)/shard_map/pallas_call | solution.py:221
  200.8 5.7 %shard_map.202 = bf16[256,2304]{1,0:T(8,128)(2,1)S(1)} custom-call(s32[2]{0:T(128)S(1)} %pad_add_fusion.pos, bf16[256,1536]{1,0:T(8,128)(2,1)S(1)} %constant_dynamic-update-slice_fusion.tokens_ref, bf16[1536,1536]{1,0:T(8,128)(2,1)} %refs_0_.31, bf16[1536,1536]{1,0:T(8,128)(2,1)} %refs_1_.23, bf16[1536,1536]{1,0:T(8,128)(2,1)} %refs_2_.23), custom_call_target="tpu_custom_call" | custom-call | flops 1 | bytes 1 | tf_op jit(solution)/shard_map/pallas_call | solution.py:221
  215.0 5.6 %collective-permute-done.48 = bf16[64,1536]{1,0:T(8,128)(2,1)S(1)} collective-permute-done((bf16[64,1536]{1,0:T(8,128)(2,1)S(1)}, bf16[64,1536]{1,0:T(8,128)(2,1)S(1)}, u32[]{:S(2)}, u32[]{:S(2)}) %collective-permute-start.48) | collective-permute-done | bytes 196640 | tf_op jit(solution)/shard_map/ppermute | solution.py:213
  244.9 5.5 %shard_map.204 = bf16[256,2304]{1,0:T(8,128)(2,1)S(1)} custom-call(s32[2]{0:T(128)S(1)} %pad_add_fusion.pos, bf16[256,1536]{1,0:T(8,128)(2,1)S(1)} %pad_maximum_fusion.2.tokens_ref, bf16[1536,1536]{1,0:T(8,128)(2,1)} %refs_0_.31, bf16[1536,1536]{1,0:T(8,128)(2,1)} %refs_1_.23, bf16[1536,1536]{1,0:T(8,128)(2,1)} %refs_2_.23), custom_call_target="tpu_custom_call" | custom-call | flops 1 | bytes 1 | tf_op jit(solution)/shard_map/pallas_call | solution.py:221
  253.4 4.0 %shard_map.205 = bf16[256,1152]{1,0:T(8,128)(2,1)S(1)} custom-call(s32[2]{0:T(128)S(1)} %pad_add_fusion.pos, bf16[256,1536]{1,0:T(8,128)(2,1)S(1)} %pad_maximum_fusion.2.tokens_ref, bf16[1536,1536]{1,0:T(8,128)(2,1)} %refs_0_.31, bf16[1536,1536]{1,0:T(8,128)(2,1)} %refs_1_.23, bf16[1536,1536]{1,0:T(8,128)(2,1)} %refs_2_.23, ...), custom_call_target="tpu_custom_call" | custom-call | flops 1 | bytes 1 | tf_op jit(solution)/shard_map/pallas_call | solution.py:221
  258.6 4.0 %shard_map.206.refs_0_.refs_2_.refs_4_ = bf16[256,1152]{1,0:T(8,128)(2,1)S(1)} custom-call(s32[2]{0:T(128)S(1)} %pad_add_fusion.pos, bf16[256,1536]{1,0:T(8,128)(2,1)S(1)} %constant_dynamic-update-slice_fusion.tokens_ref, bf16[1536,1536]{1,0:T(8,128)(2,1)} %refs_0_.31, bf16[1536,1536]{1,0:T(8,128)(2,1)} %refs_1_.23, bf16[1536,1536]{1,0:T(8,128)(2,1)} %refs_2_.23, ...), custom_call_target="tpu_custom_call" | custom-call | flops 1 | bytes 1 | tf_op jit(solution)/shard_map/pallas_call | solution.py:221
  262.7 10.1 %collective-permute-done.61.refs_6_ = bf16[256,1152]{1,0:T(8,128)(2,1)S(1)} collective-permute-done((bf16[256,1152]{1,0:T(8,128)(2,1)S(1)}, bf16[256,1152]{1,0:T(8,128)(2,1)S(1)}, u32[]{:S(2)}, u32[]{:S(2)}) %collective-permute-start.61) | collective-permute-done | bytes 589856 | tf_op jit(solution)/shard_map/ppermute | solution.py:200
  272.8 4.0 %shard_map.207.refs_1_.refs_3_.refs_5_ = bf16[256,1152]{1,0:T(8,128)(2,1)S(1)} custom-call(s32[2]{0:T(128)S(1)} %pad_add_fusion.pos, bf16[256,1536]{1,0:T(8,128)(2,1)S(1)} %pad_maximum_fusion.2.tokens_ref, bf16[1536,1536]{1,0:T(8,128)(2,1)} %refs_0_.31, bf16[1536,1536]{1,0:T(8,128)(2,1)} %refs_1_.23, bf16[1536,1536]{1,0:T(8,128)(2,1)} %refs_2_.23, ...), custom_call_target="tpu_custom_call" | custom-call | flops 1 | bytes 1 | tf_op jit(solution)/shard_map/pallas_call | solution.py:221
  281.5 9.1 %collective-permute-done.63.refs_2_ = bf16[512,384]{1,0:T(8,128)(2,1)S(1)} collective-permute-done((bf16[512,384]{1,0:T(8,128)(2,1)S(1)}, bf16[512,384]{1,0:T(8,128)(2,1)S(1)}, u32[]{:S(2)}, u32[]{:S(2)}) %collective-permute-start.63) | collective-permute-done | bytes 393248 | tf_op jit(solution)/shard_map/ppermute | solution.py:200
  292.4 6.2 %shard_map.209 = f32[512,1536]{1,0:T(8,128)S(1)} custom-call(s32[2]{0:T(128)S(1)} %pad_add_fusion.pos, bf16[1536,1536]{1,0:T(8,128)(2,1)} %weight_ref.23, bf16[512,384]{1,0:T(8,128)(2,1)S(1)} %bitcast.145, bf16[512,384]{1,0:T(8,128)(2,1)S(1)} %collective-permute-done.62.refs_1_, bf16[512,384]{1,0:T(8,128)(2,1)S(1)} %collective-permute-done.63.refs_2_, ...), custom_call_target="tpu_custom_call" | custom-call | flops 1 | bytes 1 | tf_op jit(solution)/shard_map/pallas_call | solution.py:221
  319.5 5.9 %collective-permute-done.66 = bf16[64,1536]{1,0:T(8,128)(2,1)S(1)} collective-permute-done((bf16[64,1536]{1,0:T(8,128)(2,1)S(1)}, bf16[64,1536]{1,0:T(8,128)(2,1)S(1)}, u32[]{:S(2)}, u32[]{:S(2)}) %collective-permute-start.66) | collective-permute-done | bytes 196640 | tf_op jit(solution)/shard_map/ppermute | solution.py:213
  (212 shorter events, 147.3 us)
Async XLA Ops:
  1.1 11.2 %collective-permute-start = (bf16[64,1536]{1,0:T(8,128)(2,1)S(1)}, bf16[64,1536]{1,0:T(8,128)(2,1)S(1)}, u32[]{:S(2)}, u32[]{:S(2)}) collective-permute-start(bf16[64,1536]{1,0:T(8,128)(2,1)S(1)} %get-tuple-element.192), channel_id=1, source_target_pairs={{0,1},{1,2},{2,3},{3,0},{4,5},{5,6},{6,7},{7,4},{8,9},{9,10},{10,1... | collective-permute-start | bytes 589832 | tf_op jit(solution)/shard_map/ppermute | solution.py:213
  14.7 11.4 %collective-permute-start.5 = (bf16[64,1536]{1,0:T(8,128)(2,1)S(1)}, bf16[64,1536]{1,0:T(8,128)(2,1)S(1)}, u32[]{:S(2)}, u32[]{:S(2)}) collective-permute-start(bf16[64,1536]{1,0:T(8,128)(2,1)S(1)} %get-tuple-element.192), channel_id=1, source_target_pairs={{0,2},{1,3},{2,0},{3,1},{4,6},{5,7},{6,4},{7,5},{8,10},{9,11},{10,... | collective-permute-start | bytes 589832 | tf_op jit(solution)/shard_map/ppermute | solution.py:213
  33.9 10.7 %collective-permute-start.11 = (bf16[256,2304]{1,0:T(8,128)(2,1)S(1)}, bf16[256,2304]{1,0:T(8,128)(2,1)S(1)}, u32[]{:S(2)}, u32[]{:S(2)}) collective-permute-start(bf16[256,2304]{1,0:T(8,128)(2,1)S(1)} %shard_map.181), channel_id=1, source_target_pairs={{0,4},{4,0},{8,12},{12,8},{1,5},{5,1},{9,13},{13,9},{2,6},{6,2},{1... | collective-permute-start | bytes 3538952 | tf_op jit(solution)/shard_map/ppermute | solution.py:200
  33.9 10.7 %collective-permute-start.10 = (bf16[64,1536]{1,0:T(8,128)(2,1)S(1)}, bf16[64,1536]{1,0:T(8,128)(2,1)S(1)}, u32[]{:S(2)}, u32[]{:S(2)}) collective-permute-start(bf16[64,1536]{1,0:T(8,128)(2,1)S(1)} %get-tuple-element.216), channel_id=1, source_target_pairs={{0,3},{1,0},{2,1},{3,2},{4,7},{5,4},{6,5},{7,6},{8,11},{9,8},{10,9... | collective-permute-start | bytes 589832 | tf_op jit(solution)/shard_map/ppermute | solution.py:213
  48.9 15.7 %collective-permute-start.13 = (bf16[256,1152]{1,0:T(8,128)(2,1)S(1)}, bf16[256,1152]{1,0:T(8,128)(2,1)S(1)}, u32[]{:S(2)}, u32[]{:S(2)}) collective-permute-start(bf16[256,1152]{1,0:T(8,128)(2,1)S(1)} %shard_map.183), channel_id=1, source_target_pairs={{0,8},{4,12},{8,0},{12,4},{1,9},{5,13},{9,1},{13,5},{2,10},{6,14},... | collective-permute-start | bytes 1769480 | tf_op jit(solution)/shard_map/ppermute | solution.py:200
  50.5 10.9 %collective-permute-start.14 = (bf16[64,1536]{1,0:T(8,128)(2,1)S(1)}, bf16[64,1536]{1,0:T(8,128)(2,1)S(1)}, u32[]{:S(2)}, u32[]{:S(2)}) collective-permute-start(bf16[64,1536]{1,0:T(8,128)(2,1)S(1)} %get-tuple-element.216), channel_id=1, source_target_pairs={{0,2},{1,3},{2,0},{3,1},{4,6},{5,7},{6,4},{7,5},{8,10},{9,11},{10,... | collective-permute-start | bytes 589832 | tf_op jit(solution)/shard_map/ppermute | solution.py:213
  64.5 19.6 %collective-permute-start.15 = (bf16[256,1536]{1,0:T(8,128)(2,1)S(1)}, bf16[256,1536]{1,0:T(8,128)(2,1)S(1)}, u32[]{:S(2)}, u32[]{:S(2)}) collective-permute-start(bf16[256,1536]{1,0:T(8,128)(2,1)S(1)} %shard_map.184), channel_id=1, source_target_pairs={{0,8},{4,12},{8,0},{12,4},{1,9},{5,13},{9,1},{13,5},{2,10},{6,14},... | collective-permute-start | bytes 2359304 | tf_op jit(solution)/shard_map/ppermute | solution.py:200
  91.6 18.8 %collective-permute-start.21 = (bf16[256,1536]{1,0:T(8,128)(2,1)S(1)}, bf16[256,1536]{1,0:T(8,128)(2,1)S(1)}, u32[]{:S(2)}, u32[]{:S(2)}) collective-permute-start(bf16[256,1536]{1,0:T(8,128)(2,1)S(1)} %shard_map.188.refs_0_), channel_id=1, source_target_pairs={{0,8},{4,12},{8,0},{12,4},{1,9},{5,13},{9,1},{13,5},{2,10},{6,14},... | collective-permute-start | bytes 2359304 | tf_op jit(solution)/shard_map/ppermute | solution.py:200
  92.4 18.0 %collective-permute-start.22 = (bf16[256,1536]{1,0:T(8,128)(2,1)S(1)}, bf16[256,1536]{1,0:T(8,128)(2,1)S(1)}, u32[]{:S(2)}, u32[]{:S(2)}) collective-permute-start(bf16[256,1536]{1,0:T(8,128)(2,1)S(1)} %shard_map.188.refs_0_), channel_id=1, source_target_pairs={{0,4},{4,0},{8,12},{12,8},{1,5},{5,1},{9,13},{13,9},{2,6},{6,2},{1... | collective-permute-start | bytes 2359304 | tf_op jit(solution)/shard_map/ppermute | solution.py:200
  92.4 17.7 %collective-permute-start.20 = (bf16[256,384]{1,0:T(8,128)(2,1)S(1)}, bf16[256,384]{1,0:T(8,128)(2,1)S(1)}, u32[]{:S(2)}, u32[]{:S(2)}) collective-permute-start(bf16[256,384]{1,0:T(8,128)(2,1)S(1)} %collective-permute-done.16.refs_2_), channel_id=1, source_target_pairs={{0,4},{4,0},{8,12},{12,8},{1,5},{5,1},{9,13},{13,9},{2,6},{6,2},{1... | collective-permute-start | bytes 589832 | tf_op jit(solution)/shard_map/ppermute | solution.py:200
  110.5 15.7 %collective-permute-start.24 = (bf16[256,1152]{1,0:T(8,128)(2,1)S(1)}, bf16[256,1152]{1,0:T(8,128)(2,1)S(1)}, u32[]{:S(2)}, u32[]{:S(2)}) collective-permute-start(bf16[256,1152]{1,0:T(8,128)(2,1)S(1)} %shard_map.189), channel_id=1, source_target_pairs={{0,8},{4,12},{8,0},{12,4},{1,9},{5,13},{9,1},{13,5},{2,10},{6,14},... | collective-permute-start | bytes 1769480 | tf_op jit(solution)/shard_map/ppermute | solution.py:200
  126.3 15.4 %collective-permute-start.25 = (bf16[128,1536]{1,0:T(8,128)(2,1)S(1)}, bf16[128,1536]{1,0:T(8,128)(2,1)S(1)}, u32[]{:S(2)}, u32[]{:S(2)}) collective-permute-start(bf16[128,1536]{1,0:T(8,128)(2,1)S(1)} %get-tuple-element.252), channel_id=1, source_target_pairs={{0,8},{4,12},{8,0},{12,4},{1,9},{5,13},{9,1},{13,5},{2,10},{6,14},... | collective-permute-start | bytes 1179656 | tf_op jit(solution)/shard_map/ppermute | solution.py:200
  141.7 12.2 %collective-permute-start.29 = (bf16[128,1536]{1,0:T(8,128)(2,1)S(1)}, bf16[128,1536]{1,0:T(8,128)(2,1)S(1)}, u32[]{:S(2)}, u32[]{:S(2)}) collective-permute-start(bf16[128,1536]{1,0:T(8,128)(2,1)S(1)} %get-tuple-element.260), channel_id=1, source_target_pairs={{0,8},{4,12},{8,0},{12,4},{1,9},{5,13},{9,1},{13,5},{2,10},{6,14},... | collective-permute-start | bytes 1179656 | tf_op jit(solution)/shard_map/ppermute | solution.py:200
  143.1 10.8 %collective-permute-start.32 = (bf16[64,1536]{1,0:T(8,128)(2,1)S(1)}, bf16[64,1536]{1,0:T(8,128)(2,1)S(1)}, u32[]{:S(2)}, u32[]{:S(2)}) collective-permute-start(bf16[64,1536]{1,0:T(8,128)(2,1)S(1)} %get-tuple-element.266), channel_id=1, source_target_pairs={{0,2},{1,3},{2,0},{3,1},{4,6},{5,7},{6,4},{7,5},{8,10},{9,11},{10,... | collective-permute-start | bytes 589832 | tf_op jit(solution)/shard_map/ppermute | solution.py:213
  161.1 14.7 %collective-permute-start.36 = (bf16[128,1536]{1,0:T(8,128)(2,1)S(1)}, bf16[128,1536]{1,0:T(8,128)(2,1)S(1)}, u32[]{:S(2)}, u32[]{:S(2)}) collective-permute-start(bf16[128,1536]{1,0:T(8,128)(2,1)S(1)} %get-tuple-element.282.refs_0_), channel_id=1, source_target_pairs={{0,4},{4,0},{8,12},{12,8},{1,5},{5,1},{9,13},{13,9},{2,6},{6,2},{1... | collective-permute-start | bytes 1179656 | tf_op jit(solution)/shard_map/ppermute | solution.py:200
  161.5 14.3 %collective-permute-start.38 = (bf16[128,1536]{1,0:T(8,128)(2,1)S(1)}, bf16[128,1536]{1,0:T(8,128)(2,1)S(1)}, u32[]{:S(2)}, u32[]{:S(2)}) collective-permute-start(bf16[128,1536]{1,0:T(8,128)(2,1)S(1)} %get-tuple-element.282.refs_0_), channel_id=1, source_target_pairs={{0,8},{4,12},{8,0},{12,4},{1,9},{5,13},{9,1},{13,5},{2,10},{6,14},... | collective-permute-start | bytes 1179656 | tf_op jit(solution)/shard_map/ppermute | solution.py:200
  162.4 13.3 %collective-permute-start.37 = (bf16[128,1536]{1,0:T(8,128)(2,1)S(1)}, bf16[128,1536]{1,0:T(8,128)(2,1)S(1)}, u32[]{:S(2)}, u32[]{:S(2)}) collective-permute-start(bf16[128,1536]{1,0:T(8,128)(2,1)S(1)} %get-tuple-element.294.refs_1_), channel_id=1, source_target_pairs={{0,4},{4,0},{8,12},{12,8},{1,5},{5,1},{9,13},{13,9},{2,6},{6,2},{1... | collective-permute-start | bytes 1179656 | tf_op jit(solution)/shard_map/ppermute | solution.py:200
  162.6 13.1 %collective-permute-start.39 = (bf16[64,1536]{1,0:T(8,128)(2,1)S(1)}, bf16[64,1536]{1,0:T(8,128)(2,1)S(1)}, u32[]{:S(2)}, u32[]{:S(2)}) collective-permute-start(bf16[64,1536]{1,0:T(8,128)(2,1)S(1)} %multiply_convert_fusion.4), channel_id=1, source_target_pairs={{0,1},{1,2},{2,3},{3,0},{4,5},{5,6},{6,7},{7,4},{8,9},{9,10},{10,1... | collective-permute-start | bytes 589832 | tf_op jit(solution)/shard_map/ppermute | solution.py:213
  162.7 13.1 %collective-permute-start.40 = (bf16[64,1536]{1,0:T(8,128)(2,1)S(1)}, bf16[64,1536]{1,0:T(8,128)(2,1)S(1)}, u32[]{:S(2)}, u32[]{:S(2)}) collective-permute-start(bf16[64,1536]{1,0:T(8,128)(2,1)S(1)} %multiply_convert_fusion.4), channel_id=1, source_target_pairs={{0,3},{1,0},{2,1},{3,2},{4,7},{5,4},{6,5},{7,6},{8,11},{9,8},{10,9... | collective-permute-start | bytes 589832 | tf_op jit(solution)/shard_map/ppermute | solution.py:213
  175.8 11.7 %collective-permute-start.41 = (bf16[128,1536]{1,0:T(8,128)(2,1)S(1)}, bf16[128,1536]{1,0:T(8,128)(2,1)S(1)}, u32[]{:S(2)}, u32[]{:S(2)}) collective-permute-start(bf16[128,1536]{1,0:T(8,128)(2,1)S(1)} %get-tuple-element.294.refs_1_), channel_id=1, source_target_pairs={{0,8},{4,12},{8,0},{12,4},{1,9},{5,13},{9,1},{13,5},{2,10},{6,14},... | collective-permute-start | bytes 1179656 | tf_op jit(solution)/shard_map/ppermute | solution.py:200
  197.0 11.2 %collective-permute-start.46 = (bf16[64,1536]{1,0:T(8,128)(2,1)S(1)}, bf16[64,1536]{1,0:T(8,128)(2,1)S(1)}, u32[]{:S(2)}, u32[]{:S(2)}) collective-permute-start(bf16[64,1536]{1,0:T(8,128)(2,1)S(1)} %get-tuple-element.377), channel_id=1, source_target_pairs={{0,3},{1,0},{2,1},{3,2},{4,7},{5,4},{6,5},{7,6},{8,11},{9,8},{10,9... | collective-permute-start | bytes 589832 | tf_op jit(solution)/shard_map/ppermute | solution.py:213
  208.2 12.4 %collective-permute-start.48 = (bf16[64,1536]{1,0:T(8,128)(2,1)S(1)}, bf16[64,1536]{1,0:T(8,128)(2,1)S(1)}, u32[]{:S(2)}, u32[]{:S(2)}) collective-permute-start(bf16[64,1536]{1,0:T(8,128)(2,1)S(1)} %get-tuple-element.320), channel_id=1, source_target_pairs={{0,2},{1,3},{2,0},{3,1},{4,6},{5,7},{6,4},{7,5},{8,10},{9,11},{10,... | collective-permute-start | bytes 589832 | tf_op jit(solution)/shard_map/ppermute | solution.py:213
  220.6 12.4 %collective-permute-start.49 = (bf16[128,1152]{1,0:T(8,128)(2,1)S(1)}, bf16[128,1152]{1,0:T(8,128)(2,1)S(1)}, u32[]{:S(2)}, u32[]{:S(2)}) collective-permute-start(bf16[128,1152]{1,0:T(8,128)(2,1)S(1)} %get-tuple-element.323), channel_id=1, source_target_pairs={{0,8},{4,12},{8,0},{12,4},{1,9},{5,13},{9,1},{13,5},{2,10},{6,14},... | collective-permute-start | bytes 884744 | tf_op jit(solution)/shard_map/ppermute | solution.py:200
  222.1 10.9 %collective-permute-start.51 = (bf16[64,1536]{1,0:T(8,128)(2,1)S(1)}, bf16[64,1536]{1,0:T(8,128)(2,1)S(1)}, u32[]{:S(2)}, u32[]{:S(2)}) collective-permute-start(bf16[64,1536]{1,0:T(8,128)(2,1)S(1)} %get-tuple-element.340), channel_id=1, source_target_pairs={{0,3},{1,0},{2,1},{3,2},{4,7},{5,4},{6,5},{7,6},{8,11},{9,8},{10,9... | collective-permute-start | bytes 589832 | tf_op jit(solution)/shard_map/ppermute | solution.py:213
  232.9 11.5 %collective-permute-start.55 = (bf16[128,1152]{1,0:T(8,128)(2,1)S(1)}, bf16[128,1152]{1,0:T(8,128)(2,1)S(1)}, u32[]{:S(2)}, u32[]{:S(2)}) collective-permute-start(bf16[128,1152]{1,0:T(8,128)(2,1)S(1)} %get-tuple-element.332), channel_id=1, source_target_pairs={{0,8},{4,12},{8,0},{12,4},{1,9},{5,13},{9,1},{13,5},{2,10},{6,14},... | collective-permute-start | bytes 884744 | tf_op jit(solution)/shard_map/ppermute | solution.py:200
  233.8 10.6 %collective-permute-start.56 = (bf16[64,1536]{1,0:T(8,128)(2,1)S(1)}, bf16[64,1536]{1,0:T(8,128)(2,1)S(1)}, u32[]{:S(2)}, u32[]{:S(2)}) collective-permute-start(bf16[64,1536]{1,0:T(8,128)(2,1)S(1)} %get-tuple-element.340), channel_id=1, source_target_pairs={{0,2},{1,3},{2,0},{3,1},{4,6},{5,7},{6,4},{7,5},{8,10},{9,11},{10,... | collective-permute-start | bytes 589832 | tf_op jit(solution)/shard_map/ppermute | solution.py:213
  257.4 15.4 %collective-permute-start.61 = (bf16[256,1152]{1,0:T(8,128)(2,1)S(1)}, bf16[256,1152]{1,0:T(8,128)(2,1)S(1)}, u32[]{:S(2)}, u32[]{:S(2)}) collective-permute-start(bf16[256,1152]{1,0:T(8,128)(2,1)S(1)} %shard_map.205), channel_id=1, source_target_pairs={{0,8},{4,12},{8,0},{12,4},{1,9},{5,13},{9,1},{13,5},{2,10},{6,14},... | collective-permute-start | bytes 1769480 | tf_op jit(solution)/shard_map/ppermute | solution.py:200
  299.1 12.0 %collective-permute-start.69 = (bf16[64,1536]{1,0:T(8,128)(2,1)S(1)}, bf16[64,1536]{1,0:T(8,128)(2,1)S(1)}, u32[]{:S(2)}, u32[]{:S(2)}) collective-permute-start(bf16[64,1536]{1,0:T(8,128)(2,1)S(1)} %get-tuple-element.374), channel_id=1, source_target_pairs={{0,3},{1,0},{2,1},{3,2},{4,7},{5,4},{6,5},{7,6},{8,11},{9,8},{10,9... | collective-permute-start | bytes 589832 | tf_op jit(solution)/shard_map/ppermute | solution.py:213
  302.7 14.2 %collective-permute-start.67 = (bf16[64,1536]{1,0:T(8,128)(2,1)S(1)}, bf16[64,1536]{1,0:T(8,128)(2,1)S(1)}, u32[]{:S(2)}, u32[]{:S(2)}) collective-permute-start(bf16[64,1536]{1,0:T(8,128)(2,1)S(1)} %get-tuple-element.375), channel_id=1, source_target_pairs={{0,1},{1,2},{2,3},{3,0},{4,5},{5,6},{6,7},{7,4},{8,9},{9,10},{10,1... | collective-permute-start | bytes 589832 | tf_op jit(solution)/shard_map/ppermute | solution.py:213
  302.7 16.8 %collective-permute-start.68 = (bf16[64,1536]{1,0:T(8,128)(2,1)S(1)}, bf16[64,1536]{1,0:T(8,128)(2,1)S(1)}, u32[]{:S(2)}, u32[]{:S(2)}) collective-permute-start(bf16[64,1536]{1,0:T(8,128)(2,1)S(1)} %get-tuple-element.373), channel_id=1, source_target_pairs={{0,3},{1,0},{2,1},{3,2},{4,7},{5,4},{6,5},{7,6},{8,11},{9,8},{10,9... | collective-permute-start | bytes 589832 | tf_op jit(solution)/shard_map/ppermute | solution.py:213
  311.2 14.2 %collective-permute-start.66 = (bf16[64,1536]{1,0:T(8,128)(2,1)S(1)}, bf16[64,1536]{1,0:T(8,128)(2,1)S(1)}, u32[]{:S(2)}, u32[]{:S(2)}) collective-permute-start(bf16[64,1536]{1,0:T(8,128)(2,1)S(1)} %get-tuple-element.372), channel_id=1, source_target_pairs={{0,1},{1,2},{2,3},{3,0},{4,5},{5,6},{6,7},{7,4},{8,9},{9,10},{10,1... | collective-permute-start | bytes 589832 | tf_op jit(solution)/shard_map/ppermute | solution.py:213
  313.4 13.5 %collective-permute-start.70 = (bf16[64,1536]{1,0:T(8,128)(2,1)S(1)}, bf16[64,1536]{1,0:T(8,128)(2,1)S(1)}, u32[]{:S(2)}, u32[]{:S(2)}) collective-permute-start(bf16[64,1536]{1,0:T(8,128)(2,1)S(1)} %get-tuple-element.371), channel_id=1, source_target_pairs={{0,3},{1,0},{2,1},{3,2},{4,7},{5,4},{6,5},{7,6},{8,11},{9,8},{10,9... | collective-permute-start | bytes 589832 | tf_op jit(solution)/shard_map/ppermute | solution.py:213
  (50 other events, 350.0 us)

commit v4 on v3

--- a/solution.py
+++ b/solution.py
@@ -304,32 +304,56 @@
     )
 
 
-def project_hidden(run, tokens, weight, bias, width, sub, arrived, from_side, pieces=1):
-    rows, depth = tokens.shape
+def project_hidden(run, tokens, weight, bias, width, sub, arrived, from_side, at=0):
+    depth = tokens.shape[1]
+    rows = from_side.shape[0]
     block = width // sub
-    sides = len(from_side)
-
-    def kernel(pos, tokens_ref, weight_ref, bias_ref, arrived_ref, *refs):
+
+    def kernel(pos, tokens_ref, weight_ref, bias_ref, arrived_ref, side_ref, out_ref):
         total = dot_f32(tokens_ref[...], weight_ref[...])
-        total = total + arrived_ref[...].astype(jnp.float32)
-        total = total + joined_rows(refs[:sides]).astype(jnp.float32)
+        total = total + arrived_ref[...].astype(jnp.float32) + side_ref[...].astype(jnp.float32)
         total = total + bias_ref[...]
-        unit = total * (1.0 + lax.erf(total * math.sqrt(0.5))) * 0.5
-        store_rows(refs[sides:], slice(None), unit)
+        out_ref[...] = (total * (1.0 + lax.erf(total * math.sqrt(0.5))) * 0.5).astype(jnp.bfloat16)
 
     return run(
         kernel,
         (sub,),
-        (tokens, weight, bias, arrived, *from_side),
+        (tokens, weight, bias, arrived, from_side),
+        (
+            pl.BlockSpec((rows, depth), lambda s, pos: (at, 0)),
+            pl.BlockSpec((depth, block), lambda s, pos: (0, mine_of(pos) * sub + s)),
+            pl.BlockSpec((1, block), lambda s, pos: (0, mine_of(pos) * sub + s)),
+            pl.BlockSpec((rows, block), lambda s, pos: (at, pos[1] * sub + s)),
+            pl.BlockSpec((rows, block), lambda s, pos: (0, s)),
+        ),
+        jax.ShapeDtypeStruct((rows, width), jnp.bfloat16),
+        pl.BlockSpec((rows, block), lambda s, pos: (0, s)),
+    )
+
+
+def project_keep(run, tokens, weights, width, arrived):
+    rows, depth = tokens.shape
+    wide = len(weights) * width
+
+    def kernel(pos, tokens_ref, *refs):
+        arrived_ref, out_ref = refs[len(weights) :]
+        for i in range(len(weights)):
+            at = slice(i * width, (i + 1) * width)
+            part = dot_f32(tokens_ref[...], refs[i][...])
+            out_ref[:, at] = part + arrived_ref[:, at].astype(jnp.float32)
+
+    spec = pl.BlockSpec((depth, width), lambda s, pos: (0, mine_of(pos)))
+    return run(
+        kernel,
+        (1,),
+        (tokens, *weights, arrived),
         (
             whole(tokens),
-            pl.BlockSpec((depth, block), lambda s, pos: (0, mine_of(pos) * sub + s)),
-            pl.BlockSpec((1, block), lambda s, pos: (0, mine_of(pos) * sub + s)),
-            pl.BlockSpec((rows, block), lambda s, pos: (0, pos[1] * sub + s)),
-            *[pl.BlockSpec((rows // sides, block), lambda s, pos: (0, s))] * sides,
+            *[spec] * len(weights),
+            pl.BlockSpec((rows, wide), lambda s, pos: (0, pos[1])),
         ),
-        (jax.ShapeDtypeStruct((rows // pieces, width), jnp.bfloat16),) * pieces,
-        (pl.BlockSpec((rows // pieces, block), lambda s, pos: (0, s)),) * pieces,
+        jax.ShapeDtypeStruct((rows, wide), jnp.float32),
+        pl.BlockSpec((rows, wide), lambda s, pos: (0, 0)),
     )
 
 
@@ -454,29 +478,33 @@
     )
 
 
-def join_blend(run, parts):
-    rows = sum(part.shape[0] for part in parts)
-    heads = parts[0].shape[1] // 3 // HEAD_DIM
-    count = len(parts)
+def join_blend(run, parts, kept, from_side, scales):
+    rows = parts.shape[0] + kept.shape[0]
+    heads = parts.shape[1] // 3 // HEAD_DIM
 
     def kernel(pos, *refs):
+        part_refs, kept_refs, side_refs = refs[:3], refs[3:6], refs[6:9]
+        *scale_refs, out_ref = refs[9:]
+        raws = [k[...] + s[...].astype(jnp.float32) for k, s in zip(kept_refs, side_refs)]
+        late = [unit_norm(raws[i], scale_refs[i][...]) for i in range(2)]
+        late.append(raws[2].astype(jnp.bfloat16))
         query, key, value = (
-            jnp.concatenate([ref[...] for ref in refs[i * count : (i + 1) * count]])
+            jnp.concatenate((part_refs[i][...], late[i])) for i in range(3)
+        )
+        out_ref[...] = softmax_blend(query, key, value)
+
+    def specs(array):
+        return [
+            pl.BlockSpec((array.shape[0], HEAD_DIM), lambda h, pos, i=i: (0, i * heads + h))
             for i in range(3)
-        )
-        refs[-1][...] = softmax_blend(query, key, value)
-
-    def specs(which):
-        return [
-            pl.BlockSpec((part.shape[0], HEAD_DIM), lambda h, pos: (0, which * heads + h))
-            for part in parts
         ]
 
+    scale_spec = pl.BlockSpec((1, HEAD_DIM), lambda h, pos: (0, mine_of(pos) * heads + h))
     return run(
         kernel,
         (heads,),
-        (*parts, *parts, *parts),
-        (*specs(0), *specs(1), *specs(2)),
+        (*[parts] * 3, *[kept] * 3, *[from_side] * 3, *scales),
+        (*specs(parts), *specs(kept), *specs(from_side), *[scale_spec] * 2),
         jax.ShapeDtypeStruct((rows, heads * HEAD_DIM), jnp.bfloat16),
         pl.BlockSpec((rows, HEAD_DIM), lambda h, pos: (0, h)),
     )
@@ -496,6 +524,11 @@
 
 def sent(array, shift):
     return row_shift(array.astype(jnp.bfloat16), shift)
+
+
+def sent_on(before, after):
+    half = before.shape[0] // 2
+    return sent(before[:half], 1), sent(after[half:], -1)
 
 
 def moment_shards(total):
@@ -577,10 +610,8 @@
     def units_across(tokens, arrived, pieces):
         return project_across(run, tokens, (up_weight,), unit_width, sub, arrived, pieces)
 
-    def units_end(tokens, arrived, side, pieces):
-        return project_hidden(
-            run, tokens, up_weight, bias, unit_width, sub, arrived, side, pieces
-        )
+    def units_end(tokens, arrived, side, at=0):
+        return project_hidden(run, tokens, up_weight, bias, unit_width, sub, arrived, side, at)
 
     def layer_end(start, own, *arrived):
         total = own
@@ -596,9 +627,10 @@
     )
 
     totals = moment_shards(moment_sum(pairs))
-    own_a, own_b, a_before, a_after, a_away, *totals = sync(
-        own_a, own_b, a_before, a_after, sent(own_a, 2), *totals
-    )
+    own_a, own_b, a_before, a_after, a_away0, a_away1, *totals = sync(
+        own_a, own_b, a_before, a_after, *sent_on(a_before, a_after), *totals
+    )
+    a_away = jnp.concatenate((a_away0, a_away1))
     totals_a = [total[:, :half] for total in totals]
     totals_b = [total[:, half:] for total in totals]
 
@@ -613,13 +645,16 @@
 
     uc_a = core_swap(us_a)
     (qx_a,) = heads_across(tok_a, heads_in, qc_a)
-    tok_a, own_b, qc_a, uc_a, qx_a = sync(tok_a, own_b, qc_a, uc_a, qx_a)
-
-    qy_a, b_away = y_swap(qx_a), sent(own_b, 2)
+    tok_a, own_b, b_before, b_after, qc_a, uc_a, qx_a = sync(
+        tok_a, own_b, b_before, b_after, qc_a, uc_a, qx_a
+    )
+
+    qy_a, b_away0, b_away1 = y_swap(qx_a), *sent_on(b_before, b_after)
     (ux_a,) = units_across(tok_a, uc_a, 1)
-    tok_a, qc_a, uc_a, ux_a, qy_a, own_b, b_before, b_after, b_away = sync(
-        tok_a, qc_a, uc_a, ux_a, qy_a, own_b, b_before, b_after, b_away
-    )
+    tok_a, qc_a, uc_a, ux_a, qy_a, own_b, b_before, b_after, b_away0, b_away1 = sync(
+        tok_a, qc_a, uc_a, ux_a, qy_a, own_b, b_before, b_after, b_away0, b_away1
+    )
+    b_away = jnp.concatenate((b_away0, b_away1))
 
     uy_a = y_swap(ux_a)
     tok_b = normed_shards((own_b, b_before, b_after, b_away), norm_gain, totals_b)
@@ -631,7 +666,7 @@
     )
 
     at_ya, at_ca, qc_b, uc_b = y_swap(at_a), core_swap(at_a), core_swap(qs_b), core_swap(us_b)
-    (hd_a,) = units_end(tok_a, uc_a, (uy_a,), 1)
+    hd_a = units_end(tok_a, uc_a, uy_a)
     tok_b, at_a, at_ya, at_ca, qc_b, uc_b, hd_a = sync(
         tok_b, at_a, at_ya, at_ca, qc_b, uc_b, hd_a
     )
@@ -664,65 +699,72 @@
     uy_b1, from_away, at_cb, at_fb = (
         y_swap(ux_b1), sent(away_a, 2), core_swap(at_b), core_swap(at_yb)
     )
-    tok_b, uc_b, uy_b0, uy_b1, at_b, at_cb, at_yb, at_fb, mine_a, *arrived = sync(
-        tok_b, uc_b, uy_b0, uy_b1, at_b, at_cb, at_yb, at_fb, mine_a,
-        from_before, from_after, from_away,
-    )
-
+    hd_b0 = units_end(tok_b, uc_b, uy_b0)
+    mixed_b = heads_out((at_b, at_cb, at_yb, at_fb))
+    tok_b, uc_b, uy_b1, hd_b0, mixed_b, mine_a, *arrived = sync(
+        tok_b, uc_b, uy_b1, hd_b0, mixed_b, mine_a, from_before, from_after, from_away
+    )
+
+    hd_yb0, hd_cb0 = y_swap(hd_b0), core_swap(hd_b0)
     layer_a = layer_end(start_f32[:half], mine_a, *arrived)
     pairs = moment_flips(moment_pair(layer_a.astype(jnp.float32)))
-    hd_b = units_end(tok_b, uc_b, (uy_b0, uy_b1), 2)
-    at_b, at_cb, at_yb, at_fb, hd_b0, hd_b1, layer_a, *pairs = sync(
-        at_b, at_cb, at_yb, at_fb, *hd_b, layer_a, *pairs
-    )
-
-    hd_yb0, hd_cb0, hd_cb1 = y_swap(hd_b0), core_swap(hd_b0), core_swap(hd_b1)
+    hd_b1 = units_end(tok_b, uc_b, uy_b1, 1)
+    hd_b0, hd_b1, hd_yb0, hd_cb0, mixed_b, layer_a, *pairs = sync(
+        hd_b0, hd_b1, hd_yb0, hd_cb0, mixed_b, layer_a, *pairs
+    )
+
+    hd_yb1, hd_cb1, hd_fb0 = y_swap(hd_b1), core_swap(hd_b1), core_swap(hd_yb0)
     join_a = normalize(layer_a.astype(jnp.float32), join_gain, moment_sum(pairs))
     ja_before, ja_after = sent(join_a, 1), sent(join_a, -1)
-    mixed_b = units_down(((hd_b0, hd_b1),), 0, heads_out((at_b, at_cb, at_yb, at_fb)))
-    hd_b1, hd_cb0, hd_cb1, hd_yb0, mixed_b, layer_a, join_a, ja_before, ja_after = sync(
-        hd_b1, hd_cb0, hd_cb1, hd_yb0, mixed_b, layer_a, join_a, ja_before, ja_after
-    )
-
-    hd_yb1, ja_away = y_swap(hd_b1), sent(join_a, 2)
+    mixed_b = units_down(((hd_b0, hd_b1),), 0, mixed_b)
+    hd_cb0, hd_cb1, hd_yb0, hd_yb1, hd_fb0, mixed_b, layer_a, join_a, ja_before, ja_after = sync(
+        hd_cb0, hd_cb1, hd_yb0, hd_yb1, hd_fb0, mixed_b, layer_a, join_a, ja_before, ja_after
+    )
+
+    hd_fb1 = core_swap(hd_yb1)
     mixed_b = units_down(((hd_cb0, hd_cb1),), 1, mixed_b)
-    hd_yb0, hd_yb1, mixed_b, join_a, ja_before, ja_after, ja_away = sync(
-        hd_yb0, hd_yb1, mixed_b, join_a, ja_before, ja_after, ja_away
-    )
-
-    hd_fb0, hd_fb1 = core_swap(hd_yb0), core_swap(hd_yb1)
+    hd_yb0, hd_yb1, hd_fb0, hd_fb1, mixed_b, join_a, ja_before, ja_after = sync(
+        hd_yb0, hd_yb1, hd_fb0, hd_fb1, mixed_b, join_a, ja_before, ja_after
+    )
+
+    ja_away0, ja_away1 = sent_on(ja_before, ja_after)
     mixed_b = units_down(((hd_yb0, hd_yb1), (hd_fb0, hd_fb1)), 2, mixed_b)
-    mixed_b, join_a, ja_before, ja_after, ja_away = sync(
-        mixed_b, join_a, ja_before, ja_after, ja_away
+    mixed_b, join_a, ja_before, ja_after, ja_away0, ja_away1 = sync(
+        mixed_b, join_a, ja_before, ja_after, ja_away0, ja_away1
     )
 
     mine_b, before_b, after_b, away_b = jnp.split(mixed_b, 4)
+    part = half // 2
+    to_after, to_before = sent(away_b[:part], 1), sent(away_b[part:], -1)
+    mine_b, before_b, after_b, to_after, to_before, join_a, *shards = sync(
+        mine_b, before_b, after_b, to_after, to_before, join_a,
+        ja_before, ja_after, ja_away0, ja_away1,
+    )
+
+    after_b = jnp.concatenate((after_b[:part] + to_after.astype(jnp.float32), after_b[part:]))
+    before_b = jnp.concatenate((before_b[:part], before_b[part:] + to_before.astype(jnp.float32)))
     from_before, from_after = sent(after_b, 1), sent(before_b, -1)
-    tok_ja = jnp.concatenate((join_a, ja_before, ja_after, ja_away))
+    tok_ja = jnp.concatenate((join_a, *shards))
     js_a = heads_send(tok_ja, join_in)
-    tok_ja, js_a, mine_b, away_b, from_before, from_after = sync(
-        tok_ja, js_a, mine_b, away_b.astype(jnp.bfloat16), from_before, from_after
-    )
-
-    from_away, jc_a = sent(away_b, 2), core_swap(js_a)
-    jx_a = heads_across(tok_ja, join_in, jc_a, 2)
-    tok_ja, jc_a, jx_a0, jx_a1, mine_b, *arrived = sync(
-        tok_ja, jc_a, *jx_a, mine_b, from_before, from_after, from_away
-    )
+    tok_ja, js_a, mine_b, *arrived = sync(tok_ja, js_a, mine_b, from_before, from_after)
 
     layer_b = layer_end(start_f32[half:], mine_b, *arrived)
     pairs = moment_flips(moment_pair(layer_b.astype(jnp.float32)))
-    jb_before, jb_after, jy_a0 = sent(layer_b, 1), sent(layer_b, -1), y_swap(jx_a0)
-    tok_ja, jc_a, jy_a0, jx_a1, layer_b, jb_before, jb_after, *pairs = sync(
-        tok_ja, jc_a, jy_a0, jx_a1, layer_b, jb_before, jb_after, *pairs
+    jb_before, jb_after, jc_a = sent(layer_b, 1), sent(layer_b, -1), core_swap(js_a)
+    jx_a = heads_across(tok_ja, join_in, jc_a, 2)
+    tok_ja, jc_a, jx_a0, jx_a1, layer_b, jb_before, jb_after, *pairs = sync(
+        tok_ja, jc_a, *jx_a, layer_b, jb_before, jb_after, *pairs
     )
 
     totals = moment_shards(moment_sum(pairs))
-    jb_away, jy_a1 = sent(layer_b, 2), y_swap(jx_a1)
-    tok_ja, jc_a, jy_a0, jy_a1, layer_b, jb_before, jb_after, jb_away, *totals = sync(
-        tok_ja, jc_a, jy_a0, jy_a1, layer_b, jb_before, jb_after, jb_away, *totals
-    )
-
+    jb_away0, jb_away1 = sent_on(jb_before, jb_after)
+    jy_a0 = y_swap(jx_a0)
+    tok_ja, jc_a, jy_a0, jx_a1, layer_b, jb_before, jb_after, jb_away0, jb_away1, *totals = sync(
+        tok_ja, jc_a, jy_a0, jx_a1, layer_b, jb_before, jb_after, jb_away0, jb_away1, *totals
+    )
+
+    jy_a1 = y_swap(jx_a1)
+    jb_away = jnp.concatenate((jb_away0, jb_away1))
     tok_jb = normed_shards((layer_b, jb_before, jb_after, jb_away), join_gain, totals)
     jc_b = core_swap(heads_send(tok_jb, join_in))
     (jx_b,) = heads_across(tok_jb, join_in, jc_b)
@@ -734,10 +776,10 @@
     parts_a = project_heads(
         run, tok_ja, join_in, join_scales, head_width, jc_a, (jy_a0, jy_a1), False
     )
-    tok_jb, jc_b, jy_b, parts_a = sync(tok_jb, jc_b, jy_b, parts_a)
-
-    parts_b = project_heads(run, tok_jb, join_in, join_scales, head_width, jc_b, (jy_b,), False)
-    joined = join_blend(run, (parts_a, parts_b))
+    kept_b = project_keep(run, tok_jb, join_in, head_width, jc_b)
+    jy_b, parts_a, kept_b = sync(jy_b, parts_a, kept_b)
+
+    joined = join_blend(run, parts_a, kept_b, jy_b, join_scales)
     joined = joined.reshape(2, 4, half, head_width).swapaxes(0, 1).reshape(8 * half, head_width)
     jo_y, jo_c = y_swap(joined), core_swap(joined)
     jo_f = core_swap(jo_y)

time: 332 us -> 325 us (0.979)
  waiting for transfers between devices: 104 us -> 81.9 us
  starting transfers between devices: 74.3 us -> 84.9 us
  Pallas kernels: 141 us -> 145 us
    ppermute x30 -> x35, waiting for transfers between devices: 62.9 us -> 43.9 us  [row_shift(): lax.ppermute(array, 'rows', [(i, (i + shift) % size) for i in range(size)])]
    ppermute x30 -> x35, starting transfers between devices: 50.5 us -> 62 us  [row_shift(): lax.ppermute(array, 'rows', [(i, (i + shift) % size) for i in range(size)])]
    pallas_call x29 -> x30, Pallas kernels: 141 us -> 145 us  [__call__(): pl.pallas_call(kernel, out_shape=out_shape, grid_spec=pltpu.PrefetchScala...]
  transfers between devices with their start and end apart: 71 -> 76, of which waited for: 40 -> 34; matrix products, arithmetic and copies ran while one was open for 1% -> 1% of each run, Pallas kernels for 34% -> 41%
where the time goes in v4:
time: 325 us; the launch traced here: 320 us
  Pallas kernels  145 us (45%)
  starting transfers between devices  84.9 us (26%)
  waiting for transfers between devices  81.9 us (25%)
  other arithmetic  4.87 us (1%)
    pallas_call x30, Pallas kernels, __call__(): pl.pallas_call(kernel, out_shape=out_shape, grid_spec=pltpu.PrefetchScala...  145 us
    ppermute x35, starting transfers between devices, row_shift(): lax.ppermute(array, 'rows', [(i, (i + shift) % size) for i in range(size)])  62 us
    ppermute x35, waiting for transfers between devices, row_shift(): lax.ppermute(array, 'rows', [(i, (i + shift) % size) for i in range(size)])  43.9 us
    ppermute x41, waiting for transfers between devices, flip(): return lax.ppermute(array, 'cols', [(i, i ^ mask) for i in range(size)])  38 us
    ppermute x41, starting transfers between devices, flip(): return lax.ppermute(array, 'cols', [(i, i ^ mask) for i in range(size)])  22.9 us
  transfers between devices with their start and end apart: 76, of which 34 were waited for; matrix products, arithmetic and copies ran while one was open for 1% of the time, Pallas kernels for 41%

profile of v4, /device:TPU:0, one launch (start us, length us, event | category | flops | bytes accessed | tf_op | source)
XLA Modules:
  0.0 320.0 jit_solution(4625581243639754655)
XLA Ops:
  27.5 5.5 %shard_map.181 = bf16[256,2304]{1,0:T(8,128)(2,1)S(1)} custom-call(s32[2]{0:T(128)S(1)} %pad_add_fusion.pos, bf16[256,1536]{1,0:T(8,128)(2,1)S(1)} %pad_maximum_fusion.tokens_ref, bf16[1536,1536]{1,0:T(8,128)(2,1)} %refs_0_.25, bf16[1536,1536]{1,0:T(8,128)(2,1)} %refs_1_.17, bf16[1536,1536]{1,0:T(8,128)(2,1)} %refs_2_.17), custom_call_target="tpu_custom_call" | custom-call | flops 1 | bytes 1 | tf_op jit(solution)/shard_map/pallas_call | solution.py:221
  36.0 7.4 %shard_map.182 = bf16[256,3072]{1,0:T(8,128)(2,1)S(1)} custom-call(s32[2]{0:T(128)S(1)} %pad_add_fusion.pos, bf16[256,1536]{1,0:T(8,128)(2,1)S(1)} %pad_maximum_fusion.tokens_ref, bf16[1536,6144]{1,0:T(8,128)(2,1)} %weight_ref.21), custom_call_target="tpu_custom_call" | custom-call | flops 1 | bytes 1 | tf_op jit(solution)/shard_map/pallas_call | solution.py:221
  49.3 4.0 %collective-permute-start.16 = (bf16[32,1536]{1,0:T(8,128)(2,1)S(1)}, bf16[32,1536]{1,0:T(8,128)(2,1)S(1)}, u32[]{:S(2)}, u32[]{:S(2)}) collective-permute-start(bf16[32,1536]{1,0:T(8,128)(2,1)S(1)} %slice.203), channel_id=1, source_target_pairs={{0,3},{1,0},{2,1},{3,2},{4,7},{5,4},{6,5},{7,6},{8,11},{9,8},{10,9... | collective-permute-start | bytes 294920 | tf_op jit(solution)/shard_map/ppermute | solution.py:213
  53.3 4.6 %shard_map.184 = bf16[256,1536]{1,0:T(8,128)(2,1)S(1)} custom-call(s32[2]{0:T(128)S(1)} %pad_add_fusion.pos, bf16[256,1536]{1,0:T(8,128)(2,1)S(1)} %pad_maximum_fusion.tokens_ref, bf16[1536,6144]{1,0:T(8,128)(2,1)} %weight_ref.21, bf16[256,3072]{1,0:T(8,128)(2,1)S(1)} %collective-permute-done.13.refs_1_.arrived_ref), custom_call_target="tpu_custom_call" | custom-call | flops 1 | bytes 1 | tf_op jit(solution)/shard_map/pallas_call | solution.py:221
  58.0 5.3 %collective-permute-done.14.refs_6_ = bf16[256,1152]{1,0:T(8,128)(2,1)S(1)} collective-permute-done((bf16[256,1152]{1,0:T(8,128)(2,1)S(1)}, bf16[256,1152]{1,0:T(8,128)(2,1)S(1)}, u32[]{:S(2)}, u32[]{:S(2)}) %collective-permute-start.14) | collective-permute-done | bytes 589856 | tf_op jit(solution)/shard_map/ppermute | solution.py:200
  65.5 7.4 %shard_map.186 = bf16[256,3072]{1,0:T(8,128)(2,1)S(1)} custom-call(s32[2]{0:T(128)S(1)} %pad_add_fusion.pos, bf16[256,1536]{1,0:T(8,128)(2,1)S(1)} %pad_maximum_fusion.1.tokens_ref, bf16[1536,6144]{1,0:T(8,128)(2,1)} %weight_ref.21), custom_call_target="tpu_custom_call" | custom-call | flops 1 | bytes 1 | tf_op jit(solution)/shard_map/pallas_call | solution.py:221
  72.9 5.5 %shard_map.185 = bf16[256,2304]{1,0:T(8,128)(2,1)S(1)} custom-call(s32[2]{0:T(128)S(1)} %pad_add_fusion.pos, bf16[256,1536]{1,0:T(8,128)(2,1)S(1)} %pad_maximum_fusion.1.tokens_ref, bf16[1536,1536]{1,0:T(8,128)(2,1)} %refs_0_.25, bf16[1536,1536]{1,0:T(8,128)(2,1)} %refs_1_.17, bf16[1536,1536]{1,0:T(8,128)(2,1)} %refs_2_.17), custom_call_target="tpu_custom_call" | custom-call | flops 1 | bytes 1 | tf_op jit(solution)/shard_map/pallas_call | solution.py:221
  78.5 4.4 %shard_map.187.refs_0_ = bf16[256,384]{1,0:T(8,128)(2,1)S(1)} custom-call(s32[2]{0:T(128)S(1)} %pad_add_fusion.pos, bf16[256,1536]{1,0:T(8,128)(2,1)S(1)} %pad_maximum_fusion.tokens_ref, bf16[1536,1536]{1,0:T(8,128)(2,1)} %refs_0_.25, bf16[1536,1536]{1,0:T(8,128)(2,1)} %refs_1_.17, bf16[1536,1536]{1,0:T(8,128)(2,1)} %refs_2_.17, ...), custom_call_target="tpu_custom_call" | custom-call | flops 1 | bytes 1 | tf_op jit(solution)/shard_map/pallas_call | solution.py:221
  84.3 4.8 %shard_map.188.refs_0_ = bf16[256,1536]{1,0:T(8,128)(2,1)S(1)} custom-call(s32[2]{0:T(128)S(1)} %pad_add_fusion.pos, bf16[256,1536]{1,0:T(8,128)(2,1)S(1)} %pad_maximum_fusion.tokens_ref, bf16[1536,6144]{1,0:T(8,128)(2,1)} %weight_ref.21, f32[1,6144]{1,0:T(1,128)S(1)} %bitcast.147, bf16[256,3072]{1,0:T(8,128)(2,1)S(1)} %collective-permute-done.13.refs_1_.arrived_ref, ...), custom_call_target="tpu_custom_call" | custom-call | flops 1 | bytes 1 | tf_op jit(solution)/shard_map/pallas_call | solution.py:221
  91.7 4.6 %shard_map.192 = (bf16[128,1536]{1,0:T(8,128)(2,1)S(1)}, bf16[128,1536]{1,0:T(8,128)(2,1)S(1)}) custom-call(s32[2]{0:T(128)S(1)} %pad_add_fusion.pos, bf16[256,1536]{1,0:T(8,128)(2,1)S(1)} %pad_maximum_fusion.1.tokens_ref, bf16[1536,6144]{1,0:T(8,128)(2,1)} %weight_ref.21, bf16[256,3072]{1,0:T(8,128)(2,1)S(1)} %collective-permute-done.21.refs_1_.arrived_ref), custom_call_target="tpu_custom_call" | custom-call | flops 1 | bytes 1 | tf_op jit(solution)/shard_map/pallas_call | solution.py:221
  96.3 4.0 %shard_map.189 = bf16[256,1152]{1,0:T(8,128)(2,1)S(1)} custom-call(s32[2]{0:T(128)S(1)} %pad_add_fusion.pos, bf16[256,1536]{1,0:T(8,128)(2,1)S(1)} %pad_maximum_fusion.1.tokens_ref, bf16[1536,1536]{1,0:T(8,128)(2,1)} %refs_0_.25, bf16[1536,1536]{1,0:T(8,128)(2,1)} %refs_1_.17, bf16[1536,1536]{1,0:T(8,128)(2,1)} %refs_2_.17, ...), custom_call_target="tpu_custom_call" | custom-call | flops 1 | bytes 1 | tf_op jit(solution)/shard_map/pallas_call | solution.py:221
  100.3 4.3 %shard_map.190.refs_1_ = f32[256,1536]{1,0:T(8,128)S(1)} custom-call(s32[2]{0:T(128)S(1)} %pad_add_fusion.pos, bf16[1536,1536]{1,0:T(8,128)(2,1)} %weight_ref.20, bf16[256,384]{1,0:T(8,128)(2,1)S(1)} %shard_map.187.refs_0_, bf16[256,384]{1,0:T(8,128)(2,1)S(1)} %collective-permute-done.19.refs_1_, bf16[256,384]{1,0:T(8,128)(2,1)S(1)} %collective-permute-done.18.refs_2_), custom_call_target="tpu_custom_call" | custom-call | flops 1 | bytes 1 | tf_op jit(solution)/shard_map/pallas_call | solution.py:221
  104.6 4.2 %shard_map.191.refs_1_ = f32[256,1536]{1,0:T(8,128)S(1)} custom-call(s32[2]{0:T(128)S(1)} %pad_add_fusion.pos, bf16[6144,1536]{1,0:T(8,128)(2,1)} %weight_ref.24, bf16[256,1536]{1,0:T(8,128)(2,1)S(1)} %shard_map.188.refs_0_, f32[256,1536]{1,0:T(8,128)S(1)} %shard_map.190.refs_1_), custom_call_target="tpu_custom_call" | custom-call | flops 1 | bytes 1 | tf_op jit(solution)/shard_map/pallas_call | solution.py:221
  112.8 4.2 %shard_map.194.refs_2_ = f32[256,1536]{1,0:T(8,128)S(1)} custom-call(s32[2]{0:T(128)S(1)} %pad_add_fusion.pos, bf16[6144,1536]{1,0:T(8,128)(2,1)} %weight_ref.24, bf16[256,1536]{1,0:T(8,128)(2,1)S(1)} %collective-permute-done.24.refs_0_, f32[256,1536]{1,0:T(8,128)S(1)} %shard_map.193.refs_1_), custom_call_target="tpu_custom_call" | custom-call | flops 1 | bytes 1 | tf_op jit(solution)/shard_map/pallas_call | solution.py:221
  117.1 7.4 %shard_map.195 = f32[256,1536]{1,0:T(8,128)S(1)} custom-call(s32[2]{0:T(128)S(1)} %pad_add_fusion.pos, bf16[6144,1536]{1,0:T(8,128)(2,1)} %weight_ref.24, bf16[256,1536]{1,0:T(8,128)(2,1)S(1)} %collective-permute-done.23.refs_0_, bf16[256,1536]{1,0:T(8,128)(2,1)S(1)} %collective-permute-done.25.refs_1_, f32[256,1536]{1,0:T(8,128)S(1)} %shard_map.194.refs_2_), custom_call_target="tpu_custom_call" | custom-call | flops 1 | bytes 1 | tf_op jit(solution)/shard_map/pallas_call | solution.py:221
  130.2 4.4 %shard_map.196.refs_0_ = bf16[256,384]{1,0:T(8,128)(2,1)S(1)} custom-call(s32[2]{0:T(128)S(1)} %pad_add_fusion.pos, bf16[256,1536]{1,0:T(8,128)(2,1)S(1)} %pad_maximum_fusion.1.tokens_ref, bf16[1536,1536]{1,0:T(8,128)(2,1)} %refs_0_.25, bf16[1536,1536]{1,0:T(8,128)(2,1)} %refs_1_.17, bf16[1536,1536]{1,0:T(8,128)(2,1)} %refs_2_.17, ...), custom_call_target="tpu_custom_call" | custom-call | flops 1 | bytes 1 | tf_op jit(solution)/shard_map/pallas_call | solution.py:221
  141.8 4.3 %shard_map.197.refs_0_ = bf16[128,1536]{1,0:T(8,128)(2,1)S(1)} custom-call(s32[2]{0:T(128)S(1)} %pad_add_fusion.pos, bf16[256,1536]{1,0:T(8,128)(2,1)S(1)} %pad_maximum_fusion.1.tokens_ref, bf16[1536,6144]{1,0:T(8,128)(2,1)} %weight_ref.21, f32[1,6144]{1,0:T(1,128)S(1)} %bitcast.148, bf16[256,3072]{1,0:T(8,128)(2,1)S(1)} %collective-permute-done.21.refs_1_.arrived_ref, ...), custom_call_target="tpu_custom_call" | custom-call | flops 1 | bytes 1 | tf_op jit(solution)/shard_map/pallas_call | solution.py:221
  146.2 5.0 %shard_map.198.refs_2_ = f32[256,1536]{1,0:T(8,128)S(1)} custom-call(s32[2]{0:T(128)S(1)} %pad_add_fusion.pos, bf16[1536,1536]{1,0:T(8,128)(2,1)} %weight_ref.20, bf16[256,384]{1,0:T(8,128)(2,1)S(1)} %shard_map.196.refs_0_, bf16[256,384]{1,0:T(8,128)(2,1)S(1)} %collective-permute-done.32.refs_1_, bf16[256,384]{1,0:T(8,128)(2,1)S(1)} %collective-permute-done.28.refs_2_, ...), custom_call_target="tpu_custom_call" | custom-call | flops 1 | bytes 1 | tf_op jit(solution)/shard_map/pallas_call | solution.py:221
  156.0 4.3 %shard_map.199.refs_1_ = bf16[128,1536]{1,0:T(8,128)(2,1)S(1)} custom-call(s32[2]{0:T(128)S(1)} %pad_add_fusion.pos, bf16[256,1536]{1,0:T(8,128)(2,1)S(1)} %pad_maximum_fusion.1.tokens_ref, bf16[1536,6144]{1,0:T(8,128)(2,1)} %weight_ref.21, f32[1,6144]{1,0:T(1,128)S(1)} %bitcast.149, bf16[256,3072]{1,0:T(8,128)(2,1)S(1)} %collective-permute-done.21.refs_1_.arrived_ref, ...), custom_call_target="tpu_custom_call" | custom-call | flops 1 | bytes 1 | tf_op jit(solution)/shard_map/pallas_call | solution.py:221
  169.2 4.2 %shard_map.200.refs_2_ = f32[256,1536]{1,0:T(8,128)S(1)} custom-call(s32[2]{0:T(128)S(1)} %pad_add_fusion.pos, bf16[6144,1536]{1,0:T(8,128)(2,1)} %weight_ref.24, bf16[128,1536]{1,0:T(8,128)(2,1)S(1)} %shard_map.197.refs_0_, bf16[128,1536]{1,0:T(8,128)(2,1)S(1)} %shard_map.199.refs_1_, f32[256,1536]{1,0:T(8,128)S(1)} %shard_map.198.refs_2_), custom_call_target="tpu_custom_call" | custom-call | flops 1 | bytes 1 | tf_op jit(solution)/shard_map/pallas_call | solution.py:221
  177.0 4.2 %shard_map.201.refs_4_ = f32[256,1536]{1,0:T(8,128)S(1)} custom-call(s32[2]{0:T(128)S(1)} %pad_add_fusion.pos, bf16[6144,1536]{1,0:T(8,128)(2,1)} %weight_ref.24, bf16[128,1536]{1,0:T(8,128)(2,1)S(1)} %collective-permute-done.36.refs_0_, bf16[128,1536]{1,0:T(8,128)(2,1)S(1)} %collective-permute-done.40.refs_1_, f32[256,1536]{1,0:T(8,128)S(1)} %shard_map.200.refs_2_), custom_call_target="tpu_custom_call" | custom-call | flops 1 | bytes 1 | tf_op jit(solution)/shard_map/pallas_call | solution.py:221
  185.2 7.0 %shard_map.202 = f32[256,1536]{1,0:T(8,128)S(1)} custom-call(s32[2]{0:T(128)S(1)} %pad_add_fusion.pos, bf16[6144,1536]{1,0:T(8,128)(2,1)} %weight_ref.24, bf16[128,1536]{1,0:T(8,128)(2,1)S(1)} %collective-permute-done.35.refs_0_, bf16[128,1536]{1,0:T(8,128)(2,1)S(1)} %collective-permute-done.41.refs_1_, ...), custom_call_target="tpu_custom_call" | custom-call | flops 1 | bytes 1 | tf_op jit(solution)/shard_map/pallas_call | solution.py:221
  202.9 5.7 %shard_map.203 = bf16[256,2304]{1,0:T(8,128)(2,1)S(1)} custom-call(s32[2]{0:T(128)S(1)} %pad_add_fusion.pos, bf16[256,1536]{1,0:T(8,128)(2,1)S(1)} %constant_dynamic-update-slice_fusion.tokens_ref, bf16[1536,1536]{1,0:T(8,128)(2,1)} %refs_0_.31, bf16[1536,1536]{1,0:T(8,128)(2,1)} %refs_1_.23, bf16[1536,1536]{1,0:T(8,128)(2,1)} %refs_2_.23), custom_call_target="tpu_custom_call" | custom-call | flops 1 | bytes 1 | tf_op jit(solution)/shard_map/pallas_call | solution.py:221
  234.1 4.5 %collective-permute-done.63 = f32[2,64]{1,0:T(2,128)S(1)} collective-permute-done((f32[2,64]{1,0:T(2,128)S(1)}, f32[2,64]{1,0:T(2,128)S(1)}, u32[]{:S(2)}, u32[]{:S(2)}) %collective-permute-start.63) | collective-permute-done | bytes 544 | tf_op jit(solution)/shard_map/ppermute | solution.py:213
  239.1 5.5 %shard_map.205 = bf16[256,2304]{1,0:T(8,128)(2,1)S(1)} custom-call(s32[2]{0:T(128)S(1)} %pad_add_fusion.pos, bf16[256,1536]{1,0:T(8,128)(2,1)S(1)} %pad_maximum_fusion.2.tokens_ref, bf16[1536,1536]{1,0:T(8,128)(2,1)} %refs_0_.31, bf16[1536,1536]{1,0:T(8,128)(2,1)} %refs_1_.23, bf16[1536,1536]{1,0:T(8,128)(2,1)} %refs_2_.23), custom_call_target="tpu_custom_call" | custom-call | flops 1 | bytes 1 | tf_op jit(solution)/shard_map/pallas_call | solution.py:221
  247.6 4.0 %shard_map.206 = bf16[256,1152]{1,0:T(8,128)(2,1)S(1)} custom-call(s32[2]{0:T(128)S(1)} %pad_add_fusion.pos, bf16[256,1536]{1,0:T(8,128)(2,1)S(1)} %pad_maximum_fusion.2.tokens_ref, bf16[1536,1536]{1,0:T(8,128)(2,1)} %refs_0_.31, bf16[1536,1536]{1,0:T(8,128)(2,1)} %refs_1_.23, bf16[1536,1536]{1,0:T(8,128)(2,1)} %refs_2_.23, ...), custom_call_target="tpu_custom_call" | custom-call | flops 1 | bytes 1 | tf_op jit(solution)/shard_map/pallas_call | solution.py:221
  255.2 4.0 %shard_map.208.refs_3_.refs_4_.refs_5_ = f32[256,1152]{1,0:T(8,128)S(1)} custom-call(s32[2]{0:T(128)S(1)} %pad_add_fusion.pos, bf16[256,1536]{1,0:T(8,128)(2,1)S(1)} %pad_maximum_fusion.2.tokens_ref, bf16[1536,1536]{1,0:T(8,128)(2,1)} %refs_0_.31, bf16[1536,1536]{1,0:T(8,128)(2,1)} %refs_1_.23, bf16[1536,1536]{1,0:T(8,128)(2,1)} %refs_2_.23, ...), custom_call_target="tpu_custom_call" | custom-call | flops 1 | bytes 1 | tf_op jit(solution)/shard_map/pallas_call | solution.py:221
  259.2 4.0 %shard_map.207.refs_0_.refs_1_.refs_2_ = bf16[256,1152]{1,0:T(8,128)(2,1)S(1)} custom-call(s32[2]{0:T(128)S(1)} %pad_add_fusion.pos, bf16[256,1536]{1,0:T(8,128)(2,1)S(1)} %constant_dynamic-update-slice_fusion.tokens_ref, bf16[1536,1536]{1,0:T(8,128)(2,1)} %refs_0_.31, bf16[1536,1536]{1,0:T(8,128)(2,1)} %refs_1_.23, bf16[1536,1536]{1,0:T(8,128)(2,1)} %refs_2_.23, ...), custom_call_target="tpu_custom_call" | custom-call | flops 1 | bytes 1 | tf_op jit(solution)/shard_map/pallas_call | solution.py:221
  263.2 5.8 %collective-permute-done.66.refs_6_.refs_7_.refs_8_ = bf16[256,1152]{1,0:T(8,128)(2,1)S(1)} collective-permute-done((bf16[256,1152]{1,0:T(8,128)(2,1)S(1)}, bf16[256,1152]{1,0:T(8,128)(2,1)S(1)}, u32[]{:S(2)}, u32[]{:S(2)}) %collective-permute-start.66) | collective-permute-done | bytes 589856 | tf_op jit(solution)/shard_map/ppermute | solution.py:200
  273.8 8.8 %collective-permute-done.68.refs_2_ = bf16[512,384]{1,0:T(8,128)(2,1)S(1)} collective-permute-done((bf16[512,384]{1,0:T(8,128)(2,1)S(1)}, bf16[512,384]{1,0:T(8,128)(2,1)S(1)}, u32[]{:S(2)}, u32[]{:S(2)}) %collective-permute-start.68) | collective-permute-done | bytes 393248 | tf_op jit(solution)/shard_map/ppermute | solution.py:200
  284.3 6.2 %shard_map.210 = f32[512,1536]{1,0:T(8,128)S(1)} custom-call(s32[2]{0:T(128)S(1)} %pad_add_fusion.pos, bf16[1536,1536]{1,0:T(8,128)(2,1)} %weight_ref.25, bf16[512,384]{1,0:T(8,128)(2,1)S(1)} %bitcast.145, bf16[512,384]{1,0:T(8,128)(2,1)S(1)} %collective-permute-done.67.refs_1_, bf16[512,384]{1,0:T(8,128)(2,1)S(1)} %collective-permute-done.68.refs_2_, ...), custom_call_target="tpu_custom_call" | custom-call | flops 1 | bytes 1 | tf_op jit(solution)/shard_map/pallas_call | solution.py:221
  311.3 6.1 %collective-permute-done.71 = bf16[64,1536]{1,0:T(8,128)(2,1)S(1)} collective-permute-done((bf16[64,1536]{1,0:T(8,128)(2,1)S(1)}, bf16[64,1536]{1,0:T(8,128)(2,1)S(1)}, u32[]{:S(2)}, u32[]{:S(2)}) %collective-permute-start.71) | collective-permute-done | bytes 196640 | tf_op jit(solution)/shard_map/ppermute | solution.py:213
  (238 shorter events, 153.0 us)
Async XLA Ops:
  1.1 11.2 %collective-permute-start = (bf16[64,1536]{1,0:T(8,128)(2,1)S(1)}, bf16[64,1536]{1,0:T(8,128)(2,1)S(1)}, u32[]{:S(2)}, u32[]{:S(2)}) collective-permute-start(bf16[64,1536]{1,0:T(8,128)(2,1)S(1)} %get-tuple-element.194), channel_id=1, source_target_pairs={{0,1},{1,2},{2,3},{3,0},{4,5},{5,6},{6,7},{7,4},{8,9},{9,10},{10,1... | collective-permute-start | bytes 589832 | tf_op jit(solution)/shard_map/ppermute | solution.py:213
  4.1 10.6 %collective-permute-start.1 = (bf16[64,1536]{1,0:T(8,128)(2,1)S(1)}, bf16[64,1536]{1,0:T(8,128)(2,1)S(1)}, u32[]{:S(2)}, u32[]{:S(2)}) collective-permute-start(bf16[64,1536]{1,0:T(8,128)(2,1)S(1)} %get-tuple-element.194), channel_id=1, source_target_pairs={{0,3},{1,0},{2,1},{3,2},{4,7},{5,4},{6,5},{7,6},{8,11},{9,8},{10,9... | collective-permute-start | bytes 589832 | tf_op jit(solution)/shard_map/ppermute | solution.py:213
  33.6 9.8 %collective-permute-start.12 = (bf16[256,2304]{1,0:T(8,128)(2,1)S(1)}, bf16[256,2304]{1,0:T(8,128)(2,1)S(1)}, u32[]{:S(2)}, u32[]{:S(2)}) collective-permute-start(bf16[256,2304]{1,0:T(8,128)(2,1)S(1)} %shard_map.181), channel_id=1, source_target_pairs={{0,4},{4,0},{8,12},{12,8},{1,5},{5,1},{9,13},{13,9},{2,6},{6,2},{1... | collective-permute-start | bytes 3538952 | tf_op jit(solution)/shard_map/ppermute | solution.py:200
  33.6 9.8 %collective-permute-start.11 = (bf16[64,1536]{1,0:T(8,128)(2,1)S(1)}, bf16[64,1536]{1,0:T(8,128)(2,1)S(1)}, u32[]{:S(2)}, u32[]{:S(2)}) collective-permute-start(bf16[64,1536]{1,0:T(8,128)(2,1)S(1)} %get-tuple-element.221), channel_id=1, source_target_pairs={{0,3},{1,0},{2,1},{3,2},{4,7},{5,4},{6,5},{7,6},{8,11},{9,8},{10,9... | collective-permute-start | bytes 589832 | tf_op jit(solution)/shard_map/ppermute | solution.py:213
  47.6 15.6 %collective-permute-start.14 = (bf16[256,1152]{1,0:T(8,128)(2,1)S(1)}, bf16[256,1152]{1,0:T(8,128)(2,1)S(1)}, u32[]{:S(2)}, u32[]{:S(2)}) collective-permute-start(bf16[256,1152]{1,0:T(8,128)(2,1)S(1)} %shard_map.183), channel_id=1, source_target_pairs={{0,8},{4,12},{8,0},{12,4},{1,9},{5,13},{9,1},{13,5},{2,10},{6,14},... | collective-permute-start | bytes 1769480 | tf_op jit(solution)/shard_map/ppermute | solution.py:200
  63.3 19.6 %collective-permute-start.17 = (bf16[256,1536]{1,0:T(8,128)(2,1)S(1)}, bf16[256,1536]{1,0:T(8,128)(2,1)S(1)}, u32[]{:S(2)}, u32[]{:S(2)}) collective-permute-start(bf16[256,1536]{1,0:T(8,128)(2,1)S(1)} %shard_map.184), channel_id=1, source_target_pairs={{0,8},{4,12},{8,0},{12,4},{1,9},{5,13},{9,1},{13,5},{2,10},{6,14},... | collective-permute-start | bytes 2359304 | tf_op jit(solution)/shard_map/ppermute | solution.py:200
  90.4 18.8 %collective-permute-start.23 = (bf16[256,1536]{1,0:T(8,128)(2,1)S(1)}, bf16[256,1536]{1,0:T(8,128)(2,1)S(1)}, u32[]{:S(2)}, u32[]{:S(2)}) collective-permute-start(bf16[256,1536]{1,0:T(8,128)(2,1)S(1)} %shard_map.188.refs_0_), channel_id=1, source_target_pairs={{0,8},{4,12},{8,0},{12,4},{1,9},{5,13},{9,1},{13,5},{2,10},{6,14},... | collective-permute-start | bytes 2359304 | tf_op jit(solution)/shard_map/ppermute | solution.py:200
  91.2 18.0 %collective-permute-start.24 = (bf16[256,1536]{1,0:T(8,128)(2,1)S(1)}, bf16[256,1536]{1,0:T(8,128)(2,1)S(1)}, u32[]{:S(2)}, u32[]{:S(2)}) collective-permute-start(bf16[256,1536]{1,0:T(8,128)(2,1)S(1)} %shard_map.188.refs_0_), channel_id=1, source_target_pairs={{0,4},{4,0},{8,12},{12,8},{1,5},{5,1},{9,13},{13,9},{2,6},{6,2},{1... | collective-permute-start | bytes 2359304 | tf_op jit(solution)/shard_map/ppermute | solution.py:200
  91.2 17.7 %collective-permute-start.22 = (bf16[256,384]{1,0:T(8,128)(2,1)S(1)}, bf16[256,384]{1,0:T(8,128)(2,1)S(1)}, u32[]{:S(2)}, u32[]{:S(2)}) collective-permute-start(bf16[256,384]{1,0:T(8,128)(2,1)S(1)} %collective-permute-done.18.refs_2_), channel_id=1, source_target_pairs={{0,4},{4,0},{8,12},{12,8},{1,5},{5,1},{9,13},{13,9},{2,6},{6,2},{1... | collective-permute-start | bytes 589832 | tf_op jit(solution)/shard_map/ppermute | solution.py:200
  109.2 15.7 %collective-permute-start.26 = (bf16[256,1152]{1,0:T(8,128)(2,1)S(1)}, bf16[256,1152]{1,0:T(8,128)(2,1)S(1)}, u32[]{:S(2)}, u32[]{:S(2)}) collective-permute-start(bf16[256,1152]{1,0:T(8,128)(2,1)S(1)} %shard_map.189), channel_id=1, source_target_pairs={{0,8},{4,12},{8,0},{12,4},{1,9},{5,13},{9,1},{13,5},{2,10},{6,14},... | collective-permute-start | bytes 1769480 | tf_op jit(solution)/shard_map/ppermute | solution.py:200
  125.0 15.4 %collective-permute-start.27 = (bf16[128,1536]{1,0:T(8,128)(2,1)S(1)}, bf16[128,1536]{1,0:T(8,128)(2,1)S(1)}, u32[]{:S(2)}, u32[]{:S(2)}) collective-permute-start(bf16[128,1536]{1,0:T(8,128)(2,1)S(1)} %get-tuple-element.258), channel_id=1, source_target_pairs={{0,8},{4,12},{8,0},{12,4},{1,9},{5,13},{9,1},{13,5},{2,10},{6,14},... | collective-permute-start | bytes 1179656 | tf_op jit(solution)/shard_map/ppermute | solution.py:200
  126.4 10.5 %collective-permute-start.30 = (bf16[64,1536]{1,0:T(8,128)(2,1)S(1)}, bf16[64,1536]{1,0:T(8,128)(2,1)S(1)}, u32[]{:S(2)}, u32[]{:S(2)}) collective-permute-start(bf16[64,1536]{1,0:T(8,128)(2,1)S(1)} %get-tuple-element.386), channel_id=1, source_target_pairs={{0,3},{1,0},{2,1},{3,2},{4,7},{5,4},{6,5},{7,6},{8,11},{9,8},{10,9... | collective-permute-start | bytes 589832 | tf_op jit(solution)/shard_map/ppermute | solution.py:213
  140.5 12.3 %collective-permute-start.31 = (bf16[128,1536]{1,0:T(8,128)(2,1)S(1)}, bf16[128,1536]{1,0:T(8,128)(2,1)S(1)}, u32[]{:S(2)}, u32[]{:S(2)}) collective-permute-start(bf16[128,1536]{1,0:T(8,128)(2,1)S(1)} %get-tuple-element.265), channel_id=1, source_target_pairs={{0,8},{4,12},{8,0},{12,4},{1,9},{5,13},{9,1},{13,5},{2,10},{6,14},... | collective-permute-start | bytes 1179656 | tf_op jit(solution)/shard_map/ppermute | solution.py:200
  141.8 11.0 %collective-permute-start.34 = (bf16[64,1536]{1,0:T(8,128)(2,1)S(1)}, bf16[64,1536]{1,0:T(8,128)(2,1)S(1)}, u32[]{:S(2)}, u32[]{:S(2)}) collective-permute-start(bf16[64,1536]{1,0:T(8,128)(2,1)S(1)} %get-tuple-element.272), channel_id=1, source_target_pairs={{0,2},{1,3},{2,0},{3,1},{4,6},{5,7},{6,4},{7,5},{8,10},{9,11},{10,... | collective-permute-start | bytes 589832 | tf_op jit(solution)/shard_map/ppermute | solution.py:213
  152.8 11.1 %collective-permute-start.35 = (bf16[128,1536]{1,0:T(8,128)(2,1)S(1)}, bf16[128,1536]{1,0:T(8,128)(2,1)S(1)}, u32[]{:S(2)}, u32[]{:S(2)}) collective-permute-start(bf16[128,1536]{1,0:T(8,128)(2,1)S(1)} %shard_map.197.refs_0_), channel_id=1, source_target_pairs={{0,8},{4,12},{8,0},{12,4},{1,9},{5,13},{9,1},{13,5},{2,10},{6,14},... | collective-permute-start | bytes 1179656 | tf_op jit(solution)/shard_map/ppermute | solution.py:200
  153.7 10.2 %collective-permute-start.36 = (bf16[128,1536]{1,0:T(8,128)(2,1)S(1)}, bf16[128,1536]{1,0:T(8,128)(2,1)S(1)}, u32[]{:S(2)}, u32[]{:S(2)}) collective-permute-start(bf16[128,1536]{1,0:T(8,128)(2,1)S(1)} %shard_map.197.refs_0_), channel_id=1, source_target_pairs={{0,4},{4,0},{8,12},{12,8},{1,5},{5,1},{9,13},{13,9},{2,6},{6,2},{1... | collective-permute-start | bytes 1179656 | tf_op jit(solution)/shard_map/ppermute | solution.py:200
  163.9 12.9 %collective-permute-start.40 = (bf16[128,1536]{1,0:T(8,128)(2,1)S(1)}, bf16[128,1536]{1,0:T(8,128)(2,1)S(1)}, u32[]{:S(2)}, u32[]{:S(2)}) collective-permute-start(bf16[128,1536]{1,0:T(8,128)(2,1)S(1)} %shard_map.199.refs_1_), channel_id=1, source_target_pairs={{0,4},{4,0},{8,12},{12,8},{1,5},{5,1},{9,13},{13,9},{2,6},{6,2},{1... | collective-permute-start | bytes 1179656 | tf_op jit(solution)/shard_map/ppermute | solution.py:200
  164.1 12.8 %collective-permute-start.41 = (bf16[128,1536]{1,0:T(8,128)(2,1)S(1)}, bf16[128,1536]{1,0:T(8,128)(2,1)S(1)}, u32[]{:S(2)}, u32[]{:S(2)}) collective-permute-start(bf16[128,1536]{1,0:T(8,128)(2,1)S(1)} %shard_map.199.refs_1_), channel_id=1, source_target_pairs={{0,8},{4,12},{8,0},{12,4},{1,9},{5,13},{9,1},{13,5},{2,10},{6,14},... | collective-permute-start | bytes 1179656 | tf_op jit(solution)/shard_map/ppermute | solution.py:200
  165.0 11.9 %collective-permute-start.42 = (bf16[128,1536]{1,0:T(8,128)(2,1)S(1)}, bf16[128,1536]{1,0:T(8,128)(2,1)S(1)}, u32[]{:S(2)}, u32[]{:S(2)}) collective-permute-start(bf16[128,1536]{1,0:T(8,128)(2,1)S(1)} %collective-permute-done.35.refs_0_), channel_id=1, source_target_pairs={{0,4},{4,0},{8,12},{12,8},{1,5},{5,1},{9,13},{13,9},{2,6},{6,2},{1... | collective-permute-start | bytes 1179656 | tf_op jit(solution)/shard_map/ppermute | solution.py:200
  165.8 11.1 %collective-permute-start.44 = (bf16[64,1536]{1,0:T(8,128)(2,1)S(1)}, bf16[64,1536]{1,0:T(8,128)(2,1)S(1)}, u32[]{:S(2)}, u32[]{:S(2)}) collective-permute-start(bf16[64,1536]{1,0:T(8,128)(2,1)S(1)} %multiply_convert_fusion.4), channel_id=1, source_target_pairs={{0,3},{1,0},{2,1},{3,2},{4,7},{5,4},{6,5},{7,6},{8,11},{9,8},{10,9... | collective-permute-start | bytes 589832 | tf_op jit(solution)/shard_map/ppermute | solution.py:213
  181.2 10.9 %collective-permute-start.46 = (bf16[32,1536]{1,0:T(8,128)(2,1)S(1)}, bf16[32,1536]{1,0:T(8,128)(2,1)S(1)}, u32[]{:S(2)}, u32[]{:S(2)}) collective-permute-start(bf16[32,1536]{1,0:T(8,128)(2,1)S(1)} %slice.215), channel_id=1, source_target_pairs={{0,1},{1,2},{2,3},{3,0},{4,5},{5,6},{6,7},{7,4},{8,9},{9,10},{10,1... | collective-permute-start | bytes 294920 | tf_op jit(solution)/shard_map/ppermute | solution.py:213
  212.5 11.2 %collective-permute-start.54 = (bf16[64,1536]{1,0:T(8,128)(2,1)S(1)}, bf16[64,1536]{1,0:T(8,128)(2,1)S(1)}, u32[]{:S(2)}, u32[]{:S(2)}) collective-permute-start(bf16[64,1536]{1,0:T(8,128)(2,1)S(1)} %get-tuple-element.344), channel_id=1, source_target_pairs={{0,3},{1,0},{2,1},{3,2},{4,7},{5,4},{6,5},{7,6},{8,11},{9,8},{10,9... | collective-permute-start | bytes 589832 | tf_op jit(solution)/shard_map/ppermute | solution.py:213
  223.8 14.8 %collective-permute-start.58 = (bf16[128,1152]{1,0:T(8,128)(2,1)S(1)}, bf16[128,1152]{1,0:T(8,128)(2,1)S(1)}, u32[]{:S(2)}, u32[]{:S(2)}) collective-permute-start(bf16[128,1152]{1,0:T(8,128)(2,1)S(1)} %get-tuple-element.335), channel_id=1, source_target_pairs={{0,8},{4,12},{8,0},{12,4},{1,9},{5,13},{9,1},{13,5},{2,10},{6,14},... | collective-permute-start | bytes 884744 | tf_op jit(solution)/shard_map/ppermute | solution.py:200
  224.8 13.8 %collective-permute-start.59 = (bf16[32,1536]{1,0:T(8,128)(2,1)S(1)}, bf16[32,1536]{1,0:T(8,128)(2,1)S(1)}, u32[]{:S(2)}, u32[]{:S(2)}) collective-permute-start(bf16[32,1536]{1,0:T(8,128)(2,1)S(1)} %slice.224), channel_id=1, source_target_pairs={{0,1},{1,2},{2,3},{3,0},{4,5},{5,6},{6,7},{7,4},{8,9},{9,10},{10,1... | collective-permute-start | bytes 294920 | tf_op jit(solution)/shard_map/ppermute | solution.py:213
  225.2 13.4 %collective-permute-start.60 = (bf16[32,1536]{1,0:T(8,128)(2,1)S(1)}, bf16[32,1536]{1,0:T(8,128)(2,1)S(1)}, u32[]{:S(2)}, u32[]{:S(2)}) collective-permute-start(bf16[32,1536]{1,0:T(8,128)(2,1)S(1)} %slice.225), channel_id=1, source_target_pairs={{0,3},{1,0},{2,1},{3,2},{4,7},{5,4},{6,5},{7,6},{8,11},{9,8},{10,9... | collective-permute-start | bytes 294920 | tf_op jit(solution)/shard_map/ppermute | solution.py:213
  254.2 14.9 %collective-permute-start.66 = (bf16[256,1152]{1,0:T(8,128)(2,1)S(1)}, bf16[256,1152]{1,0:T(8,128)(2,1)S(1)}, u32[]{:S(2)}, u32[]{:S(2)}) collective-permute-start(bf16[256,1152]{1,0:T(8,128)(2,1)S(1)} %shard_map.206), channel_id=1, source_target_pairs={{0,8},{4,12},{8,0},{12,4},{1,9},{5,13},{9,1},{13,5},{2,10},{6,14},... | collective-permute-start | bytes 1769480 | tf_op jit(solution)/shard_map/ppermute | solution.py:200
  272.8 9.9 %collective-permute-start.68 = (bf16[512,384]{1,0:T(8,128)(2,1)S(1)}, bf16[512,384]{1,0:T(8,128)(2,1)S(1)}, u32[]{:S(2)}, u32[]{:S(2)}) collective-permute-start(bf16[512,384]{1,0:T(8,128)(2,1)S(1)} %bitcast.143), channel_id=1, source_target_pairs={{0,8},{4,12},{8,0},{12,4},{1,9},{5,13},{9,1},{13,5},{2,10},{6,14},... | collective-permute-start | bytes 1179656 | tf_op jit(solution)/shard_map/ppermute | solution.py:200
  290.9 12.0 %collective-permute-start.74 = (bf16[64,1536]{1,0:T(8,128)(2,1)S(1)}, bf16[64,1536]{1,0:T(8,128)(2,1)S(1)}, u32[]{:S(2)}, u32[]{:S(2)}) collective-permute-start(bf16[64,1536]{1,0:T(8,128)(2,1)S(1)} %get-tuple-element.378), channel_id=1, source_target_pairs={{0,3},{1,0},{2,1},{3,2},{4,7},{5,4},{6,5},{7,6},{8,11},{9,8},{10,9... | collective-permute-start | bytes 589832 | tf_op jit(solution)/shard_map/ppermute | solution.py:213
  294.7 14.2 %collective-permute-start.72 = (bf16[64,1536]{1,0:T(8,128)(2,1)S(1)}, bf16[64,1536]{1,0:T(8,128)(2,1)S(1)}, u32[]{:S(2)}, u32[]{:S(2)}) collective-permute-start(bf16[64,1536]{1,0:T(8,128)(2,1)S(1)} %get-tuple-element.379), channel_id=1, source_target_pairs={{0,1},{1,2},{2,3},{3,0},{4,5},{5,6},{6,7},{7,4},{8,9},{9,10},{10,1... | collective-permute-start | bytes 589832 | tf_op jit(solution)/shard_map/ppermute | solution.py:213
  294.7 16.6 %collective-permute-start.73 = (bf16[64,1536]{1,0:T(8,128)(2,1)S(1)}, bf16[64,1536]{1,0:T(8,128)(2,1)S(1)}, u32[]{:S(2)}, u32[]{:S(2)}) collective-permute-start(bf16[64,1536]{1,0:T(8,128)(2,1)S(1)} %get-tuple-element.377), channel_id=1, source_target_pairs={{0,3},{1,0},{2,1},{3,2},{4,7},{5,4},{6,5},{7,6},{8,11},{9,8},{10,9... | collective-permute-start | bytes 589832 | tf_op jit(solution)/shard_map/ppermute | solution.py:213
  303.0 14.4 %collective-permute-start.71 = (bf16[64,1536]{1,0:T(8,128)(2,1)S(1)}, bf16[64,1536]{1,0:T(8,128)(2,1)S(1)}, u32[]{:S(2)}, u32[]{:S(2)}) collective-permute-start(bf16[64,1536]{1,0:T(8,128)(2,1)S(1)} %get-tuple-element.376), channel_id=1, source_target_pairs={{0,1},{1,2},{2,3},{3,0},{4,5},{5,6},{6,7},{7,4},{8,9},{9,10},{10,1... | collective-permute-start | bytes 589832 | tf_op jit(solution)/shard_map/ppermute | solution.py:213
  303.5 15.4 %collective-permute-start.75 = (bf16[64,1536]{1,0:T(8,128)(2,1)S(1)}, bf16[64,1536]{1,0:T(8,128)(2,1)S(1)}, u32[]{:S(2)}, u32[]{:S(2)}) collective-permute-start(bf16[64,1536]{1,0:T(8,128)(2,1)S(1)} %get-tuple-element.375), channel_id=1, source_target_pairs={{0,3},{1,0},{2,1},{3,2},{4,7},{5,4},{6,5},{7,6},{8,11},{9,8},{10,9... | collective-permute-start | bytes 589832 | tf_op jit(solution)/shard_map/ppermute | solution.py:213
  (55 other events, 403.6 us)

commit v5 on v4

--- a/solution.py
+++ b/solution.py
@@ -640,19 +640,23 @@
     tok_a, own_b, b_before, qs_a = sync(tok_a, own_b, b_before, qs_a)
 
     b_after, qc_a = sent(own_b, -1), core_swap(qs_a)
+    qx_a = heads_across(tok_a, heads_in, qc_a, 2)
+    tok_a, own_b, b_before, b_after, qc_a, qx_a0, qx_a1 = sync(
+        tok_a, own_b, b_before, b_after, qc_a, *qx_a
+    )
+
+    qy_a0 = y_swap(qx_a0)
     us_a = units_send(tok_a)
-    tok_a, own_b, b_after, qc_a, us_a = sync(tok_a, own_b, b_after, qc_a, us_a)
-
-    uc_a = core_swap(us_a)
-    (qx_a,) = heads_across(tok_a, heads_in, qc_a)
-    tok_a, own_b, b_before, b_after, qc_a, uc_a, qx_a = sync(
-        tok_a, own_b, b_before, b_after, qc_a, uc_a, qx_a
-    )
-
-    qy_a, b_away0, b_away1 = y_swap(qx_a), *sent_on(b_before, b_after)
+    tok_a, own_b, b_before, b_after, qc_a, us_a, qy_a0, qx_a1 = sync(
+        tok_a, own_b, b_before, b_after, qc_a, us_a, qy_a0, qx_a1
+    )
+
+    uc_a, qy_a1, b_away0, b_away1 = (
+        core_swap(us_a), y_swap(qx_a1), *sent_on(b_before, b_after)
+    )
     (ux_a,) = units_across(tok_a, uc_a, 1)
-    tok_a, qc_a, uc_a, ux_a, qy_a, own_b, b_before, b_after, b_away0, b_away1 = sync(
-        tok_a, qc_a, uc_a, ux_a, qy_a, own_b, b_before, b_after, b_away0, b_away1
+    tok_a, qc_a, uc_a, ux_a, qy_a0, qy_a1, own_b, b_before, b_after, b_away0, b_away1 = sync(
+        tok_a, qc_a, uc_a, ux_a, qy_a0, qy_a1, own_b, b_before, b_after, b_away0, b_away1
     )
     b_away = jnp.concatenate((b_away0, b_away1))
 
@@ -660,7 +664,7 @@
     tok_b = normed_shards((own_b, b_before, b_after, b_away), norm_gain, totals_b)
     qs_b = heads_send(tok_b, heads_in)
     us_b = units_send(tok_b)
-    at_a = project_heads(run, tok_a, heads_in, scales, head_width, qc_a, (qy_a,), True)
+    at_a = project_heads(run, tok_a, heads_in, scales, head_width, qc_a, (qy_a0, qy_a1), True)
     tok_a, tok_b, qs_b, us_b, at_a, uc_a, uy_a = sync(
         tok_a, tok_b, qs_b, us_b, at_a, uc_a, uy_a
     )
@@ -680,8 +684,8 @@
     )
 
     qy_b, hd_fa = y_swap(qx_b), core_swap(hd_ya)
-    mixed_a = units_down(((hd_ca,),), 1, heads_out((at_fa,), 3, mixed_a))
-    mixed_a = units_down(((hd_ya,), (hd_fa,)), 2, mixed_a)
+    mixed_a = heads_out((at_fa,), 3, mixed_a)
+    mixed_a = units_down(((hd_ca,), (hd_ya,), (hd_fa,)), 1, mixed_a)
     tok_b, mixed_a, qc_b, qy_b, uc_b, ux_b0, ux_b1 = sync(
         tok_b, mixed_a, qc_b, qy_b, uc_b, *ux_b
     )
@@ -746,17 +750,17 @@
     from_before, from_after = sent(after_b, 1), sent(before_b, -1)
     tok_ja = jnp.concatenate((join_a, *shards))
     js_a = heads_send(tok_ja, join_in)
-    tok_ja, js_a, mine_b, *arrived = sync(tok_ja, js_a, mine_b, from_before, from_after)
+    jc_a = core_swap(js_a)
+    tok_ja, jc_a, mine_b, *arrived = sync(tok_ja, jc_a, mine_b, from_before, from_after)
 
     layer_b = layer_end(start_f32[half:], mine_b, *arrived)
-    pairs = moment_flips(moment_pair(layer_b.astype(jnp.float32)))
-    jb_before, jb_after, jc_a = sent(layer_b, 1), sent(layer_b, -1), core_swap(js_a)
+    totals = moment_shards(moment_sum(moment_flips(moment_pair(layer_b.astype(jnp.float32)))))
+    jb_before, jb_after = sent(layer_b, 1), sent(layer_b, -1)
     jx_a = heads_across(tok_ja, join_in, jc_a, 2)
-    tok_ja, jc_a, jx_a0, jx_a1, layer_b, jb_before, jb_after, *pairs = sync(
-        tok_ja, jc_a, *jx_a, layer_b, jb_before, jb_after, *pairs
-    )
-
-    totals = moment_shards(moment_sum(pairs))
+    tok_ja, jc_a, jx_a0, jx_a1, layer_b, jb_before, jb_after, *totals = sync(
+        tok_ja, jc_a, *jx_a, layer_b, jb_before, jb_after, *totals
+    )
+
     jb_away0, jb_away1 = sent_on(jb_before, jb_after)
     jy_a0 = y_swap(jx_a0)
     tok_ja, jc_a, jy_a0, jx_a1, layer_b, jb_before, jb_after, jb_away0, jb_away1, *totals = sync(
@@ -783,7 +787,8 @@
     joined = joined.reshape(2, 4, half, head_width).swapaxes(0, 1).reshape(8 * half, head_width)
     jo_y, jo_c = y_swap(joined), core_swap(joined)
     jo_f = core_swap(jo_y)
-    result = contract(run, ((joined,), (jo_c,), (jo_y,), (jo_f,)), join_out, 1)
+    result = contract(run, ((joined,), (jo_c,)), join_out, 1)
+    result = contract(run, ((jo_y,), (jo_f,)), join_out, 1, 2, result)
     summed = scatter_rows_long(result)
     layer_own = jnp.concatenate((layer_a, layer_b))
     return (layer_own.astype(jnp.float32) + summed).astype(jnp.bfloat16)

time: 325 us -> 330 us (1.015)
    ppermute x41 -> x42, waiting for transfers between devices: 38 us -> 32.9 us  [flip(): return lax.ppermute(array, 'cols', [(i, i ^ mask) for i in range(size)])]
    ppermute x35, waiting for transfers between devices: 43.9 us -> 48.6 us  [row_shift(): lax.ppermute(array, 'rows', [(i, (i + shift) % size) for i in range(size)])]
    ppermute x41 -> x42, starting transfers between devices: 22.9 us -> 24.4 us  [flip(): return lax.ppermute(array, 'cols', [(i, i ^ mask) for i in range(size)])]
  transfers between devices with their start and end apart: 76 -> 77, of which waited for: 34 -> 36; matrix products, arithmetic and copies ran while one was open for 1% -> 1% of each run, Pallas kernels for 41% -> 39%
where the time goes in v5:
time: 330 us; the launch traced here: 325 us
  Pallas kernels  146 us (44%)
  starting transfers between devices  88.1 us (27%)
  waiting for transfers between devices  81.5 us (25%)
  other arithmetic  4.86 us (1%)
  local copies, waits for them, and re-layouts  3.44 us (1%)
    pallas_call x30, Pallas kernels, __call__(): pl.pallas_call(kernel, out_shape=out_shape, grid_spec=pltpu.PrefetchScala...  146 us
    ppermute x35, starting transfers between devices, row_shift(): lax.ppermute(array, 'rows', [(i, (i + shift) % size) for i in range(size)])  63.8 us
    ppermute x35, waiting for transfers between devices, row_shift(): lax.ppermute(array, 'rows', [(i, (i + shift) % size) for i in range(size)])  48.6 us
    ppermute x42, waiting for transfers between devices, flip(): return lax.ppermute(array, 'cols', [(i, i ^ mask) for i in range(size)])  32.9 us
    ppermute x42, starting transfers between devices, flip(): return lax.ppermute(array, 'cols', [(i, i ^ mask) for i in range(size)])  24.4 us
  transfers between devices with their start and end apart: 77, of which 36 were waited for; matrix products, arithmetic and copies ran while one was open for 1% of the time, Pallas kernels for 39%

profile of v5, /device:TPU:0, one launch (start us, length us, event | category | flops | bytes accessed | tf_op | source)
XLA Modules:
  0.0 324.8 jit_solution(5914469340615300919)
XLA Ops:
  27.5 5.5 %shard_map.181 = bf16[256,2304]{1,0:T(8,128)(2,1)S(1)} custom-call(s32[2]{0:T(128)S(1)} %pad_add_fusion.pos, bf16[256,1536]{1,0:T(8,128)(2,1)S(1)} %pad_maximum_fusion.tokens_ref, bf16[1536,1536]{1,0:T(8,128)(2,1)} %refs_0_.25, bf16[1536,1536]{1,0:T(8,128)(2,1)} %refs_1_.17, bf16[1536,1536]{1,0:T(8,128)(2,1)} %refs_2_.17), custom_call_target="tpu_custom_call" | custom-call | flops 1 | bytes 1 | tf_op jit(solution)/shard_map/pallas_call | solution.py:221
  36.4 4.0 %shard_map.182 = (bf16[128,1152]{1,0:T(8,128)(2,1)S(1)}, bf16[128,1152]{1,0:T(8,128)(2,1)S(1)}) custom-call(s32[2]{0:T(128)S(1)} %pad_add_fusion.pos, bf16[256,1536]{1,0:T(8,128)(2,1)S(1)} %pad_maximum_fusion.tokens_ref, bf16[1536,1536]{1,0:T(8,128)(2,1)} %refs_0_.25, bf16[1536,1536]{1,0:T(8,128)(2,1)} %refs_1_.17, bf16[1536,1536]{1,0:T(8,128)(2,1)} %refs_2_.17, ...), custom_call_target="tpu_custom_call" | custom-call | flops 1 | bytes 1 | tf_op jit(solution)/shard_map/pallas_call | solution.py:221
  42.4 7.4 %shard_map.183 = bf16[256,3072]{1,0:T(8,128)(2,1)S(1)} custom-call(s32[2]{0:T(128)S(1)} %pad_add_fusion.pos, bf16[256,1536]{1,0:T(8,128)(2,1)S(1)} %pad_maximum_fusion.tokens_ref, bf16[1536,6144]{1,0:T(8,128)(2,1)} %weight_ref.20), custom_call_target="tpu_custom_call" | custom-call | flops 1 | bytes 1 | tf_op jit(solution)/shard_map/pallas_call | solution.py:221
  55.5 4.6 %shard_map.184 = bf16[256,1536]{1,0:T(8,128)(2,1)S(1)} custom-call(s32[2]{0:T(128)S(1)} %pad_add_fusion.pos, bf16[256,1536]{1,0:T(8,128)(2,1)S(1)} %pad_maximum_fusion.tokens_ref, bf16[1536,6144]{1,0:T(8,128)(2,1)} %weight_ref.20, bf16[256,3072]{1,0:T(8,128)(2,1)S(1)} %collective-permute-done.14.refs_1_.arrived_ref), custom_call_target="tpu_custom_call" | custom-call | flops 1 | bytes 1 | tf_op jit(solution)/shard_map/pallas_call | solution.py:221
  61.9 7.4 %shard_map.186 = bf16[256,3072]{1,0:T(8,128)(2,1)S(1)} custom-call(s32[2]{0:T(128)S(1)} %pad_add_fusion.pos, bf16[256,1536]{1,0:T(8,128)(2,1)S(1)} %pad_maximum_fusion.1.tokens_ref, bf16[1536,6144]{1,0:T(8,128)(2,1)} %weight_ref.20), custom_call_target="tpu_custom_call" | custom-call | flops 1 | bytes 1 | tf_op jit(solution)/shard_map/pallas_call | solution.py:221
  69.3 5.5 %shard_map.185 = bf16[256,2304]{1,0:T(8,128)(2,1)S(1)} custom-call(s32[2]{0:T(128)S(1)} %pad_add_fusion.pos, bf16[256,1536]{1,0:T(8,128)(2,1)S(1)} %pad_maximum_fusion.1.tokens_ref, bf16[1536,1536]{1,0:T(8,128)(2,1)} %refs_0_.25, bf16[1536,1536]{1,0:T(8,128)(2,1)} %refs_1_.17, bf16[1536,1536]{1,0:T(8,128)(2,1)} %refs_2_.17), custom_call_target="tpu_custom_call" | custom-call | flops 1 | bytes 1 | tf_op jit(solution)/shard_map/pallas_call | solution.py:221
  74.8 4.4 %shard_map.187.refs_0_ = bf16[256,384]{1,0:T(8,128)(2,1)S(1)} custom-call(s32[2]{0:T(128)S(1)} %pad_add_fusion.pos, bf16[256,1536]{1,0:T(8,128)(2,1)S(1)} %pad_maximum_fusion.tokens_ref, bf16[1536,1536]{1,0:T(8,128)(2,1)} %refs_0_.25, bf16[1536,1536]{1,0:T(8,128)(2,1)} %refs_1_.17, bf16[1536,1536]{1,0:T(8,128)(2,1)} %refs_2_.17, ...), custom_call_target="tpu_custom_call" | custom-call | flops 1 | bytes 1 | tf_op jit(solution)/shard_map/pallas_call | solution.py:221
  81.0 4.8 %shard_map.188.refs_0_ = bf16[256,1536]{1,0:T(8,128)(2,1)S(1)} custom-call(s32[2]{0:T(128)S(1)} %pad_add_fusion.pos, bf16[256,1536]{1,0:T(8,128)(2,1)S(1)} %pad_maximum_fusion.tokens_ref, bf16[1536,6144]{1,0:T(8,128)(2,1)} %weight_ref.20, f32[1,6144]{1,0:T(1,128)S(1)} %bitcast.147, bf16[256,3072]{1,0:T(8,128)(2,1)S(1)} %collective-permute-done.14.refs_1_.arrived_ref, ...), custom_call_target="tpu_custom_call" | custom-call | flops 1 | bytes 1 | tf_op jit(solution)/shard_map/pallas_call | solution.py:221
  88.4 4.6 %shard_map.192 = (bf16[128,1536]{1,0:T(8,128)(2,1)S(1)}, bf16[128,1536]{1,0:T(8,128)(2,1)S(1)}) custom-call(s32[2]{0:T(128)S(1)} %pad_add_fusion.pos, bf16[256,1536]{1,0:T(8,128)(2,1)S(1)} %pad_maximum_fusion.1.tokens_ref, bf16[1536,6144]{1,0:T(8,128)(2,1)} %weight_ref.20, bf16[256,3072]{1,0:T(8,128)(2,1)S(1)} %collective-permute-done.22.refs_1_.arrived_ref), custom_call_target="tpu_custom_call" | custom-call | flops 1 | bytes 1 | tf_op jit(solution)/shard_map/pallas_call | solution.py:221
  93.0 4.0 %shard_map.189 = bf16[256,1152]{1,0:T(8,128)(2,1)S(1)} custom-call(s32[2]{0:T(128)S(1)} %pad_add_fusion.pos, bf16[256,1536]{1,0:T(8,128)(2,1)S(1)} %pad_maximum_fusion.1.tokens_ref, bf16[1536,1536]{1,0:T(8,128)(2,1)} %refs_0_.25, bf16[1536,1536]{1,0:T(8,128)(2,1)} %refs_1_.17, bf16[1536,1536]{1,0:T(8,128)(2,1)} %refs_2_.17, ...), custom_call_target="tpu_custom_call" | custom-call | flops 1 | bytes 1 | tf_op jit(solution)/shard_map/pallas_call | solution.py:221
  97.0 4.3 %shard_map.190.refs_1_ = f32[256,1536]{1,0:T(8,128)S(1)} custom-call(s32[2]{0:T(128)S(1)} %pad_add_fusion.pos, bf16[1536,1536]{1,0:T(8,128)(2,1)} %weight_ref.19, bf16[256,384]{1,0:T(8,128)(2,1)S(1)} %shard_map.187.refs_0_, bf16[256,384]{1,0:T(8,128)(2,1)S(1)} %collective-permute-done.20.refs_1_, bf16[256,384]{1,0:T(8,128)(2,1)S(1)} %collective-permute-done.19.refs_2_), custom_call_target="tpu_custom_call" | custom-call | flops 1 | bytes 1 | tf_op jit(solution)/shard_map/pallas_call | solution.py:221
  101.3 4.2 %shard_map.191.refs_1_ = f32[256,1536]{1,0:T(8,128)S(1)} custom-call(s32[2]{0:T(128)S(1)} %pad_add_fusion.pos, bf16[6144,1536]{1,0:T(8,128)(2,1)} %weight_ref.23, bf16[256,1536]{1,0:T(8,128)(2,1)S(1)} %shard_map.188.refs_0_, f32[256,1536]{1,0:T(8,128)S(1)} %shard_map.190.refs_1_), custom_call_target="tpu_custom_call" | custom-call | flops 1 | bytes 1 | tf_op jit(solution)/shard_map/pallas_call | solution.py:221
  109.4 9.6 %shard_map.194 = f32[256,1536]{1,0:T(8,128)S(1)} custom-call(s32[2]{0:T(128)S(1)} %pad_add_fusion.pos, bf16[6144,1536]{1,0:T(8,128)(2,1)} %weight_ref.23, bf16[256,1536]{1,0:T(8,128)(2,1)S(1)} %collective-permute-done.25.refs_0_, bf16[256,1536]{1,0:T(8,128)(2,1)S(1)} %collective-permute-done.24.refs_1_, ...), custom_call_target="tpu_custom_call" | custom-call | flops 1 | bytes 1 | tf_op jit(solution)/shard_map/pallas_call | solution.py:221
  127.3 4.4 %shard_map.195.refs_0_ = bf16[256,384]{1,0:T(8,128)(2,1)S(1)} custom-call(s32[2]{0:T(128)S(1)} %pad_add_fusion.pos, bf16[256,1536]{1,0:T(8,128)(2,1)S(1)} %pad_maximum_fusion.1.tokens_ref, bf16[1536,1536]{1,0:T(8,128)(2,1)} %refs_0_.25, bf16[1536,1536]{1,0:T(8,128)(2,1)} %refs_1_.17, bf16[1536,1536]{1,0:T(8,128)(2,1)} %refs_2_.17, ...), custom_call_target="tpu_custom_call" | custom-call | flops 1 | bytes 1 | tf_op jit(solution)/shard_map/pallas_call | solution.py:221
  139.8 4.3 %shard_map.196.refs_0_ = bf16[128,1536]{1,0:T(8,128)(2,1)S(1)} custom-call(s32[2]{0:T(128)S(1)} %pad_add_fusion.pos, bf16[256,1536]{1,0:T(8,128)(2,1)S(1)} %pad_maximum_fusion.1.tokens_ref, bf16[1536,6144]{1,0:T(8,128)(2,1)} %weight_ref.20, f32[1,6144]{1,0:T(1,128)S(1)} %bitcast.148, bf16[256,3072]{1,0:T(8,128)(2,1)S(1)} %collective-permute-done.22.refs_1_.arrived_ref, ...), custom_call_target="tpu_custom_call" | custom-call | flops 1 | bytes 1 | tf_op jit(solution)/shard_map/pallas_call | solution.py:221
  144.2 5.0 %shard_map.197.refs_2_ = f32[256,1536]{1,0:T(8,128)S(1)} custom-call(s32[2]{0:T(128)S(1)} %pad_add_fusion.pos, bf16[1536,1536]{1,0:T(8,128)(2,1)} %weight_ref.19, bf16[256,384]{1,0:T(8,128)(2,1)S(1)} %shard_map.195.refs_0_, bf16[256,384]{1,0:T(8,128)(2,1)S(1)} %collective-permute-done.33.refs_1_, bf16[256,384]{1,0:T(8,128)(2,1)S(1)} %collective-permute-done.29.refs_2_, ...), custom_call_target="tpu_custom_call" | custom-call | flops 1 | bytes 1 | tf_op jit(solution)/shard_map/pallas_call | solution.py:221
  154.2 4.3 %shard_map.198.refs_1_ = bf16[128,1536]{1,0:T(8,128)(2,1)S(1)} custom-call(s32[2]{0:T(128)S(1)} %pad_add_fusion.pos, bf16[256,1536]{1,0:T(8,128)(2,1)S(1)} %pad_maximum_fusion.1.tokens_ref, bf16[1536,6144]{1,0:T(8,128)(2,1)} %weight_ref.20, f32[1,6144]{1,0:T(1,128)S(1)} %bitcast.149, bf16[256,3072]{1,0:T(8,128)(2,1)S(1)} %collective-permute-done.22.refs_1_.arrived_ref, ...), custom_call_target="tpu_custom_call" | custom-call | flops 1 | bytes 1 | tf_op jit(solution)/shard_map/pallas_call | solution.py:221
  167.3 4.2 %shard_map.199.refs_2_ = f32[256,1536]{1,0:T(8,128)S(1)} custom-call(s32[2]{0:T(128)S(1)} %pad_add_fusion.pos, bf16[6144,1536]{1,0:T(8,128)(2,1)} %weight_ref.23, bf16[128,1536]{1,0:T(8,128)(2,1)S(1)} %shard_map.196.refs_0_, bf16[128,1536]{1,0:T(8,128)(2,1)S(1)} %shard_map.198.refs_1_, f32[256,1536]{1,0:T(8,128)S(1)} %shard_map.197.refs_2_), custom_call_target="tpu_custom_call" | custom-call | flops 1 | bytes 1 | tf_op jit(solution)/shard_map/pallas_call | solution.py:221
  175.2 4.2 %shard_map.200.refs_4_ = f32[256,1536]{1,0:T(8,128)S(1)} custom-call(s32[2]{0:T(128)S(1)} %pad_add_fusion.pos, bf16[6144,1536]{1,0:T(8,128)(2,1)} %weight_ref.23, bf16[128,1536]{1,0:T(8,128)(2,1)S(1)} %collective-permute-done.37.refs_0_, bf16[128,1536]{1,0:T(8,128)(2,1)S(1)} %collective-permute-done.41.refs_1_, f32[256,1536]{1,0:T(8,128)S(1)} %shard_map.199.refs_2_), custom_call_target="tpu_custom_call" | custom-call | flops 1 | bytes 1 | tf_op jit(solution)/shard_map/pallas_call | solution.py:221
  183.4 7.0 %shard_map.201 = f32[256,1536]{1,0:T(8,128)S(1)} custom-call(s32[2]{0:T(128)S(1)} %pad_add_fusion.pos, bf16[6144,1536]{1,0:T(8,128)(2,1)} %weight_ref.23, bf16[128,1536]{1,0:T(8,128)(2,1)S(1)} %collective-permute-done.36.refs_0_, bf16[128,1536]{1,0:T(8,128)(2,1)S(1)} %collective-permute-done.42.refs_1_, ...), custom_call_target="tpu_custom_call" | custom-call | flops 1 | bytes 1 | tf_op jit(solution)/shard_map/pallas_call | solution.py:221
  198.1 5.5 %shard_map.202 = bf16[256,2304]{1,0:T(8,128)(2,1)S(1)} custom-call(s32[2]{0:T(128)S(1)} %pad_add_fusion.pos, bf16[256,1536]{1,0:T(8,128)(2,1)S(1)} %constant_dynamic-update-slice_fusion.tokens_ref, bf16[1536,1536]{1,0:T(8,128)(2,1)} %refs_0_.31, bf16[1536,1536]{1,0:T(8,128)(2,1)} %refs_1_.23, bf16[1536,1536]{1,0:T(8,128)(2,1)} %refs_2_.23), custom_call_target="tpu_custom_call" | custom-call | flops 1 | bytes 1 | tf_op jit(solution)/shard_map/pallas_call | solution.py:221
  206.7 5.1 %collective-permute-done.53 = bf16[64,1536]{1,0:T(8,128)(2,1)S(1)} collective-permute-done((bf16[64,1536]{1,0:T(8,128)(2,1)S(1)}, bf16[64,1536]{1,0:T(8,128)(2,1)S(1)}, u32[]{:S(2)}, u32[]{:S(2)}) %collective-permute-start.53) | collective-permute-done | bytes 196640 | tf_op jit(solution)/shard_map/ppermute | solution.py:213
  211.9 4.6 %collective-permute-done.52 = bf16[64,1536]{1,0:T(8,128)(2,1)S(1)} collective-permute-done((bf16[64,1536]{1,0:T(8,128)(2,1)S(1)}, bf16[64,1536]{1,0:T(8,128)(2,1)S(1)}, u32[]{:S(2)}, u32[]{:S(2)}) %collective-permute-start.52) | collective-permute-done | bytes 196640 | tf_op jit(solution)/shard_map/ppermute | solution.py:213
  226.5 4.0 %shard_map.203 = (bf16[128,1152]{1,0:T(8,128)(2,1)S(1)}, bf16[128,1152]{1,0:T(8,128)(2,1)S(1)}) custom-call(s32[2]{0:T(128)S(1)} %pad_add_fusion.pos, bf16[256,1536]{1,0:T(8,128)(2,1)S(1)} %constant_dynamic-update-slice_fusion.tokens_ref, bf16[1536,1536]{1,0:T(8,128)(2,1)} %refs_0_.31, bf16[1536,1536]{1,0:T(8,128)(2,1)} %refs_1_.23, ...), custom_call_target="tpu_custom_call" | custom-call | flops 1 | bytes 1 | tf_op jit(solution)/shard_map/pallas_call | solution.py:221
  240.8 5.5 %shard_map.204 = bf16[256,2304]{1,0:T(8,128)(2,1)S(1)} custom-call(s32[2]{0:T(128)S(1)} %pad_add_fusion.pos, bf16[256,1536]{1,0:T(8,128)(2,1)S(1)} %pad_maximum_fusion.2.tokens_ref, bf16[1536,1536]{1,0:T(8,128)(2,1)} %refs_0_.31, bf16[1536,1536]{1,0:T(8,128)(2,1)} %refs_1_.23, bf16[1536,1536]{1,0:T(8,128)(2,1)} %refs_2_.23), custom_call_target="tpu_custom_call" | custom-call | flops 1 | bytes 1 | tf_op jit(solution)/shard_map/pallas_call | solution.py:221
  249.3 4.0 %shard_map.205 = bf16[256,1152]{1,0:T(8,128)(2,1)S(1)} custom-call(s32[2]{0:T(128)S(1)} %pad_add_fusion.pos, bf16[256,1536]{1,0:T(8,128)(2,1)S(1)} %pad_maximum_fusion.2.tokens_ref, bf16[1536,1536]{1,0:T(8,128)(2,1)} %refs_0_.31, bf16[1536,1536]{1,0:T(8,128)(2,1)} %refs_1_.23, bf16[1536,1536]{1,0:T(8,128)(2,1)} %refs_2_.23, ...), custom_call_target="tpu_custom_call" | custom-call | flops 1 | bytes 1 | tf_op jit(solution)/shard_map/pallas_call | solution.py:221
  257.0 4.0 %shard_map.207.refs_3_.refs_4_.refs_5_ = f32[256,1152]{1,0:T(8,128)S(1)} custom-call(s32[2]{0:T(128)S(1)} %pad_add_fusion.pos, bf16[256,1536]{1,0:T(8,128)(2,1)S(1)} %pad_maximum_fusion.2.tokens_ref, bf16[1536,1536]{1,0:T(8,128)(2,1)} %refs_0_.31, bf16[1536,1536]{1,0:T(8,128)(2,1)} %refs_1_.23, bf16[1536,1536]{1,0:T(8,128)(2,1)} %refs_2_.23, ...), custom_call_target="tpu_custom_call" | custom-call | flops 1 | bytes 1 | tf_op jit(solution)/shard_map/pallas_call | solution.py:221
  261.0 4.0 %shard_map.206.refs_0_.refs_1_.refs_2_ = bf16[256,1152]{1,0:T(8,128)(2,1)S(1)} custom-call(s32[2]{0:T(128)S(1)} %pad_add_fusion.pos, bf16[256,1536]{1,0:T(8,128)(2,1)S(1)} %constant_dynamic-update-slice_fusion.tokens_ref, bf16[1536,1536]{1,0:T(8,128)(2,1)} %refs_0_.31, bf16[1536,1536]{1,0:T(8,128)(2,1)} %refs_1_.23, bf16[1536,1536]{1,0:T(8,128)(2,1)} %refs_2_.23, ...), custom_call_target="tpu_custom_call" | custom-call | flops 1 | bytes 1 | tf_op jit(solution)/shard_map/pallas_call | solution.py:221
  265.0 5.8 %collective-permute-done.67.refs_6_.refs_7_.refs_8_ = bf16[256,1152]{1,0:T(8,128)(2,1)S(1)} collective-permute-done((bf16[256,1152]{1,0:T(8,128)(2,1)S(1)}, bf16[256,1152]{1,0:T(8,128)(2,1)S(1)}, u32[]{:S(2)}, u32[]{:S(2)}) %collective-permute-start.67) | collective-permute-done | bytes 589856 | tf_op jit(solution)/shard_map/ppermute | solution.py:200
  275.6 8.7 %collective-permute-done.68.refs_0_ = bf16[512,384]{1,0:T(8,128)(2,1)S(1)} collective-permute-done((bf16[512,384]{1,0:T(8,128)(2,1)S(1)}, bf16[512,384]{1,0:T(8,128)(2,1)S(1)}, u32[]{:S(2)}, u32[]{:S(2)}) %collective-permute-start.68) | collective-permute-done | bytes 393248 | tf_op jit(solution)/shard_map/ppermute | solution.py:200
  289.8 4.9 %shard_map.210 = f32[512,1536]{1,0:T(8,128)S(1)} custom-call(s32[2]{0:T(128)S(1)} %pad_add_fusion.pos, bf16[1536,1536]{1,0:T(8,128)(2,1)} %weight_ref.25, bf16[512,384]{1,0:T(8,128)(2,1)S(1)} %collective-permute-done.68.refs_0_, bf16[512,384]{1,0:T(8,128)(2,1)S(1)} %collective-permute-done.69.refs_1_, f32[512,1536]{1,0:T(8,128)} %copy-done), custom_call_target="tpu_custom_call" | custom-call | flops 1 | bytes 1 | tf_op jit(solution)/shard_map/pallas_call | solution.py:221
  316.0 5.5 %collective-permute-done.72 = bf16[64,1536]{1,0:T(8,128)(2,1)S(1)} collective-permute-done((bf16[64,1536]{1,0:T(8,128)(2,1)S(1)}, bf16[64,1536]{1,0:T(8,128)(2,1)S(1)}, u32[]{:S(2)}, u32[]{:S(2)}) %collective-permute-start.72) | collective-permute-done | bytes 196640 | tf_op jit(solution)/shard_map/ppermute | solution.py:213
  (242 shorter events, 158.2 us)
Async XLA Ops:
  1.1 11.2 %collective-permute-start = (bf16[64,1536]{1,0:T(8,128)(2,1)S(1)}, bf16[64,1536]{1,0:T(8,128)(2,1)S(1)}, u32[]{:S(2)}, u32[]{:S(2)}) collective-permute-start(bf16[64,1536]{1,0:T(8,128)(2,1)S(1)} %get-tuple-element.200), channel_id=1, source_target_pairs={{0,1},{1,2},{2,3},{3,0},{4,5},{5,6},{6,7},{7,4},{8,9},{9,10},{10,1... | collective-permute-start | bytes 589832 | tf_op jit(solution)/shard_map/ppermute | solution.py:213
  4.1 10.6 %collective-permute-start.1 = (bf16[64,1536]{1,0:T(8,128)(2,1)S(1)}, bf16[64,1536]{1,0:T(8,128)(2,1)S(1)}, u32[]{:S(2)}, u32[]{:S(2)}) collective-permute-start(bf16[64,1536]{1,0:T(8,128)(2,1)S(1)} %get-tuple-element.200), channel_id=1, source_target_pairs={{0,3},{1,0},{2,1},{3,2},{4,7},{5,4},{6,5},{7,6},{8,11},{9,8},{10,9... | collective-permute-start | bytes 589832 | tf_op jit(solution)/shard_map/ppermute | solution.py:213
  49.9 10.2 %collective-permute-start.15 = (bf16[128,1152]{1,0:T(8,128)(2,1)S(1)}, bf16[128,1152]{1,0:T(8,128)(2,1)S(1)}, u32[]{:S(2)}, u32[]{:S(2)}) collective-permute-start(bf16[128,1152]{1,0:T(8,128)(2,1)S(1)} %get-tuple-element.227), channel_id=1, source_target_pairs={{0,8},{4,12},{8,0},{12,4},{1,9},{5,13},{9,1},{13,5},{2,10},{6,14},... | collective-permute-start | bytes 884744 | tf_op jit(solution)/shard_map/ppermute | solution.py:200
  60.1 19.5 %collective-permute-start.18 = (bf16[256,1536]{1,0:T(8,128)(2,1)S(1)}, bf16[256,1536]{1,0:T(8,128)(2,1)S(1)}, u32[]{:S(2)}, u32[]{:S(2)}) collective-permute-start(bf16[256,1536]{1,0:T(8,128)(2,1)S(1)} %shard_map.184), channel_id=1, source_target_pairs={{0,8},{4,12},{8,0},{12,4},{1,9},{5,13},{9,1},{13,5},{2,10},{6,14},... | collective-permute-start | bytes 2359304 | tf_op jit(solution)/shard_map/ppermute | solution.py:200
  86.9 19.0 %collective-permute-start.24 = (bf16[256,1536]{1,0:T(8,128)(2,1)S(1)}, bf16[256,1536]{1,0:T(8,128)(2,1)S(1)}, u32[]{:S(2)}, u32[]{:S(2)}) collective-permute-start(bf16[256,1536]{1,0:T(8,128)(2,1)S(1)} %shard_map.188.refs_0_), channel_id=1, source_target_pairs={{0,8},{4,12},{8,0},{12,4},{1,9},{5,13},{9,1},{13,5},{2,10},{6,14},... | collective-permute-start | bytes 2359304 | tf_op jit(solution)/shard_map/ppermute | solution.py:200
  87.9 18.0 %collective-permute-start.25 = (bf16[256,1536]{1,0:T(8,128)(2,1)S(1)}, bf16[256,1536]{1,0:T(8,128)(2,1)S(1)}, u32[]{:S(2)}, u32[]{:S(2)}) collective-permute-start(bf16[256,1536]{1,0:T(8,128)(2,1)S(1)} %shard_map.188.refs_0_), channel_id=1, source_target_pairs={{0,4},{4,0},{8,12},{12,8},{1,5},{5,1},{9,13},{13,9},{2,6},{6,2},{1... | collective-permute-start | bytes 2359304 | tf_op jit(solution)/shard_map/ppermute | solution.py:200
  87.9 17.7 %collective-permute-start.23 = (bf16[256,384]{1,0:T(8,128)(2,1)S(1)}, bf16[256,384]{1,0:T(8,128)(2,1)S(1)}, u32[]{:S(2)}, u32[]{:S(2)}) collective-permute-start(bf16[256,384]{1,0:T(8,128)(2,1)S(1)} %collective-permute-done.19.refs_2_), channel_id=1, source_target_pairs={{0,4},{4,0},{8,12},{12,8},{1,5},{5,1},{9,13},{13,9},{2,6},{6,2},{1... | collective-permute-start | bytes 589832 | tf_op jit(solution)/shard_map/ppermute | solution.py:200
  105.9 15.7 %collective-permute-start.27 = (bf16[256,1152]{1,0:T(8,128)(2,1)S(1)}, bf16[256,1152]{1,0:T(8,128)(2,1)S(1)}, u32[]{:S(2)}, u32[]{:S(2)}) collective-permute-start(bf16[256,1152]{1,0:T(8,128)(2,1)S(1)} %shard_map.189), channel_id=1, source_target_pairs={{0,8},{4,12},{8,0},{12,4},{1,9},{5,13},{9,1},{13,5},{2,10},{6,14},... | collective-permute-start | bytes 1769480 | tf_op jit(solution)/shard_map/ppermute | solution.py:200
  121.8 15.7 %collective-permute-start.28 = (bf16[128,1536]{1,0:T(8,128)(2,1)S(1)}, bf16[128,1536]{1,0:T(8,128)(2,1)S(1)}, u32[]{:S(2)}, u32[]{:S(2)}) collective-permute-start(bf16[128,1536]{1,0:T(8,128)(2,1)S(1)} %get-tuple-element.270), channel_id=1, source_target_pairs={{0,8},{4,12},{8,0},{12,4},{1,9},{5,13},{9,1},{13,5},{2,10},{6,14},... | collective-permute-start | bytes 1179656 | tf_op jit(solution)/shard_map/ppermute | solution.py:200
  123.0 10.1 %collective-permute-start.30 = (bf16[64,1536]{1,0:T(8,128)(2,1)S(1)}, bf16[64,1536]{1,0:T(8,128)(2,1)S(1)}, u32[]{:S(2)}, u32[]{:S(2)}) collective-permute-start(bf16[64,1536]{1,0:T(8,128)(2,1)S(1)} %get-tuple-element.399), channel_id=1, source_target_pairs={{0,1},{1,2},{2,3},{3,0},{4,5},{5,6},{6,7},{7,4},{8,9},{9,10},{10,1... | collective-permute-start | bytes 589832 | tf_op jit(solution)/shard_map/ppermute | solution.py:213
  124.4 10.2 %collective-permute-start.31 = (bf16[64,1536]{1,0:T(8,128)(2,1)S(1)}, bf16[64,1536]{1,0:T(8,128)(2,1)S(1)}, u32[]{:S(2)}, u32[]{:S(2)}) collective-permute-start(bf16[64,1536]{1,0:T(8,128)(2,1)S(1)} %get-tuple-element.398), channel_id=1, source_target_pairs={{0,3},{1,0},{2,1},{3,2},{4,7},{5,4},{6,5},{7,6},{8,11},{9,8},{10,9... | collective-permute-start | bytes 589832 | tf_op jit(solution)/shard_map/ppermute | solution.py:213
  137.5 13.4 %collective-permute-start.32 = (bf16[128,1536]{1,0:T(8,128)(2,1)S(1)}, bf16[128,1536]{1,0:T(8,128)(2,1)S(1)}, u32[]{:S(2)}, u32[]{:S(2)}) collective-permute-start(bf16[128,1536]{1,0:T(8,128)(2,1)S(1)} %get-tuple-element.277), channel_id=1, source_target_pairs={{0,8},{4,12},{8,0},{12,4},{1,9},{5,13},{9,1},{13,5},{2,10},{6,14},... | collective-permute-start | bytes 1179656 | tf_op jit(solution)/shard_map/ppermute | solution.py:200
  138.9 11.9 %collective-permute-start.35 = (bf16[64,1536]{1,0:T(8,128)(2,1)S(1)}, bf16[64,1536]{1,0:T(8,128)(2,1)S(1)}, u32[]{:S(2)}, u32[]{:S(2)}) collective-permute-start(bf16[64,1536]{1,0:T(8,128)(2,1)S(1)} %get-tuple-element.284), channel_id=1, source_target_pairs={{0,2},{1,3},{2,0},{3,1},{4,6},{5,7},{6,4},{7,5},{8,10},{9,11},{10,... | collective-permute-start | bytes 589832 | tf_op jit(solution)/shard_map/ppermute | solution.py:213
  150.8 11.1 %collective-permute-start.36 = (bf16[128,1536]{1,0:T(8,128)(2,1)S(1)}, bf16[128,1536]{1,0:T(8,128)(2,1)S(1)}, u32[]{:S(2)}, u32[]{:S(2)}) collective-permute-start(bf16[128,1536]{1,0:T(8,128)(2,1)S(1)} %shard_map.196.refs_0_), channel_id=1, source_target_pairs={{0,8},{4,12},{8,0},{12,4},{1,9},{5,13},{9,1},{13,5},{2,10},{6,14},... | collective-permute-start | bytes 1179656 | tf_op jit(solution)/shard_map/ppermute | solution.py:200
  151.8 10.0 %collective-permute-start.37 = (bf16[128,1536]{1,0:T(8,128)(2,1)S(1)}, bf16[128,1536]{1,0:T(8,128)(2,1)S(1)}, u32[]{:S(2)}, u32[]{:S(2)}) collective-permute-start(bf16[128,1536]{1,0:T(8,128)(2,1)S(1)} %shard_map.196.refs_0_), channel_id=1, source_target_pairs={{0,4},{4,0},{8,12},{12,8},{1,5},{5,1},{9,13},{13,9},{2,6},{6,2},{1... | collective-permute-start | bytes 1179656 | tf_op jit(solution)/shard_map/ppermute | solution.py:200
  161.9 13.1 %collective-permute-start.41 = (bf16[128,1536]{1,0:T(8,128)(2,1)S(1)}, bf16[128,1536]{1,0:T(8,128)(2,1)S(1)}, u32[]{:S(2)}, u32[]{:S(2)}) collective-permute-start(bf16[128,1536]{1,0:T(8,128)(2,1)S(1)} %shard_map.198.refs_1_), channel_id=1, source_target_pairs={{0,4},{4,0},{8,12},{12,8},{1,5},{5,1},{9,13},{13,9},{2,6},{6,2},{1... | collective-permute-start | bytes 1179656 | tf_op jit(solution)/shard_map/ppermute | solution.py:200
  162.1 13.0 %collective-permute-start.42 = (bf16[128,1536]{1,0:T(8,128)(2,1)S(1)}, bf16[128,1536]{1,0:T(8,128)(2,1)S(1)}, u32[]{:S(2)}, u32[]{:S(2)}) collective-permute-start(bf16[128,1536]{1,0:T(8,128)(2,1)S(1)} %shard_map.198.refs_1_), channel_id=1, source_target_pairs={{0,8},{4,12},{8,0},{12,4},{1,9},{5,13},{9,1},{13,5},{2,10},{6,14},... | collective-permute-start | bytes 1179656 | tf_op jit(solution)/shard_map/ppermute | solution.py:200
  163.2 11.9 %collective-permute-start.43 = (bf16[128,1536]{1,0:T(8,128)(2,1)S(1)}, bf16[128,1536]{1,0:T(8,128)(2,1)S(1)}, u32[]{:S(2)}, u32[]{:S(2)}) collective-permute-start(bf16[128,1536]{1,0:T(8,128)(2,1)S(1)} %collective-permute-done.36.refs_0_), channel_id=1, source_target_pairs={{0,4},{4,0},{8,12},{12,8},{1,5},{5,1},{9,13},{13,9},{2,6},{6,2},{1... | collective-permute-start | bytes 1179656 | tf_op jit(solution)/shard_map/ppermute | solution.py:200
  164.0 11.1 %collective-permute-start.45 = (bf16[64,1536]{1,0:T(8,128)(2,1)S(1)}, bf16[64,1536]{1,0:T(8,128)(2,1)S(1)}, u32[]{:S(2)}, u32[]{:S(2)}) collective-permute-start(bf16[64,1536]{1,0:T(8,128)(2,1)S(1)} %multiply_convert_fusion.4), channel_id=1, source_target_pairs={{0,3},{1,0},{2,1},{3,2},{4,7},{5,4},{6,5},{7,6},{8,11},{9,8},{10,9... | collective-permute-start | bytes 589832 | tf_op jit(solution)/shard_map/ppermute | solution.py:213
  179.4 10.9 %collective-permute-start.47 = (bf16[32,1536]{1,0:T(8,128)(2,1)S(1)}, bf16[32,1536]{1,0:T(8,128)(2,1)S(1)}, u32[]{:S(2)}, u32[]{:S(2)}) collective-permute-start(bf16[32,1536]{1,0:T(8,128)(2,1)S(1)} %slice.215), channel_id=1, source_target_pairs={{0,1},{1,2},{2,3},{3,0},{4,5},{5,6},{6,7},{7,4},{8,9},{9,10},{10,1... | collective-permute-start | bytes 294920 | tf_op jit(solution)/shard_map/ppermute | solution.py:213
  180.1 10.2 %collective-permute-start.48 = (bf16[32,1536]{1,0:T(8,128)(2,1)S(1)}, bf16[32,1536]{1,0:T(8,128)(2,1)S(1)}, u32[]{:S(2)}, u32[]{:S(2)}) collective-permute-start(bf16[32,1536]{1,0:T(8,128)(2,1)S(1)} %slice.216), channel_id=1, source_target_pairs={{0,3},{1,0},{2,1},{3,2},{4,7},{5,4},{6,5},{7,6},{8,11},{9,8},{10,9... | collective-permute-start | bytes 294920 | tf_op jit(solution)/shard_map/ppermute | solution.py:213
  203.6 12.8 %collective-permute-start.51 = (bf16[256,2304]{1,0:T(8,128)(2,1)S(1)}, bf16[256,2304]{1,0:T(8,128)(2,1)S(1)}, u32[]{:S(2)}, u32[]{:S(2)}) collective-permute-start(bf16[256,2304]{1,0:T(8,128)(2,1)S(1)} %shard_map.202), channel_id=1, source_target_pairs={{0,4},{4,0},{8,12},{12,8},{1,5},{5,1},{9,13},{13,9},{2,6},{6,2},{1... | collective-permute-start | bytes 3538952 | tf_op jit(solution)/shard_map/ppermute | solution.py:200
  206.7 9.8 %collective-permute-start.52 = (bf16[64,1536]{1,0:T(8,128)(2,1)S(1)}, bf16[64,1536]{1,0:T(8,128)(2,1)S(1)}, u32[]{:S(2)}, u32[]{:S(2)}) collective-permute-start(bf16[64,1536]{1,0:T(8,128)(2,1)S(1)} %pad_maximum_fusion.3), channel_id=1, source_target_pairs={{0,1},{1,2},{2,3},{3,0},{4,5},{5,6},{6,7},{7,4},{8,9},{9,10},{10,1... | collective-permute-start | bytes 589832 | tf_op jit(solution)/shard_map/ppermute | solution.py:213
  218.6 13.4 %collective-permute-start.54 = (bf16[64,1536]{1,0:T(8,128)(2,1)S(1)}, bf16[64,1536]{1,0:T(8,128)(2,1)S(1)}, u32[]{:S(2)}, u32[]{:S(2)}) collective-permute-start(bf16[64,1536]{1,0:T(8,128)(2,1)S(1)} %get-tuple-element.356), channel_id=1, source_target_pairs={{0,1},{1,2},{2,3},{3,0},{4,5},{5,6},{6,7},{7,4},{8,9},{9,10},{10,1... | collective-permute-start | bytes 589832 | tf_op jit(solution)/shard_map/ppermute | solution.py:213
  220.5 11.6 %collective-permute-start.55 = (bf16[64,1536]{1,0:T(8,128)(2,1)S(1)}, bf16[64,1536]{1,0:T(8,128)(2,1)S(1)}, u32[]{:S(2)}, u32[]{:S(2)}) collective-permute-start(bf16[64,1536]{1,0:T(8,128)(2,1)S(1)} %get-tuple-element.356), channel_id=1, source_target_pairs={{0,3},{1,0},{2,1},{3,2},{4,7},{5,4},{6,5},{7,6},{8,11},{9,8},{10,9... | collective-permute-start | bytes 589832 | tf_op jit(solution)/shard_map/ppermute | solution.py:213
  255.9 14.9 %collective-permute-start.67 = (bf16[256,1152]{1,0:T(8,128)(2,1)S(1)}, bf16[256,1152]{1,0:T(8,128)(2,1)S(1)}, u32[]{:S(2)}, u32[]{:S(2)}) collective-permute-start(bf16[256,1152]{1,0:T(8,128)(2,1)S(1)} %shard_map.205), channel_id=1, source_target_pairs={{0,8},{4,12},{8,0},{12,4},{1,9},{5,13},{9,1},{13,5},{2,10},{6,14},... | collective-permute-start | bytes 1769480 | tf_op jit(solution)/shard_map/ppermute | solution.py:200
  274.5 9.9 %collective-permute-start.68 = (bf16[512,384]{1,0:T(8,128)(2,1)S(1)}, bf16[512,384]{1,0:T(8,128)(2,1)S(1)}, u32[]{:S(2)}, u32[]{:S(2)}) collective-permute-start(bf16[512,384]{1,0:T(8,128)(2,1)S(1)} %bitcast.143), channel_id=1, source_target_pairs={{0,8},{4,12},{8,0},{12,4},{1,9},{5,13},{9,1},{13,5},{2,10},{6,14},... | collective-permute-start | bytes 1179656 | tf_op jit(solution)/shard_map/ppermute | solution.py:200
  295.6 11.9 %collective-permute-start.75 = (bf16[64,1536]{1,0:T(8,128)(2,1)S(1)}, bf16[64,1536]{1,0:T(8,128)(2,1)S(1)}, u32[]{:S(2)}, u32[]{:S(2)}) collective-permute-start(bf16[64,1536]{1,0:T(8,128)(2,1)S(1)} %get-tuple-element.390), channel_id=1, source_target_pairs={{0,3},{1,0},{2,1},{3,2},{4,7},{5,4},{6,5},{7,6},{8,11},{9,8},{10,9... | collective-permute-start | bytes 589832 | tf_op jit(solution)/shard_map/ppermute | solution.py:213
  298.8 14.2 %collective-permute-start.73 = (bf16[64,1536]{1,0:T(8,128)(2,1)S(1)}, bf16[64,1536]{1,0:T(8,128)(2,1)S(1)}, u32[]{:S(2)}, u32[]{:S(2)}) collective-permute-start(bf16[64,1536]{1,0:T(8,128)(2,1)S(1)} %get-tuple-element.391), channel_id=1, source_target_pairs={{0,1},{1,2},{2,3},{3,0},{4,5},{5,6},{6,7},{7,4},{8,9},{9,10},{10,1... | collective-permute-start | bytes 589832 | tf_op jit(solution)/shard_map/ppermute | solution.py:213
  298.8 17.2 %collective-permute-start.74 = (bf16[64,1536]{1,0:T(8,128)(2,1)S(1)}, bf16[64,1536]{1,0:T(8,128)(2,1)S(1)}, u32[]{:S(2)}, u32[]{:S(2)}) collective-permute-start(bf16[64,1536]{1,0:T(8,128)(2,1)S(1)} %get-tuple-element.389), channel_id=1, source_target_pairs={{0,3},{1,0},{2,1},{3,2},{4,7},{5,4},{6,5},{7,6},{8,11},{9,8},{10,9... | collective-permute-start | bytes 589832 | tf_op jit(solution)/shard_map/ppermute | solution.py:213
  307.6 13.8 %collective-permute-start.72 = (bf16[64,1536]{1,0:T(8,128)(2,1)S(1)}, bf16[64,1536]{1,0:T(8,128)(2,1)S(1)}, u32[]{:S(2)}, u32[]{:S(2)}) collective-permute-start(bf16[64,1536]{1,0:T(8,128)(2,1)S(1)} %get-tuple-element.388), channel_id=1, source_target_pairs={{0,1},{1,2},{2,3},{3,0},{4,5},{5,6},{6,7},{7,4},{8,9},{9,10},{10,1... | collective-permute-start | bytes 589832 | tf_op jit(solution)/shard_map/ppermute | solution.py:213
  309.5 14.2 %collective-permute-start.76 = (bf16[64,1536]{1,0:T(8,128)(2,1)S(1)}, bf16[64,1536]{1,0:T(8,128)(2,1)S(1)}, u32[]{:S(2)}, u32[]{:S(2)}) collective-permute-start(bf16[64,1536]{1,0:T(8,128)(2,1)S(1)} %get-tuple-element.387), channel_id=1, source_target_pairs={{0,3},{1,0},{2,1},{3,2},{4,7},{5,4},{6,5},{7,6},{8,11},{9,8},{10,9... | collective-permute-start | bytes 589832 | tf_op jit(solution)/shard_map/ppermute | solution.py:213
  (57 other events, 409.7 us)

commit v6 on v5

--- a/solution.py
+++ b/solution.py
@@ -526,11 +526,6 @@
     return row_shift(array.astype(jnp.bfloat16), shift)
 
 
-def sent_on(before, after):
-    half = before.shape[0] // 2
-    return sent(before[:half], 1), sent(after[half:], -1)
-
-
 def moment_shards(total):
     return total, row_shift(total, 1), row_shift(total, -1), row_shift(total, 2)
 
@@ -545,18 +540,11 @@
     return lax.optimization_barrier(values)
 
 
-def scatter_rows_long(terms):
+def scatter_rows(terms):
     own, before, after, away = jnp.split(terms, 4)
-    half = own.shape[0] // 2
-
-    def send(array, shift):
-        return row_shift(array.astype(jnp.bfloat16), shift).astype(jnp.float32)
-
-    to_after = send(away[:half], 1)
-    to_before = send(away[half:], -1)
-    from_before = jnp.concatenate((send(after[:half] + to_after, 1), send(after[half:], 1)))
-    from_after = jnp.concatenate((send(before[:half], -1), send(before[half:] + to_before, -1)))
-    return own + from_before + from_after
+    to_after, from_after = sent(away, 1), sent(before, -1)
+    from_before = sent(after + to_after.astype(jnp.float32), 1)
+    return own + from_before.astype(jnp.float32) + from_after.astype(jnp.float32)
 
 
 def fast_body(
@@ -627,10 +615,9 @@
     )
 
     totals = moment_shards(moment_sum(pairs))
-    own_a, own_b, a_before, a_after, a_away0, a_away1, *totals = sync(
-        own_a, own_b, a_before, a_after, *sent_on(a_before, a_after), *totals
-    )
-    a_away = jnp.concatenate((a_away0, a_away1))
+    own_a, own_b, a_before, a_after, a_away, *totals = sync(
+        own_a, own_b, a_before, a_after, sent(a_before, 1), *totals
+    )
     totals_a = [total[:, :half] for total in totals]
     totals_b = [total[:, half:] for total in totals]
 
@@ -651,14 +638,11 @@
         tok_a, own_b, b_before, b_after, qc_a, us_a, qy_a0, qx_a1
     )
 
-    uc_a, qy_a1, b_away0, b_away1 = (
-        core_swap(us_a), y_swap(qx_a1), *sent_on(b_before, b_after)
-    )
+    uc_a, qy_a1, b_away = core_swap(us_a), y_swap(qx_a1), sent(b_before, 1)
     (ux_a,) = units_across(tok_a, uc_a, 1)
-    tok_a, qc_a, uc_a, ux_a, qy_a0, qy_a1, own_b, b_before, b_after, b_away0, b_away1 = sync(
-        tok_a, qc_a, uc_a, ux_a, qy_a0, qy_a1, own_b, b_before, b_after, b_away0, b_away1
-    )
-    b_away = jnp.concatenate((b_away0, b_away1))
+    tok_a, qc_a, uc_a, ux_a, qy_a0, qy_a1, own_b, b_before, b_after, b_away = sync(
+        tok_a, qc_a, uc_a, ux_a, qy_a0, qy_a1, own_b, b_before, b_after, b_away
+    )
 
     uy_a = y_swap(ux_a)
     tok_b = normed_shards((own_b, b_before, b_after, b_away), norm_gain, totals_b)
@@ -692,83 +676,78 @@
 
     uy_b0 = y_swap(ux_b0)
     mine_a, before_a, after_a, away_a = jnp.split(mixed_a, 4)
-    from_before, from_after = sent(after_a, 1), sent(before_a, -1)
+    to_after, from_after = sent(away_a, 1), sent(before_a, -1)
     at_b = project_heads(run, tok_b, heads_in, scales, head_width, qc_b, (qy_b,), True)
-    at_yb = y_swap(at_b)
-    tok_b, uc_b, uy_b0, ux_b1, at_b, at_yb, mine_a, away_a, from_before, from_after = sync(
-        tok_b, uc_b, uy_b0, ux_b1, at_b, at_yb, mine_a, away_a.astype(jnp.bfloat16),
-        from_before, from_after,
-    )
-
-    uy_b1, from_away, at_cb, at_fb = (
-        y_swap(ux_b1), sent(away_a, 2), core_swap(at_b), core_swap(at_yb)
-    )
+    tok_b, uc_b, uy_b0, ux_b1, at_b, mine_a, after_a, to_after, from_after = sync(
+        tok_b, uc_b, uy_b0, ux_b1, at_b, mine_a, after_a, to_after, from_after
+    )
+
+    from_before = sent(after_a + to_after.astype(jnp.float32), 1)
+    uy_b1, at_yb, at_cb = y_swap(ux_b1), y_swap(at_b), core_swap(at_b)
     hd_b0 = units_end(tok_b, uc_b, uy_b0)
-    mixed_b = heads_out((at_b, at_cb, at_yb, at_fb))
-    tok_b, uc_b, uy_b1, hd_b0, mixed_b, mine_a, *arrived = sync(
-        tok_b, uc_b, uy_b1, hd_b0, mixed_b, mine_a, from_before, from_after, from_away
-    )
-
-    hd_yb0, hd_cb0 = y_swap(hd_b0), core_swap(hd_b0)
+    mixed_b = heads_out((at_b, at_cb))
+    tok_b, uc_b, uy_b1, hd_b0, at_yb, mixed_b, mine_a, *arrived = sync(
+        tok_b, uc_b, uy_b1, hd_b0, at_yb, mixed_b, mine_a, from_before, from_after
+    )
+
+    hd_yb0, at_fb = y_swap(hd_b0), core_swap(at_yb)
     layer_a = layer_end(start_f32[:half], mine_a, *arrived)
     pairs = moment_flips(moment_pair(layer_a.astype(jnp.float32)))
     hd_b1 = units_end(tok_b, uc_b, uy_b1, 1)
-    hd_b0, hd_b1, hd_yb0, hd_cb0, mixed_b, layer_a, *pairs = sync(
-        hd_b0, hd_b1, hd_yb0, hd_cb0, mixed_b, layer_a, *pairs
-    )
-
-    hd_yb1, hd_cb1, hd_fb0 = y_swap(hd_b1), core_swap(hd_b1), core_swap(hd_yb0)
+    mixed_b = heads_out((at_yb, at_fb), 2, mixed_b)
+    hd_b0, hd_b1, hd_yb0, mixed_b, layer_a, *pairs = sync(
+        hd_b0, hd_b1, hd_yb0, mixed_b, layer_a, *pairs
+    )
+
+    hd_yb1, hd_cb0, hd_cb1 = y_swap(hd_b1), core_swap(hd_b0), core_swap(hd_b1)
     join_a = normalize(layer_a.astype(jnp.float32), join_gain, moment_sum(pairs))
     ja_before, ja_after = sent(join_a, 1), sent(join_a, -1)
     mixed_b = units_down(((hd_b0, hd_b1),), 0, mixed_b)
-    hd_cb0, hd_cb1, hd_yb0, hd_yb1, hd_fb0, mixed_b, layer_a, join_a, ja_before, ja_after = sync(
-        hd_cb0, hd_cb1, hd_yb0, hd_yb1, hd_fb0, mixed_b, layer_a, join_a, ja_before, ja_after
-    )
-
+    hd_cb0, hd_cb1, hd_yb0, hd_yb1, mixed_b, layer_a, join_a, ja_before, ja_after = sync(
+        hd_cb0, hd_cb1, hd_yb0, hd_yb1, mixed_b, layer_a, join_a, ja_before, ja_after
+    )
+
+    hd_fb0 = core_swap(hd_yb0)
     hd_fb1 = core_swap(hd_yb1)
     mixed_b = units_down(((hd_cb0, hd_cb1),), 1, mixed_b)
     hd_yb0, hd_yb1, hd_fb0, hd_fb1, mixed_b, join_a, ja_before, ja_after = sync(
         hd_yb0, hd_yb1, hd_fb0, hd_fb1, mixed_b, join_a, ja_before, ja_after
     )
 
-    ja_away0, ja_away1 = sent_on(ja_before, ja_after)
+    ja_away = sent(ja_before, 1)
     mixed_b = units_down(((hd_yb0, hd_yb1), (hd_fb0, hd_fb1)), 2, mixed_b)
-    mixed_b, join_a, ja_before, ja_after, ja_away0, ja_away1 = sync(
-        mixed_b, join_a, ja_before, ja_after, ja_away0, ja_away1
+    mixed_b, join_a, ja_before, ja_after, ja_away = sync(
+        mixed_b, join_a, ja_before, ja_after, ja_away
     )
 
     mine_b, before_b, after_b, away_b = jnp.split(mixed_b, 4)
-    part = half // 2
-    to_after, to_before = sent(away_b[:part], 1), sent(away_b[part:], -1)
-    mine_b, before_b, after_b, to_after, to_before, join_a, *shards = sync(
-        mine_b, before_b, after_b, to_after, to_before, join_a,
-        ja_before, ja_after, ja_away0, ja_away1,
-    )
-
-    after_b = jnp.concatenate((after_b[:part] + to_after.astype(jnp.float32), after_b[part:]))
-    before_b = jnp.concatenate((before_b[:part], before_b[part:] + to_before.astype(jnp.float32)))
-    from_before, from_after = sent(after_b, 1), sent(before_b, -1)
-    tok_ja = jnp.concatenate((join_a, *shards))
+    to_after, from_after = sent(away_b, 1), sent(before_b, -1)
+    tok_ja = jnp.concatenate((join_a, ja_before, ja_after, ja_away))
     js_a = heads_send(tok_ja, join_in)
-    jc_a = core_swap(js_a)
-    tok_ja, jc_a, mine_b, *arrived = sync(tok_ja, jc_a, mine_b, from_before, from_after)
+    mine_b, after_b, to_after, from_after, tok_ja, js_a = sync(
+        mine_b, after_b, to_after, from_after, tok_ja, js_a
+    )
+
+    from_before, jc_a = sent(after_b + to_after.astype(jnp.float32), 1), core_swap(js_a)
+    jx_a = heads_across(tok_ja, join_in, jc_a, 2)
+    tok_ja, jc_a, jx_a0, jx_a1, mine_b, *arrived = sync(
+        tok_ja, jc_a, *jx_a, mine_b, from_before, from_after
+    )
 
     layer_b = layer_end(start_f32[half:], mine_b, *arrived)
     totals = moment_shards(moment_sum(moment_flips(moment_pair(layer_b.astype(jnp.float32)))))
     jb_before, jb_after = sent(layer_b, 1), sent(layer_b, -1)
-    jx_a = heads_across(tok_ja, join_in, jc_a, 2)
     tok_ja, jc_a, jx_a0, jx_a1, layer_b, jb_before, jb_after, *totals = sync(
-        tok_ja, jc_a, *jx_a, layer_b, jb_before, jb_after, *totals
-    )
-
-    jb_away0, jb_away1 = sent_on(jb_before, jb_after)
+        tok_ja, jc_a, jx_a0, jx_a1, layer_b, jb_before, jb_after, *totals
+    )
+
+    jb_away = sent(jb_before, 1)
     jy_a0 = y_swap(jx_a0)
-    tok_ja, jc_a, jy_a0, jx_a1, layer_b, jb_before, jb_after, jb_away0, jb_away1, *totals = sync(
-        tok_ja, jc_a, jy_a0, jx_a1, layer_b, jb_before, jb_after, jb_away0, jb_away1, *totals
+    tok_ja, jc_a, jy_a0, jx_a1, layer_b, jb_before, jb_after, jb_away, *totals = sync(
+        tok_ja, jc_a, jy_a0, jx_a1, layer_b, jb_before, jb_after, jb_away, *totals
     )
 
     jy_a1 = y_swap(jx_a1)
-    jb_away = jnp.concatenate((jb_away0, jb_away1))
     tok_jb = normed_shards((layer_b, jb_before, jb_after, jb_away), join_gain, totals)
     jc_b = core_swap(heads_send(tok_jb, join_in))
     (jx_b,) = heads_across(tok_jb, join_in, jc_b)
@@ -787,9 +766,8 @@
     joined = joined.reshape(2, 4, half, head_width).swapaxes(0, 1).reshape(8 * half, head_width)
     jo_y, jo_c = y_swap(joined), core_swap(joined)
     jo_f = core_swap(jo_y)
-    result = contract(run, ((joined,), (jo_c,)), join_out, 1)
-    result = contract(run, ((jo_y,), (jo_f,)), join_out, 1, 2, result)
-    summed = scatter_rows_long(result)
+    result = contract(run, ((joined,), (jo_c,), (jo_y,), (jo_f,)), join_out, 1)
+    summed = scatter_rows(result)
     layer_own = jnp.concatenate((layer_a, layer_b))
     return (layer_own.astype(jnp.float32) + summed).astype(jnp.bfloat16)
 

time: 330 us -> 323 us (0.979)
  starting transfers between devices: 88.1 us -> 63 us
  waiting for transfers between devices: 81.5 us -> 102 us
    ppermute x35 -> x27, starting transfers between devices: 63.8 us -> 38.5 us  [row_shift(): lax.ppermute(array, 'rows', [(i, (i + shift) % size) for i in range(size)])]
    ppermute x35 -> x27, waiting for transfers between devices: 48.6 us -> 61.4 us  [row_shift(): lax.ppermute(array, 'rows', [(i, (i + shift) % size) for i in range(size)])]
    ppermute x42, waiting for transfers between devices: 32.9 us -> 41 us  [flip(): return lax.ppermute(array, 'cols', [(i, i ^ mask) for i in range(size)])]
  transfers between devices with their start and end apart: 77 -> 69, of which waited for: 36 -> 34; matrix products, arithmetic and copies ran while one was open for 1% -> 1% of each run, Pallas kernels for 39% -> 41%
where the time goes in v6:
time: 323 us; the launch traced here: 318 us
  Pallas kernels  144 us (45%)
  waiting for transfers between devices  102 us (32%)
  starting transfers between devices  63 us (20%)
  other arithmetic  5.55 us (2%)
    pallas_call x30, Pallas kernels, __call__(): pl.pallas_call(kernel, out_shape=out_shape, grid_spec=pltpu.PrefetchScala...  144 us
    ppermute x27, waiting for transfers between devices, row_shift(): lax.ppermute(array, 'rows', [(i, (i + shift) % size) for i in range(size)])  61.4 us
    ppermute x42, waiting for transfers between devices, flip(): return lax.ppermute(array, 'cols', [(i, i ^ mask) for i in range(size)])  41 us
    ppermute x27, starting transfers between devices, row_shift(): lax.ppermute(array, 'rows', [(i, (i + shift) % size) for i in range(size)])  38.5 us
    ppermute x42, starting transfers between devices, flip(): return lax.ppermute(array, 'cols', [(i, i ^ mask) for i in range(size)])  24.6 us
  transfers between devices with their start and end apart: 69, of which 34 were waited for; matrix products, arithmetic and copies ran while one was open for 1% of the time, Pallas kernels for 41%

profile of v6, /device:TPU:0, one launch (start us, length us, event | category | flops | bytes accessed | tf_op | source)
XLA Modules:
  0.0 318.1 jit_solution(18080252300825702972)
XLA Ops:
  25.5 5.5 %shard_map.181 = bf16[256,2304]{1,0:T(8,128)(2,1)S(1)} custom-call(s32[2]{0:T(128)S(1)} %pad_add_fusion.pos, bf16[256,1536]{1,0:T(8,128)(2,1)S(1)} %pad_maximum_fusion.tokens_ref, bf16[1536,1536]{1,0:T(8,128)(2,1)} %refs_0_.25, bf16[1536,1536]{1,0:T(8,128)(2,1)} %refs_1_.17, bf16[1536,1536]{1,0:T(8,128)(2,1)} %refs_2_.17), custom_call_target="tpu_custom_call" | custom-call | flops 1 | bytes 1 | tf_op jit(solution)/shard_map/pallas_call | solution.py:221
  41.3 7.4 %shard_map.183 = bf16[256,3072]{1,0:T(8,128)(2,1)S(1)} custom-call(s32[2]{0:T(128)S(1)} %pad_add_fusion.pos, bf16[256,1536]{1,0:T(8,128)(2,1)S(1)} %pad_maximum_fusion.tokens_ref, bf16[1536,6144]{1,0:T(8,128)(2,1)} %weight_ref.20), custom_call_target="tpu_custom_call" | custom-call | flops 1 | bytes 1 | tf_op jit(solution)/shard_map/pallas_call | solution.py:221
  52.2 4.6 %shard_map.184 = bf16[256,1536]{1,0:T(8,128)(2,1)S(1)} custom-call(s32[2]{0:T(128)S(1)} %pad_add_fusion.pos, bf16[256,1536]{1,0:T(8,128)(2,1)S(1)} %pad_maximum_fusion.tokens_ref, bf16[1536,6144]{1,0:T(8,128)(2,1)} %weight_ref.20, bf16[256,3072]{1,0:T(8,128)(2,1)S(1)} %collective-permute-done.13.refs_1_.arrived_ref), custom_call_target="tpu_custom_call" | custom-call | flops 1 | bytes 1 | tf_op jit(solution)/shard_map/pallas_call | solution.py:221
  61.3 7.4 %shard_map.186 = bf16[256,3072]{1,0:T(8,128)(2,1)S(1)} custom-call(s32[2]{0:T(128)S(1)} %pad_add_fusion.pos, bf16[256,1536]{1,0:T(8,128)(2,1)S(1)} %pad_maximum_fusion.1.tokens_ref, bf16[1536,6144]{1,0:T(8,128)(2,1)} %weight_ref.20), custom_call_target="tpu_custom_call" | custom-call | flops 1 | bytes 1 | tf_op jit(solution)/shard_map/pallas_call | solution.py:221
  68.7 5.5 %shard_map.185 = bf16[256,2304]{1,0:T(8,128)(2,1)S(1)} custom-call(s32[2]{0:T(128)S(1)} %pad_add_fusion.pos, bf16[256,1536]{1,0:T(8,128)(2,1)S(1)} %pad_maximum_fusion.1.tokens_ref, bf16[1536,1536]{1,0:T(8,128)(2,1)} %refs_0_.25, bf16[1536,1536]{1,0:T(8,128)(2,1)} %refs_1_.17, bf16[1536,1536]{1,0:T(8,128)(2,1)} %refs_2_.17), custom_call_target="tpu_custom_call" | custom-call | flops 1 | bytes 1 | tf_op jit(solution)/shard_map/pallas_call | solution.py:221
  74.3 4.4 %shard_map.187.refs_0_ = bf16[256,384]{1,0:T(8,128)(2,1)S(1)} custom-call(s32[2]{0:T(128)S(1)} %pad_add_fusion.pos, bf16[256,1536]{1,0:T(8,128)(2,1)S(1)} %pad_maximum_fusion.tokens_ref, bf16[1536,1536]{1,0:T(8,128)(2,1)} %refs_0_.25, bf16[1536,1536]{1,0:T(8,128)(2,1)} %refs_1_.17, bf16[1536,1536]{1,0:T(8,128)(2,1)} %refs_2_.17, ...), custom_call_target="tpu_custom_call" | custom-call | flops 1 | bytes 1 | tf_op jit(solution)/shard_map/pallas_call | solution.py:221
  80.4 4.8 %shard_map.188.refs_0_ = bf16[256,1536]{1,0:T(8,128)(2,1)S(1)} custom-call(s32[2]{0:T(128)S(1)} %pad_add_fusion.pos, bf16[256,1536]{1,0:T(8,128)(2,1)S(1)} %pad_maximum_fusion.tokens_ref, bf16[1536,6144]{1,0:T(8,128)(2,1)} %weight_ref.20, f32[1,6144]{1,0:T(1,128)S(1)} %bitcast.147, bf16[256,3072]{1,0:T(8,128)(2,1)S(1)} %collective-permute-done.13.refs_1_.arrived_ref, ...), custom_call_target="tpu_custom_call" | custom-call | flops 1 | bytes 1 | tf_op jit(solution)/shard_map/pallas_call | solution.py:221
  87.8 4.6 %shard_map.192 = (bf16[128,1536]{1,0:T(8,128)(2,1)S(1)}, bf16[128,1536]{1,0:T(8,128)(2,1)S(1)}) custom-call(s32[2]{0:T(128)S(1)} %pad_add_fusion.pos, bf16[256,1536]{1,0:T(8,128)(2,1)S(1)} %pad_maximum_fusion.1.tokens_ref, bf16[1536,6144]{1,0:T(8,128)(2,1)} %weight_ref.20, bf16[256,3072]{1,0:T(8,128)(2,1)S(1)} %collective-permute-done.20.refs_1_.arrived_ref), custom_call_target="tpu_custom_call" | custom-call | flops 1 | bytes 1 | tf_op jit(solution)/shard_map/pallas_call | solution.py:221
  92.5 4.0 %shard_map.189 = bf16[256,1152]{1,0:T(8,128)(2,1)S(1)} custom-call(s32[2]{0:T(128)S(1)} %pad_add_fusion.pos, bf16[256,1536]{1,0:T(8,128)(2,1)S(1)} %pad_maximum_fusion.1.tokens_ref, bf16[1536,1536]{1,0:T(8,128)(2,1)} %refs_0_.25, bf16[1536,1536]{1,0:T(8,128)(2,1)} %refs_1_.17, bf16[1536,1536]{1,0:T(8,128)(2,1)} %refs_2_.17, ...), custom_call_target="tpu_custom_call" | custom-call | flops 1 | bytes 1 | tf_op jit(solution)/shard_map/pallas_call | solution.py:221
  96.4 4.3 %shard_map.190.refs_1_ = f32[256,1536]{1,0:T(8,128)S(1)} custom-call(s32[2]{0:T(128)S(1)} %pad_add_fusion.pos, bf16[1536,1536]{1,0:T(8,128)(2,1)} %weight_ref.21, bf16[256,384]{1,0:T(8,128)(2,1)S(1)} %shard_map.187.refs_0_, bf16[256,384]{1,0:T(8,128)(2,1)S(1)} %collective-permute-done.18.refs_1_, bf16[256,384]{1,0:T(8,128)(2,1)S(1)} %collective-permute-done.17.refs_2_), custom_call_target="tpu_custom_call" | custom-call | flops 1 | bytes 1 | tf_op jit(solution)/shard_map/pallas_call | solution.py:221
  100.7 4.2 %shard_map.191.refs_1_ = f32[256,1536]{1,0:T(8,128)S(1)} custom-call(s32[2]{0:T(128)S(1)} %pad_add_fusion.pos, bf16[6144,1536]{1,0:T(8,128)(2,1)} %weight_ref.24, bf16[256,1536]{1,0:T(8,128)(2,1)S(1)} %shard_map.188.refs_0_, f32[256,1536]{1,0:T(8,128)S(1)} %shard_map.190.refs_1_), custom_call_target="tpu_custom_call" | custom-call | flops 1 | bytes 1 | tf_op jit(solution)/shard_map/pallas_call | solution.py:221
  108.7 9.6 %shard_map.194 = f32[256,1536]{1,0:T(8,128)S(1)} custom-call(s32[2]{0:T(128)S(1)} %pad_add_fusion.pos, bf16[6144,1536]{1,0:T(8,128)(2,1)} %weight_ref.24, bf16[256,1536]{1,0:T(8,128)(2,1)S(1)} %collective-permute-done.23.refs_0_, bf16[256,1536]{1,0:T(8,128)(2,1)S(1)} %collective-permute-done.22.refs_1_, ...), custom_call_target="tpu_custom_call" | custom-call | flops 1 | bytes 1 | tf_op jit(solution)/shard_map/pallas_call | solution.py:221
  121.2 4.2 %collective-permute-start.28 = (bf16[64,1536]{1,0:T(8,128)(2,1)S(1)}, bf16[64,1536]{1,0:T(8,128)(2,1)S(1)}, u32[]{:S(2)}, u32[]{:S(2)}) collective-permute-start(bf16[64,1536]{1,0:T(8,128)(2,1)S(1)} %get-tuple-element.377), channel_id=1, source_target_pairs={{0,3},{1,0},{2,1},{3,2},{4,7},{5,4},{6,5},{7,6},{8,11},{9,8},{10,9... | collective-permute-start | bytes 589832 | tf_op jit(solution)/shard_map/ppermute | solution.py:213
  126.5 4.4 %shard_map.195.refs_0_ = bf16[256,384]{1,0:T(8,128)(2,1)S(1)} custom-call(s32[2]{0:T(128)S(1)} %pad_add_fusion.pos, bf16[256,1536]{1,0:T(8,128)(2,1)S(1)} %pad_maximum_fusion.1.tokens_ref, bf16[1536,1536]{1,0:T(8,128)(2,1)} %refs_0_.25, bf16[1536,1536]{1,0:T(8,128)(2,1)} %refs_1_.17, bf16[1536,1536]{1,0:T(8,128)(2,1)} %refs_2_.17, ...), custom_call_target="tpu_custom_call" | custom-call | flops 1 | bytes 1 | tf_op jit(solution)/shard_map/pallas_call | solution.py:221
  137.8 4.3 %shard_map.196.refs_0_ = bf16[128,1536]{1,0:T(8,128)(2,1)S(1)} custom-call(s32[2]{0:T(128)S(1)} %pad_add_fusion.pos, bf16[256,1536]{1,0:T(8,128)(2,1)S(1)} %pad_maximum_fusion.1.tokens_ref, bf16[1536,6144]{1,0:T(8,128)(2,1)} %weight_ref.20, f32[1,6144]{1,0:T(1,128)S(1)} %bitcast.148, bf16[256,3072]{1,0:T(8,128)(2,1)S(1)} %collective-permute-done.20.refs_1_.arrived_ref, ...), custom_call_target="tpu_custom_call" | custom-call | flops 1 | bytes 1 | tf_op jit(solution)/shard_map/pallas_call | solution.py:221
  145.5 5.8 %collective-permute-done.30.refs_0_ = bf16[256,384]{1,0:T(8,128)(2,1)S(1)} collective-permute-done((bf16[256,384]{1,0:T(8,128)(2,1)S(1)}, bf16[256,384]{1,0:T(8,128)(2,1)S(1)}, u32[]{:S(2)}, u32[]{:S(2)}) %collective-permute-start.30) | collective-permute-done | bytes 196640 | tf_op jit(solution)/shard_map/ppermute | solution.py:200
  154.8 4.3 %shard_map.198.refs_1_ = bf16[128,1536]{1,0:T(8,128)(2,1)S(1)} custom-call(s32[2]{0:T(128)S(1)} %pad_add_fusion.pos, bf16[256,1536]{1,0:T(8,128)(2,1)S(1)} %pad_maximum_fusion.1.tokens_ref, bf16[1536,6144]{1,0:T(8,128)(2,1)} %weight_ref.20, f32[1,6144]{1,0:T(1,128)S(1)} %bitcast.149, bf16[256,3072]{1,0:T(8,128)(2,1)S(1)} %collective-permute-done.20.refs_1_.arrived_ref, ...), custom_call_target="tpu_custom_call" | custom-call | flops 1 | bytes 1 | tf_op jit(solution)/shard_map/pallas_call | solution.py:221
  168.1 4.2 %shard_map.200.refs_2_ = f32[256,1536]{1,0:T(8,128)S(1)} custom-call(s32[2]{0:T(128)S(1)} %pad_add_fusion.pos, bf16[6144,1536]{1,0:T(8,128)(2,1)} %weight_ref.24, bf16[128,1536]{1,0:T(8,128)(2,1)S(1)} %shard_map.196.refs_0_, bf16[128,1536]{1,0:T(8,128)(2,1)S(1)} %shard_map.198.refs_1_, f32[256,1536]{1,0:T(8,128)S(1)} %shard_map.199.refs_2_), custom_call_target="tpu_custom_call" | custom-call | flops 1 | bytes 1 | tf_op jit(solution)/shard_map/pallas_call | solution.py:221
  176.5 4.2 %shard_map.201.refs_4_ = f32[256,1536]{1,0:T(8,128)S(1)} custom-call(s32[2]{0:T(128)S(1)} %pad_add_fusion.pos, bf16[6144,1536]{1,0:T(8,128)(2,1)} %weight_ref.24, bf16[128,1536]{1,0:T(8,128)(2,1)S(1)} %collective-permute-done.38.refs_0_, bf16[128,1536]{1,0:T(8,128)(2,1)S(1)} %collective-permute-done.39.refs_1_, f32[256,1536]{1,0:T(8,128)S(1)} %shard_map.200.refs_2_), custom_call_target="tpu_custom_call" | custom-call | flops 1 | bytes 1 | tf_op jit(solution)/shard_map/pallas_call | solution.py:221
  181.0 7.0 %shard_map.202 = f32[256,1536]{1,0:T(8,128)S(1)} custom-call(s32[2]{0:T(128)S(1)} %pad_add_fusion.pos, bf16[6144,1536]{1,0:T(8,128)(2,1)} %weight_ref.24, bf16[128,1536]{1,0:T(8,128)(2,1)S(1)} %collective-permute-done.33.refs_0_, bf16[128,1536]{1,0:T(8,128)(2,1)S(1)} %collective-permute-done.40.refs_1_, ...), custom_call_target="tpu_custom_call" | custom-call | flops 1 | bytes 1 | tf_op jit(solution)/shard_map/pallas_call | solution.py:221
  193.6 5.5 %shard_map.203 = bf16[256,2304]{1,0:T(8,128)(2,1)S(1)} custom-call(s32[2]{0:T(128)S(1)} %pad_add_fusion.pos, bf16[256,1536]{1,0:T(8,128)(2,1)S(1)} %constant_dynamic-update-slice_fusion.tokens_ref, bf16[1536,1536]{1,0:T(8,128)(2,1)} %refs_0_.31, bf16[1536,1536]{1,0:T(8,128)(2,1)} %refs_1_.23, bf16[1536,1536]{1,0:T(8,128)(2,1)} %refs_2_.23), custom_call_target="tpu_custom_call" | custom-call | flops 1 | bytes 1 | tf_op jit(solution)/shard_map/pallas_call | solution.py:221
  220.8 5.5 %collective-permute-done.55 = f32[2,64]{1,0:T(2,128)S(1)} collective-permute-done((f32[2,64]{1,0:T(2,128)S(1)}, f32[2,64]{1,0:T(2,128)S(1)}, u32[]{:S(2)}, u32[]{:S(2)}) %collective-permute-start.55) | collective-permute-done | bytes 544 | tf_op jit(solution)/shard_map/ppermute | solution.py:213
  227.9 7.0 %collective-permute-done.59 = bf16[64,1536]{1,0:T(8,128)(2,1)S(1)} collective-permute-done((bf16[64,1536]{1,0:T(8,128)(2,1)S(1)}, bf16[64,1536]{1,0:T(8,128)(2,1)S(1)}, u32[]{:S(2)}, u32[]{:S(2)}) %collective-permute-start.59) | collective-permute-done | bytes 196640 | tf_op jit(solution)/shard_map/ppermute | solution.py:213
  235.4 5.5 %shard_map.205 = bf16[256,2304]{1,0:T(8,128)(2,1)S(1)} custom-call(s32[2]{0:T(128)S(1)} %pad_add_fusion.pos, bf16[256,1536]{1,0:T(8,128)(2,1)S(1)} %pad_maximum_fusion.2.tokens_ref, bf16[1536,1536]{1,0:T(8,128)(2,1)} %refs_0_.31, bf16[1536,1536]{1,0:T(8,128)(2,1)} %refs_1_.23, bf16[1536,1536]{1,0:T(8,128)(2,1)} %refs_2_.23), custom_call_target="tpu_custom_call" | custom-call | flops 1 | bytes 1 | tf_op jit(solution)/shard_map/pallas_call | solution.py:221
  251.5 4.0 %shard_map.208.refs_3_.refs_4_.refs_5_ = f32[256,1152]{1,0:T(8,128)S(1)} custom-call(s32[2]{0:T(128)S(1)} %pad_add_fusion.pos, bf16[256,1536]{1,0:T(8,128)(2,1)S(1)} %pad_maximum_fusion.2.tokens_ref, bf16[1536,1536]{1,0:T(8,128)(2,1)} %refs_0_.31, bf16[1536,1536]{1,0:T(8,128)(2,1)} %refs_1_.23, bf16[1536,1536]{1,0:T(8,128)(2,1)} %refs_2_.23, ...), custom_call_target="tpu_custom_call" | custom-call | flops 1 | bytes 1 | tf_op jit(solution)/shard_map/pallas_call | solution.py:221
  255.5 4.0 %shard_map.207.refs_0_.refs_1_.refs_2_ = bf16[256,1152]{1,0:T(8,128)(2,1)S(1)} custom-call(s32[2]{0:T(128)S(1)} %pad_add_fusion.pos, bf16[256,1536]{1,0:T(8,128)(2,1)S(1)} %constant_dynamic-update-slice_fusion.tokens_ref, bf16[1536,1536]{1,0:T(8,128)(2,1)} %refs_0_.31, bf16[1536,1536]{1,0:T(8,128)(2,1)} %refs_1_.23, bf16[1536,1536]{1,0:T(8,128)(2,1)} %refs_2_.23, ...), custom_call_target="tpu_custom_call" | custom-call | flops 1 | bytes 1 | tf_op jit(solution)/shard_map/pallas_call | solution.py:221
  259.6 5.8 %collective-permute-done.62.refs_6_.refs_7_.refs_8_ = bf16[256,1152]{1,0:T(8,128)(2,1)S(1)} collective-permute-done((bf16[256,1152]{1,0:T(8,128)(2,1)S(1)}, bf16[256,1152]{1,0:T(8,128)(2,1)S(1)}, u32[]{:S(2)}, u32[]{:S(2)}) %collective-permute-start.62) | collective-permute-done | bytes 589856 | tf_op jit(solution)/shard_map/ppermute | solution.py:200
  270.2 8.7 %collective-permute-done.64.refs_2_ = bf16[512,384]{1,0:T(8,128)(2,1)S(1)} collective-permute-done((bf16[512,384]{1,0:T(8,128)(2,1)S(1)}, bf16[512,384]{1,0:T(8,128)(2,1)S(1)}, u32[]{:S(2)}, u32[]{:S(2)}) %collective-permute-start.64) | collective-permute-done | bytes 393248 | tf_op jit(solution)/shard_map/ppermute | solution.py:200
  280.6 6.2 %shard_map.210 = f32[512,1536]{1,0:T(8,128)S(1)} custom-call(s32[2]{0:T(128)S(1)} %pad_add_fusion.pos, bf16[1536,1536]{1,0:T(8,128)(2,1)} %weight_ref.25, bf16[512,384]{1,0:T(8,128)(2,1)S(1)} %bitcast.145, bf16[512,384]{1,0:T(8,128)(2,1)S(1)} %collective-permute-done.63.refs_1_, bf16[512,384]{1,0:T(8,128)(2,1)S(1)} %collective-permute-done.64.refs_2_, ...), custom_call_target="tpu_custom_call" | custom-call | flops 1 | bytes 1 | tf_op jit(solution)/shard_map/pallas_call | solution.py:221
  291.0 10.0 %collective-permute-done.66 = bf16[128,1536]{1,0:T(8,128)(2,1)S(1)} collective-permute-done((bf16[128,1536]{1,0:T(8,128)(2,1)S(1)}, bf16[128,1536]{1,0:T(8,128)(2,1)S(1)}, u32[]{:S(2)}, u32[]{:S(2)}) %collective-permute-start.66) | collective-permute-done | bytes 393248 | tf_op jit(solution)/shard_map/ppermute | solution.py:213
  301.1 5.7 %collective-permute-done.68 = bf16[128,1536]{1,0:T(8,128)(2,1)S(1)} collective-permute-done((bf16[128,1536]{1,0:T(8,128)(2,1)S(1)}, bf16[128,1536]{1,0:T(8,128)(2,1)S(1)}, u32[]{:S(2)}, u32[]{:S(2)}) %collective-permute-start.68) | collective-permute-done | bytes 393248 | tf_op jit(solution)/shard_map/ppermute | solution.py:213
  306.8 10.2 %collective-permute-done.67 = bf16[128,1536]{1,0:T(8,128)(2,1)S(1)} collective-permute-done((bf16[128,1536]{1,0:T(8,128)(2,1)S(1)}, bf16[128,1536]{1,0:T(8,128)(2,1)S(1)}, u32[]{:S(2)}, u32[]{:S(2)}) %collective-permute-start.67) | collective-permute-done | bytes 393248 | tf_op jit(solution)/shard_map/ppermute | solution.py:213
  (208 shorter events, 133.7 us)
Async XLA Ops:
  1.1 11.2 %collective-permute-start = (bf16[64,1536]{1,0:T(8,128)(2,1)S(1)}, bf16[64,1536]{1,0:T(8,128)(2,1)S(1)}, u32[]{:S(2)}, u32[]{:S(2)}) collective-permute-start(bf16[64,1536]{1,0:T(8,128)(2,1)S(1)} %get-tuple-element.191), channel_id=1, source_target_pairs={{0,1},{1,2},{2,3},{3,0},{4,5},{5,6},{6,7},{7,4},{8,9},{9,10},{10,1... | collective-permute-start | bytes 589832 | tf_op jit(solution)/shard_map/ppermute | solution.py:213
  4.1 10.6 %collective-permute-start.1 = (bf16[64,1536]{1,0:T(8,128)(2,1)S(1)}, bf16[64,1536]{1,0:T(8,128)(2,1)S(1)}, u32[]{:S(2)}, u32[]{:S(2)}) collective-permute-start(bf16[64,1536]{1,0:T(8,128)(2,1)S(1)} %get-tuple-element.191), channel_id=1, source_target_pairs={{0,3},{1,0},{2,1},{3,2},{4,7},{5,4},{6,5},{7,6},{8,11},{9,8},{10,9... | collective-permute-start | bytes 589832 | tf_op jit(solution)/shard_map/ppermute | solution.py:213
  14.7 9.4 %collective-permute-start.5 = (bf16[64,1536]{1,0:T(8,128)(2,1)S(1)}, bf16[64,1536]{1,0:T(8,128)(2,1)S(1)}, u32[]{:S(2)}, u32[]{:S(2)}) collective-permute-start(bf16[64,1536]{1,0:T(8,128)(2,1)S(1)} %collective-permute-done), channel_id=1, source_target_pairs={{0,1},{1,2},{2,3},{3,0},{4,5},{5,6},{6,7},{7,4},{8,9},{9,10},{10,1... | collective-permute-start | bytes 589832 | tf_op jit(solution)/shard_map/ppermute | solution.py:213
  48.8 10.8 %collective-permute-start.14 = (bf16[128,1152]{1,0:T(8,128)(2,1)S(1)}, bf16[128,1152]{1,0:T(8,128)(2,1)S(1)}, u32[]{:S(2)}, u32[]{:S(2)}) collective-permute-start(bf16[128,1152]{1,0:T(8,128)(2,1)S(1)} %get-tuple-element.217), channel_id=1, source_target_pairs={{0,8},{4,12},{8,0},{12,4},{1,9},{5,13},{9,1},{13,5},{2,10},{6,14},... | collective-permute-start | bytes 884744 | tf_op jit(solution)/shard_map/ppermute | solution.py:200
  49.9 9.7 %collective-permute-start.15 = (bf16[64,1536]{1,0:T(8,128)(2,1)S(1)}, bf16[64,1536]{1,0:T(8,128)(2,1)S(1)}, u32[]{:S(2)}, u32[]{:S(2)}) collective-permute-start(bf16[64,1536]{1,0:T(8,128)(2,1)S(1)} %collective-permute-done.9), channel_id=1, source_target_pairs={{0,1},{1,2},{2,3},{3,0},{4,5},{5,6},{6,7},{7,4},{8,9},{9,10},{10,1... | collective-permute-start | bytes 589832 | tf_op jit(solution)/shard_map/ppermute | solution.py:213
  59.6 19.2 %collective-permute-start.16 = (bf16[256,1536]{1,0:T(8,128)(2,1)S(1)}, bf16[256,1536]{1,0:T(8,128)(2,1)S(1)}, u32[]{:S(2)}, u32[]{:S(2)}) collective-permute-start(bf16[256,1536]{1,0:T(8,128)(2,1)S(1)} %shard_map.184), channel_id=1, source_target_pairs={{0,8},{4,12},{8,0},{12,4},{1,9},{5,13},{9,1},{13,5},{2,10},{6,14},... | collective-permute-start | bytes 2359304 | tf_op jit(solution)/shard_map/ppermute | solution.py:200
  86.2 19.1 %collective-permute-start.22 = (bf16[256,1536]{1,0:T(8,128)(2,1)S(1)}, bf16[256,1536]{1,0:T(8,128)(2,1)S(1)}, u32[]{:S(2)}, u32[]{:S(2)}) collective-permute-start(bf16[256,1536]{1,0:T(8,128)(2,1)S(1)} %shard_map.188.refs_0_), channel_id=1, source_target_pairs={{0,8},{4,12},{8,0},{12,4},{1,9},{5,13},{9,1},{13,5},{2,10},{6,14},... | collective-permute-start | bytes 2359304 | tf_op jit(solution)/shard_map/ppermute | solution.py:200
  87.3 17.9 %collective-permute-start.23 = (bf16[256,1536]{1,0:T(8,128)(2,1)S(1)}, bf16[256,1536]{1,0:T(8,128)(2,1)S(1)}, u32[]{:S(2)}, u32[]{:S(2)}) collective-permute-start(bf16[256,1536]{1,0:T(8,128)(2,1)S(1)} %shard_map.188.refs_0_), channel_id=1, source_target_pairs={{0,4},{4,0},{8,12},{12,8},{1,5},{5,1},{9,13},{13,9},{2,6},{6,2},{1... | collective-permute-start | bytes 2359304 | tf_op jit(solution)/shard_map/ppermute | solution.py:200
  87.3 17.7 %collective-permute-start.21 = (bf16[256,384]{1,0:T(8,128)(2,1)S(1)}, bf16[256,384]{1,0:T(8,128)(2,1)S(1)}, u32[]{:S(2)}, u32[]{:S(2)}) collective-permute-start(bf16[256,384]{1,0:T(8,128)(2,1)S(1)} %collective-permute-done.17.refs_2_), channel_id=1, source_target_pairs={{0,4},{4,0},{8,12},{12,8},{1,5},{5,1},{9,13},{13,9},{2,6},{6,2},{1... | collective-permute-start | bytes 589832 | tf_op jit(solution)/shard_map/ppermute | solution.py:200
  105.3 15.7 %collective-permute-start.25 = (bf16[256,1152]{1,0:T(8,128)(2,1)S(1)}, bf16[256,1152]{1,0:T(8,128)(2,1)S(1)}, u32[]{:S(2)}, u32[]{:S(2)}) collective-permute-start(bf16[256,1152]{1,0:T(8,128)(2,1)S(1)} %shard_map.189), channel_id=1, source_target_pairs={{0,8},{4,12},{8,0},{12,4},{1,9},{5,13},{9,1},{13,5},{2,10},{6,14},... | collective-permute-start | bytes 1769480 | tf_op jit(solution)/shard_map/ppermute | solution.py:200
  121.1 9.8 %collective-permute-start.27 = (bf16[64,1536]{1,0:T(8,128)(2,1)S(1)}, bf16[64,1536]{1,0:T(8,128)(2,1)S(1)}, u32[]{:S(2)}, u32[]{:S(2)}) collective-permute-start(bf16[64,1536]{1,0:T(8,128)(2,1)S(1)} %get-tuple-element.378), channel_id=1, source_target_pairs={{0,1},{1,2},{2,3},{3,0},{4,5},{5,6},{6,7},{7,4},{8,9},{9,10},{10,1... | collective-permute-start | bytes 589832 | tf_op jit(solution)/shard_map/ppermute | solution.py:213
  121.2 11.2 %collective-permute-start.28 = (bf16[64,1536]{1,0:T(8,128)(2,1)S(1)}, bf16[64,1536]{1,0:T(8,128)(2,1)S(1)}, u32[]{:S(2)}, u32[]{:S(2)}) collective-permute-start(bf16[64,1536]{1,0:T(8,128)(2,1)S(1)} %get-tuple-element.377), channel_id=1, source_target_pairs={{0,3},{1,0},{2,1},{3,2},{4,7},{5,4},{6,5},{7,6},{8,11},{9,8},{10,9... | collective-permute-start | bytes 589832 | tf_op jit(solution)/shard_map/ppermute | solution.py:213
  125.4 10.2 %collective-permute-start.26 = (bf16[128,1536]{1,0:T(8,128)(2,1)S(1)}, bf16[128,1536]{1,0:T(8,128)(2,1)S(1)}, u32[]{:S(2)}, u32[]{:S(2)}) collective-permute-start(bf16[128,1536]{1,0:T(8,128)(2,1)S(1)} %get-tuple-element.259), channel_id=1, source_target_pairs={{0,8},{4,12},{8,0},{12,4},{1,9},{5,13},{9,1},{13,5},{2,10},{6,14},... | collective-permute-start | bytes 1179656 | tf_op jit(solution)/shard_map/ppermute | solution.py:200
  135.6 15.7 %collective-permute-start.29 = (bf16[128,1536]{1,0:T(8,128)(2,1)S(1)}, bf16[128,1536]{1,0:T(8,128)(2,1)S(1)}, u32[]{:S(2)}, u32[]{:S(2)}) collective-permute-start(bf16[128,1536]{1,0:T(8,128)(2,1)S(1)} %get-tuple-element.266), channel_id=1, source_target_pairs={{0,8},{4,12},{8,0},{12,4},{1,9},{5,13},{9,1},{13,5},{2,10},{6,14},... | collective-permute-start | bytes 1179656 | tf_op jit(solution)/shard_map/ppermute | solution.py:200
  136.7 14.7 %collective-permute-start.30 = (bf16[256,384]{1,0:T(8,128)(2,1)S(1)}, bf16[256,384]{1,0:T(8,128)(2,1)S(1)}, u32[]{:S(2)}, u32[]{:S(2)}) collective-permute-start(bf16[256,384]{1,0:T(8,128)(2,1)S(1)} %shard_map.195.refs_0_), channel_id=1, source_target_pairs={{0,8},{4,12},{8,0},{12,4},{1,9},{5,13},{9,1},{13,5},{2,10},{6,14},... | collective-permute-start | bytes 589832 | tf_op jit(solution)/shard_map/ppermute | solution.py:200
  151.4 10.8 %collective-permute-start.33 = (bf16[128,1536]{1,0:T(8,128)(2,1)S(1)}, bf16[128,1536]{1,0:T(8,128)(2,1)S(1)}, u32[]{:S(2)}, u32[]{:S(2)}) collective-permute-start(bf16[128,1536]{1,0:T(8,128)(2,1)S(1)} %shard_map.196.refs_0_), channel_id=1, source_target_pairs={{0,8},{4,12},{8,0},{12,4},{1,9},{5,13},{9,1},{13,5},{2,10},{6,14},... | collective-permute-start | bytes 1179656 | tf_op jit(solution)/shard_map/ppermute | solution.py:200
  152.8 9.4 %collective-permute-start.35 = (f32[2,64]{1,0:T(2,128)S(1)}, f32[2,64]{1,0:T(2,128)S(1)}, u32[]{:S(2)}, u32[]{:S(2)}) collective-permute-start(f32[2,64]{1,0:T(2,128)S(1)} %pad_maximum_fusion.4), channel_id=1, source_target_pairs={{0,4},{4,0},{8,12},{12,8},{1,5},{5,1},{9,13},{13,9},{2,6},{6,2},{1... | collective-permute-start | bytes 1544 | tf_op jit(solution)/shard_map/ppermute | solution.py:200
  162.3 13.6 %collective-permute-start.39 = (bf16[128,1536]{1,0:T(8,128)(2,1)S(1)}, bf16[128,1536]{1,0:T(8,128)(2,1)S(1)}, u32[]{:S(2)}, u32[]{:S(2)}) collective-permute-start(bf16[128,1536]{1,0:T(8,128)(2,1)S(1)} %shard_map.198.refs_1_), channel_id=1, source_target_pairs={{0,4},{4,0},{8,12},{12,8},{1,5},{5,1},{9,13},{13,9},{2,6},{6,2},{1... | collective-permute-start | bytes 1179656 | tf_op jit(solution)/shard_map/ppermute | solution.py:200
  163.0 12.8 %collective-permute-start.40 = (bf16[128,1536]{1,0:T(8,128)(2,1)S(1)}, bf16[128,1536]{1,0:T(8,128)(2,1)S(1)}, u32[]{:S(2)}, u32[]{:S(2)}) collective-permute-start(bf16[128,1536]{1,0:T(8,128)(2,1)S(1)} %shard_map.198.refs_1_), channel_id=1, source_target_pairs={{0,8},{4,12},{8,0},{12,4},{1,9},{5,13},{9,1},{13,5},{2,10},{6,14},... | collective-permute-start | bytes 1179656 | tf_op jit(solution)/shard_map/ppermute | solution.py:200
  164.1 11.8 %collective-permute-start.38 = (bf16[128,1536]{1,0:T(8,128)(2,1)S(1)}, bf16[128,1536]{1,0:T(8,128)(2,1)S(1)}, u32[]{:S(2)}, u32[]{:S(2)}) collective-permute-start(bf16[128,1536]{1,0:T(8,128)(2,1)S(1)} %shard_map.196.refs_0_), channel_id=1, source_target_pairs={{0,4},{4,0},{8,12},{12,8},{1,5},{5,1},{9,13},{13,9},{2,6},{6,2},{1... | collective-permute-start | bytes 1179656 | tf_op jit(solution)/shard_map/ppermute | solution.py:200
  164.2 9.6 %collective-permute-start.41 = (bf16[64,1536]{1,0:T(8,128)(2,1)S(1)}, bf16[64,1536]{1,0:T(8,128)(2,1)S(1)}, u32[]{:S(2)}, u32[]{:S(2)}) collective-permute-start(bf16[64,1536]{1,0:T(8,128)(2,1)S(1)} %multiply_convert_fusion.4), channel_id=1, source_target_pairs={{0,1},{1,2},{2,3},{3,0},{4,5},{5,6},{6,7},{7,4},{8,9},{9,10},{10,1... | collective-permute-start | bytes 589832 | tf_op jit(solution)/shard_map/ppermute | solution.py:213
  164.3 11.6 %collective-permute-start.42 = (bf16[64,1536]{1,0:T(8,128)(2,1)S(1)}, bf16[64,1536]{1,0:T(8,128)(2,1)S(1)}, u32[]{:S(2)}, u32[]{:S(2)}) collective-permute-start(bf16[64,1536]{1,0:T(8,128)(2,1)S(1)} %multiply_convert_fusion.4), channel_id=1, source_target_pairs={{0,3},{1,0},{2,1},{3,2},{4,7},{5,4},{6,5},{7,6},{8,11},{9,8},{10,9... | collective-permute-start | bytes 589832 | tf_op jit(solution)/shard_map/ppermute | solution.py:213
  189.7 9.7 %collective-permute-start.46 = (bf16[64,1536]{1,0:T(8,128)(2,1)S(1)}, bf16[64,1536]{1,0:T(8,128)(2,1)S(1)}, u32[]{:S(2)}, u32[]{:S(2)}) collective-permute-start(bf16[64,1536]{1,0:T(8,128)(2,1)S(1)} %get-tuple-element.376), channel_id=1, source_target_pairs={{0,1},{1,2},{2,3},{3,0},{4,5},{5,6},{6,7},{7,4},{8,9},{9,10},{10,1... | collective-permute-start | bytes 589832 | tf_op jit(solution)/shard_map/ppermute | solution.py:213
  190.9 10.5 %collective-permute-start.47 = (bf16[64,1536]{1,0:T(8,128)(2,1)S(1)}, bf16[64,1536]{1,0:T(8,128)(2,1)S(1)}, u32[]{:S(2)}, u32[]{:S(2)}) collective-permute-start(bf16[64,1536]{1,0:T(8,128)(2,1)S(1)} %get-tuple-element.375), channel_id=1, source_target_pairs={{0,3},{1,0},{2,1},{3,2},{4,7},{5,4},{6,5},{7,6},{8,11},{9,8},{10,9... | collective-permute-start | bytes 589832 | tf_op jit(solution)/shard_map/ppermute | solution.py:213
  213.0 13.3 %collective-permute-start.50 = (bf16[64,1536]{1,0:T(8,128)(2,1)S(1)}, bf16[64,1536]{1,0:T(8,128)(2,1)S(1)}, u32[]{:S(2)}, u32[]{:S(2)}) collective-permute-start(bf16[64,1536]{1,0:T(8,128)(2,1)S(1)} %get-tuple-element.339), channel_id=1, source_target_pairs={{0,1},{1,2},{2,3},{3,0},{4,5},{5,6},{6,7},{7,4},{8,9},{9,10},{10,1... | collective-permute-start | bytes 589832 | tf_op jit(solution)/shard_map/ppermute | solution.py:213
  213.0 13.3 %collective-permute-start.51 = (bf16[64,1536]{1,0:T(8,128)(2,1)S(1)}, bf16[64,1536]{1,0:T(8,128)(2,1)S(1)}, u32[]{:S(2)}, u32[]{:S(2)}) collective-permute-start(bf16[64,1536]{1,0:T(8,128)(2,1)S(1)} %get-tuple-element.339), channel_id=1, source_target_pairs={{0,3},{1,0},{2,1},{3,2},{4,7},{5,4},{6,5},{7,6},{8,11},{9,8},{10,9... | collective-permute-start | bytes 589832 | tf_op jit(solution)/shard_map/ppermute | solution.py:213
  241.0 9.4 %collective-permute-start.60 = (bf16[128,1152]{1,0:T(8,128)(2,1)S(1)}, bf16[128,1152]{1,0:T(8,128)(2,1)S(1)}, u32[]{:S(2)}, u32[]{:S(2)}) collective-permute-start(bf16[128,1152]{1,0:T(8,128)(2,1)S(1)} %get-tuple-element.343), channel_id=1, source_target_pairs={{0,8},{4,12},{8,0},{12,4},{1,9},{5,13},{9,1},{13,5},{2,10},{6,14},... | collective-permute-start | bytes 884744 | tf_op jit(solution)/shard_map/ppermute | solution.py:200
  250.5 14.9 %collective-permute-start.62 = (bf16[256,1152]{1,0:T(8,128)(2,1)S(1)}, bf16[256,1152]{1,0:T(8,128)(2,1)S(1)}, u32[]{:S(2)}, u32[]{:S(2)}) collective-permute-start(bf16[256,1152]{1,0:T(8,128)(2,1)S(1)} %shard_map.206), channel_id=1, source_target_pairs={{0,8},{4,12},{8,0},{12,4},{1,9},{5,13},{9,1},{13,5},{2,10},{6,14},... | collective-permute-start | bytes 1769480 | tf_op jit(solution)/shard_map/ppermute | solution.py:200
  269.1 9.9 %collective-permute-start.64 = (bf16[512,384]{1,0:T(8,128)(2,1)S(1)}, bf16[512,384]{1,0:T(8,128)(2,1)S(1)}, u32[]{:S(2)}, u32[]{:S(2)}) collective-permute-start(bf16[512,384]{1,0:T(8,128)(2,1)S(1)} %bitcast.143), channel_id=1, source_target_pairs={{0,8},{4,12},{8,0},{12,4},{1,9},{5,13},{9,1},{13,5},{2,10},{6,14},... | collective-permute-start | bytes 1179656 | tf_op jit(solution)/shard_map/ppermute | solution.py:200
  287.1 13.9 %collective-permute-start.66 = (bf16[128,1536]{1,0:T(8,128)(2,1)S(1)}, bf16[128,1536]{1,0:T(8,128)(2,1)S(1)}, u32[]{:S(2)}, u32[]{:S(2)}) collective-permute-start(bf16[128,1536]{1,0:T(8,128)(2,1)S(1)} %get-tuple-element.369), channel_id=1, source_target_pairs={{0,1},{1,2},{2,3},{3,0},{4,5},{5,6},{6,7},{7,4},{8,9},{9,10},{10,1... | collective-permute-start | bytes 1179656 | tf_op jit(solution)/shard_map/ppermute | solution.py:213
  287.3 19.5 %collective-permute-start.68 = (bf16[128,1536]{1,0:T(8,128)(2,1)S(1)}, bf16[128,1536]{1,0:T(8,128)(2,1)S(1)}, u32[]{:S(2)}, u32[]{:S(2)}) collective-permute-start(bf16[128,1536]{1,0:T(8,128)(2,1)S(1)} %get-tuple-element.370), channel_id=1, source_target_pairs={{0,3},{1,0},{2,1},{3,2},{4,7},{5,4},{6,5},{7,6},{8,11},{9,8},{10,9... | collective-permute-start | bytes 1179656 | tf_op jit(solution)/shard_map/ppermute | solution.py:213
  301.0 16.0 %collective-permute-start.67 = (bf16[128,1536]{1,0:T(8,128)(2,1)S(1)}, bf16[128,1536]{1,0:T(8,128)(2,1)S(1)}, u32[]{:S(2)}, u32[]{:S(2)}) collective-permute-start(bf16[128,1536]{1,0:T(8,128)(2,1)S(1)} %fusion), channel_id=1, source_target_pairs={{0,1},{1,2},{2,3},{3,0},{4,5},{5,6},{6,7},{7,4},{8,9},{9,10},{10,1... | collective-permute-start | bytes 1179656 | tf_op jit(solution)/shard_map/ppermute | solution.py:213
  (46 other events, 304.4 us)

commit v7 on v6

--- a/solution.py
+++ b/solution.py
@@ -542,9 +542,16 @@
 
 def scatter_rows(terms):
     own, before, after, away = jnp.split(terms, 4)
-    to_after, from_after = sent(away, 1), sent(before, -1)
-    from_before = sent(after + to_after.astype(jnp.float32), 1)
-    return own + from_before.astype(jnp.float32) + from_after.astype(jnp.float32)
+    half = own.shape[0] // 2
+
+    def send(array, shift):
+        return sent(array, shift).astype(jnp.float32)
+
+    to_after = send(away[:half], 1)
+    to_before = send(away[half:], -1)
+    from_before = jnp.concatenate((send(after[:half] + to_after, 1), send(after[half:], 1)))
+    from_after = jnp.concatenate((send(before[:half], -1), send(before[half:] + to_before, -1)))
+    return own + from_before + from_after
 
 
 def fast_body(
@@ -676,13 +683,14 @@
 
     uy_b0 = y_swap(ux_b0)
     mine_a, before_a, after_a, away_a = jnp.split(mixed_a, 4)
-    to_after, from_after = sent(away_a, 1), sent(before_a, -1)
+    to_after = sent(away_a, 1)
     at_b = project_heads(run, tok_b, heads_in, scales, head_width, qc_b, (qy_b,), True)
-    tok_b, uc_b, uy_b0, ux_b1, at_b, mine_a, after_a, to_after, from_after = sync(
-        tok_b, uc_b, uy_b0, ux_b1, at_b, mine_a, after_a, to_after, from_after
+    tok_b, uc_b, uy_b0, ux_b1, at_b, mine_a, before_a, after_a, to_after = sync(
+        tok_b, uc_b, uy_b0, ux_b1, at_b, mine_a, before_a, after_a, to_after
     )
 
     from_before = sent(after_a + to_after.astype(jnp.float32), 1)
+    from_after = sent(before_a, -1)
     uy_b1, at_yb, at_cb = y_swap(ux_b1), y_swap(at_b), core_swap(at_b)
     hd_b0 = units_end(tok_b, uc_b, uy_b0)
     mixed_b = heads_out((at_b, at_cb))
@@ -721,25 +729,26 @@
     )
 
     mine_b, before_b, after_b, away_b = jnp.split(mixed_b, 4)
-    to_after, from_after = sent(away_b, 1), sent(before_b, -1)
+    to_after = sent(away_b, 1)
+    mine_b, before_b, after_b, to_after, join_a, ja_before, ja_after, ja_away = sync(
+        mine_b, before_b, after_b, to_after, join_a, ja_before, ja_after, ja_away
+    )
+
+    from_before = sent(after_b + to_after.astype(jnp.float32), 1)
+    from_after = sent(before_b, -1)
     tok_ja = jnp.concatenate((join_a, ja_before, ja_after, ja_away))
     js_a = heads_send(tok_ja, join_in)
-    mine_b, after_b, to_after, from_after, tok_ja, js_a = sync(
-        mine_b, after_b, to_after, from_after, tok_ja, js_a
-    )
-
-    from_before, jc_a = sent(after_b + to_after.astype(jnp.float32), 1), core_swap(js_a)
+    tok_ja, js_a, mine_b, *arrived = sync(tok_ja, js_a, mine_b, from_before, from_after)
+
+    layer_b = layer_end(start_f32[half:], mine_b, *arrived)
+    pairs = moment_flips(moment_pair(layer_b.astype(jnp.float32)))
+    jb_before, jb_after, jc_a = sent(layer_b, 1), sent(layer_b, -1), core_swap(js_a)
     jx_a = heads_across(tok_ja, join_in, jc_a, 2)
-    tok_ja, jc_a, jx_a0, jx_a1, mine_b, *arrived = sync(
-        tok_ja, jc_a, *jx_a, mine_b, from_before, from_after
-    )
-
-    layer_b = layer_end(start_f32[half:], mine_b, *arrived)
-    totals = moment_shards(moment_sum(moment_flips(moment_pair(layer_b.astype(jnp.float32)))))
-    jb_before, jb_after = sent(layer_b, 1), sent(layer_b, -1)
-    tok_ja, jc_a, jx_a0, jx_a1, layer_b, jb_before, jb_after, *totals = sync(
-        tok_ja, jc_a, jx_a0, jx_a1, layer_b, jb_before, jb_after, *totals
-    )
+    tok_ja, jc_a, jx_a0, jx_a1, layer_b, jb_before, jb_after, *pairs = sync(
+        tok_ja, jc_a, *jx_a, layer_b, jb_before, jb_after, *pairs
+    )
+
+    totals = moment_shards(moment_sum(pairs))
 
     jb_away = sent(jb_before, 1)
     jy_a0 = y_swap(jx_a0)

time: 323 us -> 315 us (0.975)
  waiting for transfers between devices: 102 us -> 85.8 us
  starting transfers between devices: 63 us -> 72 us
    ppermute x27 -> x30, starting transfers between devices: 38.5 us -> 47.7 us  [row_shift(): lax.ppermute(array, 'rows', [(i, (i + shift) % size) for i in range(size)])]
    ppermute x27 -> x30, waiting for transfers between devices: 61.4 us -> 52.4 us  [row_shift(): lax.ppermute(array, 'rows', [(i, (i + shift) % size) for i in range(size)])]
    ppermute x42, waiting for transfers between devices: 41 us -> 33.4 us  [flip(): return lax.ppermute(array, 'cols', [(i, i ^ mask) for i in range(size)])]
  transfers between devices with their start and end apart: 69 -> 72, of which waited for: 34 -> 35; matrix products, arithmetic and copies ran while one was open for 1% -> 1% of each run, Pallas kernels for 41% -> 42%
where the time goes in v7:
time: 315 us; the launch traced here: 310 us
  Pallas kernels  144 us (46%)
  waiting for transfers between devices  85.8 us (27%)
  starting transfers between devices  72 us (23%)
  other arithmetic  5.38 us (2%)
    pallas_call x30, Pallas kernels, __call__(): pl.pallas_call(kernel, out_shape=out_shape, grid_spec=pltpu.PrefetchScala...  144 us
    ppermute x30, waiting for transfers between devices, row_shift(): lax.ppermute(array, 'rows', [(i, (i + shift) % size) for i in range(size)])  52.4 us
    ppermute x30, starting transfers between devices, row_shift(): lax.ppermute(array, 'rows', [(i, (i + shift) % size) for i in range(size)])  47.7 us
    ppermute x42, waiting for transfers between devices, flip(): return lax.ppermute(array, 'cols', [(i, i ^ mask) for i in range(size)])  33.4 us
    ppermute x42, starting transfers between devices, flip(): return lax.ppermute(array, 'cols', [(i, i ^ mask) for i in range(size)])  24.3 us
  transfers between devices with their start and end apart: 72, of which 35 were waited for; matrix products, arithmetic and copies ran while one was open for 1% of the time, Pallas kernels for 42%

profile of v7, /device:TPU:0, one launch (start us, length us, event | category | flops | bytes accessed | tf_op | source)
XLA Modules:
  0.0 310.3 jit_solution(4115884028986310007)
XLA Ops:
  25.5 5.5 %shard_map.181 = bf16[256,2304]{1,0:T(8,128)(2,1)S(1)} custom-call(s32[2]{0:T(128)S(1)} %pad_add_fusion.pos, bf16[256,1536]{1,0:T(8,128)(2,1)S(1)} %pad_maximum_fusion.tokens_ref, bf16[1536,1536]{1,0:T(8,128)(2,1)} %refs_0_.25, bf16[1536,1536]{1,0:T(8,128)(2,1)} %refs_1_.17, bf16[1536,1536]{1,0:T(8,128)(2,1)} %refs_2_.17), custom_call_target="tpu_custom_call" | custom-call | flops 1 | bytes 1 | tf_op jit(solution)/shard_map/pallas_call | solution.py:221
  35.0 4.0 %shard_map.182 = (bf16[128,1152]{1,0:T(8,128)(2,1)S(1)}, bf16[128,1152]{1,0:T(8,128)(2,1)S(1)}) custom-call(s32[2]{0:T(128)S(1)} %pad_add_fusion.pos, bf16[256,1536]{1,0:T(8,128)(2,1)S(1)} %pad_maximum_fusion.tokens_ref, bf16[1536,1536]{1,0:T(8,128)(2,1)} %refs_0_.25, bf16[1536,1536]{1,0:T(8,128)(2,1)} %refs_1_.17, bf16[1536,1536]{1,0:T(8,128)(2,1)} %refs_2_.17, ...), custom_call_target="tpu_custom_call" | custom-call | flops 1 | bytes 1 | tf_op jit(solution)/shard_map/pallas_call | solution.py:221
  41.3 7.4 %shard_map.183 = bf16[256,3072]{1,0:T(8,128)(2,1)S(1)} custom-call(s32[2]{0:T(128)S(1)} %pad_add_fusion.pos, bf16[256,1536]{1,0:T(8,128)(2,1)S(1)} %pad_maximum_fusion.tokens_ref, bf16[1536,6144]{1,0:T(8,128)(2,1)} %weight_ref.20), custom_call_target="tpu_custom_call" | custom-call | flops 1 | bytes 1 | tf_op jit(solution)/shard_map/pallas_call | solution.py:221
  52.2 4.6 %shard_map.184 = bf16[256,1536]{1,0:T(8,128)(2,1)S(1)} custom-call(s32[2]{0:T(128)S(1)} %pad_add_fusion.pos, bf16[256,1536]{1,0:T(8,128)(2,1)S(1)} %pad_maximum_fusion.tokens_ref, bf16[1536,6144]{1,0:T(8,128)(2,1)} %weight_ref.20, bf16[256,3072]{1,0:T(8,128)(2,1)S(1)} %collective-permute-done.13.refs_1_.arrived_ref), custom_call_target="tpu_custom_call" | custom-call | flops 1 | bytes 1 | tf_op jit(solution)/shard_map/pallas_call | solution.py:221
  61.3 7.4 %shard_map.186 = bf16[256,3072]{1,0:T(8,128)(2,1)S(1)} custom-call(s32[2]{0:T(128)S(1)} %pad_add_fusion.pos, bf16[256,1536]{1,0:T(8,128)(2,1)S(1)} %pad_maximum_fusion.1.tokens_ref, bf16[1536,6144]{1,0:T(8,128)(2,1)} %weight_ref.20), custom_call_target="tpu_custom_call" | custom-call | flops 1 | bytes 1 | tf_op jit(solution)/shard_map/pallas_call | solution.py:221
  68.7 5.5 %shard_map.185 = bf16[256,2304]{1,0:T(8,128)(2,1)S(1)} custom-call(s32[2]{0:T(128)S(1)} %pad_add_fusion.pos, bf16[256,1536]{1,0:T(8,128)(2,1)S(1)} %pad_maximum_fusion.1.tokens_ref, bf16[1536,1536]{1,0:T(8,128)(2,1)} %refs_0_.25, bf16[1536,1536]{1,0:T(8,128)(2,1)} %refs_1_.17, bf16[1536,1536]{1,0:T(8,128)(2,1)} %refs_2_.17), custom_call_target="tpu_custom_call" | custom-call | flops 1 | bytes 1 | tf_op jit(solution)/shard_map/pallas_call | solution.py:221
  74.3 4.4 %shard_map.187.refs_0_ = bf16[256,384]{1,0:T(8,128)(2,1)S(1)} custom-call(s32[2]{0:T(128)S(1)} %pad_add_fusion.pos, bf16[256,1536]{1,0:T(8,128)(2,1)S(1)} %pad_maximum_fusion.tokens_ref, bf16[1536,1536]{1,0:T(8,128)(2,1)} %refs_0_.25, bf16[1536,1536]{1,0:T(8,128)(2,1)} %refs_1_.17, bf16[1536,1536]{1,0:T(8,128)(2,1)} %refs_2_.17, ...), custom_call_target="tpu_custom_call" | custom-call | flops 1 | bytes 1 | tf_op jit(solution)/shard_map/pallas_call | solution.py:221
  80.4 4.8 %shard_map.188.refs_0_ = bf16[256,1536]{1,0:T(8,128)(2,1)S(1)} custom-call(s32[2]{0:T(128)S(1)} %pad_add_fusion.pos, bf16[256,1536]{1,0:T(8,128)(2,1)S(1)} %pad_maximum_fusion.tokens_ref, bf16[1536,6144]{1,0:T(8,128)(2,1)} %weight_ref.20, f32[1,6144]{1,0:T(1,128)S(1)} %bitcast.147, bf16[256,3072]{1,0:T(8,128)(2,1)S(1)} %collective-permute-done.13.refs_1_.arrived_ref, ...), custom_call_target="tpu_custom_call" | custom-call | flops 1 | bytes 1 | tf_op jit(solution)/shard_map/pallas_call | solution.py:221
  87.8 4.6 %shard_map.192 = (bf16[128,1536]{1,0:T(8,128)(2,1)S(1)}, bf16[128,1536]{1,0:T(8,128)(2,1)S(1)}) custom-call(s32[2]{0:T(128)S(1)} %pad_add_fusion.pos, bf16[256,1536]{1,0:T(8,128)(2,1)S(1)} %pad_maximum_fusion.1.tokens_ref, bf16[1536,6144]{1,0:T(8,128)(2,1)} %weight_ref.20, bf16[256,3072]{1,0:T(8,128)(2,1)S(1)} %collective-permute-done.20.refs_1_.arrived_ref), custom_call_target="tpu_custom_call" | custom-call | flops 1 | bytes 1 | tf_op jit(solution)/shard_map/pallas_call | solution.py:221
  92.5 4.0 %shard_map.189 = bf16[256,1152]{1,0:T(8,128)(2,1)S(1)} custom-call(s32[2]{0:T(128)S(1)} %pad_add_fusion.pos, bf16[256,1536]{1,0:T(8,128)(2,1)S(1)} %pad_maximum_fusion.1.tokens_ref, bf16[1536,1536]{1,0:T(8,128)(2,1)} %refs_0_.25, bf16[1536,1536]{1,0:T(8,128)(2,1)} %refs_1_.17, bf16[1536,1536]{1,0:T(8,128)(2,1)} %refs_2_.17, ...), custom_call_target="tpu_custom_call" | custom-call | flops 1 | bytes 1 | tf_op jit(solution)/shard_map/pallas_call | solution.py:221
  96.4 4.3 %shard_map.190.refs_1_ = f32[256,1536]{1,0:T(8,128)S(1)} custom-call(s32[2]{0:T(128)S(1)} %pad_add_fusion.pos, bf16[1536,1536]{1,0:T(8,128)(2,1)} %weight_ref.21, bf16[256,384]{1,0:T(8,128)(2,1)S(1)} %shard_map.187.refs_0_, bf16[256,384]{1,0:T(8,128)(2,1)S(1)} %collective-permute-done.18.refs_1_, bf16[256,384]{1,0:T(8,128)(2,1)S(1)} %collective-permute-done.17.refs_2_), custom_call_target="tpu_custom_call" | custom-call | flops 1 | bytes 1 | tf_op jit(solution)/shard_map/pallas_call | solution.py:221
  100.7 4.2 %shard_map.191.refs_1_ = f32[256,1536]{1,0:T(8,128)S(1)} custom-call(s32[2]{0:T(128)S(1)} %pad_add_fusion.pos, bf16[6144,1536]{1,0:T(8,128)(2,1)} %weight_ref.24, bf16[256,1536]{1,0:T(8,128)(2,1)S(1)} %shard_map.188.refs_0_, f32[256,1536]{1,0:T(8,128)S(1)} %shard_map.190.refs_1_), custom_call_target="tpu_custom_call" | custom-call | flops 1 | bytes 1 | tf_op jit(solution)/shard_map/pallas_call | solution.py:221
  108.7 9.6 %shard_map.194 = f32[256,1536]{1,0:T(8,128)S(1)} custom-call(s32[2]{0:T(128)S(1)} %pad_add_fusion.pos, bf16[6144,1536]{1,0:T(8,128)(2,1)} %weight_ref.24, bf16[256,1536]{1,0:T(8,128)(2,1)S(1)} %collective-permute-done.23.refs_0_, bf16[256,1536]{1,0:T(8,128)(2,1)S(1)} %collective-permute-done.22.refs_1_, ...), custom_call_target="tpu_custom_call" | custom-call | flops 1 | bytes 1 | tf_op jit(solution)/shard_map/pallas_call | solution.py:221
  122.6 4.4 %shard_map.195.refs_0_ = bf16[256,384]{1,0:T(8,128)(2,1)S(1)} custom-call(s32[2]{0:T(128)S(1)} %pad_add_fusion.pos, bf16[256,1536]{1,0:T(8,128)(2,1)S(1)} %pad_maximum_fusion.1.tokens_ref, bf16[1536,1536]{1,0:T(8,128)(2,1)} %refs_0_.25, bf16[1536,1536]{1,0:T(8,128)(2,1)} %refs_1_.17, bf16[1536,1536]{1,0:T(8,128)(2,1)} %refs_2_.17, ...), custom_call_target="tpu_custom_call" | custom-call | flops 1 | bytes 1 | tf_op jit(solution)/shard_map/pallas_call | solution.py:221
  138.3 4.3 %shard_map.196.refs_0_ = bf16[128,1536]{1,0:T(8,128)(2,1)S(1)} custom-call(s32[2]{0:T(128)S(1)} %pad_add_fusion.pos, bf16[256,1536]{1,0:T(8,128)(2,1)S(1)} %pad_maximum_fusion.1.tokens_ref, bf16[1536,6144]{1,0:T(8,128)(2,1)} %weight_ref.20, f32[1,6144]{1,0:T(1,128)S(1)} %bitcast.148, bf16[256,3072]{1,0:T(8,128)(2,1)S(1)} %collective-permute-done.20.refs_1_.arrived_ref, ...), custom_call_target="tpu_custom_call" | custom-call | flops 1 | bytes 1 | tf_op jit(solution)/shard_map/pallas_call | solution.py:221
  151.5 4.3 %shard_map.198.refs_1_ = bf16[128,1536]{1,0:T(8,128)(2,1)S(1)} custom-call(s32[2]{0:T(128)S(1)} %pad_add_fusion.pos, bf16[256,1536]{1,0:T(8,128)(2,1)S(1)} %pad_maximum_fusion.1.tokens_ref, bf16[1536,6144]{1,0:T(8,128)(2,1)} %weight_ref.20, f32[1,6144]{1,0:T(1,128)S(1)} %bitcast.149, bf16[256,3072]{1,0:T(8,128)(2,1)S(1)} %collective-permute-done.20.refs_1_.arrived_ref, ...), custom_call_target="tpu_custom_call" | custom-call | flops 1 | bytes 1 | tf_op jit(solution)/shard_map/pallas_call | solution.py:221
  164.8 4.2 %shard_map.200.refs_2_ = f32[256,1536]{1,0:T(8,128)S(1)} custom-call(s32[2]{0:T(128)S(1)} %pad_add_fusion.pos, bf16[6144,1536]{1,0:T(8,128)(2,1)} %weight_ref.24, bf16[128,1536]{1,0:T(8,128)(2,1)S(1)} %shard_map.196.refs_0_, bf16[128,1536]{1,0:T(8,128)(2,1)S(1)} %shard_map.198.refs_1_, f32[256,1536]{1,0:T(8,128)S(1)} %shard_map.199.refs_2_), custom_call_target="tpu_custom_call" | custom-call | flops 1 | bytes 1 | tf_op jit(solution)/shard_map/pallas_call | solution.py:221
  174.8 4.2 %shard_map.201.refs_4_ = f32[256,1536]{1,0:T(8,128)S(1)} custom-call(s32[2]{0:T(128)S(1)} %pad_add_fusion.pos, bf16[6144,1536]{1,0:T(8,128)(2,1)} %weight_ref.24, bf16[128,1536]{1,0:T(8,128)(2,1)S(1)} %collective-permute-done.38.refs_0_, bf16[128,1536]{1,0:T(8,128)(2,1)S(1)} %collective-permute-done.39.refs_1_, f32[256,1536]{1,0:T(8,128)S(1)} %shard_map.200.refs_2_), custom_call_target="tpu_custom_call" | custom-call | flops 1 | bytes 1 | tf_op jit(solution)/shard_map/pallas_call | solution.py:221
  179.8 7.0 %shard_map.202 = f32[256,1536]{1,0:T(8,128)S(1)} custom-call(s32[2]{0:T(128)S(1)} %pad_add_fusion.pos, bf16[6144,1536]{1,0:T(8,128)(2,1)} %weight_ref.24, bf16[128,1536]{1,0:T(8,128)(2,1)S(1)} %collective-permute-done.33.refs_0_, bf16[128,1536]{1,0:T(8,128)(2,1)S(1)} %collective-permute-done.40.refs_1_, ...), custom_call_target="tpu_custom_call" | custom-call | flops 1 | bytes 1 | tf_op jit(solution)/shard_map/pallas_call | solution.py:221
  188.2 7.5 %collective-permute-done.46 = bf16[64,1536]{1,0:T(8,128)(2,1)S(1)} collective-permute-done((bf16[64,1536]{1,0:T(8,128)(2,1)S(1)}, bf16[64,1536]{1,0:T(8,128)(2,1)S(1)}, u32[]{:S(2)}, u32[]{:S(2)}) %collective-permute-start.46) | collective-permute-done | bytes 196640 | tf_op jit(solution)/shard_map/ppermute | solution.py:213
  195.8 3.9 %collective-permute-start.48 = (bf16[64,1536]{1,0:T(8,128)(2,1)S(1)}, bf16[64,1536]{1,0:T(8,128)(2,1)S(1)}, u32[]{:S(2)}, u32[]{:S(2)}) collective-permute-start(bf16[64,1536]{1,0:T(8,128)(2,1)S(1)} %get-tuple-element.320), channel_id=1, source_target_pairs={{0,3},{1,0},{2,1},{3,2},{4,7},{5,4},{6,5},{7,6},{8,11},{9,8},{10,9... | collective-permute-start | bytes 589832 | tf_op jit(solution)/shard_map/ppermute | solution.py:213
  199.8 5.5 %shard_map.203 = bf16[256,2304]{1,0:T(8,128)(2,1)S(1)} custom-call(s32[2]{0:T(128)S(1)} %pad_add_fusion.pos, bf16[256,1536]{1,0:T(8,128)(2,1)S(1)} %constant_dynamic-update-slice_fusion.tokens_ref, bf16[1536,1536]{1,0:T(8,128)(2,1)} %refs_0_.31, bf16[1536,1536]{1,0:T(8,128)(2,1)} %refs_1_.23, bf16[1536,1536]{1,0:T(8,128)(2,1)} %refs_2_.23), custom_call_target="tpu_custom_call" | custom-call | flops 1 | bytes 1 | tf_op jit(solution)/shard_map/pallas_call | solution.py:221
  211.5 4.0 %shard_map.204 = (bf16[128,1152]{1,0:T(8,128)(2,1)S(1)}, bf16[128,1152]{1,0:T(8,128)(2,1)S(1)}) custom-call(s32[2]{0:T(128)S(1)} %pad_add_fusion.pos, bf16[256,1536]{1,0:T(8,128)(2,1)S(1)} %constant_dynamic-update-slice_fusion.tokens_ref, bf16[1536,1536]{1,0:T(8,128)(2,1)} %refs_0_.31, bf16[1536,1536]{1,0:T(8,128)(2,1)} %refs_1_.23, ...), custom_call_target="tpu_custom_call" | custom-call | flops 1 | bytes 1 | tf_op jit(solution)/shard_map/pallas_call | solution.py:221
  229.4 5.5 %shard_map.205 = bf16[256,2304]{1,0:T(8,128)(2,1)S(1)} custom-call(s32[2]{0:T(128)S(1)} %pad_add_fusion.pos, bf16[256,1536]{1,0:T(8,128)(2,1)S(1)} %pad_maximum_fusion.2.tokens_ref, bf16[1536,1536]{1,0:T(8,128)(2,1)} %refs_0_.31, bf16[1536,1536]{1,0:T(8,128)(2,1)} %refs_1_.23, bf16[1536,1536]{1,0:T(8,128)(2,1)} %refs_2_.23), custom_call_target="tpu_custom_call" | custom-call | flops 1 | bytes 1 | tf_op jit(solution)/shard_map/pallas_call | solution.py:221
  237.9 4.0 %shard_map.206 = bf16[256,1152]{1,0:T(8,128)(2,1)S(1)} custom-call(s32[2]{0:T(128)S(1)} %pad_add_fusion.pos, bf16[256,1536]{1,0:T(8,128)(2,1)S(1)} %pad_maximum_fusion.2.tokens_ref, bf16[1536,1536]{1,0:T(8,128)(2,1)} %refs_0_.31, bf16[1536,1536]{1,0:T(8,128)(2,1)} %refs_1_.23, bf16[1536,1536]{1,0:T(8,128)(2,1)} %refs_2_.23, ...), custom_call_target="tpu_custom_call" | custom-call | flops 1 | bytes 1 | tf_op jit(solution)/shard_map/pallas_call | solution.py:221
  245.5 4.0 %shard_map.208.refs_3_.refs_4_.refs_5_ = f32[256,1152]{1,0:T(8,128)S(1)} custom-call(s32[2]{0:T(128)S(1)} %pad_add_fusion.pos, bf16[256,1536]{1,0:T(8,128)(2,1)S(1)} %pad_maximum_fusion.2.tokens_ref, bf16[1536,1536]{1,0:T(8,128)(2,1)} %refs_0_.31, bf16[1536,1536]{1,0:T(8,128)(2,1)} %refs_1_.23, bf16[1536,1536]{1,0:T(8,128)(2,1)} %refs_2_.23, ...), custom_call_target="tpu_custom_call" | custom-call | flops 1 | bytes 1 | tf_op jit(solution)/shard_map/pallas_call | solution.py:221
  249.5 4.0 %shard_map.207.refs_0_.refs_1_.refs_2_ = bf16[256,1152]{1,0:T(8,128)(2,1)S(1)} custom-call(s32[2]{0:T(128)S(1)} %pad_add_fusion.pos, bf16[256,1536]{1,0:T(8,128)(2,1)S(1)} %constant_dynamic-update-slice_fusion.tokens_ref, bf16[1536,1536]{1,0:T(8,128)(2,1)} %refs_0_.31, bf16[1536,1536]{1,0:T(8,128)(2,1)} %refs_1_.23, bf16[1536,1536]{1,0:T(8,128)(2,1)} %refs_2_.23, ...), custom_call_target="tpu_custom_call" | custom-call | flops 1 | bytes 1 | tf_op jit(solution)/shard_map/pallas_call | solution.py:221
  253.5 5.9 %collective-permute-done.62.refs_6_.refs_7_.refs_8_ = bf16[256,1152]{1,0:T(8,128)(2,1)S(1)} collective-permute-done((bf16[256,1152]{1,0:T(8,128)(2,1)S(1)}, bf16[256,1152]{1,0:T(8,128)(2,1)S(1)}, u32[]{:S(2)}, u32[]{:S(2)}) %collective-permute-start.62) | collective-permute-done | bytes 589856 | tf_op jit(solution)/shard_map/ppermute | solution.py:200
  264.1 8.8 %collective-permute-done.64.refs_2_ = bf16[512,384]{1,0:T(8,128)(2,1)S(1)} collective-permute-done((bf16[512,384]{1,0:T(8,128)(2,1)S(1)}, bf16[512,384]{1,0:T(8,128)(2,1)S(1)}, u32[]{:S(2)}, u32[]{:S(2)}) %collective-permute-start.64) | collective-permute-done | bytes 393248 | tf_op jit(solution)/shard_map/ppermute | solution.py:200
  274.6 6.2 %shard_map.210 = f32[512,1536]{1,0:T(8,128)S(1)} custom-call(s32[2]{0:T(128)S(1)} %pad_add_fusion.pos, bf16[1536,1536]{1,0:T(8,128)(2,1)} %weight_ref.25, bf16[512,384]{1,0:T(8,128)(2,1)S(1)} %bitcast.145, bf16[512,384]{1,0:T(8,128)(2,1)S(1)} %collective-permute-done.63.refs_1_, bf16[512,384]{1,0:T(8,128)(2,1)S(1)} %collective-permute-done.64.refs_2_, ...), custom_call_target="tpu_custom_call" | custom-call | flops 1 | bytes 1 | tf_op jit(solution)/shard_map/pallas_call | solution.py:221
  285.0 3.8 %collective-permute-start.69 = (bf16[64,1536]{1,0:T(8,128)(2,1)S(1)}, bf16[64,1536]{1,0:T(8,128)(2,1)S(1)}, u32[]{:S(2)}, u32[]{:S(2)}) collective-permute-start(bf16[64,1536]{1,0:T(8,128)(2,1)S(1)} %get-tuple-element.371), channel_id=1, source_target_pairs={{0,3},{1,0},{2,1},{3,2},{4,7},{5,4},{6,5},{7,6},{8,11},{9,8},{10,9... | collective-permute-start | bytes 589832 | tf_op jit(solution)/shard_map/ppermute | solution.py:213
  301.6 6.1 %collective-permute-done.67 = bf16[64,1536]{1,0:T(8,128)(2,1)S(1)} collective-permute-done((bf16[64,1536]{1,0:T(8,128)(2,1)S(1)}, bf16[64,1536]{1,0:T(8,128)(2,1)S(1)}, u32[]{:S(2)}, u32[]{:S(2)}) %collective-permute-start.67) | collective-permute-done | bytes 196640 | tf_op jit(solution)/shard_map/ppermute | solution.py:213
  (212 shorter events, 141.2 us)
Async XLA Ops:
  1.1 11.2 %collective-permute-start = (bf16[64,1536]{1,0:T(8,128)(2,1)S(1)}, bf16[64,1536]{1,0:T(8,128)(2,1)S(1)}, u32[]{:S(2)}, u32[]{:S(2)}) collective-permute-start(bf16[64,1536]{1,0:T(8,128)(2,1)S(1)} %get-tuple-element.191), channel_id=1, source_target_pairs={{0,1},{1,2},{2,3},{3,0},{4,5},{5,6},{6,7},{7,4},{8,9},{9,10},{10,1... | collective-permute-start | bytes 589832 | tf_op jit(solution)/shard_map/ppermute | solution.py:213
  4.1 10.6 %collective-permute-start.1 = (bf16[64,1536]{1,0:T(8,128)(2,1)S(1)}, bf16[64,1536]{1,0:T(8,128)(2,1)S(1)}, u32[]{:S(2)}, u32[]{:S(2)}) collective-permute-start(bf16[64,1536]{1,0:T(8,128)(2,1)S(1)} %get-tuple-element.191), channel_id=1, source_target_pairs={{0,3},{1,0},{2,1},{3,2},{4,7},{5,4},{6,5},{7,6},{8,11},{9,8},{10,9... | collective-permute-start | bytes 589832 | tf_op jit(solution)/shard_map/ppermute | solution.py:213
  48.8 10.8 %collective-permute-start.14 = (bf16[128,1152]{1,0:T(8,128)(2,1)S(1)}, bf16[128,1152]{1,0:T(8,128)(2,1)S(1)}, u32[]{:S(2)}, u32[]{:S(2)}) collective-permute-start(bf16[128,1152]{1,0:T(8,128)(2,1)S(1)} %get-tuple-element.217), channel_id=1, source_target_pairs={{0,8},{4,12},{8,0},{12,4},{1,9},{5,13},{9,1},{13,5},{2,10},{6,14},... | collective-permute-start | bytes 884744 | tf_op jit(solution)/shard_map/ppermute | solution.py:200
  49.9 9.7 %collective-permute-start.15 = (bf16[64,1536]{1,0:T(8,128)(2,1)S(1)}, bf16[64,1536]{1,0:T(8,128)(2,1)S(1)}, u32[]{:S(2)}, u32[]{:S(2)}) collective-permute-start(bf16[64,1536]{1,0:T(8,128)(2,1)S(1)} %collective-permute-done.9), channel_id=1, source_target_pairs={{0,1},{1,2},{2,3},{3,0},{4,5},{5,6},{6,7},{7,4},{8,9},{9,10},{10,1... | collective-permute-start | bytes 589832 | tf_op jit(solution)/shard_map/ppermute | solution.py:213
  59.6 19.2 %collective-permute-start.16 = (bf16[256,1536]{1,0:T(8,128)(2,1)S(1)}, bf16[256,1536]{1,0:T(8,128)(2,1)S(1)}, u32[]{:S(2)}, u32[]{:S(2)}) collective-permute-start(bf16[256,1536]{1,0:T(8,128)(2,1)S(1)} %shard_map.184), channel_id=1, source_target_pairs={{0,8},{4,12},{8,0},{12,4},{1,9},{5,13},{9,1},{13,5},{2,10},{6,14},... | collective-permute-start | bytes 2359304 | tf_op jit(solution)/shard_map/ppermute | solution.py:200
  86.2 19.1 %collective-permute-start.22 = (bf16[256,1536]{1,0:T(8,128)(2,1)S(1)}, bf16[256,1536]{1,0:T(8,128)(2,1)S(1)}, u32[]{:S(2)}, u32[]{:S(2)}) collective-permute-start(bf16[256,1536]{1,0:T(8,128)(2,1)S(1)} %shard_map.188.refs_0_), channel_id=1, source_target_pairs={{0,8},{4,12},{8,0},{12,4},{1,9},{5,13},{9,1},{13,5},{2,10},{6,14},... | collective-permute-start | bytes 2359304 | tf_op jit(solution)/shard_map/ppermute | solution.py:200
  87.3 17.9 %collective-permute-start.23 = (bf16[256,1536]{1,0:T(8,128)(2,1)S(1)}, bf16[256,1536]{1,0:T(8,128)(2,1)S(1)}, u32[]{:S(2)}, u32[]{:S(2)}) collective-permute-start(bf16[256,1536]{1,0:T(8,128)(2,1)S(1)} %shard_map.188.refs_0_), channel_id=1, source_target_pairs={{0,4},{4,0},{8,12},{12,8},{1,5},{5,1},{9,13},{13,9},{2,6},{6,2},{1... | collective-permute-start | bytes 2359304 | tf_op jit(solution)/shard_map/ppermute | solution.py:200
  87.3 17.7 %collective-permute-start.21 = (bf16[256,384]{1,0:T(8,128)(2,1)S(1)}, bf16[256,384]{1,0:T(8,128)(2,1)S(1)}, u32[]{:S(2)}, u32[]{:S(2)}) collective-permute-start(bf16[256,384]{1,0:T(8,128)(2,1)S(1)} %collective-permute-done.17.refs_2_), channel_id=1, source_target_pairs={{0,4},{4,0},{8,12},{12,8},{1,5},{5,1},{9,13},{13,9},{2,6},{6,2},{1... | collective-permute-start | bytes 589832 | tf_op jit(solution)/shard_map/ppermute | solution.py:200
  105.3 15.7 %collective-permute-start.25 = (bf16[256,1152]{1,0:T(8,128)(2,1)S(1)}, bf16[256,1152]{1,0:T(8,128)(2,1)S(1)}, u32[]{:S(2)}, u32[]{:S(2)}) collective-permute-start(bf16[256,1152]{1,0:T(8,128)(2,1)S(1)} %shard_map.189), channel_id=1, source_target_pairs={{0,8},{4,12},{8,0},{12,4},{1,9},{5,13},{9,1},{13,5},{2,10},{6,14},... | collective-permute-start | bytes 1769480 | tf_op jit(solution)/shard_map/ppermute | solution.py:200
  121.5 10.8 %collective-permute-start.26 = (bf16[128,1536]{1,0:T(8,128)(2,1)S(1)}, bf16[128,1536]{1,0:T(8,128)(2,1)S(1)}, u32[]{:S(2)}, u32[]{:S(2)}) collective-permute-start(bf16[128,1536]{1,0:T(8,128)(2,1)S(1)} %get-tuple-element.259), channel_id=1, source_target_pairs={{0,8},{4,12},{8,0},{12,4},{1,9},{5,13},{9,1},{13,5},{2,10},{6,14},... | collective-permute-start | bytes 1179656 | tf_op jit(solution)/shard_map/ppermute | solution.py:200
  132.3 10.3 %collective-permute-start.30 = (bf16[256,384]{1,0:T(8,128)(2,1)S(1)}, bf16[256,384]{1,0:T(8,128)(2,1)S(1)}, u32[]{:S(2)}, u32[]{:S(2)}) collective-permute-start(bf16[256,384]{1,0:T(8,128)(2,1)S(1)} %shard_map.195.refs_0_), channel_id=1, source_target_pairs={{0,4},{4,0},{8,12},{12,8},{1,5},{5,1},{9,13},{13,9},{2,6},{6,2},{1... | collective-permute-start | bytes 589832 | tf_op jit(solution)/shard_map/ppermute | solution.py:200
  132.3 13.4 %collective-permute-start.29 = (bf16[256,384]{1,0:T(8,128)(2,1)S(1)}, bf16[256,384]{1,0:T(8,128)(2,1)S(1)}, u32[]{:S(2)}, u32[]{:S(2)}) collective-permute-start(bf16[256,384]{1,0:T(8,128)(2,1)S(1)} %shard_map.195.refs_0_), channel_id=1, source_target_pairs={{0,8},{4,12},{8,0},{12,4},{1,9},{5,13},{9,1},{13,5},{2,10},{6,14},... | collective-permute-start | bytes 589832 | tf_op jit(solution)/shard_map/ppermute | solution.py:200
  133.3 14.8 %collective-permute-start.28 = (bf16[128,1536]{1,0:T(8,128)(2,1)S(1)}, bf16[128,1536]{1,0:T(8,128)(2,1)S(1)}, u32[]{:S(2)}, u32[]{:S(2)}) collective-permute-start(bf16[128,1536]{1,0:T(8,128)(2,1)S(1)} %get-tuple-element.266), channel_id=1, source_target_pairs={{0,8},{4,12},{8,0},{12,4},{1,9},{5,13},{9,1},{13,5},{2,10},{6,14},... | collective-permute-start | bytes 1179656 | tf_op jit(solution)/shard_map/ppermute | solution.py:200
  134.4 11.3 %collective-permute-start.31 = (bf16[64,1536]{1,0:T(8,128)(2,1)S(1)}, bf16[64,1536]{1,0:T(8,128)(2,1)S(1)}, u32[]{:S(2)}, u32[]{:S(2)}) collective-permute-start(bf16[64,1536]{1,0:T(8,128)(2,1)S(1)} %add_convert_fusion.1), channel_id=1, source_target_pairs={{0,1},{1,2},{2,3},{3,0},{4,5},{5,6},{6,7},{7,4},{8,9},{9,10},{10,1... | collective-permute-start | bytes 589832 | tf_op jit(solution)/shard_map/ppermute | solution.py:213
  134.8 12.3 %collective-permute-start.32 = (bf16[64,1536]{1,0:T(8,128)(2,1)S(1)}, bf16[64,1536]{1,0:T(8,128)(2,1)S(1)}, u32[]{:S(2)}, u32[]{:S(2)}) collective-permute-start(bf16[64,1536]{1,0:T(8,128)(2,1)S(1)} %get-tuple-element.272), channel_id=1, source_target_pairs={{0,3},{1,0},{2,1},{3,2},{4,7},{5,4},{6,5},{7,6},{8,11},{9,8},{10,9... | collective-permute-start | bytes 589832 | tf_op jit(solution)/shard_map/ppermute | solution.py:213
  148.1 10.8 %collective-permute-start.33 = (bf16[128,1536]{1,0:T(8,128)(2,1)S(1)}, bf16[128,1536]{1,0:T(8,128)(2,1)S(1)}, u32[]{:S(2)}, u32[]{:S(2)}) collective-permute-start(bf16[128,1536]{1,0:T(8,128)(2,1)S(1)} %shard_map.196.refs_0_), channel_id=1, source_target_pairs={{0,8},{4,12},{8,0},{12,4},{1,9},{5,13},{9,1},{13,5},{2,10},{6,14},... | collective-permute-start | bytes 1179656 | tf_op jit(solution)/shard_map/ppermute | solution.py:200
  159.0 15.2 %collective-permute-start.39 = (bf16[128,1536]{1,0:T(8,128)(2,1)S(1)}, bf16[128,1536]{1,0:T(8,128)(2,1)S(1)}, u32[]{:S(2)}, u32[]{:S(2)}) collective-permute-start(bf16[128,1536]{1,0:T(8,128)(2,1)S(1)} %shard_map.198.refs_1_), channel_id=1, source_target_pairs={{0,4},{4,0},{8,12},{12,8},{1,5},{5,1},{9,13},{13,9},{2,6},{6,2},{1... | collective-permute-start | bytes 1179656 | tf_op jit(solution)/shard_map/ppermute | solution.py:200
  159.7 14.4 %collective-permute-start.40 = (bf16[128,1536]{1,0:T(8,128)(2,1)S(1)}, bf16[128,1536]{1,0:T(8,128)(2,1)S(1)}, u32[]{:S(2)}, u32[]{:S(2)}) collective-permute-start(bf16[128,1536]{1,0:T(8,128)(2,1)S(1)} %shard_map.198.refs_1_), channel_id=1, source_target_pairs={{0,8},{4,12},{8,0},{12,4},{1,9},{5,13},{9,1},{13,5},{2,10},{6,14},... | collective-permute-start | bytes 1179656 | tf_op jit(solution)/shard_map/ppermute | solution.py:200
  160.8 13.4 %collective-permute-start.38 = (bf16[128,1536]{1,0:T(8,128)(2,1)S(1)}, bf16[128,1536]{1,0:T(8,128)(2,1)S(1)}, u32[]{:S(2)}, u32[]{:S(2)}) collective-permute-start(bf16[128,1536]{1,0:T(8,128)(2,1)S(1)} %shard_map.196.refs_0_), channel_id=1, source_target_pairs={{0,4},{4,0},{8,12},{12,8},{1,5},{5,1},{9,13},{13,9},{2,6},{6,2},{1... | collective-permute-start | bytes 1179656 | tf_op jit(solution)/shard_map/ppermute | solution.py:200
  161.3 12.8 %collective-permute-start.42 = (bf16[64,1536]{1,0:T(8,128)(2,1)S(1)}, bf16[64,1536]{1,0:T(8,128)(2,1)S(1)}, u32[]{:S(2)}, u32[]{:S(2)}) collective-permute-start(bf16[64,1536]{1,0:T(8,128)(2,1)S(1)} %multiply_convert_fusion.4), channel_id=1, source_target_pairs={{0,3},{1,0},{2,1},{3,2},{4,7},{5,4},{6,5},{7,6},{8,11},{9,8},{10,9... | collective-permute-start | bytes 589832 | tf_op jit(solution)/shard_map/ppermute | solution.py:213
  205.6 9.9 %collective-permute-start.50 = (bf16[64,1536]{1,0:T(8,128)(2,1)S(1)}, bf16[64,1536]{1,0:T(8,128)(2,1)S(1)}, u32[]{:S(2)}, u32[]{:S(2)}) collective-permute-start(bf16[64,1536]{1,0:T(8,128)(2,1)S(1)} %get-tuple-element.339), channel_id=1, source_target_pairs={{0,1},{1,2},{2,3},{3,0},{4,5},{5,6},{6,7},{7,4},{8,9},{9,10},{10,1... | collective-permute-start | bytes 589832 | tf_op jit(solution)/shard_map/ppermute | solution.py:213
  206.1 12.0 %collective-permute-start.51 = (bf16[64,1536]{1,0:T(8,128)(2,1)S(1)}, bf16[64,1536]{1,0:T(8,128)(2,1)S(1)}, u32[]{:S(2)}, u32[]{:S(2)}) collective-permute-start(bf16[64,1536]{1,0:T(8,128)(2,1)S(1)} %get-tuple-element.339), channel_id=1, source_target_pairs={{0,3},{1,0},{2,1},{3,2},{4,7},{5,4},{6,5},{7,6},{8,11},{9,8},{10,9... | collective-permute-start | bytes 589832 | tf_op jit(solution)/shard_map/ppermute | solution.py:213
  218.0 10.9 %collective-permute-start.55 = (bf16[128,1152]{1,0:T(8,128)(2,1)S(1)}, bf16[128,1152]{1,0:T(8,128)(2,1)S(1)}, u32[]{:S(2)}, u32[]{:S(2)}) collective-permute-start(bf16[128,1152]{1,0:T(8,128)(2,1)S(1)} %get-tuple-element.330), channel_id=1, source_target_pairs={{0,8},{4,12},{8,0},{12,4},{1,9},{5,13},{9,1},{13,5},{2,10},{6,14},... | collective-permute-start | bytes 884744 | tf_op jit(solution)/shard_map/ppermute | solution.py:200
  219.1 9.8 %collective-permute-start.56 = (bf16[64,1536]{1,0:T(8,128)(2,1)S(1)}, bf16[64,1536]{1,0:T(8,128)(2,1)S(1)}, u32[]{:S(2)}, u32[]{:S(2)}) collective-permute-start(bf16[64,1536]{1,0:T(8,128)(2,1)S(1)} %collective-permute-done.50), channel_id=1, source_target_pairs={{0,1},{1,2},{2,3},{3,0},{4,5},{5,6},{6,7},{7,4},{8,9},{9,10},{10,1... | collective-permute-start | bytes 589832 | tf_op jit(solution)/shard_map/ppermute | solution.py:213
  244.5 14.9 %collective-permute-start.62 = (bf16[256,1152]{1,0:T(8,128)(2,1)S(1)}, bf16[256,1152]{1,0:T(8,128)(2,1)S(1)}, u32[]{:S(2)}, u32[]{:S(2)}) collective-permute-start(bf16[256,1152]{1,0:T(8,128)(2,1)S(1)} %shard_map.206), channel_id=1, source_target_pairs={{0,8},{4,12},{8,0},{12,4},{1,9},{5,13},{9,1},{13,5},{2,10},{6,14},... | collective-permute-start | bytes 1769480 | tf_op jit(solution)/shard_map/ppermute | solution.py:200
  263.1 9.9 %collective-permute-start.64 = (bf16[512,384]{1,0:T(8,128)(2,1)S(1)}, bf16[512,384]{1,0:T(8,128)(2,1)S(1)}, u32[]{:S(2)}, u32[]{:S(2)}) collective-permute-start(bf16[512,384]{1,0:T(8,128)(2,1)S(1)} %bitcast.143), channel_id=1, source_target_pairs={{0,8},{4,12},{8,0},{12,4},{1,9},{5,13},{9,1},{13,5},{2,10},{6,14},... | collective-permute-start | bytes 1179656 | tf_op jit(solution)/shard_map/ppermute | solution.py:200
  281.1 9.6 %collective-permute-start.66 = (bf16[64,1536]{1,0:T(8,128)(2,1)S(1)}, bf16[64,1536]{1,0:T(8,128)(2,1)S(1)}, u32[]{:S(2)}, u32[]{:S(2)}) collective-permute-start(bf16[64,1536]{1,0:T(8,128)(2,1)S(1)} %get-tuple-element.374), channel_id=1, source_target_pairs={{0,1},{1,2},{2,3},{3,0},{4,5},{5,6},{6,7},{7,4},{8,9},{9,10},{10,1... | collective-permute-start | bytes 589832 | tf_op jit(solution)/shard_map/ppermute | solution.py:213
  281.2 12.0 %collective-permute-start.70 = (bf16[64,1536]{1,0:T(8,128)(2,1)S(1)}, bf16[64,1536]{1,0:T(8,128)(2,1)S(1)}, u32[]{:S(2)}, u32[]{:S(2)}) collective-permute-start(bf16[64,1536]{1,0:T(8,128)(2,1)S(1)} %get-tuple-element.372), channel_id=1, source_target_pairs={{0,3},{1,0},{2,1},{3,2},{4,7},{5,4},{6,5},{7,6},{8,11},{9,8},{10,9... | collective-permute-start | bytes 589832 | tf_op jit(solution)/shard_map/ppermute | solution.py:213
  285.0 14.2 %collective-permute-start.68 = (bf16[64,1536]{1,0:T(8,128)(2,1)S(1)}, bf16[64,1536]{1,0:T(8,128)(2,1)S(1)}, u32[]{:S(2)}, u32[]{:S(2)}) collective-permute-start(bf16[64,1536]{1,0:T(8,128)(2,1)S(1)} %get-tuple-element.373), channel_id=1, source_target_pairs={{0,1},{1,2},{2,3},{3,0},{4,5},{5,6},{6,7},{7,4},{8,9},{9,10},{10,1... | collective-permute-start | bytes 589832 | tf_op jit(solution)/shard_map/ppermute | solution.py:213
  285.0 16.6 %collective-permute-start.69 = (bf16[64,1536]{1,0:T(8,128)(2,1)S(1)}, bf16[64,1536]{1,0:T(8,128)(2,1)S(1)}, u32[]{:S(2)}, u32[]{:S(2)}) collective-permute-start(bf16[64,1536]{1,0:T(8,128)(2,1)S(1)} %get-tuple-element.371), channel_id=1, source_target_pairs={{0,3},{1,0},{2,1},{3,2},{4,7},{5,4},{6,5},{7,6},{8,11},{9,8},{10,9... | collective-permute-start | bytes 589832 | tf_op jit(solution)/shard_map/ppermute | solution.py:213
  293.3 14.4 %collective-permute-start.67 = (bf16[64,1536]{1,0:T(8,128)(2,1)S(1)}, bf16[64,1536]{1,0:T(8,128)(2,1)S(1)}, u32[]{:S(2)}, u32[]{:S(2)}) collective-permute-start(bf16[64,1536]{1,0:T(8,128)(2,1)S(1)} %get-tuple-element.370), channel_id=1, source_target_pairs={{0,1},{1,2},{2,3},{3,0},{4,5},{5,6},{6,7},{7,4},{8,9},{9,10},{10,1... | collective-permute-start | bytes 589832 | tf_op jit(solution)/shard_map/ppermute | solution.py:213
  293.9 15.4 %collective-permute-start.71 = (bf16[64,1536]{1,0:T(8,128)(2,1)S(1)}, bf16[64,1536]{1,0:T(8,128)(2,1)S(1)}, u32[]{:S(2)}, u32[]{:S(2)}) collective-permute-start(bf16[64,1536]{1,0:T(8,128)(2,1)S(1)} %get-tuple-element.369), channel_id=1, source_target_pairs={{0,3},{1,0},{2,1},{3,2},{4,7},{5,4},{6,5},{7,6},{8,11},{9,8},{10,9... | collective-permute-start | bytes 589832 | tf_op jit(solution)/shard_map/ppermute | solution.py:213
  (49 other events, 325.3 us)

commit v8 on v7

--- a/solution.py
+++ b/solution.py
@@ -580,7 +580,7 @@
     run = Runner(jnp.stack((index & 1, index >> 1)).astype(jnp.int32))
     head_width = query_weight.shape[1] // 4
     unit_width = up_weight.shape[1] // 4
-    sub = 3 if unit_width % (3 * 256) == 0 else 1
+    sub = 2 if unit_width % 256 == 0 else 1
     heads_in = (query_weight, key_weight, value_weight)
     join_in = (join_query, join_key, join_value)
     scales = (query_gain[None], key_gain[None])
@@ -597,10 +597,10 @@
         return contract(run, [(part,) for part in parts], out_weight, 1, first, start)
 
     def units_down(parts, first, start):
-        return contract(run, parts, down_weight, 2, first, start)
+        return contract(run, parts, down_weight, 1 if len(parts) > 1 else 2, first, start)
 
     def units_send(tokens):
-        return project_send(run, tokens, (up_weight,), unit_width, sub)
+        return project_send(run, tokens, (up_weight,), unit_width, 1)
 
     def units_across(tokens, arrived, pieces):
         return project_across(run, tokens, (up_weight,), unit_width, sub, arrived, pieces)

time: 315 us -> 314 us (level)
  waiting for transfers between devices: 85.8 us -> 96.5 us
  Pallas kernels: 144 us -> 136 us
  starting transfers between devices: 72 us -> 68.7 us
    pallas_call x30, Pallas kernels: 144 us -> 136 us  [__call__(): pl.pallas_call(kernel, out_shape=out_shape, grid_spec=pltpu.PrefetchScala...]
    ppermute x42, waiting for transfers between devices: 33.4 us -> 40.7 us  [flip(): return lax.ppermute(array, 'cols', [(i, i ^ mask) for i in range(size)])]
    ppermute x30, waiting for transfers between devices: 52.4 us -> 55.8 us  [row_shift(): lax.ppermute(array, 'rows', [(i, (i + shift) % size) for i in range(size)])]
  transfers between devices with their start and end apart: 72 -> 72, of which waited for: 35 -> 37; matrix products, arithmetic and copies ran while one was open for 1% -> 1% of each run, Pallas kernels for 42% -> 39%
where the time goes in v8:
time: 314 us; the launch traced here: 309 us
  Pallas kernels  136 us (43%)
  waiting for transfers between devices  96.5 us (31%)
  starting transfers between devices  68.7 us (22%)
  other arithmetic  5.38 us (2%)
    pallas_call x30, Pallas kernels, __call__(): pl.pallas_call(kernel, out_shape=out_shape, grid_spec=pltpu.PrefetchScala...  136 us
    ppermute x30, waiting for transfers between devices, row_shift(): lax.ppermute(array, 'rows', [(i, (i + shift) % size) for i in range(size)])  55.8 us
    ppermute x30, starting transfers between devices, row_shift(): lax.ppermute(array, 'rows', [(i, (i + shift) % size) for i in range(size)])  46.7 us
    ppermute x42, waiting for transfers between devices, flip(): return lax.ppermute(array, 'cols', [(i, i ^ mask) for i in range(size)])  40.7 us
    ppermute x42, starting transfers between devices, flip(): return lax.ppermute(array, 'cols', [(i, i ^ mask) for i in range(size)])  22 us
  transfers between devices with their start and end apart: 72, of which 37 were waited for; matrix products, arithmetic and copies ran while one was open for 1% of the time, Pallas kernels for 39%

profile of v8, /device:TPU:0, one launch (start us, length us, event | category | flops | bytes accessed | tf_op | source)
XLA Modules:
  0.0 308.8 jit_solution(11529572084637641722)
XLA Ops:
  25.5 5.5 %shard_map.181 = bf16[256,2304]{1,0:T(8,128)(2,1)S(1)} custom-call(s32[2]{0:T(128)S(1)} %pad_add_fusion.pos, bf16[256,1536]{1,0:T(8,128)(2,1)S(1)} %pad_maximum_fusion.tokens_ref, bf16[1536,1536]{1,0:T(8,128)(2,1)} %refs_0_.25, bf16[1536,1536]{1,0:T(8,128)(2,1)} %refs_1_.17, bf16[1536,1536]{1,0:T(8,128)(2,1)} %refs_2_.17), custom_call_target="tpu_custom_call" | custom-call | flops 1 | bytes 1 | tf_op jit(solution)/shard_map/pallas_call | solution.py:221
  35.0 4.0 %shard_map.182 = (bf16[128,1152]{1,0:T(8,128)(2,1)S(1)}, bf16[128,1152]{1,0:T(8,128)(2,1)S(1)}) custom-call(s32[2]{0:T(128)S(1)} %pad_add_fusion.pos, bf16[256,1536]{1,0:T(8,128)(2,1)S(1)} %pad_maximum_fusion.tokens_ref, bf16[1536,1536]{1,0:T(8,128)(2,1)} %refs_0_.25, bf16[1536,1536]{1,0:T(8,128)(2,1)} %refs_1_.17, bf16[1536,1536]{1,0:T(8,128)(2,1)} %refs_2_.17, ...), custom_call_target="tpu_custom_call" | custom-call | flops 1 | bytes 1 | tf_op jit(solution)/shard_map/pallas_call | solution.py:221
  41.3 5.8 %shard_map.183 = bf16[256,3072]{1,0:T(8,128)(2,1)S(1)} custom-call(s32[2]{0:T(128)S(1)} %pad_add_fusion.pos, bf16[256,1536]{1,0:T(8,128)(2,1)S(1)} %pad_maximum_fusion.tokens_ref, bf16[1536,6144]{1,0:T(8,128)(2,1)} %weight_ref.20), custom_call_target="tpu_custom_call" | custom-call | flops 1 | bytes 1 | tf_op jit(solution)/shard_map/pallas_call | solution.py:221
  51.8 3.9 %shard_map.184 = bf16[256,1536]{1,0:T(8,128)(2,1)S(1)} custom-call(s32[2]{0:T(128)S(1)} %pad_add_fusion.pos, bf16[256,1536]{1,0:T(8,128)(2,1)S(1)} %pad_maximum_fusion.tokens_ref, bf16[1536,6144]{1,0:T(8,128)(2,1)} %weight_ref.20, bf16[256,3072]{1,0:T(8,128)(2,1)S(1)} %collective-permute-done.13.refs_1_.arrived_ref), custom_call_target="tpu_custom_call" | custom-call | flops 1 | bytes 1 | tf_op jit(solution)/shard_map/pallas_call | solution.py:221
  55.7 3.9 %collective-permute-done.15 = bf16[64,1536]{1,0:T(8,128)(2,1)S(1)} collective-permute-done((bf16[64,1536]{1,0:T(8,128)(2,1)S(1)}, bf16[64,1536]{1,0:T(8,128)(2,1)S(1)}, u32[]{:S(2)}, u32[]{:S(2)}) %collective-permute-start.15) | collective-permute-done | bytes 196640 | tf_op jit(solution)/shard_map/ppermute | solution.py:213
  60.9 5.8 %shard_map.186 = bf16[256,3072]{1,0:T(8,128)(2,1)S(1)} custom-call(s32[2]{0:T(128)S(1)} %pad_add_fusion.pos, bf16[256,1536]{1,0:T(8,128)(2,1)S(1)} %pad_maximum_fusion.1.tokens_ref, bf16[1536,6144]{1,0:T(8,128)(2,1)} %weight_ref.20), custom_call_target="tpu_custom_call" | custom-call | flops 1 | bytes 1 | tf_op jit(solution)/shard_map/pallas_call | solution.py:221
  66.7 5.5 %shard_map.185 = bf16[256,2304]{1,0:T(8,128)(2,1)S(1)} custom-call(s32[2]{0:T(128)S(1)} %pad_add_fusion.pos, bf16[256,1536]{1,0:T(8,128)(2,1)S(1)} %pad_maximum_fusion.1.tokens_ref, bf16[1536,1536]{1,0:T(8,128)(2,1)} %refs_0_.25, bf16[1536,1536]{1,0:T(8,128)(2,1)} %refs_1_.17, bf16[1536,1536]{1,0:T(8,128)(2,1)} %refs_2_.17), custom_call_target="tpu_custom_call" | custom-call | flops 1 | bytes 1 | tf_op jit(solution)/shard_map/pallas_call | solution.py:221
  72.2 4.4 %shard_map.187.refs_0_ = bf16[256,384]{1,0:T(8,128)(2,1)S(1)} custom-call(s32[2]{0:T(128)S(1)} %pad_add_fusion.pos, bf16[256,1536]{1,0:T(8,128)(2,1)S(1)} %pad_maximum_fusion.tokens_ref, bf16[1536,1536]{1,0:T(8,128)(2,1)} %refs_0_.25, bf16[1536,1536]{1,0:T(8,128)(2,1)} %refs_1_.17, bf16[1536,1536]{1,0:T(8,128)(2,1)} %refs_2_.17, ...), custom_call_target="tpu_custom_call" | custom-call | flops 1 | bytes 1 | tf_op jit(solution)/shard_map/pallas_call | solution.py:221
  79.8 4.1 %shard_map.188.refs_0_ = bf16[256,1536]{1,0:T(8,128)(2,1)S(1)} custom-call(s32[2]{0:T(128)S(1)} %pad_add_fusion.pos, bf16[256,1536]{1,0:T(8,128)(2,1)S(1)} %pad_maximum_fusion.tokens_ref, bf16[1536,6144]{1,0:T(8,128)(2,1)} %weight_ref.20, f32[1,6144]{1,0:T(1,128)S(1)} %bitcast.147, bf16[256,3072]{1,0:T(8,128)(2,1)S(1)} %collective-permute-done.13.refs_1_.arrived_ref, ...), custom_call_target="tpu_custom_call" | custom-call | flops 1 | bytes 1 | tf_op jit(solution)/shard_map/pallas_call | solution.py:221
  87.2 3.9 %shard_map.192 = (bf16[128,1536]{1,0:T(8,128)(2,1)S(1)}, bf16[128,1536]{1,0:T(8,128)(2,1)S(1)}) custom-call(s32[2]{0:T(128)S(1)} %pad_add_fusion.pos, bf16[256,1536]{1,0:T(8,128)(2,1)S(1)} %pad_maximum_fusion.1.tokens_ref, bf16[1536,6144]{1,0:T(8,128)(2,1)} %weight_ref.20, bf16[256,3072]{1,0:T(8,128)(2,1)S(1)} %collective-permute-done.20.refs_1_.arrived_ref), custom_call_target="tpu_custom_call" | custom-call | flops 1 | bytes 1 | tf_op jit(solution)/shard_map/pallas_call | solution.py:221
  91.1 4.0 %shard_map.189 = bf16[256,1152]{1,0:T(8,128)(2,1)S(1)} custom-call(s32[2]{0:T(128)S(1)} %pad_add_fusion.pos, bf16[256,1536]{1,0:T(8,128)(2,1)S(1)} %pad_maximum_fusion.1.tokens_ref, bf16[1536,1536]{1,0:T(8,128)(2,1)} %refs_0_.25, bf16[1536,1536]{1,0:T(8,128)(2,1)} %refs_1_.17, bf16[1536,1536]{1,0:T(8,128)(2,1)} %refs_2_.17, ...), custom_call_target="tpu_custom_call" | custom-call | flops 1 | bytes 1 | tf_op jit(solution)/shard_map/pallas_call | solution.py:221
  95.1 4.3 %shard_map.190.refs_1_ = f32[256,1536]{1,0:T(8,128)S(1)} custom-call(s32[2]{0:T(128)S(1)} %pad_add_fusion.pos, bf16[1536,1536]{1,0:T(8,128)(2,1)} %weight_ref.21, bf16[256,384]{1,0:T(8,128)(2,1)S(1)} %shard_map.187.refs_0_, bf16[256,384]{1,0:T(8,128)(2,1)S(1)} %collective-permute-done.18.refs_1_, bf16[256,384]{1,0:T(8,128)(2,1)S(1)} %collective-permute-done.17.refs_2_), custom_call_target="tpu_custom_call" | custom-call | flops 1 | bytes 1 | tf_op jit(solution)/shard_map/pallas_call | solution.py:221
  99.4 4.2 %shard_map.191.refs_1_ = f32[256,1536]{1,0:T(8,128)S(1)} custom-call(s32[2]{0:T(128)S(1)} %pad_add_fusion.pos, bf16[6144,1536]{1,0:T(8,128)(2,1)} %weight_ref.24, bf16[256,1536]{1,0:T(8,128)(2,1)S(1)} %shard_map.188.refs_0_, f32[256,1536]{1,0:T(8,128)S(1)} %shard_map.190.refs_1_), custom_call_target="tpu_custom_call" | custom-call | flops 1 | bytes 1 | tf_op jit(solution)/shard_map/pallas_call | solution.py:221
  108.0 8.3 %shard_map.194 = f32[256,1536]{1,0:T(8,128)S(1)} custom-call(s32[2]{0:T(128)S(1)} %pad_add_fusion.pos, bf16[6144,1536]{1,0:T(8,128)(2,1)} %weight_ref.24, bf16[256,1536]{1,0:T(8,128)(2,1)S(1)} %collective-permute-done.23.refs_0_, bf16[256,1536]{1,0:T(8,128)(2,1)S(1)} %collective-permute-done.22.refs_1_, ...), custom_call_target="tpu_custom_call" | custom-call | flops 1 | bytes 1 | tf_op jit(solution)/shard_map/pallas_call | solution.py:221
  116.3 4.3 %collective-permute-done.25.refs_6_ = bf16[256,1152]{1,0:T(8,128)(2,1)S(1)} collective-permute-done((bf16[256,1152]{1,0:T(8,128)(2,1)S(1)}, bf16[256,1152]{1,0:T(8,128)(2,1)S(1)}, u32[]{:S(2)}, u32[]{:S(2)}) %collective-permute-start.25) | collective-permute-done | bytes 589856 | tf_op jit(solution)/shard_map/ppermute | solution.py:200
  121.5 4.4 %shard_map.195.refs_0_ = bf16[256,384]{1,0:T(8,128)(2,1)S(1)} custom-call(s32[2]{0:T(128)S(1)} %pad_add_fusion.pos, bf16[256,1536]{1,0:T(8,128)(2,1)S(1)} %pad_maximum_fusion.1.tokens_ref, bf16[1536,1536]{1,0:T(8,128)(2,1)} %refs_0_.25, bf16[1536,1536]{1,0:T(8,128)(2,1)} %refs_1_.17, bf16[1536,1536]{1,0:T(8,128)(2,1)} %refs_2_.17, ...), custom_call_target="tpu_custom_call" | custom-call | flops 1 | bytes 1 | tf_op jit(solution)/shard_map/pallas_call | solution.py:221
  163.1 4.2 %shard_map.200.refs_2_ = f32[256,1536]{1,0:T(8,128)S(1)} custom-call(s32[2]{0:T(128)S(1)} %pad_add_fusion.pos, bf16[6144,1536]{1,0:T(8,128)(2,1)} %weight_ref.24, bf16[128,1536]{1,0:T(8,128)(2,1)S(1)} %shard_map.196.refs_0_, bf16[128,1536]{1,0:T(8,128)(2,1)S(1)} %shard_map.198.refs_1_, f32[256,1536]{1,0:T(8,128)S(1)} %shard_map.199.refs_2_), custom_call_target="tpu_custom_call" | custom-call | flops 1 | bytes 1 | tf_op jit(solution)/shard_map/pallas_call | solution.py:221
  173.2 4.2 %shard_map.201.refs_4_ = f32[256,1536]{1,0:T(8,128)S(1)} custom-call(s32[2]{0:T(128)S(1)} %pad_add_fusion.pos, bf16[6144,1536]{1,0:T(8,128)(2,1)} %weight_ref.24, bf16[128,1536]{1,0:T(8,128)(2,1)S(1)} %collective-permute-done.38.refs_0_, bf16[128,1536]{1,0:T(8,128)(2,1)S(1)} %collective-permute-done.39.refs_1_, f32[256,1536]{1,0:T(8,128)S(1)} %shard_map.200.refs_2_), custom_call_target="tpu_custom_call" | custom-call | flops 1 | bytes 1 | tf_op jit(solution)/shard_map/pallas_call | solution.py:221
  178.1 6.2 %shard_map.202 = f32[256,1536]{1,0:T(8,128)S(1)} custom-call(s32[2]{0:T(128)S(1)} %pad_add_fusion.pos, bf16[6144,1536]{1,0:T(8,128)(2,1)} %weight_ref.24, bf16[128,1536]{1,0:T(8,128)(2,1)S(1)} %collective-permute-done.33.refs_0_, bf16[128,1536]{1,0:T(8,128)(2,1)S(1)} %collective-permute-done.40.refs_1_, ...), custom_call_target="tpu_custom_call" | custom-call | flops 1 | bytes 1 | tf_op jit(solution)/shard_map/pallas_call | solution.py:221
  186.4 7.8 %collective-permute-done.46 = bf16[64,1536]{1,0:T(8,128)(2,1)S(1)} collective-permute-done((bf16[64,1536]{1,0:T(8,128)(2,1)S(1)}, bf16[64,1536]{1,0:T(8,128)(2,1)S(1)}, u32[]{:S(2)}, u32[]{:S(2)}) %collective-permute-start.46) | collective-permute-done | bytes 196640 | tf_op jit(solution)/shard_map/ppermute | solution.py:213
  194.3 3.9 %collective-permute-start.48 = (bf16[64,1536]{1,0:T(8,128)(2,1)S(1)}, bf16[64,1536]{1,0:T(8,128)(2,1)S(1)}, u32[]{:S(2)}, u32[]{:S(2)}) collective-permute-start(bf16[64,1536]{1,0:T(8,128)(2,1)S(1)} %get-tuple-element.320), channel_id=1, source_target_pairs={{0,3},{1,0},{2,1},{3,2},{4,7},{5,4},{6,5},{7,6},{8,11},{9,8},{10,9... | collective-permute-start | bytes 589832 | tf_op jit(solution)/shard_map/ppermute | solution.py:213
  198.2 5.5 %shard_map.203 = bf16[256,2304]{1,0:T(8,128)(2,1)S(1)} custom-call(s32[2]{0:T(128)S(1)} %pad_add_fusion.pos, bf16[256,1536]{1,0:T(8,128)(2,1)S(1)} %constant_dynamic-update-slice_fusion.tokens_ref, bf16[1536,1536]{1,0:T(8,128)(2,1)} %refs_0_.31, bf16[1536,1536]{1,0:T(8,128)(2,1)} %refs_1_.23, bf16[1536,1536]{1,0:T(8,128)(2,1)} %refs_2_.23), custom_call_target="tpu_custom_call" | custom-call | flops 1 | bytes 1 | tf_op jit(solution)/shard_map/pallas_call | solution.py:221
  209.8 4.0 %shard_map.204 = (bf16[128,1152]{1,0:T(8,128)(2,1)S(1)}, bf16[128,1152]{1,0:T(8,128)(2,1)S(1)}) custom-call(s32[2]{0:T(128)S(1)} %pad_add_fusion.pos, bf16[256,1536]{1,0:T(8,128)(2,1)S(1)} %constant_dynamic-update-slice_fusion.tokens_ref, bf16[1536,1536]{1,0:T(8,128)(2,1)} %refs_0_.31, bf16[1536,1536]{1,0:T(8,128)(2,1)} %refs_1_.23, ...), custom_call_target="tpu_custom_call" | custom-call | flops 1 | bytes 1 | tf_op jit(solution)/shard_map/pallas_call | solution.py:221
  227.7 5.7 %shard_map.205 = bf16[256,2304]{1,0:T(8,128)(2,1)S(1)} custom-call(s32[2]{0:T(128)S(1)} %pad_add_fusion.pos, bf16[256,1536]{1,0:T(8,128)(2,1)S(1)} %pad_maximum_fusion.2.tokens_ref, bf16[1536,1536]{1,0:T(8,128)(2,1)} %refs_0_.31, bf16[1536,1536]{1,0:T(8,128)(2,1)} %refs_1_.23, bf16[1536,1536]{1,0:T(8,128)(2,1)} %refs_2_.23), custom_call_target="tpu_custom_call" | custom-call | flops 1 | bytes 1 | tf_op jit(solution)/shard_map/pallas_call | solution.py:221
  236.4 4.0 %shard_map.206 = bf16[256,1152]{1,0:T(8,128)(2,1)S(1)} custom-call(s32[2]{0:T(128)S(1)} %pad_add_fusion.pos, bf16[256,1536]{1,0:T(8,128)(2,1)S(1)} %pad_maximum_fusion.2.tokens_ref, bf16[1536,1536]{1,0:T(8,128)(2,1)} %refs_0_.31, bf16[1536,1536]{1,0:T(8,128)(2,1)} %refs_1_.23, bf16[1536,1536]{1,0:T(8,128)(2,1)} %refs_2_.23, ...), custom_call_target="tpu_custom_call" | custom-call | flops 1 | bytes 1 | tf_op jit(solution)/shard_map/pallas_call | solution.py:221
  244.1 4.0 %shard_map.208.refs_3_.refs_4_.refs_5_ = f32[256,1152]{1,0:T(8,128)S(1)} custom-call(s32[2]{0:T(128)S(1)} %pad_add_fusion.pos, bf16[256,1536]{1,0:T(8,128)(2,1)S(1)} %pad_maximum_fusion.2.tokens_ref, bf16[1536,1536]{1,0:T(8,128)(2,1)} %refs_0_.31, bf16[1536,1536]{1,0:T(8,128)(2,1)} %refs_1_.23, bf16[1536,1536]{1,0:T(8,128)(2,1)} %refs_2_.23, ...), custom_call_target="tpu_custom_call" | custom-call | flops 1 | bytes 1 | tf_op jit(solution)/shard_map/pallas_call | solution.py:221
  248.1 4.0 %shard_map.207.refs_0_.refs_1_.refs_2_ = bf16[256,1152]{1,0:T(8,128)(2,1)S(1)} custom-call(s32[2]{0:T(128)S(1)} %pad_add_fusion.pos, bf16[256,1536]{1,0:T(8,128)(2,1)S(1)} %constant_dynamic-update-slice_fusion.tokens_ref, bf16[1536,1536]{1,0:T(8,128)(2,1)} %refs_0_.31, bf16[1536,1536]{1,0:T(8,128)(2,1)} %refs_1_.23, bf16[1536,1536]{1,0:T(8,128)(2,1)} %refs_2_.23, ...), custom_call_target="tpu_custom_call" | custom-call | flops 1 | bytes 1 | tf_op jit(solution)/shard_map/pallas_call | solution.py:221
  252.2 5.7 %collective-permute-done.62.refs_6_.refs_7_.refs_8_ = bf16[256,1152]{1,0:T(8,128)(2,1)S(1)} collective-permute-done((bf16[256,1152]{1,0:T(8,128)(2,1)S(1)}, bf16[256,1152]{1,0:T(8,128)(2,1)S(1)}, u32[]{:S(2)}, u32[]{:S(2)}) %collective-permute-start.62) | collective-permute-done | bytes 589856 | tf_op jit(solution)/shard_map/ppermute | solution.py:200
  262.7 8.7 %collective-permute-done.64.refs_2_ = bf16[512,384]{1,0:T(8,128)(2,1)S(1)} collective-permute-done((bf16[512,384]{1,0:T(8,128)(2,1)S(1)}, bf16[512,384]{1,0:T(8,128)(2,1)S(1)}, u32[]{:S(2)}, u32[]{:S(2)}) %collective-permute-start.64) | collective-permute-done | bytes 393248 | tf_op jit(solution)/shard_map/ppermute | solution.py:200
  273.1 6.2 %shard_map.210 = f32[512,1536]{1,0:T(8,128)S(1)} custom-call(s32[2]{0:T(128)S(1)} %pad_add_fusion.pos, bf16[1536,1536]{1,0:T(8,128)(2,1)} %weight_ref.25, bf16[512,384]{1,0:T(8,128)(2,1)S(1)} %bitcast.145, bf16[512,384]{1,0:T(8,128)(2,1)S(1)} %collective-permute-done.63.refs_1_, bf16[512,384]{1,0:T(8,128)(2,1)S(1)} %collective-permute-done.64.refs_2_, ...), custom_call_target="tpu_custom_call" | custom-call | flops 1 | bytes 1 | tf_op jit(solution)/shard_map/pallas_call | solution.py:221
  283.5 3.8 %collective-permute-start.69 = (bf16[64,1536]{1,0:T(8,128)(2,1)S(1)}, bf16[64,1536]{1,0:T(8,128)(2,1)S(1)}, u32[]{:S(2)}, u32[]{:S(2)}) collective-permute-start(bf16[64,1536]{1,0:T(8,128)(2,1)S(1)} %get-tuple-element.371), channel_id=1, source_target_pairs={{0,3},{1,0},{2,1},{3,2},{4,7},{5,4},{6,5},{7,6},{8,11},{9,8},{10,9... | collective-permute-start | bytes 589832 | tf_op jit(solution)/shard_map/ppermute | solution.py:213
  300.1 6.1 %collective-permute-done.67 = bf16[64,1536]{1,0:T(8,128)(2,1)S(1)} collective-permute-done((bf16[64,1536]{1,0:T(8,128)(2,1)S(1)}, bf16[64,1536]{1,0:T(8,128)(2,1)S(1)}, u32[]{:S(2)}, u32[]{:S(2)}) %collective-permute-start.67) | collective-permute-done | bytes 196640 | tf_op jit(solution)/shard_map/ppermute | solution.py:213
  (212 shorter events, 147.4 us)
Async XLA Ops:
  1.1 11.2 %collective-permute-start = (bf16[64,1536]{1,0:T(8,128)(2,1)S(1)}, bf16[64,1536]{1,0:T(8,128)(2,1)S(1)}, u32[]{:S(2)}, u32[]{:S(2)}) collective-permute-start(bf16[64,1536]{1,0:T(8,128)(2,1)S(1)} %get-tuple-element.191), channel_id=1, source_target_pairs={{0,1},{1,2},{2,3},{3,0},{4,5},{5,6},{6,7},{7,4},{8,9},{9,10},{10,1... | collective-permute-start | bytes 589832 | tf_op jit(solution)/shard_map/ppermute | solution.py:213
  4.1 10.6 %collective-permute-start.1 = (bf16[64,1536]{1,0:T(8,128)(2,1)S(1)}, bf16[64,1536]{1,0:T(8,128)(2,1)S(1)}, u32[]{:S(2)}, u32[]{:S(2)}) collective-permute-start(bf16[64,1536]{1,0:T(8,128)(2,1)S(1)} %get-tuple-element.191), channel_id=1, source_target_pairs={{0,3},{1,0},{2,1},{3,2},{4,7},{5,4},{6,5},{7,6},{8,11},{9,8},{10,9... | collective-permute-start | bytes 589832 | tf_op jit(solution)/shard_map/ppermute | solution.py:213
  48.4 11.2 %collective-permute-start.14 = (bf16[128,1152]{1,0:T(8,128)(2,1)S(1)}, bf16[128,1152]{1,0:T(8,128)(2,1)S(1)}, u32[]{:S(2)}, u32[]{:S(2)}) collective-permute-start(bf16[128,1152]{1,0:T(8,128)(2,1)S(1)} %get-tuple-element.217), channel_id=1, source_target_pairs={{0,8},{4,12},{8,0},{12,4},{1,9},{5,13},{9,1},{13,5},{2,10},{6,14},... | collective-permute-start | bytes 884744 | tf_op jit(solution)/shard_map/ppermute | solution.py:200
  49.9 9.7 %collective-permute-start.15 = (bf16[64,1536]{1,0:T(8,128)(2,1)S(1)}, bf16[64,1536]{1,0:T(8,128)(2,1)S(1)}, u32[]{:S(2)}, u32[]{:S(2)}) collective-permute-start(bf16[64,1536]{1,0:T(8,128)(2,1)S(1)} %collective-permute-done.9), channel_id=1, source_target_pairs={{0,1},{1,2},{2,3},{3,0},{4,5},{5,6},{6,7},{7,4},{8,9},{9,10},{10,1... | collective-permute-start | bytes 589832 | tf_op jit(solution)/shard_map/ppermute | solution.py:213
  59.6 19.2 %collective-permute-start.16 = (bf16[256,1536]{1,0:T(8,128)(2,1)S(1)}, bf16[256,1536]{1,0:T(8,128)(2,1)S(1)}, u32[]{:S(2)}, u32[]{:S(2)}) collective-permute-start(bf16[256,1536]{1,0:T(8,128)(2,1)S(1)} %shard_map.184), channel_id=1, source_target_pairs={{0,8},{4,12},{8,0},{12,4},{1,9},{5,13},{9,1},{13,5},{2,10},{6,14},... | collective-permute-start | bytes 2359304 | tf_op jit(solution)/shard_map/ppermute | solution.py:200
  86.1 18.7 %collective-permute-start.22 = (bf16[256,1536]{1,0:T(8,128)(2,1)S(1)}, bf16[256,1536]{1,0:T(8,128)(2,1)S(1)}, u32[]{:S(2)}, u32[]{:S(2)}) collective-permute-start(bf16[256,1536]{1,0:T(8,128)(2,1)S(1)} %shard_map.188.refs_0_), channel_id=1, source_target_pairs={{0,8},{4,12},{8,0},{12,4},{1,9},{5,13},{9,1},{13,5},{2,10},{6,14},... | collective-permute-start | bytes 2359304 | tf_op jit(solution)/shard_map/ppermute | solution.py:200
  86.7 18.1 %collective-permute-start.23 = (bf16[256,1536]{1,0:T(8,128)(2,1)S(1)}, bf16[256,1536]{1,0:T(8,128)(2,1)S(1)}, u32[]{:S(2)}, u32[]{:S(2)}) collective-permute-start(bf16[256,1536]{1,0:T(8,128)(2,1)S(1)} %shard_map.188.refs_0_), channel_id=1, source_target_pairs={{0,4},{4,0},{8,12},{12,8},{1,5},{5,1},{9,13},{13,9},{2,6},{6,2},{1... | collective-permute-start | bytes 2359304 | tf_op jit(solution)/shard_map/ppermute | solution.py:200
  86.7 16.9 %collective-permute-start.21 = (bf16[256,384]{1,0:T(8,128)(2,1)S(1)}, bf16[256,384]{1,0:T(8,128)(2,1)S(1)}, u32[]{:S(2)}, u32[]{:S(2)}) collective-permute-start(bf16[256,384]{1,0:T(8,128)(2,1)S(1)} %collective-permute-done.17.refs_2_), channel_id=1, source_target_pairs={{0,4},{4,0},{8,12},{12,8},{1,5},{5,1},{9,13},{13,9},{2,6},{6,2},{1... | collective-permute-start | bytes 589832 | tf_op jit(solution)/shard_map/ppermute | solution.py:200
  104.8 15.7 %collective-permute-start.25 = (bf16[256,1152]{1,0:T(8,128)(2,1)S(1)}, bf16[256,1152]{1,0:T(8,128)(2,1)S(1)}, u32[]{:S(2)}, u32[]{:S(2)}) collective-permute-start(bf16[256,1152]{1,0:T(8,128)(2,1)S(1)} %shard_map.189), channel_id=1, source_target_pairs={{0,8},{4,12},{8,0},{12,4},{1,9},{5,13},{9,1},{13,5},{2,10},{6,14},... | collective-permute-start | bytes 1769480 | tf_op jit(solution)/shard_map/ppermute | solution.py:200
  120.7 10.8 %collective-permute-start.26 = (bf16[128,1536]{1,0:T(8,128)(2,1)S(1)}, bf16[128,1536]{1,0:T(8,128)(2,1)S(1)}, u32[]{:S(2)}, u32[]{:S(2)}) collective-permute-start(bf16[128,1536]{1,0:T(8,128)(2,1)S(1)} %get-tuple-element.259), channel_id=1, source_target_pairs={{0,8},{4,12},{8,0},{12,4},{1,9},{5,13},{9,1},{13,5},{2,10},{6,14},... | collective-permute-start | bytes 1179656 | tf_op jit(solution)/shard_map/ppermute | solution.py:200
  131.5 12.6 %collective-permute-start.29 = (bf16[256,384]{1,0:T(8,128)(2,1)S(1)}, bf16[256,384]{1,0:T(8,128)(2,1)S(1)}, u32[]{:S(2)}, u32[]{:S(2)}) collective-permute-start(bf16[256,384]{1,0:T(8,128)(2,1)S(1)} %shard_map.195.refs_0_), channel_id=1, source_target_pairs={{0,8},{4,12},{8,0},{12,4},{1,9},{5,13},{9,1},{13,5},{2,10},{6,14},... | collective-permute-start | bytes 589832 | tf_op jit(solution)/shard_map/ppermute | solution.py:200
  132.2 15.0 %collective-permute-start.28 = (bf16[128,1536]{1,0:T(8,128)(2,1)S(1)}, bf16[128,1536]{1,0:T(8,128)(2,1)S(1)}, u32[]{:S(2)}, u32[]{:S(2)}) collective-permute-start(bf16[128,1536]{1,0:T(8,128)(2,1)S(1)} %get-tuple-element.266), channel_id=1, source_target_pairs={{0,8},{4,12},{8,0},{12,4},{1,9},{5,13},{9,1},{13,5},{2,10},{6,14},... | collective-permute-start | bytes 1179656 | tf_op jit(solution)/shard_map/ppermute | solution.py:200
  133.5 10.5 %collective-permute-start.31 = (bf16[64,1536]{1,0:T(8,128)(2,1)S(1)}, bf16[64,1536]{1,0:T(8,128)(2,1)S(1)}, u32[]{:S(2)}, u32[]{:S(2)}) collective-permute-start(bf16[64,1536]{1,0:T(8,128)(2,1)S(1)} %add_convert_fusion.1), channel_id=1, source_target_pairs={{0,1},{1,2},{2,3},{3,0},{4,5},{5,6},{6,7},{7,4},{8,9},{9,10},{10,1... | collective-permute-start | bytes 589832 | tf_op jit(solution)/shard_map/ppermute | solution.py:213
  133.7 12.3 %collective-permute-start.32 = (bf16[64,1536]{1,0:T(8,128)(2,1)S(1)}, bf16[64,1536]{1,0:T(8,128)(2,1)S(1)}, u32[]{:S(2)}, u32[]{:S(2)}) collective-permute-start(bf16[64,1536]{1,0:T(8,128)(2,1)S(1)} %get-tuple-element.272), channel_id=1, source_target_pairs={{0,3},{1,0},{2,1},{3,2},{4,7},{5,4},{6,5},{7,6},{8,11},{9,8},{10,9... | collective-permute-start | bytes 589832 | tf_op jit(solution)/shard_map/ppermute | solution.py:213
  147.2 10.8 %collective-permute-start.33 = (bf16[128,1536]{1,0:T(8,128)(2,1)S(1)}, bf16[128,1536]{1,0:T(8,128)(2,1)S(1)}, u32[]{:S(2)}, u32[]{:S(2)}) collective-permute-start(bf16[128,1536]{1,0:T(8,128)(2,1)S(1)} %shard_map.196.refs_0_), channel_id=1, source_target_pairs={{0,8},{4,12},{8,0},{12,4},{1,9},{5,13},{9,1},{13,5},{2,10},{6,14},... | collective-permute-start | bytes 1179656 | tf_op jit(solution)/shard_map/ppermute | solution.py:200
  158.1 14.6 %collective-permute-start.39 = (bf16[128,1536]{1,0:T(8,128)(2,1)S(1)}, bf16[128,1536]{1,0:T(8,128)(2,1)S(1)}, u32[]{:S(2)}, u32[]{:S(2)}) collective-permute-start(bf16[128,1536]{1,0:T(8,128)(2,1)S(1)} %shard_map.198.refs_1_), channel_id=1, source_target_pairs={{0,4},{4,0},{8,12},{12,8},{1,5},{5,1},{9,13},{13,9},{2,6},{6,2},{1... | collective-permute-start | bytes 1179656 | tf_op jit(solution)/shard_map/ppermute | solution.py:200
  158.2 14.5 %collective-permute-start.40 = (bf16[128,1536]{1,0:T(8,128)(2,1)S(1)}, bf16[128,1536]{1,0:T(8,128)(2,1)S(1)}, u32[]{:S(2)}, u32[]{:S(2)}) collective-permute-start(bf16[128,1536]{1,0:T(8,128)(2,1)S(1)} %shard_map.198.refs_1_), channel_id=1, source_target_pairs={{0,8},{4,12},{8,0},{12,4},{1,9},{5,13},{9,1},{13,5},{2,10},{6,14},... | collective-permute-start | bytes 1179656 | tf_op jit(solution)/shard_map/ppermute | solution.py:200
  159.1 13.5 %collective-permute-start.38 = (bf16[128,1536]{1,0:T(8,128)(2,1)S(1)}, bf16[128,1536]{1,0:T(8,128)(2,1)S(1)}, u32[]{:S(2)}, u32[]{:S(2)}) collective-permute-start(bf16[128,1536]{1,0:T(8,128)(2,1)S(1)} %shard_map.196.refs_0_), channel_id=1, source_target_pairs={{0,4},{4,0},{8,12},{12,8},{1,5},{5,1},{9,13},{13,9},{2,6},{6,2},{1... | collective-permute-start | bytes 1179656 | tf_op jit(solution)/shard_map/ppermute | solution.py:200
  159.3 9.6 %collective-permute-start.41 = (bf16[64,1536]{1,0:T(8,128)(2,1)S(1)}, bf16[64,1536]{1,0:T(8,128)(2,1)S(1)}, u32[]{:S(2)}, u32[]{:S(2)}) collective-permute-start(bf16[64,1536]{1,0:T(8,128)(2,1)S(1)} %multiply_convert_fusion.4), channel_id=1, source_target_pairs={{0,1},{1,2},{2,3},{3,0},{4,5},{5,6},{6,7},{7,4},{8,9},{9,10},{10,1... | collective-permute-start | bytes 589832 | tf_op jit(solution)/shard_map/ppermute | solution.py:213
  160.0 12.7 %collective-permute-start.42 = (bf16[64,1536]{1,0:T(8,128)(2,1)S(1)}, bf16[64,1536]{1,0:T(8,128)(2,1)S(1)}, u32[]{:S(2)}, u32[]{:S(2)}) collective-permute-start(bf16[64,1536]{1,0:T(8,128)(2,1)S(1)} %multiply_convert_fusion.4), channel_id=1, source_target_pairs={{0,3},{1,0},{2,1},{3,2},{4,7},{5,4},{6,5},{7,6},{8,11},{9,8},{10,9... | collective-permute-start | bytes 589832 | tf_op jit(solution)/shard_map/ppermute | solution.py:213
  204.1 9.8 %collective-permute-start.50 = (bf16[64,1536]{1,0:T(8,128)(2,1)S(1)}, bf16[64,1536]{1,0:T(8,128)(2,1)S(1)}, u32[]{:S(2)}, u32[]{:S(2)}) collective-permute-start(bf16[64,1536]{1,0:T(8,128)(2,1)S(1)} %get-tuple-element.339), channel_id=1, source_target_pairs={{0,1},{1,2},{2,3},{3,0},{4,5},{5,6},{6,7},{7,4},{8,9},{9,10},{10,1... | collective-permute-start | bytes 589832 | tf_op jit(solution)/shard_map/ppermute | solution.py:213
  204.2 12.2 %collective-permute-start.51 = (bf16[64,1536]{1,0:T(8,128)(2,1)S(1)}, bf16[64,1536]{1,0:T(8,128)(2,1)S(1)}, u32[]{:S(2)}, u32[]{:S(2)}) collective-permute-start(bf16[64,1536]{1,0:T(8,128)(2,1)S(1)} %get-tuple-element.339), channel_id=1, source_target_pairs={{0,3},{1,0},{2,1},{3,2},{4,7},{5,4},{6,5},{7,6},{8,11},{9,8},{10,9... | collective-permute-start | bytes 589832 | tf_op jit(solution)/shard_map/ppermute | solution.py:213
  216.4 10.9 %collective-permute-start.55 = (bf16[128,1152]{1,0:T(8,128)(2,1)S(1)}, bf16[128,1152]{1,0:T(8,128)(2,1)S(1)}, u32[]{:S(2)}, u32[]{:S(2)}) collective-permute-start(bf16[128,1152]{1,0:T(8,128)(2,1)S(1)} %get-tuple-element.330), channel_id=1, source_target_pairs={{0,8},{4,12},{8,0},{12,4},{1,9},{5,13},{9,1},{13,5},{2,10},{6,14},... | collective-permute-start | bytes 884744 | tf_op jit(solution)/shard_map/ppermute | solution.py:200
  217.3 10.0 %collective-permute-start.56 = (bf16[64,1536]{1,0:T(8,128)(2,1)S(1)}, bf16[64,1536]{1,0:T(8,128)(2,1)S(1)}, u32[]{:S(2)}, u32[]{:S(2)}) collective-permute-start(bf16[64,1536]{1,0:T(8,128)(2,1)S(1)} %collective-permute-done.50), channel_id=1, source_target_pairs={{0,1},{1,2},{2,3},{3,0},{4,5},{5,6},{6,7},{7,4},{8,9},{9,10},{10,1... | collective-permute-start | bytes 589832 | tf_op jit(solution)/shard_map/ppermute | solution.py:213
  243.0 14.9 %collective-permute-start.62 = (bf16[256,1152]{1,0:T(8,128)(2,1)S(1)}, bf16[256,1152]{1,0:T(8,128)(2,1)S(1)}, u32[]{:S(2)}, u32[]{:S(2)}) collective-permute-start(bf16[256,1152]{1,0:T(8,128)(2,1)S(1)} %shard_map.206), channel_id=1, source_target_pairs={{0,8},{4,12},{8,0},{12,4},{1,9},{5,13},{9,1},{13,5},{2,10},{6,14},... | collective-permute-start | bytes 1769480 | tf_op jit(solution)/shard_map/ppermute | solution.py:200
  261.6 9.9 %collective-permute-start.64 = (bf16[512,384]{1,0:T(8,128)(2,1)S(1)}, bf16[512,384]{1,0:T(8,128)(2,1)S(1)}, u32[]{:S(2)}, u32[]{:S(2)}) collective-permute-start(bf16[512,384]{1,0:T(8,128)(2,1)S(1)} %bitcast.143), channel_id=1, source_target_pairs={{0,8},{4,12},{8,0},{12,4},{1,9},{5,13},{9,1},{13,5},{2,10},{6,14},... | collective-permute-start | bytes 1179656 | tf_op jit(solution)/shard_map/ppermute | solution.py:200
  279.6 9.6 %collective-permute-start.66 = (bf16[64,1536]{1,0:T(8,128)(2,1)S(1)}, bf16[64,1536]{1,0:T(8,128)(2,1)S(1)}, u32[]{:S(2)}, u32[]{:S(2)}) collective-permute-start(bf16[64,1536]{1,0:T(8,128)(2,1)S(1)} %get-tuple-element.374), channel_id=1, source_target_pairs={{0,1},{1,2},{2,3},{3,0},{4,5},{5,6},{6,7},{7,4},{8,9},{9,10},{10,1... | collective-permute-start | bytes 589832 | tf_op jit(solution)/shard_map/ppermute | solution.py:213
  279.7 12.0 %collective-permute-start.70 = (bf16[64,1536]{1,0:T(8,128)(2,1)S(1)}, bf16[64,1536]{1,0:T(8,128)(2,1)S(1)}, u32[]{:S(2)}, u32[]{:S(2)}) collective-permute-start(bf16[64,1536]{1,0:T(8,128)(2,1)S(1)} %get-tuple-element.372), channel_id=1, source_target_pairs={{0,3},{1,0},{2,1},{3,2},{4,7},{5,4},{6,5},{7,6},{8,11},{9,8},{10,9... | collective-permute-start | bytes 589832 | tf_op jit(solution)/shard_map/ppermute | solution.py:213
  283.5 14.2 %collective-permute-start.68 = (bf16[64,1536]{1,0:T(8,128)(2,1)S(1)}, bf16[64,1536]{1,0:T(8,128)(2,1)S(1)}, u32[]{:S(2)}, u32[]{:S(2)}) collective-permute-start(bf16[64,1536]{1,0:T(8,128)(2,1)S(1)} %get-tuple-element.373), channel_id=1, source_target_pairs={{0,1},{1,2},{2,3},{3,0},{4,5},{5,6},{6,7},{7,4},{8,9},{9,10},{10,1... | collective-permute-start | bytes 589832 | tf_op jit(solution)/shard_map/ppermute | solution.py:213
  283.5 16.6 %collective-permute-start.69 = (bf16[64,1536]{1,0:T(8,128)(2,1)S(1)}, bf16[64,1536]{1,0:T(8,128)(2,1)S(1)}, u32[]{:S(2)}, u32[]{:S(2)}) collective-permute-start(bf16[64,1536]{1,0:T(8,128)(2,1)S(1)} %get-tuple-element.371), channel_id=1, source_target_pairs={{0,3},{1,0},{2,1},{3,2},{4,7},{5,4},{6,5},{7,6},{8,11},{9,8},{10,9... | collective-permute-start | bytes 589832 | tf_op jit(solution)/shard_map/ppermute | solution.py:213
  291.8 14.4 %collective-permute-start.67 = (bf16[64,1536]{1,0:T(8,128)(2,1)S(1)}, bf16[64,1536]{1,0:T(8,128)(2,1)S(1)}, u32[]{:S(2)}, u32[]{:S(2)}) collective-permute-start(bf16[64,1536]{1,0:T(8,128)(2,1)S(1)} %get-tuple-element.370), channel_id=1, source_target_pairs={{0,1},{1,2},{2,3},{3,0},{4,5},{5,6},{6,7},{7,4},{8,9},{9,10},{10,1... | collective-permute-start | bytes 589832 | tf_op jit(solution)/shard_map/ppermute | solution.py:213
  292.4 15.4 %collective-permute-start.71 = (bf16[64,1536]{1,0:T(8,128)(2,1)S(1)}, bf16[64,1536]{1,0:T(8,128)(2,1)S(1)}, u32[]{:S(2)}, u32[]{:S(2)}) collective-permute-start(bf16[64,1536]{1,0:T(8,128)(2,1)S(1)} %get-tuple-element.369), channel_id=1, source_target_pairs={{0,3},{1,0},{2,1},{3,2},{4,7},{5,4},{6,5},{7,6},{8,11},{9,8},{10,9... | collective-permute-start | bytes 589832 | tf_op jit(solution)/shard_map/ppermute | solution.py:213
  (49 other events, 327.9 us)

commit v9 on v8

--- a/solution.py
+++ b/solution.py
@@ -730,33 +730,34 @@
 
     mine_b, before_b, after_b, away_b = jnp.split(mixed_b, 4)
     to_after = sent(away_b, 1)
-    mine_b, before_b, after_b, to_after, join_a, ja_before, ja_after, ja_away = sync(
-        mine_b, before_b, after_b, to_after, join_a, ja_before, ja_after, ja_away
-    )
-
-    from_before = sent(after_b + to_after.astype(jnp.float32), 1)
-    from_after = sent(before_b, -1)
     tok_ja = jnp.concatenate((join_a, ja_before, ja_after, ja_away))
     js_a = heads_send(tok_ja, join_in)
-    tok_ja, js_a, mine_b, *arrived = sync(tok_ja, js_a, mine_b, from_before, from_after)
+    mine_b, before_b, after_b, to_after, tok_ja, js_a = sync(
+        mine_b, before_b, after_b, to_after, tok_ja, js_a
+    )
+
+    from_before = sent(after_b + to_after.astype(jnp.float32), 1)
+    from_after, jc_a = sent(before_b, -1), core_swap(js_a)
+    jx_a = heads_across(tok_ja, join_in, jc_a, 2)
+    tok_ja, jc_a, jx_a0, jx_a1, mine_b, *arrived = sync(
+        tok_ja, jc_a, *jx_a, mine_b, from_before, from_after
+    )
 
     layer_b = layer_end(start_f32[half:], mine_b, *arrived)
-    pairs = moment_flips(moment_pair(layer_b.astype(jnp.float32)))
-    jb_before, jb_after, jc_a = sent(layer_b, 1), sent(layer_b, -1), core_swap(js_a)
-    jx_a = heads_across(tok_ja, join_in, jc_a, 2)
-    tok_ja, jc_a, jx_a0, jx_a1, layer_b, jb_before, jb_after, *pairs = sync(
-        tok_ja, jc_a, *jx_a, layer_b, jb_before, jb_after, *pairs
-    )
-
-    totals = moment_shards(moment_sum(pairs))
-
+    pair = moment_pair(layer_b.astype(jnp.float32))
+    pair = pair + flip(pair, 1)
+    jb_before, jb_after, jy_a0 = sent(layer_b, 1), sent(layer_b, -1), y_swap(jx_a0)
+    tok_ja, jc_a, jy_a0, jx_a1, layer_b, jb_before, jb_after, *pairs = sync(
+        tok_ja, jc_a, jy_a0, jx_a1, layer_b, jb_before, jb_after, pair, flip(pair, 2)
+    )
+
+    totals = moment_shards(pairs[0] + pairs[1])
     jb_away = sent(jb_before, 1)
-    jy_a0 = y_swap(jx_a0)
-    tok_ja, jc_a, jy_a0, jx_a1, layer_b, jb_before, jb_after, jb_away, *totals = sync(
-        tok_ja, jc_a, jy_a0, jx_a1, layer_b, jb_before, jb_after, jb_away, *totals
-    )
-
     jy_a1 = y_swap(jx_a1)
+    tok_ja, jc_a, jy_a0, jy_a1, layer_b, jb_before, jb_after, jb_away, *totals = sync(
+        tok_ja, jc_a, jy_a0, jy_a1, layer_b, jb_before, jb_after, jb_away, *totals
+    )
+
     tok_jb = normed_shards((layer_b, jb_before, jb_after, jb_away), join_gain, totals)
     jc_b = core_swap(heads_send(tok_jb, join_in))
     (jx_b,) = heads_across(tok_jb, join_in, jc_b)

time: 314 us -> 316 us (level)
    ppermute x42 -> x41, waiting for transfers between devices: 40.7 us -> 43.1 us  [flip(): return lax.ppermute(array, 'cols', [(i, i ^ mask) for i in range(size)])]
    ppermute x42 -> x41, starting transfers between devices: 22 us -> 21 us  [flip(): return lax.ppermute(array, 'cols', [(i, i ^ mask) for i in range(size)])]
  transfers between devices with their start and end apart: 72 -> 71, of which waited for: 37 -> 40; matrix products, arithmetic and copies ran while one was open for 1% -> 1% of each run, Pallas kernels for 39% -> 37%
where the time goes in v9:
time: 316 us; the launch traced here: 311 us
  Pallas kernels  136 us (43%)
  waiting for transfers between devices  99.5 us (31%)
  starting transfers between devices  67.4 us (21%)
  other arithmetic  5.4 us (2%)
    pallas_call x30, Pallas kernels, __call__(): pl.pallas_call(kernel, out_shape=out_shape, grid_spec=pltpu.PrefetchScala...  136 us
    ppermute x30, waiting for transfers between devices, row_shift(): lax.ppermute(array, 'rows', [(i, (i + shift) % size) for i in range(size)])  56.4 us
    ppermute x30, starting transfers between devices, row_shift(): lax.ppermute(array, 'rows', [(i, (i + shift) % size) for i in range(size)])  46.5 us
    ppermute x41, waiting for transfers between devices, flip(): return lax.ppermute(array, 'cols', [(i, i ^ mask) for i in range(size)])  43.1 us
    ppermute x41, starting transfers between devices, flip(): return lax.ppermute(array, 'cols', [(i, i ^ mask) for i in range(size)])  21 us
  transfers between devices with their start and end apart: 71, of which 40 were waited for; matrix products, arithmetic and copies ran while one was open for 1% of the time, Pallas kernels for 37%

profile of v9, /device:TPU:0, one launch (start us, length us, event | category | flops | bytes accessed | tf_op | source)
XLA Modules:
  0.0 310.5 jit_solution(3630206229575323546)
XLA Ops:
  25.5 5.5 %shard_map.181 = bf16[256,2304]{1,0:T(8,128)(2,1)S(1)} custom-call(s32[2]{0:T(128)S(1)} %pad_add_fusion.pos, bf16[256,1536]{1,0:T(8,128)(2,1)S(1)} %pad_maximum_fusion.tokens_ref, bf16[1536,1536]{1,0:T(8,128)(2,1)} %refs_0_.25, bf16[1536,1536]{1,0:T(8,128)(2,1)} %refs_1_.17, bf16[1536,1536]{1,0:T(8,128)(2,1)} %refs_2_.17), custom_call_target="tpu_custom_call" | custom-call | flops 1 | bytes 1 | tf_op jit(solution)/shard_map/pallas_call | solution.py:221
  35.0 4.0 %shard_map.182 = (bf16[128,1152]{1,0:T(8,128)(2,1)S(1)}, bf16[128,1152]{1,0:T(8,128)(2,1)S(1)}) custom-call(s32[2]{0:T(128)S(1)} %pad_add_fusion.pos, bf16[256,1536]{1,0:T(8,128)(2,1)S(1)} %pad_maximum_fusion.tokens_ref, bf16[1536,1536]{1,0:T(8,128)(2,1)} %refs_0_.25, bf16[1536,1536]{1,0:T(8,128)(2,1)} %refs_1_.17, bf16[1536,1536]{1,0:T(8,128)(2,1)} %refs_2_.17, ...), custom_call_target="tpu_custom_call" | custom-call | flops 1 | bytes 1 | tf_op jit(solution)/shard_map/pallas_call | solution.py:221
  41.3 5.8 %shard_map.183 = bf16[256,3072]{1,0:T(8,128)(2,1)S(1)} custom-call(s32[2]{0:T(128)S(1)} %pad_add_fusion.pos, bf16[256,1536]{1,0:T(8,128)(2,1)S(1)} %pad_maximum_fusion.tokens_ref, bf16[1536,6144]{1,0:T(8,128)(2,1)} %weight_ref.20), custom_call_target="tpu_custom_call" | custom-call | flops 1 | bytes 1 | tf_op jit(solution)/shard_map/pallas_call | solution.py:221
  51.8 3.9 %shard_map.184 = bf16[256,1536]{1,0:T(8,128)(2,1)S(1)} custom-call(s32[2]{0:T(128)S(1)} %pad_add_fusion.pos, bf16[256,1536]{1,0:T(8,128)(2,1)S(1)} %pad_maximum_fusion.tokens_ref, bf16[1536,6144]{1,0:T(8,128)(2,1)} %weight_ref.20, bf16[256,3072]{1,0:T(8,128)(2,1)S(1)} %collective-permute-done.13.refs_1_.arrived_ref), custom_call_target="tpu_custom_call" | custom-call | flops 1 | bytes 1 | tf_op jit(solution)/shard_map/pallas_call | solution.py:221
  55.7 3.9 %collective-permute-done.15 = bf16[64,1536]{1,0:T(8,128)(2,1)S(1)} collective-permute-done((bf16[64,1536]{1,0:T(8,128)(2,1)S(1)}, bf16[64,1536]{1,0:T(8,128)(2,1)S(1)}, u32[]{:S(2)}, u32[]{:S(2)}) %collective-permute-start.15) | collective-permute-done | bytes 196640 | tf_op jit(solution)/shard_map/ppermute | solution.py:213
  60.9 5.8 %shard_map.186 = bf16[256,3072]{1,0:T(8,128)(2,1)S(1)} custom-call(s32[2]{0:T(128)S(1)} %pad_add_fusion.pos, bf16[256,1536]{1,0:T(8,128)(2,1)S(1)} %pad_maximum_fusion.1.tokens_ref, bf16[1536,6144]{1,0:T(8,128)(2,1)} %weight_ref.20), custom_call_target="tpu_custom_call" | custom-call | flops 1 | bytes 1 | tf_op jit(solution)/shard_map/pallas_call | solution.py:221
  66.7 5.5 %shard_map.185 = bf16[256,2304]{1,0:T(8,128)(2,1)S(1)} custom-call(s32[2]{0:T(128)S(1)} %pad_add_fusion.pos, bf16[256,1536]{1,0:T(8,128)(2,1)S(1)} %pad_maximum_fusion.1.tokens_ref, bf16[1536,1536]{1,0:T(8,128)(2,1)} %refs_0_.25, bf16[1536,1536]{1,0:T(8,128)(2,1)} %refs_1_.17, bf16[1536,1536]{1,0:T(8,128)(2,1)} %refs_2_.17), custom_call_target="tpu_custom_call" | custom-call | flops 1 | bytes 1 | tf_op jit(solution)/shard_map/pallas_call | solution.py:221
  72.2 4.4 %shard_map.187.refs_0_ = bf16[256,384]{1,0:T(8,128)(2,1)S(1)} custom-call(s32[2]{0:T(128)S(1)} %pad_add_fusion.pos, bf16[256,1536]{1,0:T(8,128)(2,1)S(1)} %pad_maximum_fusion.tokens_ref, bf16[1536,1536]{1,0:T(8,128)(2,1)} %refs_0_.25, bf16[1536,1536]{1,0:T(8,128)(2,1)} %refs_1_.17, bf16[1536,1536]{1,0:T(8,128)(2,1)} %refs_2_.17, ...), custom_call_target="tpu_custom_call" | custom-call | flops 1 | bytes 1 | tf_op jit(solution)/shard_map/pallas_call | solution.py:221
  79.8 4.1 %shard_map.188.refs_0_ = bf16[256,1536]{1,0:T(8,128)(2,1)S(1)} custom-call(s32[2]{0:T(128)S(1)} %pad_add_fusion.pos, bf16[256,1536]{1,0:T(8,128)(2,1)S(1)} %pad_maximum_fusion.tokens_ref, bf16[1536,6144]{1,0:T(8,128)(2,1)} %weight_ref.20, f32[1,6144]{1,0:T(1,128)S(1)} %bitcast.147, bf16[256,3072]{1,0:T(8,128)(2,1)S(1)} %collective-permute-done.13.refs_1_.arrived_ref, ...), custom_call_target="tpu_custom_call" | custom-call | flops 1 | bytes 1 | tf_op jit(solution)/shard_map/pallas_call | solution.py:221
  87.2 3.9 %shard_map.192 = (bf16[128,1536]{1,0:T(8,128)(2,1)S(1)}, bf16[128,1536]{1,0:T(8,128)(2,1)S(1)}) custom-call(s32[2]{0:T(128)S(1)} %pad_add_fusion.pos, bf16[256,1536]{1,0:T(8,128)(2,1)S(1)} %pad_maximum_fusion.1.tokens_ref, bf16[1536,6144]{1,0:T(8,128)(2,1)} %weight_ref.20, bf16[256,3072]{1,0:T(8,128)(2,1)S(1)} %collective-permute-done.20.refs_1_.arrived_ref), custom_call_target="tpu_custom_call" | custom-call | flops 1 | bytes 1 | tf_op jit(solution)/shard_map/pallas_call | solution.py:221
  91.1 4.0 %shard_map.189 = bf16[256,1152]{1,0:T(8,128)(2,1)S(1)} custom-call(s32[2]{0:T(128)S(1)} %pad_add_fusion.pos, bf16[256,1536]{1,0:T(8,128)(2,1)S(1)} %pad_maximum_fusion.1.tokens_ref, bf16[1536,1536]{1,0:T(8,128)(2,1)} %refs_0_.25, bf16[1536,1536]{1,0:T(8,128)(2,1)} %refs_1_.17, bf16[1536,1536]{1,0:T(8,128)(2,1)} %refs_2_.17, ...), custom_call_target="tpu_custom_call" | custom-call | flops 1 | bytes 1 | tf_op jit(solution)/shard_map/pallas_call | solution.py:221
  95.1 4.3 %shard_map.190.refs_1_ = f32[256,1536]{1,0:T(8,128)S(1)} custom-call(s32[2]{0:T(128)S(1)} %pad_add_fusion.pos, bf16[1536,1536]{1,0:T(8,128)(2,1)} %weight_ref.21, bf16[256,384]{1,0:T(8,128)(2,1)S(1)} %shard_map.187.refs_0_, bf16[256,384]{1,0:T(8,128)(2,1)S(1)} %collective-permute-done.18.refs_1_, bf16[256,384]{1,0:T(8,128)(2,1)S(1)} %collective-permute-done.17.refs_2_), custom_call_target="tpu_custom_call" | custom-call | flops 1 | bytes 1 | tf_op jit(solution)/shard_map/pallas_call | solution.py:221
  99.4 4.2 %shard_map.191.refs_1_ = f32[256,1536]{1,0:T(8,128)S(1)} custom-call(s32[2]{0:T(128)S(1)} %pad_add_fusion.pos, bf16[6144,1536]{1,0:T(8,128)(2,1)} %weight_ref.24, bf16[256,1536]{1,0:T(8,128)(2,1)S(1)} %shard_map.188.refs_0_, f32[256,1536]{1,0:T(8,128)S(1)} %shard_map.190.refs_1_), custom_call_target="tpu_custom_call" | custom-call | flops 1 | bytes 1 | tf_op jit(solution)/shard_map/pallas_call | solution.py:221
  108.0 8.3 %shard_map.194 = f32[256,1536]{1,0:T(8,128)S(1)} custom-call(s32[2]{0:T(128)S(1)} %pad_add_fusion.pos, bf16[6144,1536]{1,0:T(8,128)(2,1)} %weight_ref.24, bf16[256,1536]{1,0:T(8,128)(2,1)S(1)} %collective-permute-done.23.refs_0_, bf16[256,1536]{1,0:T(8,128)(2,1)S(1)} %collective-permute-done.22.refs_1_, ...), custom_call_target="tpu_custom_call" | custom-call | flops 1 | bytes 1 | tf_op jit(solution)/shard_map/pallas_call | solution.py:221
  116.3 4.3 %collective-permute-done.25.refs_6_ = bf16[256,1152]{1,0:T(8,128)(2,1)S(1)} collective-permute-done((bf16[256,1152]{1,0:T(8,128)(2,1)S(1)}, bf16[256,1152]{1,0:T(8,128)(2,1)S(1)}, u32[]{:S(2)}, u32[]{:S(2)}) %collective-permute-start.25) | collective-permute-done | bytes 589856 | tf_op jit(solution)/shard_map/ppermute | solution.py:200
  121.5 4.4 %shard_map.195.refs_0_ = bf16[256,384]{1,0:T(8,128)(2,1)S(1)} custom-call(s32[2]{0:T(128)S(1)} %pad_add_fusion.pos, bf16[256,1536]{1,0:T(8,128)(2,1)S(1)} %pad_maximum_fusion.1.tokens_ref, bf16[1536,1536]{1,0:T(8,128)(2,1)} %refs_0_.25, bf16[1536,1536]{1,0:T(8,128)(2,1)} %refs_1_.17, bf16[1536,1536]{1,0:T(8,128)(2,1)} %refs_2_.17, ...), custom_call_target="tpu_custom_call" | custom-call | flops 1 | bytes 1 | tf_op jit(solution)/shard_map/pallas_call | solution.py:221
  163.1 4.2 %shard_map.200.refs_2_ = f32[256,1536]{1,0:T(8,128)S(1)} custom-call(s32[2]{0:T(128)S(1)} %pad_add_fusion.pos, bf16[6144,1536]{1,0:T(8,128)(2,1)} %weight_ref.24, bf16[128,1536]{1,0:T(8,128)(2,1)S(1)} %shard_map.196.refs_0_, bf16[128,1536]{1,0:T(8,128)(2,1)S(1)} %shard_map.198.refs_1_, f32[256,1536]{1,0:T(8,128)S(1)} %shard_map.199.refs_2_), custom_call_target="tpu_custom_call" | custom-call | flops 1 | bytes 1 | tf_op jit(solution)/shard_map/pallas_call | solution.py:221
  173.2 4.2 %shard_map.201.refs_4_ = f32[256,1536]{1,0:T(8,128)S(1)} custom-call(s32[2]{0:T(128)S(1)} %pad_add_fusion.pos, bf16[6144,1536]{1,0:T(8,128)(2,1)} %weight_ref.24, bf16[128,1536]{1,0:T(8,128)(2,1)S(1)} %collective-permute-done.38.refs_0_, bf16[128,1536]{1,0:T(8,128)(2,1)S(1)} %collective-permute-done.39.refs_1_, f32[256,1536]{1,0:T(8,128)S(1)} %shard_map.200.refs_2_), custom_call_target="tpu_custom_call" | custom-call | flops 1 | bytes 1 | tf_op jit(solution)/shard_map/pallas_call | solution.py:221
  178.1 6.2 %shard_map.202 = f32[256,1536]{1,0:T(8,128)S(1)} custom-call(s32[2]{0:T(128)S(1)} %pad_add_fusion.pos, bf16[6144,1536]{1,0:T(8,128)(2,1)} %weight_ref.24, bf16[128,1536]{1,0:T(8,128)(2,1)S(1)} %collective-permute-done.33.refs_0_, bf16[128,1536]{1,0:T(8,128)(2,1)S(1)} %collective-permute-done.40.refs_1_, ...), custom_call_target="tpu_custom_call" | custom-call | flops 1 | bytes 1 | tf_op jit(solution)/shard_map/pallas_call | solution.py:221
  186.5 5.5 %shard_map.203 = bf16[256,2304]{1,0:T(8,128)(2,1)S(1)} custom-call(s32[2]{0:T(128)S(1)} %pad_add_fusion.pos, bf16[256,1536]{1,0:T(8,128)(2,1)S(1)} %constant_dynamic-update-slice_fusion.tokens_ref, bf16[1536,1536]{1,0:T(8,128)(2,1)} %refs_0_.31, bf16[1536,1536]{1,0:T(8,128)(2,1)} %refs_1_.23, bf16[1536,1536]{1,0:T(8,128)(2,1)} %refs_2_.23), custom_call_target="tpu_custom_call" | custom-call | flops 1 | bytes 1 | tf_op jit(solution)/shard_map/pallas_call | solution.py:221
  194.4 3.8 %collective-permute-start.49 = (bf16[64,1536]{1,0:T(8,128)(2,1)S(1)}, bf16[64,1536]{1,0:T(8,128)(2,1)S(1)}, u32[]{:S(2)}, u32[]{:S(2)}) collective-permute-start(bf16[64,1536]{1,0:T(8,128)(2,1)S(1)} %get-tuple-element.318), channel_id=1, source_target_pairs={{0,3},{1,0},{2,1},{3,2},{4,7},{5,4},{6,5},{7,6},{8,11},{9,8},{10,9... | collective-permute-start | bytes 589832 | tf_op jit(solution)/shard_map/ppermute | solution.py:213
  198.2 4.0 %shard_map.204 = (bf16[128,1152]{1,0:T(8,128)(2,1)S(1)}, bf16[128,1152]{1,0:T(8,128)(2,1)S(1)}) custom-call(s32[2]{0:T(128)S(1)} %pad_add_fusion.pos, bf16[256,1536]{1,0:T(8,128)(2,1)S(1)} %constant_dynamic-update-slice_fusion.tokens_ref, bf16[1536,1536]{1,0:T(8,128)(2,1)} %refs_0_.31, bf16[1536,1536]{1,0:T(8,128)(2,1)} %refs_1_.23, ...), custom_call_target="tpu_custom_call" | custom-call | flops 1 | bytes 1 | tf_op jit(solution)/shard_map/pallas_call | solution.py:221
  231.0 5.7 %shard_map.205 = bf16[256,2304]{1,0:T(8,128)(2,1)S(1)} custom-call(s32[2]{0:T(128)S(1)} %pad_add_fusion.pos, bf16[256,1536]{1,0:T(8,128)(2,1)S(1)} %pad_maximum_fusion.2.tokens_ref, bf16[1536,1536]{1,0:T(8,128)(2,1)} %refs_0_.31, bf16[1536,1536]{1,0:T(8,128)(2,1)} %refs_1_.23, bf16[1536,1536]{1,0:T(8,128)(2,1)} %refs_2_.23), custom_call_target="tpu_custom_call" | custom-call | flops 1 | bytes 1 | tf_op jit(solution)/shard_map/pallas_call | solution.py:221
  239.6 4.0 %shard_map.206 = bf16[256,1152]{1,0:T(8,128)(2,1)S(1)} custom-call(s32[2]{0:T(128)S(1)} %pad_add_fusion.pos, bf16[256,1536]{1,0:T(8,128)(2,1)S(1)} %pad_maximum_fusion.2.tokens_ref, bf16[1536,1536]{1,0:T(8,128)(2,1)} %refs_0_.31, bf16[1536,1536]{1,0:T(8,128)(2,1)} %refs_1_.23, bf16[1536,1536]{1,0:T(8,128)(2,1)} %refs_2_.23, ...), custom_call_target="tpu_custom_call" | custom-call | flops 1 | bytes 1 | tf_op jit(solution)/shard_map/pallas_call | solution.py:221
  244.6 4.0 %shard_map.208.refs_3_.refs_4_.refs_5_ = f32[256,1152]{1,0:T(8,128)S(1)} custom-call(s32[2]{0:T(128)S(1)} %pad_add_fusion.pos, bf16[256,1536]{1,0:T(8,128)(2,1)S(1)} %pad_maximum_fusion.2.tokens_ref, bf16[1536,1536]{1,0:T(8,128)(2,1)} %refs_0_.31, bf16[1536,1536]{1,0:T(8,128)(2,1)} %refs_1_.23, bf16[1536,1536]{1,0:T(8,128)(2,1)} %refs_2_.23, ...), custom_call_target="tpu_custom_call" | custom-call | flops 1 | bytes 1 | tf_op jit(solution)/shard_map/pallas_call | solution.py:221
  248.6 4.0 %shard_map.207.refs_0_.refs_1_.refs_2_ = bf16[256,1152]{1,0:T(8,128)(2,1)S(1)} custom-call(s32[2]{0:T(128)S(1)} %pad_add_fusion.pos, bf16[256,1536]{1,0:T(8,128)(2,1)S(1)} %constant_dynamic-update-slice_fusion.tokens_ref, bf16[1536,1536]{1,0:T(8,128)(2,1)} %refs_0_.31, bf16[1536,1536]{1,0:T(8,128)(2,1)} %refs_1_.23, bf16[1536,1536]{1,0:T(8,128)(2,1)} %refs_2_.23, ...), custom_call_target="tpu_custom_call" | custom-call | flops 1 | bytes 1 | tf_op jit(solution)/shard_map/pallas_call | solution.py:221
  252.7 6.4 %collective-permute-done.61.refs_6_.refs_7_.refs_8_ = bf16[256,1152]{1,0:T(8,128)(2,1)S(1)} collective-permute-done((bf16[256,1152]{1,0:T(8,128)(2,1)S(1)}, bf16[256,1152]{1,0:T(8,128)(2,1)S(1)}, u32[]{:S(2)}, u32[]{:S(2)}) %collective-permute-start.61) | collective-permute-done | bytes 589856 | tf_op jit(solution)/shard_map/ppermute | solution.py:200
  263.7 9.4 %collective-permute-done.63.refs_2_ = bf16[512,384]{1,0:T(8,128)(2,1)S(1)} collective-permute-done((bf16[512,384]{1,0:T(8,128)(2,1)S(1)}, bf16[512,384]{1,0:T(8,128)(2,1)S(1)}, u32[]{:S(2)}, u32[]{:S(2)}) %collective-permute-start.63) | collective-permute-done | bytes 393248 | tf_op jit(solution)/shard_map/ppermute | solution.py:200
  274.9 6.2 %shard_map.210 = f32[512,1536]{1,0:T(8,128)S(1)} custom-call(s32[2]{0:T(128)S(1)} %pad_add_fusion.pos, bf16[1536,1536]{1,0:T(8,128)(2,1)} %weight_ref.25, bf16[512,384]{1,0:T(8,128)(2,1)S(1)} %bitcast.145, bf16[512,384]{1,0:T(8,128)(2,1)S(1)} %collective-permute-done.62.refs_1_, bf16[512,384]{1,0:T(8,128)(2,1)S(1)} %collective-permute-done.63.refs_2_, ...), custom_call_target="tpu_custom_call" | custom-call | flops 1 | bytes 1 | tf_op jit(solution)/shard_map/pallas_call | solution.py:221
  281.4 3.8 %collective-permute-start.69 = (bf16[64,1536]{1,0:T(8,128)(2,1)S(1)}, bf16[64,1536]{1,0:T(8,128)(2,1)S(1)}, u32[]{:S(2)}, u32[]{:S(2)}) collective-permute-start(bf16[64,1536]{1,0:T(8,128)(2,1)S(1)} %get-tuple-element.368), channel_id=1, source_target_pairs={{0,3},{1,0},{2,1},{3,2},{4,7},{5,4},{6,5},{7,6},{8,11},{9,8},{10,9... | collective-permute-start | bytes 589832 | tf_op jit(solution)/shard_map/ppermute | solution.py:213
  285.2 3.8 %collective-permute-start.68 = (bf16[64,1536]{1,0:T(8,128)(2,1)S(1)}, bf16[64,1536]{1,0:T(8,128)(2,1)S(1)}, u32[]{:S(2)}, u32[]{:S(2)}) collective-permute-start(bf16[64,1536]{1,0:T(8,128)(2,1)S(1)} %get-tuple-element.367), channel_id=1, source_target_pairs={{0,3},{1,0},{2,1},{3,2},{4,7},{5,4},{6,5},{7,6},{8,11},{9,8},{10,9... | collective-permute-start | bytes 589832 | tf_op jit(solution)/shard_map/ppermute | solution.py:213
  301.8 6.1 %collective-permute-done.66 = bf16[64,1536]{1,0:T(8,128)(2,1)S(1)} collective-permute-done((bf16[64,1536]{1,0:T(8,128)(2,1)S(1)}, bf16[64,1536]{1,0:T(8,128)(2,1)S(1)}, u32[]{:S(2)}, u32[]{:S(2)}) %collective-permute-start.66) | collective-permute-done | bytes 196640 | tf_op jit(solution)/shard_map/ppermute | solution.py:213
  (211 shorter events, 151.8 us)
Async XLA Ops:
  1.1 11.2 %collective-permute-start = (bf16[64,1536]{1,0:T(8,128)(2,1)S(1)}, bf16[64,1536]{1,0:T(8,128)(2,1)S(1)}, u32[]{:S(2)}, u32[]{:S(2)}) collective-permute-start(bf16[64,1536]{1,0:T(8,128)(2,1)S(1)} %get-tuple-element.189), channel_id=1, source_target_pairs={{0,1},{1,2},{2,3},{3,0},{4,5},{5,6},{6,7},{7,4},{8,9},{9,10},{10,1... | collective-permute-start | bytes 589832 | tf_op jit(solution)/shard_map/ppermute | solution.py:213
  4.1 10.6 %collective-permute-start.1 = (bf16[64,1536]{1,0:T(8,128)(2,1)S(1)}, bf16[64,1536]{1,0:T(8,128)(2,1)S(1)}, u32[]{:S(2)}, u32[]{:S(2)}) collective-permute-start(bf16[64,1536]{1,0:T(8,128)(2,1)S(1)} %get-tuple-element.189), channel_id=1, source_target_pairs={{0,3},{1,0},{2,1},{3,2},{4,7},{5,4},{6,5},{7,6},{8,11},{9,8},{10,9... | collective-permute-start | bytes 589832 | tf_op jit(solution)/shard_map/ppermute | solution.py:213
  48.4 11.2 %collective-permute-start.14 = (bf16[128,1152]{1,0:T(8,128)(2,1)S(1)}, bf16[128,1152]{1,0:T(8,128)(2,1)S(1)}, u32[]{:S(2)}, u32[]{:S(2)}) collective-permute-start(bf16[128,1152]{1,0:T(8,128)(2,1)S(1)} %get-tuple-element.215), channel_id=1, source_target_pairs={{0,8},{4,12},{8,0},{12,4},{1,9},{5,13},{9,1},{13,5},{2,10},{6,14},... | collective-permute-start | bytes 884744 | tf_op jit(solution)/shard_map/ppermute | solution.py:200
  49.9 9.7 %collective-permute-start.15 = (bf16[64,1536]{1,0:T(8,128)(2,1)S(1)}, bf16[64,1536]{1,0:T(8,128)(2,1)S(1)}, u32[]{:S(2)}, u32[]{:S(2)}) collective-permute-start(bf16[64,1536]{1,0:T(8,128)(2,1)S(1)} %collective-permute-done.9), channel_id=1, source_target_pairs={{0,1},{1,2},{2,3},{3,0},{4,5},{5,6},{6,7},{7,4},{8,9},{9,10},{10,1... | collective-permute-start | bytes 589832 | tf_op jit(solution)/shard_map/ppermute | solution.py:213
  59.6 19.2 %collective-permute-start.16 = (bf16[256,1536]{1,0:T(8,128)(2,1)S(1)}, bf16[256,1536]{1,0:T(8,128)(2,1)S(1)}, u32[]{:S(2)}, u32[]{:S(2)}) collective-permute-start(bf16[256,1536]{1,0:T(8,128)(2,1)S(1)} %shard_map.184), channel_id=1, source_target_pairs={{0,8},{4,12},{8,0},{12,4},{1,9},{5,13},{9,1},{13,5},{2,10},{6,14},... | collective-permute-start | bytes 2359304 | tf_op jit(solution)/shard_map/ppermute | solution.py:200
  86.1 18.7 %collective-permute-start.22 = (bf16[256,1536]{1,0:T(8,128)(2,1)S(1)}, bf16[256,1536]{1,0:T(8,128)(2,1)S(1)}, u32[]{:S(2)}, u32[]{:S(2)}) collective-permute-start(bf16[256,1536]{1,0:T(8,128)(2,1)S(1)} %shard_map.188.refs_0_), channel_id=1, source_target_pairs={{0,8},{4,12},{8,0},{12,4},{1,9},{5,13},{9,1},{13,5},{2,10},{6,14},... | collective-permute-start | bytes 2359304 | tf_op jit(solution)/shard_map/ppermute | solution.py:200
  86.7 18.1 %collective-permute-start.23 = (bf16[256,1536]{1,0:T(8,128)(2,1)S(1)}, bf16[256,1536]{1,0:T(8,128)(2,1)S(1)}, u32[]{:S(2)}, u32[]{:S(2)}) collective-permute-start(bf16[256,1536]{1,0:T(8,128)(2,1)S(1)} %shard_map.188.refs_0_), channel_id=1, source_target_pairs={{0,4},{4,0},{8,12},{12,8},{1,5},{5,1},{9,13},{13,9},{2,6},{6,2},{1... | collective-permute-start | bytes 2359304 | tf_op jit(solution)/shard_map/ppermute | solution.py:200
  86.7 16.9 %collective-permute-start.21 = (bf16[256,384]{1,0:T(8,128)(2,1)S(1)}, bf16[256,384]{1,0:T(8,128)(2,1)S(1)}, u32[]{:S(2)}, u32[]{:S(2)}) collective-permute-start(bf16[256,384]{1,0:T(8,128)(2,1)S(1)} %collective-permute-done.17.refs_2_), channel_id=1, source_target_pairs={{0,4},{4,0},{8,12},{12,8},{1,5},{5,1},{9,13},{13,9},{2,6},{6,2},{1... | collective-permute-start | bytes 589832 | tf_op jit(solution)/shard_map/ppermute | solution.py:200
  104.8 15.7 %collective-permute-start.25 = (bf16[256,1152]{1,0:T(8,128)(2,1)S(1)}, bf16[256,1152]{1,0:T(8,128)(2,1)S(1)}, u32[]{:S(2)}, u32[]{:S(2)}) collective-permute-start(bf16[256,1152]{1,0:T(8,128)(2,1)S(1)} %shard_map.189), channel_id=1, source_target_pairs={{0,8},{4,12},{8,0},{12,4},{1,9},{5,13},{9,1},{13,5},{2,10},{6,14},... | collective-permute-start | bytes 1769480 | tf_op jit(solution)/shard_map/ppermute | solution.py:200
  120.7 10.8 %collective-permute-start.26 = (bf16[128,1536]{1,0:T(8,128)(2,1)S(1)}, bf16[128,1536]{1,0:T(8,128)(2,1)S(1)}, u32[]{:S(2)}, u32[]{:S(2)}) collective-permute-start(bf16[128,1536]{1,0:T(8,128)(2,1)S(1)} %get-tuple-element.257), channel_id=1, source_target_pairs={{0,8},{4,12},{8,0},{12,4},{1,9},{5,13},{9,1},{13,5},{2,10},{6,14},... | collective-permute-start | bytes 1179656 | tf_op jit(solution)/shard_map/ppermute | solution.py:200
  131.5 12.6 %collective-permute-start.29 = (bf16[256,384]{1,0:T(8,128)(2,1)S(1)}, bf16[256,384]{1,0:T(8,128)(2,1)S(1)}, u32[]{:S(2)}, u32[]{:S(2)}) collective-permute-start(bf16[256,384]{1,0:T(8,128)(2,1)S(1)} %shard_map.195.refs_0_), channel_id=1, source_target_pairs={{0,8},{4,12},{8,0},{12,4},{1,9},{5,13},{9,1},{13,5},{2,10},{6,14},... | collective-permute-start | bytes 589832 | tf_op jit(solution)/shard_map/ppermute | solution.py:200
  132.2 15.0 %collective-permute-start.28 = (bf16[128,1536]{1,0:T(8,128)(2,1)S(1)}, bf16[128,1536]{1,0:T(8,128)(2,1)S(1)}, u32[]{:S(2)}, u32[]{:S(2)}) collective-permute-start(bf16[128,1536]{1,0:T(8,128)(2,1)S(1)} %get-tuple-element.264), channel_id=1, source_target_pairs={{0,8},{4,12},{8,0},{12,4},{1,9},{5,13},{9,1},{13,5},{2,10},{6,14},... | collective-permute-start | bytes 1179656 | tf_op jit(solution)/shard_map/ppermute | solution.py:200
  133.5 10.5 %collective-permute-start.31 = (bf16[64,1536]{1,0:T(8,128)(2,1)S(1)}, bf16[64,1536]{1,0:T(8,128)(2,1)S(1)}, u32[]{:S(2)}, u32[]{:S(2)}) collective-permute-start(bf16[64,1536]{1,0:T(8,128)(2,1)S(1)} %add_convert_fusion.1), channel_id=1, source_target_pairs={{0,1},{1,2},{2,3},{3,0},{4,5},{5,6},{6,7},{7,4},{8,9},{9,10},{10,1... | collective-permute-start | bytes 589832 | tf_op jit(solution)/shard_map/ppermute | solution.py:213
  133.7 12.3 %collective-permute-start.32 = (bf16[64,1536]{1,0:T(8,128)(2,1)S(1)}, bf16[64,1536]{1,0:T(8,128)(2,1)S(1)}, u32[]{:S(2)}, u32[]{:S(2)}) collective-permute-start(bf16[64,1536]{1,0:T(8,128)(2,1)S(1)} %get-tuple-element.270), channel_id=1, source_target_pairs={{0,3},{1,0},{2,1},{3,2},{4,7},{5,4},{6,5},{7,6},{8,11},{9,8},{10,9... | collective-permute-start | bytes 589832 | tf_op jit(solution)/shard_map/ppermute | solution.py:213
  147.2 10.8 %collective-permute-start.33 = (bf16[128,1536]{1,0:T(8,128)(2,1)S(1)}, bf16[128,1536]{1,0:T(8,128)(2,1)S(1)}, u32[]{:S(2)}, u32[]{:S(2)}) collective-permute-start(bf16[128,1536]{1,0:T(8,128)(2,1)S(1)} %shard_map.196.refs_0_), channel_id=1, source_target_pairs={{0,8},{4,12},{8,0},{12,4},{1,9},{5,13},{9,1},{13,5},{2,10},{6,14},... | collective-permute-start | bytes 1179656 | tf_op jit(solution)/shard_map/ppermute | solution.py:200
  158.1 14.6 %collective-permute-start.39 = (bf16[128,1536]{1,0:T(8,128)(2,1)S(1)}, bf16[128,1536]{1,0:T(8,128)(2,1)S(1)}, u32[]{:S(2)}, u32[]{:S(2)}) collective-permute-start(bf16[128,1536]{1,0:T(8,128)(2,1)S(1)} %shard_map.198.refs_1_), channel_id=1, source_target_pairs={{0,4},{4,0},{8,12},{12,8},{1,5},{5,1},{9,13},{13,9},{2,6},{6,2},{1... | collective-permute-start | bytes 1179656 | tf_op jit(solution)/shard_map/ppermute | solution.py:200
  158.2 14.5 %collective-permute-start.40 = (bf16[128,1536]{1,0:T(8,128)(2,1)S(1)}, bf16[128,1536]{1,0:T(8,128)(2,1)S(1)}, u32[]{:S(2)}, u32[]{:S(2)}) collective-permute-start(bf16[128,1536]{1,0:T(8,128)(2,1)S(1)} %shard_map.198.refs_1_), channel_id=1, source_target_pairs={{0,8},{4,12},{8,0},{12,4},{1,9},{5,13},{9,1},{13,5},{2,10},{6,14},... | collective-permute-start | bytes 1179656 | tf_op jit(solution)/shard_map/ppermute | solution.py:200
  159.1 13.5 %collective-permute-start.38 = (bf16[128,1536]{1,0:T(8,128)(2,1)S(1)}, bf16[128,1536]{1,0:T(8,128)(2,1)S(1)}, u32[]{:S(2)}, u32[]{:S(2)}) collective-permute-start(bf16[128,1536]{1,0:T(8,128)(2,1)S(1)} %shard_map.196.refs_0_), channel_id=1, source_target_pairs={{0,4},{4,0},{8,12},{12,8},{1,5},{5,1},{9,13},{13,9},{2,6},{6,2},{1... | collective-permute-start | bytes 1179656 | tf_op jit(solution)/shard_map/ppermute | solution.py:200
  160.0 12.7 %collective-permute-start.42 = (bf16[64,1536]{1,0:T(8,128)(2,1)S(1)}, bf16[64,1536]{1,0:T(8,128)(2,1)S(1)}, u32[]{:S(2)}, u32[]{:S(2)}) collective-permute-start(bf16[64,1536]{1,0:T(8,128)(2,1)S(1)} %multiply_convert_fusion.4), channel_id=1, source_target_pairs={{0,3},{1,0},{2,1},{3,2},{4,7},{5,4},{6,5},{7,6},{8,11},{9,8},{10,9... | collective-permute-start | bytes 589832 | tf_op jit(solution)/shard_map/ppermute | solution.py:213
  194.4 11.6 %collective-permute-start.49 = (bf16[64,1536]{1,0:T(8,128)(2,1)S(1)}, bf16[64,1536]{1,0:T(8,128)(2,1)S(1)}, u32[]{:S(2)}, u32[]{:S(2)}) collective-permute-start(bf16[64,1536]{1,0:T(8,128)(2,1)S(1)} %get-tuple-element.318), channel_id=1, source_target_pairs={{0,3},{1,0},{2,1},{3,2},{4,7},{5,4},{6,5},{7,6},{8,11},{9,8},{10,9... | collective-permute-start | bytes 589832 | tf_op jit(solution)/shard_map/ppermute | solution.py:213
  206.0 13.6 %collective-permute-start.50 = (bf16[128,1152]{1,0:T(8,128)(2,1)S(1)}, bf16[128,1152]{1,0:T(8,128)(2,1)S(1)}, u32[]{:S(2)}, u32[]{:S(2)}) collective-permute-start(bf16[128,1152]{1,0:T(8,128)(2,1)S(1)} %get-tuple-element.321), channel_id=1, source_target_pairs={{0,8},{4,12},{8,0},{12,4},{1,9},{5,13},{9,1},{13,5},{2,10},{6,14},... | collective-permute-start | bytes 884744 | tf_op jit(solution)/shard_map/ppermute | solution.py:200
  208.0 11.6 %collective-permute-start.52 = (bf16[64,1536]{1,0:T(8,128)(2,1)S(1)}, bf16[64,1536]{1,0:T(8,128)(2,1)S(1)}, u32[]{:S(2)}, u32[]{:S(2)}) collective-permute-start(bf16[64,1536]{1,0:T(8,128)(2,1)S(1)} %get-tuple-element.335), channel_id=1, source_target_pairs={{0,3},{1,0},{2,1},{3,2},{4,7},{5,4},{6,5},{7,6},{8,11},{9,8},{10,9... | collective-permute-start | bytes 589832 | tf_op jit(solution)/shard_map/ppermute | solution.py:213
  219.6 10.9 %collective-permute-start.55 = (bf16[128,1152]{1,0:T(8,128)(2,1)S(1)}, bf16[128,1152]{1,0:T(8,128)(2,1)S(1)}, u32[]{:S(2)}, u32[]{:S(2)}) collective-permute-start(bf16[128,1152]{1,0:T(8,128)(2,1)S(1)} %get-tuple-element.329), channel_id=1, source_target_pairs={{0,8},{4,12},{8,0},{12,4},{1,9},{5,13},{9,1},{13,5},{2,10},{6,14},... | collective-permute-start | bytes 884744 | tf_op jit(solution)/shard_map/ppermute | solution.py:200
  220.7 9.8 %collective-permute-start.56 = (bf16[64,1536]{1,0:T(8,128)(2,1)S(1)}, bf16[64,1536]{1,0:T(8,128)(2,1)S(1)}, u32[]{:S(2)}, u32[]{:S(2)}) collective-permute-start(bf16[64,1536]{1,0:T(8,128)(2,1)S(1)} %collective-permute-done.51), channel_id=1, source_target_pairs={{0,1},{1,2},{2,3},{3,0},{4,5},{5,6},{6,7},{7,4},{8,9},{9,10},{10,1... | collective-permute-start | bytes 589832 | tf_op jit(solution)/shard_map/ppermute | solution.py:213
  243.6 15.4 %collective-permute-start.61 = (bf16[256,1152]{1,0:T(8,128)(2,1)S(1)}, bf16[256,1152]{1,0:T(8,128)(2,1)S(1)}, u32[]{:S(2)}, u32[]{:S(2)}) collective-permute-start(bf16[256,1152]{1,0:T(8,128)(2,1)S(1)} %shard_map.206), channel_id=1, source_target_pairs={{0,8},{4,12},{8,0},{12,4},{1,9},{5,13},{9,1},{13,5},{2,10},{6,14},... | collective-permute-start | bytes 1769480 | tf_op jit(solution)/shard_map/ppermute | solution.py:200
  262.7 10.4 %collective-permute-start.63 = (bf16[512,384]{1,0:T(8,128)(2,1)S(1)}, bf16[512,384]{1,0:T(8,128)(2,1)S(1)}, u32[]{:S(2)}, u32[]{:S(2)}) collective-permute-start(bf16[512,384]{1,0:T(8,128)(2,1)S(1)} %bitcast.143), channel_id=1, source_target_pairs={{0,8},{4,12},{8,0},{12,4},{1,9},{5,13},{9,1},{13,5},{2,10},{6,14},... | collective-permute-start | bytes 1179656 | tf_op jit(solution)/shard_map/ppermute | solution.py:200
  281.3 9.6 %collective-permute-start.65 = (bf16[64,1536]{1,0:T(8,128)(2,1)S(1)}, bf16[64,1536]{1,0:T(8,128)(2,1)S(1)}, u32[]{:S(2)}, u32[]{:S(2)}) collective-permute-start(bf16[64,1536]{1,0:T(8,128)(2,1)S(1)} %get-tuple-element.370), channel_id=1, source_target_pairs={{0,1},{1,2},{2,3},{3,0},{4,5},{5,6},{6,7},{7,4},{8,9},{9,10},{10,1... | collective-permute-start | bytes 589832 | tf_op jit(solution)/shard_map/ppermute | solution.py:213
  281.4 12.0 %collective-permute-start.69 = (bf16[64,1536]{1,0:T(8,128)(2,1)S(1)}, bf16[64,1536]{1,0:T(8,128)(2,1)S(1)}, u32[]{:S(2)}, u32[]{:S(2)}) collective-permute-start(bf16[64,1536]{1,0:T(8,128)(2,1)S(1)} %get-tuple-element.368), channel_id=1, source_target_pairs={{0,3},{1,0},{2,1},{3,2},{4,7},{5,4},{6,5},{7,6},{8,11},{9,8},{10,9... | collective-permute-start | bytes 589832 | tf_op jit(solution)/shard_map/ppermute | solution.py:213
  285.2 14.2 %collective-permute-start.67 = (bf16[64,1536]{1,0:T(8,128)(2,1)S(1)}, bf16[64,1536]{1,0:T(8,128)(2,1)S(1)}, u32[]{:S(2)}, u32[]{:S(2)}) collective-permute-start(bf16[64,1536]{1,0:T(8,128)(2,1)S(1)} %get-tuple-element.369), channel_id=1, source_target_pairs={{0,1},{1,2},{2,3},{3,0},{4,5},{5,6},{6,7},{7,4},{8,9},{9,10},{10,1... | collective-permute-start | bytes 589832 | tf_op jit(solution)/shard_map/ppermute | solution.py:213
  285.2 16.6 %collective-permute-start.68 = (bf16[64,1536]{1,0:T(8,128)(2,1)S(1)}, bf16[64,1536]{1,0:T(8,128)(2,1)S(1)}, u32[]{:S(2)}, u32[]{:S(2)}) collective-permute-start(bf16[64,1536]{1,0:T(8,128)(2,1)S(1)} %get-tuple-element.367), channel_id=1, source_target_pairs={{0,3},{1,0},{2,1},{3,2},{4,7},{5,4},{6,5},{7,6},{8,11},{9,8},{10,9... | collective-permute-start | bytes 589832 | tf_op jit(solution)/shard_map/ppermute | solution.py:213
  293.5 14.4 %collective-permute-start.66 = (bf16[64,1536]{1,0:T(8,128)(2,1)S(1)}, bf16[64,1536]{1,0:T(8,128)(2,1)S(1)}, u32[]{:S(2)}, u32[]{:S(2)}) collective-permute-start(bf16[64,1536]{1,0:T(8,128)(2,1)S(1)} %get-tuple-element.366), channel_id=1, source_target_pairs={{0,1},{1,2},{2,3},{3,0},{4,5},{5,6},{6,7},{7,4},{8,9},{9,10},{10,1... | collective-permute-start | bytes 589832 | tf_op jit(solution)/shard_map/ppermute | solution.py:213
  294.1 15.4 %collective-permute-start.70 = (bf16[64,1536]{1,0:T(8,128)(2,1)S(1)}, bf16[64,1536]{1,0:T(8,128)(2,1)S(1)}, u32[]{:S(2)}, u32[]{:S(2)}) collective-permute-start(bf16[64,1536]{1,0:T(8,128)(2,1)S(1)} %get-tuple-element.365), channel_id=1, source_target_pairs={{0,3},{1,0},{2,1},{3,2},{4,7},{5,4},{6,5},{7,6},{8,11},{9,8},{10,9... | collective-permute-start | bytes 589832 | tf_op jit(solution)/shard_map/ppermute | solution.py:213
  (48 other events, 313.5 us)
